TPU v7x, 32 devices: a whole 2x2x4 slice. The times are simulated.
32 devices in a mesh: parts: 1, grid: 32 (over z, y, x, core).
Axes of the slice: x: 2, y: 2, z: 4, core: 2. Of those that a mesh axis runs over, the one named last changes fastest.
Arguments:
- tokens: bfloat16 [128, 32, 1024], P(('parts', 'grid')), may hold values from -6 to 6
- cotangent: bfloat16 [128, 32, 1024], P(('parts', 'grid')), may hold values from -6 to 6
- w_sqkv: bfloat16 [1024, 3072], P('grid'), may hold values from -0.1875 to 0.1875
- w_so: bfloat16 [1024, 1024], P('grid'), may hold values from -0.1875 to 0.1875
- w_gqkv: bfloat16 [1024, 3072], P('grid'), may hold values from -0.1875 to 0.1875
- w_go: bfloat16 [1024, 1024], P('grid'), may hold values from -0.1875 to 0.1875
- keep: int32 [32, 128], P(None, 'parts'), may hold values from 0 to 1, as said below
Outputs:
- mixed: bfloat16 [128, 32, 1024], P(('parts', 'grid'))
- token_grad: bfloat16 [128, 32, 1024], P(('parts', 'grid'))
Inputs may be any that keep to these rules, and one draw needn't show every extreme that they name: `keep`: every band group keeps at least one patch; the kept share differs from group to group.
All inputs are finite; a program needn't handle non-finite values.
Results may differ from a plain program's by a relative error of at most 0.017.
Values may be sent and summed in bfloat16 or wider, within the bound.
No kernel may reach another device: no remote copies, remote signals or barrier semaphores. Data moves between devices by JAX's collectives and lax.ppermute only.
A program may use at most 192 MiB of HBM per device.

v0:
```python
from functools import partial

import jax
import jax.numpy as jnp
from jax import lax
from jax.sharding import PartitionSpec as P

H = 16
G = 32


def rms_normalize(values):
    wide = values.astype(jnp.float32)
    meansq = jnp.mean(wide * wide, axis=-1, keepdims=True)
    return (wide * lax.rsqrt(meansq + 1e-06)).astype(jnp.bfloat16)


def project_spatial(tokens, weight):
    patches, groups, width = tokens.shape
    normed = rms_normalize(tokens).reshape(patches * groups, width)
    stacked = jnp.dot(normed, weight, preferred_element_type=jnp.float32).astype(jnp.bfloat16)
    stacked = stacked.reshape(patches, groups, 3, width).transpose(2, 0, 1, 3)
    return stacked.reshape(3, patches, groups * width)


def pair_attention(operands):
    stacked, keep_row = operands
    query, keyed, valued = (stacked[0], stacked[1], stacked[2])
    scale = query.shape[-1] ** (-0.5)
    scores = jnp.dot(query, keyed.T, preferred_element_type=jnp.float32) * scale
    weights = jnp.exp(scores) * keep_row[None, :]
    probs = (weights / jnp.sum(weights, axis=-1, keepdims=True)).astype(jnp.bfloat16)
    return jnp.dot(probs, valued, preferred_element_type=jnp.float32).astype(jnp.bfloat16)


def spatial_attention(stacked, keep_rows, attend):
    three, patches, columns = stacked.shape
    pairs = keep_rows.shape[0]
    split = stacked.reshape(3, patches, pairs, columns // pairs).transpose(2, 0, 1, 3)
    result = lax.map(attend, (split, keep_rows))
    return result.transpose(1, 0, 2).reshape(patches, columns)


def block_group(tokens, attended, w_so, w_gqkv, w_go):
    patches, groups, width = tokens.shape
    rows = patches * groups
    heads = H
    y_first = (
        tokens.reshape(rows, width).astype(jnp.float32)
        + jnp.dot(attended.reshape(rows, width), w_so, preferred_element_type=jnp.float32)
    ).astype(jnp.bfloat16)
    normed = rms_normalize(y_first)
    stacked = jnp.dot(normed, w_gqkv, preferred_element_type=jnp.float32).astype(jnp.bfloat16)
    stacked = stacked.reshape(patches, groups, 3, heads, width // heads)
    query = stacked[:, :, 0].astype(jnp.float32)
    keyed = stacked[:, :, 1].astype(jnp.float32)
    valued = stacked[:, :, 2].astype(jnp.float32)
    scale = (width // heads) ** (-0.5)
    scores = jnp.einsum("pgne,pkne->pngk", query, keyed) * scale
    weights = jnp.exp(scores)
    probs = (weights / jnp.sum(weights, axis=-1, keepdims=True)).astype(jnp.bfloat16)
    result = jnp.einsum("pngk,pkne->pgne", probs.astype(jnp.float32), valued).astype(jnp.bfloat16)
    result = result.reshape(rows, width)
    mixed = (
        y_first.astype(jnp.float32) + jnp.dot(result, w_go, preferred_element_type=jnp.float32)
    ).astype(jnp.bfloat16)
    return mixed.reshape(patches, groups, width)


def local(tokens, cotangent, w_sqkv, w_so, w_gqkv, w_go, keep):
    grid_size = lax.axis_size("grid")
    position = lax.axis_index("grid")
    full_sqkv, full_so, full_gqkv, full_go = (
        lax.all_gather(w_sqkv, "grid", axis=0, tiled=True),
        lax.all_gather(w_so, "grid", axis=0, tiled=True),
        lax.all_gather(w_gqkv, "grid", axis=0, tiled=True),
        lax.all_gather(w_go, "grid", axis=0, tiled=True),
    )
    stacked, pull_first = jax.vjp(partial(project_spatial, weight=full_sqkv), tokens)
    banded = lax.all_to_all(stacked, "grid", split_axis=2, concat_axis=1, tiled=True)
    pairs = G * H // grid_size
    pair_ids = position * pairs + jnp.arange(pairs, dtype=jnp.int32)
    select = (pair_ids[:, None] // H == jnp.arange(G, dtype=jnp.int32)[None, :]).astype(jnp.float32)
    keep_rows = jnp.dot(select, keep.astype(jnp.float32), precision=lax.Precision.HIGHEST)
    attend = jax.checkpoint(pair_attention)
    attended_bands, pull_spatial = jax.vjp(
        partial(spatial_attention, keep_rows=keep_rows, attend=attend), banded
    )
    attended = lax.all_to_all(attended_bands, "grid", split_axis=0, concat_axis=1, tiled=True)
    mixed, pull_group = jax.vjp(
        partial(block_group, w_so=full_so, w_gqkv=full_gqkv, w_go=full_go), tokens, attended
    )
    grad_direct, grad_attended = pull_group(cotangent)
    grad_bands = lax.all_to_all(grad_attended, "grid", split_axis=1, concat_axis=0, tiled=True)
    (grad_banded,) = pull_spatial(grad_bands)
    grad_stacked = lax.all_to_all(grad_banded, "grid", split_axis=1, concat_axis=2, tiled=True)
    (grad_first,) = pull_first(grad_stacked)
    return (mixed, grad_direct + grad_first)


def solution(mesh):
    placed = (
        P(("parts", "grid"), None, None),
        P(("parts", "grid"), None, None),
        P("grid", None),
        P("grid", None),
        P("grid", None),
        P("grid", None),
        P(None, "parts"),
    )
    return jax.shard_map(
        local,
        mesh=mesh,
        in_specs=placed,
        out_specs=(P(("parts", "grid"), None, None), P(("parts", "grid"), None, None)),
        check_vma=False,
    )
```

profile of v0, /device:TPU:0, one launch (start us, length us, event | category | flops | bytes accessed | tf_op | source)
XLA Modules:
  0.0 408.1 jit_solution(649732156367251045)
XLA Ops:
  10.0 1.1 fusion.43
  11.1 1.1 fusion.44
  12.1 71.0 %all-gather.5.cloned.1.call-done = bf16[1024,3072]{1,0:T(8,128)(2,1)} async-done(((bf16[32,3072]{1,0:T(8,128)(2,1)}), bf16[1024,3072]{1,0:T(8,128)(2,1)}) %all-gather.5.cloned.1.call-update) | async-done | bytes 6291472 | tf_op jit(solution)/shard_map/all_gather | solution.py:74
  83.1 3.8 convolution_convert_fusion.6
  86.9 1.2 reshape.171
  88.1 33.8 %copy.75 = bf16[3,4,32,1024]{1,0,3,2:T(4,128)(2,1)} copy(bf16[3,4,32,1024]{3,0,2,1:T(4,128)(2,1)S(1)} %bitcast.189) | data formatting | bytes 1572864 | tf_op jit(solution)/shard_map/jvp()/reshape | solution.py:23
  121.8 36.9 %reshape.187 = bf16[32,2,6144]{2,1,0:T(2,128)(2,1)} reshape(bf16[32768,3,4]{2,1,0:T(4,128)(2,1)} %bitcast.185) | data formatting | bytes 1572864
  158.7 3.0 all-to-all-start
  162.0 23.2 %all-to-all-done = bf16[32,2,6144]{2,1,0:T(2,128)(2,1)S(1)} async-done(((bf16[32,2,6144]{2,1,0:T(2,128)(2,1)}), bf16[32,2,6144]{2,1,0:T(2,128)(2,1)S(1)}, u32[]{:S(2)}, u32[]{:S(2)}) %all-to-all-start) | async-done | bytes 786464 | tf_op jit(solution)/shard_map/all_to_all | solution.py:80
  185.1 31.4 %reshape.188 = bf16[32768,3,4]{2,1,0:T(4,128)(2,1)} reshape(bf16[32,2,6144]{2,1,0:T(2,128)(2,1)S(1)} %all-to-all-done) | data formatting | bytes 1572864
  216.5 42.8 %copy.54 = bf16[3,4,32,1024]{3,1,2,0:T(4,128)(2,1)S(1)} copy(bf16[3,4,32,1024]{1,0,3,2:T(4,128)(2,1)} %bitcast.186) | data formatting | bytes 1572864 | tf_op jit(solution)/shard_map/all_to_all | solution.py:80
  259.4 1.0 reshape.173
  260.8 16.3 %while.24 = (s32[]{:T(128)}, bf16[16,128,64]{1,2,0:T(8,128)(2,1)}, bf16[16,3,128,64]{3,2,1,0:T(8,128)(2,1)S(1)}, f32[16,128]{1,0:T(8,128)S(1)}, s32[]{:T(128)}, /*index=5*/s32[]{:T(128)}, s32[]{}, s32[]{}) while((s32[]{:T(128)}, bf16[16,128,64]{1,2,0:T(8,128)(2,1)}, bf16[16,3,128,64]{3,2,1,0:T(8,128)(2,1)S(1)}, f32[16,128]{1,0:T(8,128)S(1)}, ...), condition=%wide.region_3.4_spmd, body=%wide.region_1.3_spmd.sunk | while | flops 4284292 | bytes 250489 | solution.py:40
  261.0 0.8 fusion.90
  262.0 0.8 fusion.90
  263.0 0.8 fusion.90
  264.1 0.8 fusion.90
  265.1 0.8 fusion.90
  266.1 0.8 fusion.90
  267.1 0.8 fusion.90
  268.1 0.8 fusion.90
  269.1 0.8 fusion.90
  270.1 0.8 fusion.90
  271.2 0.8 fusion.90
  277.1 1.5 copy.56
  278.6 1.0 all_to_all.47
  279.6 3.4 all-to-all-start.1
  283.1 2.5 convolution_convert_fusion.15
  285.9 7.6 %all-to-all-done.1 = bf16[32,4,1024]{2,1,0:T(4,128)(2,1)S(1)} async-done(((bf16[32,4,1024]{2,1,0:T(4,128)(2,1)}), bf16[32,4,1024]{2,1,0:T(4,128)(2,1)S(1)}, u32[]{:S(2)}, u32[]{:S(2)}) %all-to-all-start.1) | async-done | bytes 262176 | tf_op jit(solution)/shard_map/all_to_all | solution.py:89
  293.6 2.1 multiply_reduce_fusion.3
  295.8 4.7 %convolution_convert_fusion.5 = bf16[128,3072]{1,0:T(8,128)(2,1)} fusion(bf16[1024,3072]{1,0:T(8,128)(2,1)} %all-gather.9.cloned.1.call-done, f32[128,1024]{1,0:T(8,128)S(1)} %get-tuple-element.187, f32[128]{0:T(128)S(1)} %fusion.54), kind=kOutput, calls=%fused_computation.45 | convolution fusion | flops 805961728 | bytes 7602688 | tf_op jit(solution)/shard_map/jvp()/dot_general | solution.py:53
  300.4 2.1 reshape.175
  305.5 1.8 copy.65
  307.2 2.3 reshape.180
  309.5 5.2 %multiply_reduce_fusion.2 = (f32[128]{0:T(128)S(1)}, f32[128,1024]{1,0:T(8,128)S(1)}) fusion(f32[128,1024]{1,0:T(8,128)S(1)} %get-tuple-element.187, bf16[128,3072]{1,0:T(8,128)(2,1)S(1)} %reshape.180, bf16[1024,3072]{1,0:T(8,128)(2,1)} %all-gather.9.cloned.1.call-done), kind=kOutput, calls=%fused_computation.94 | convolution fusion | flops 805830528 | bytes 8126976 | tf_op jit(solution)/shard_map/transpose(jvp())/dot_general | solution.py:53
  315.0 0.8 convolution_convert_fusion.13
  316.0 12.8 %all_to_all.59 = bf16[4,32,1024]{2,0,1:T(4,128)(2,1)S(1)} all-to-all(bf16[4,32,1024]{2,0,1:T(4,128)(2,1)S(1)} %copy.66), channel_id=1, replica_groups=mesh['parts'=1,'grid'=32] {'grid'}, dimensions={1} | all-to-all | bytes 524288 | tf_op jit(solution)/shard_map/all_to_all | solution.py:94
  329.5 32.7 %while.25 = (s32[]{:T(128)}, bf16[16,3,128,64]{2,3,0,1:T(8,128)(2,1)S(1)}, bf16[16,3,128,64]{3,2,1,0:T(8,128)(2,1)}, f32[16,128]{1,0:T(8,128)S(1)}, bf16[16,128,64]{2,1,0:T(8,128)(2,1)S(1)}, /*index=5*/s32[]{:T(128)}, s32[]{:T(128)}) while((s32[]{:T(128)}, bf16[16,3,128,64]{2,3,0,1:T(8,128)(2,1)S(1)}, bf16[16,3,128,64]{3,2,1,0:T(8,128)(2,1)}, ...), condition=%wide.region_11.12_spmd, body=%wide.region_8.11_spmd.sunk | while | flops 11018371 | bytes 1025641 | solution.py:40
  329.5 0.9 dynamic-slice_bitcast_fusion.12
  331.6 0.9 dynamic-slice_bitcast_fusion.12
  333.6 0.9 dynamic-slice_bitcast_fusion.12
  335.7 0.9 dynamic-slice_bitcast_fusion.12
  337.7 0.9 dynamic-slice_bitcast_fusion.12
  339.8 0.9 dynamic-slice_bitcast_fusion.12
  341.8 0.9 dynamic-slice_bitcast_fusion.12
  343.8 0.9 dynamic-slice_bitcast_fusion.12
  345.9 0.9 dynamic-slice_bitcast_fusion.12
  347.9 0.9 dynamic-slice_bitcast_fusion.12
  350.0 0.9 dynamic-slice_bitcast_fusion.12
  352.0 0.9 dynamic-slice_bitcast_fusion.12
  354.1 0.9 dynamic-slice_bitcast_fusion.12
  356.1 0.9 dynamic-slice_bitcast_fusion.12
  358.1 0.9 dynamic-slice_bitcast_fusion.12
  360.2 0.9 dynamic-slice_bitcast_fusion.12
  362.2 1.7 copy.70
  363.9 3.6 all-to-all-start.3
  367.5 1.9 fusion.27
  369.4 1.0 copy.62
  370.5 1.4 reshape.176
  371.9 1.2 fusion.32
  373.1 20.4 %all-to-all-done.3 = bf16[3,128,1024]{2,0,1:T(4,128)(2,1)} async-done(((bf16[3,128,1024]{2,0,1:T(4,128)(2,1)}), bf16[3,128,1024]{2,0,1:T(4,128)(2,1)}, u32[]{:S(2)}, u32[]{:S(2)}) %all-to-all-start.3) | async-done | bytes 786464 | tf_op jit(solution)/shard_map/all_to_all | solution.py:96
  393.5 1.6 copy.72
  395.5 5.0 %convolution_convert_fusion.12 = bf16[128,1024]{1,0:T(8,128)(2,1)S(1)} fusion(bf16[128,3072]{1,0:T(8,128)(2,1)S(1)} %bitcast.191, bf16[1024,3072]{1,0:T(8,128)(2,1)} %all-gather.5.cloned.1.call-done), kind=kOutput, calls=%fused_computation.63 | convolution fusion | flops 805437440 | bytes 7340032 | tf_op jit(solution)/shard_map/transpose(jvp())/dot_general | solution.py:21
  400.6 0.9 fusion.47
  (250 shorter events, 33.0 us)
Async XLA Ops:
  7.2 75.9 %all-gather.5.cloned.1.call-start = ((), (), s32[]{:S(2)}) async-start(), calls=%async_computation.4 | async-start | bytes 6488064 | tf_op jit(solution)/shard_map/all_gather | solution.py:74
  7.9 275.2 %all-gather.11.cloned.1.call-start = ((), (), s32[]{:S(2)}) async-start(), calls=%async_computation.7 | async-start | bytes 2162688 | tf_op jit(solution)/shard_map/all_gather | solution.py:77
  8.6 284.9 %all-gather.7.cloned.1.call-start = ((), (), s32[]{:S(2)}) async-start(), calls=%async_computation.5 | async-start | bytes 2162688 | tf_op jit(solution)/shard_map/all_gather | solution.py:75
  9.4 286.4 %all-gather.9.cloned.1.call-start = ((), (), s32[]{:S(2)}) async-start(), calls=%async_computation.6 | async-start | bytes 6488064 | tf_op jit(solution)/shard_map/all_gather | solution.py:76
  121.8 40.0 %copy-start.7 = (s32[32,128]{1,0:T(8,128)S(1)}, s32[32,128]{1,0:T(8,128)}, u32[]{:S(2)}) copy-start(s32[32,128]{1,0:T(8,128)} %param.17) | copy-start | bytes 49156
  158.7 26.4 %all-to-all-start = ((bf16[32,2,6144]{2,1,0:T(2,128)(2,1)}), bf16[32,2,6144]{2,1,0:T(2,128)(2,1)S(1)}, u32[]{:S(2)}, u32[]{:S(2)}) async-start(bf16[32,2,6144]{2,1,0:T(2,128)(2,1)} %reshape.187), calls=%async_computation | async-start | bytes 1572864 | tf_op jit(solution)/shard_map/all_to_all | solution.py:80
  260.8 22.3 %copy-start.6 = (bf16[4,32,1024]{2,1,0:T(8,128)(2,1)S(1)}, bf16[4,32,1024]{2,1,0:T(8,128)(2,1)}, u32[]{:S(2)}) copy-start(bf16[4,32,1024]{2,1,0:T(8,128)(2,1)} %param.12) | copy-start | bytes 786436
  277.1 2.5 copy-start.4
  279.6 13.9 %all-to-all-start.1 = ((bf16[32,4,1024]{2,1,0:T(4,128)(2,1)}), bf16[32,4,1024]{2,1,0:T(4,128)(2,1)S(1)}, u32[]{:S(2)}, u32[]{:S(2)}) async-start(bf16[32,4,1024]{2,1,0:T(4,128)(2,1)} %all_to_all.47), calls=%async_computation.1 | async-start | bytes 524288 | tf_op jit(solution)/shard_map/all_to_all | solution.py:89
  283.0 10.5 %copy-start.2 = (bf16[4,32,1024]{2,1,0:T(8,128)(2,1)S(1)}, bf16[4,32,1024]{2,1,0:T(8,128)(2,1)}, u32[]{:S(2)}) copy-start(bf16[4,32,1024]{2,1,0:T(8,128)(2,1)} %param.11) | copy-start | bytes 786436
  302.9 0.8 copy-start.5
  303.4 1.2 copy-start.3
  309.5 5.4 %copy-start.1 = (bf16[1024,1024]{1,0:T(8,128)(2,1)S(1)}, bf16[1024,1024]{1,0:T(8,128)(2,1)}, u32[]{:S(2)}) copy-start(bf16[1024,1024]{1,0:T(8,128)(2,1)} %all-gather.7.cloned.1.call-done) | copy-start | bytes 6291460
  363.9 29.6 %all-to-all-start.3 = ((bf16[3,128,1024]{2,0,1:T(4,128)(2,1)}), bf16[3,128,1024]{2,0,1:T(4,128)(2,1)}, u32[]{:S(2)}, u32[]{:S(2)}) async-start(bf16[3,128,1024]{2,0,1:T(4,128)(2,1)} %copy.70), calls=%async_computation.3 | async-start | bytes 2097152 | tf_op jit(solution)/shard_map/all_to_all | solution.py:96
  367.5 4.4 %copy-start = (bf16[1024,1024]{1,0:T(8,128)(2,1)S(1)}, bf16[1024,1024]{1,0:T(8,128)(2,1)}, u32[]{:S(2)}) copy-start(bf16[1024,1024]{1,0:T(8,128)(2,1)} %all-gather.11.cloned.1.call-done) | copy-start | bytes 6291460
Sparse Core Ops, SparseCore 0:
  10.9 72.1 all-gather.4
  86.0 54.8 all-gather.10
  143.7 57.2 all-gather.6
  203.7 68.3 all-gather.8
where the time goes:
time: 411 us; the launch traced here: 408 us
  local copies, waits for them, and re-layouts  179 us (44%)
  waiting for transfers between devices  125 us (30%)
  matrix products  62.1 us (15%)
  between operations  14.2 us (3%)
  blocking collectives  12.8 us (3%)
  starting transfers between devices  10.2 us (2%)
  other arithmetic  4.5 us (1%)
    all_gather x1, waiting for transfers between devices, local(): lax.all_gather(w_sqkv, 'grid', axis=0, tiled=True)  71 us
    unnamed x19, local copies, waits for them, and re-layouts  68.7 us
    all_to_all x1, local copies, waits for them, and re-layouts, local(): lax.all_to_all(stacked, 'grid', split_axis=2, concat_axis=1, tiled=True)  42.8 us
    reshape x1, local copies, waits for them, and re-layouts, project_spatial(): return stacked.reshape(3, patches, groups * width)  33.8 us
    all_to_all x1, waiting for transfers between devices, local(): lax.all_to_all(stacked, 'grid', split_axis=2, concat_axis=1, tiled=True)  23.2 us
    all_to_all x1, waiting for transfers between devices, local(): lax.all_to_all(grad_banded, 'grid', split_axis=1, concat_axis=2, tiled=True)  20.4 us
    dot_general x48, matrix products, pair_attention(): jnp.dot(probs, valued, preferred_element_type=jnp.float32)  19.4 us
    squeeze x48, local copies, waits for them, and re-layouts, spatial_attention(): result = lax.map(attend, (split, keep_rows))  14.7 us
  transfers between devices with their start and end apart: 7, of which 4 were waited for; matrix products, arithmetic and copies ran while one was open for 45% of the time, Pallas kernels for 0%

commit v1 on v0

--- a/solution.py
+++ b/solution.py
@@ -3,6 +3,8 @@
 import jax
 import jax.numpy as jnp
 from jax import lax
+from jax.experimental import pallas as pl
+from jax.experimental.pallas import tpu as pltpu
 from jax.sharding import PartitionSpec as P
 
 H = 16
@@ -67,7 +69,7 @@
     return mixed.reshape(patches, groups, width)
 
 
-def local(tokens, cotangent, w_sqkv, w_so, w_gqkv, w_go, keep):
+def general_layer(tokens, cotangent, w_sqkv, w_so, w_gqkv, w_go, keep):
     grid_size = lax.axis_size("grid")
     position = lax.axis_index("grid")
     full_sqkv, full_so, full_gqkv, full_go = (
@@ -98,6 +100,265 @@
     return (mixed, grad_direct + grad_first)
 
 
+def nt(a, b):
+    return lax.dot_general(a, b, (((1,), (1,)), ((), ())), preferred_element_type=jnp.float32)
+
+
+def tn(a, b):
+    return lax.dot_general(a, b, (((0,), (0,)), ((), ())), preferred_element_type=jnp.float32)
+
+
+def nn(a, b):
+    return jnp.dot(a, b, preferred_element_type=jnp.float32)
+
+
+def inverse_rms(wide):
+    return lax.rsqrt(jnp.mean(wide * wide, axis=-1, keepdims=True) + 1e-06)
+
+
+def norm_grad(wide, inverse, grad):
+    inner = jnp.mean(grad * wide, axis=-1, keepdims=True)
+    return grad * inverse - wide * (inverse * inverse * inverse * inner)
+
+
+def head_pair(values, low):
+    zero = jnp.zeros_like(values)
+    return jnp.concatenate([jnp.where(low, values, zero), jnp.where(low, zero, values)], axis=0)
+
+
+def join_pair(stacked, low):
+    rows = stacked.shape[0] // 2
+    return jnp.where(low, stacked[:rows], stacked[rows:])
+
+
+def halves(values):
+    width = values.shape[1] // 2
+    first = jnp.sum(values[:, :width], axis=-1, keepdims=True)
+    second = jnp.sum(values[:, width:], axis=-1, keepdims=True)
+    rows = values.shape[0]
+    return jnp.concatenate(
+        [jnp.broadcast_to(first, (rows, width)), jnp.broadcast_to(second, (rows, width))], axis=1
+    )
+
+
+def low_lanes(rows):
+    return lax.broadcasted_iota(jnp.int32, (rows, 128), 1) < 64
+
+
+def pair_forward(qkv, allowed, low, width, pair):
+    query = qkv[:, pair * 128 : pair * 128 + 128]
+    keyed = head_pair(qkv[:, width + pair * 128 : width + pair * 128 + 128], low)
+    valued = head_pair(qkv[:, 2 * width + pair * 128 : 2 * width + pair * 128 + 128], low)
+    weights = jnp.where(allowed, jnp.exp(nt(query, keyed) * 0.125), 0.0)
+    probs = weights / halves(weights)
+    result = nn(probs.astype(jnp.bfloat16), valued).astype(jnp.bfloat16)
+    return probs, result
+
+
+def pair_backward(qkv, probs, grad, low, width, pair):
+    query = qkv[:, pair * 128 : pair * 128 + 128]
+    keyed = head_pair(qkv[:, width + pair * 128 : width + pair * 128 + 128], low)
+    valued = head_pair(qkv[:, 2 * width + pair * 128 : 2 * width + pair * 128 + 128], low)
+    grad_probs = nt(grad, valued).astype(jnp.bfloat16).astype(jnp.float32)
+    grad_scores = probs * (grad_probs - halves(grad_probs * probs))
+    grad_scores = (grad_scores * 0.125).astype(jnp.bfloat16)
+    grad_value = join_pair(tn(probs.astype(jnp.bfloat16), grad), low).astype(jnp.bfloat16)
+    grad_query = nn(grad_scores, keyed).astype(jnp.bfloat16)
+    grad_key = join_pair(tn(grad_scores, query), low).astype(jnp.bfloat16)
+    return grad_query, grad_key, grad_value
+
+
+def spatial_forward(tokens, keep, w_qkv, w_out, y_out, qkv_out, probs_out, qkv_buf, out_buf, sems):
+    rows, width = tokens.shape
+    span = 2 * rows
+    load_qkv = pltpu.make_async_copy(w_qkv, qkv_buf, sems.at[0])
+    load_out = pltpu.make_async_copy(w_out, out_buf, sems.at[1])
+    load_qkv.start()
+    load_out.start()
+    wide = tokens[...].astype(jnp.float32)
+    normed = (wide * inverse_rms(wide)).astype(jnp.bfloat16)
+    allowed = keep[...] > 0
+    low = low_lanes(rows)
+    load_qkv.wait()
+    qkv_out[...] = nn(normed, qkv_buf[...]).astype(jnp.bfloat16)
+    results = []
+    for pair in range(width // 128):
+        probs, result = pair_forward(qkv_out, allowed, low, width, pair)
+        probs_out[:, pair * span : pair * span + span] = probs
+        results.append(result)
+    load_out.wait()
+    total = wide + nn(jnp.concatenate(results, axis=1), out_buf[...])
+    y_out[...] = total.astype(jnp.bfloat16)
+
+
+def spatial_backward(tokens, grad, qkv, probs, w_qkv, w_out, grad_out, qkv_buf, out_buf, grads, sems):
+    rows, width = tokens.shape
+    span = 2 * rows
+    load_out = pltpu.make_async_copy(w_out, out_buf, sems.at[1])
+    load_qkv = pltpu.make_async_copy(w_qkv, qkv_buf, sems.at[0])
+    load_out.start()
+    load_qkv.start()
+    low = low_lanes(rows)
+    load_out.wait()
+    grad_attended = nt(grad[...], out_buf[...]).astype(jnp.bfloat16)
+    for pair in range(width // 128):
+        at = pair * 128
+        parts = pair_backward(
+            qkv, probs[:, pair * span : pair * span + span], grad_attended[:, at : at + 128], low, width, pair
+        )
+        for which, part in enumerate(parts):
+            grads[:, which * width + at : which * width + at + 128] = part
+    wide = tokens[...].astype(jnp.float32)
+    inverse = inverse_rms(wide)
+    load_qkv.wait()
+    grad_normed = nt(grads[...], qkv_buf[...]).astype(jnp.bfloat16).astype(jnp.float32)
+    grad_out[...] = norm_grad(wide, inverse, grad_normed).astype(jnp.bfloat16)
+
+
+def reorder(patches, groups, backward):
+    rows = patches * groups
+    here = lax.broadcasted_iota(jnp.int32, (rows, rows), 1 if backward else 0)
+    there = lax.broadcasted_iota(jnp.int32, (rows, rows), 0 if backward else 1)
+    patch, group = here // groups, here % groups
+    return (there == group * patches + patch).astype(jnp.bfloat16)
+
+
+def group_layer(
+    patches, y_in, cotangent, w_qkv, w_out, mixed, grad_y, grad_bands, qkv_buf, out_buf, qkv, grads, probs_buf, sems
+):
+    rows, width = y_in.shape
+    groups = rows // patches
+    span = 2 * rows
+    load_qkv = pltpu.make_async_copy(w_qkv, qkv_buf, sems.at[0])
+    load_out = pltpu.make_async_copy(w_out, out_buf, sems.at[1])
+    load_qkv.start()
+    load_out.start()
+    y_first = nn(reorder(patches, groups, False), y_in[...]).astype(jnp.bfloat16)
+    wide = y_first.astype(jnp.float32)
+    inverse = inverse_rms(wide)
+    normed = (wide * inverse).astype(jnp.bfloat16)
+    low = low_lanes(rows)
+    row_patch = lax.broadcasted_iota(jnp.int32, (rows, 2 * rows), 0) // groups
+    column_patch = (lax.broadcasted_iota(jnp.int32, (rows, 2 * rows), 1) % rows) // groups
+    allowed = row_patch == column_patch
+    load_qkv.wait()
+    qkv[...] = nn(normed, qkv_buf[...]).astype(jnp.bfloat16)
+    results = []
+    for pair in range(width // 128):
+        probs, result = pair_forward(qkv, allowed, low, width, pair)
+        probs_buf[:, pair * span : pair * span + span] = probs
+        results.append(result)
+    load_out.wait()
+    mixed[...] = (wide + nn(jnp.concatenate(results, axis=1), out_buf[...])).astype(jnp.bfloat16)
+    grad_attended = nt(cotangent[...], out_buf[...]).astype(jnp.bfloat16)
+    for pair in range(width // 128):
+        at = pair * 128
+        parts = pair_backward(
+            qkv, probs_buf[:, pair * span : pair * span + span], grad_attended[:, at : at + 128], low, width, pair
+        )
+        for which, part in enumerate(parts):
+            grads[:, which * width + at : which * width + at + 128] = part
+    grad_normed = nt(grads[...], qkv_buf[...]).astype(jnp.bfloat16).astype(jnp.float32)
+    through = norm_grad(wide, inverse, grad_normed).astype(jnp.bfloat16)
+    total = cotangent[...] + through
+    grad_y[...] = total
+    grad_bands[...] = nn(reorder(patches, groups, True), total).astype(jnp.bfloat16)
+
+
+VMEM_SPEC = pl.BlockSpec(memory_space=pltpu.VMEM)
+ANY_SPEC = pl.BlockSpec(memory_space=pl.ANY)
+PARAMS = pltpu.CompilerParams(vmem_limit_bytes=44 * 1024 * 1024)
+
+
+def shape(rows, columns, dtype=jnp.bfloat16):
+    return jax.ShapeDtypeStruct((rows, columns), dtype)
+
+
+def weight_scratch(width):
+    return [pltpu.VMEM((width, 3 * width), jnp.bfloat16), pltpu.VMEM((width, width), jnp.bfloat16)]
+
+
+def cost(rows, width, passes):
+    return pl.CostEstimate(
+        flops=passes * 8 * rows * width * width, bytes_accessed=8 * width * width, transcendentals=16 * rows * rows
+    )
+
+
+def exchange(values):
+    return lax.all_to_all(values, "grid", split_axis=0, concat_axis=0, tiled=True)
+
+
+def banded_layer(tokens, cotangent, w_sqkv, w_so, w_gqkv, w_go, keep):
+    patches, groups, width = tokens.shape
+    rows = patches * groups
+    all_patches = patches * lax.axis_size("grid")
+    position = lax.axis_index("grid")
+    full_sqkv, full_so, full_gqkv, full_go = (
+        lax.all_gather(w_sqkv, "grid", axis=0, tiled=True),
+        lax.all_gather(w_so, "grid", axis=0, tiled=True),
+        lax.all_gather(w_gqkv, "grid", axis=0, tiled=True),
+        lax.all_gather(w_go, "grid", axis=0, tiled=True),
+    )
+    banded = exchange(tokens.transpose(1, 0, 2)).reshape(all_patches, width)
+    keep_row = lax.dynamic_slice_in_dim(keep, position, 1, 0)
+    keep_row = jnp.concatenate([keep_row, keep_row], axis=1)
+    pairs = width // 128
+    y_bands, qkv, probs = pl.pallas_call(
+        spatial_forward,
+        out_shape=(
+            shape(all_patches, width),
+            shape(all_patches, 3 * width),
+            shape(all_patches, 2 * pairs * all_patches, jnp.float32),
+        ),
+        in_specs=[VMEM_SPEC, VMEM_SPEC, ANY_SPEC, ANY_SPEC],
+        out_specs=(VMEM_SPEC,) * 3,
+        scratch_shapes=weight_scratch(width) + [pltpu.SemaphoreType.DMA((2,))],
+        compiler_params=PARAMS,
+        cost_estimate=cost(all_patches, width, 1),
+        name="spatial_forward",
+    )(banded, keep_row, full_sqkv, full_so)
+    y_rows = exchange(y_bands.reshape(groups, patches, width)).reshape(rows, width)
+    mixed, grad_y, grad_bands = pl.pallas_call(
+        partial(group_layer, patches),
+        out_shape=(shape(rows, width),) * 3,
+        in_specs=[VMEM_SPEC, VMEM_SPEC, ANY_SPEC, ANY_SPEC],
+        out_specs=(VMEM_SPEC,) * 3,
+        scratch_shapes=weight_scratch(width)
+        + [
+            pltpu.VMEM((rows, 3 * width), jnp.bfloat16),
+            pltpu.VMEM((rows, 3 * width), jnp.bfloat16),
+            pltpu.VMEM((rows, 2 * pairs * rows), jnp.float32),
+            pltpu.SemaphoreType.DMA((2,)),
+        ],
+        compiler_params=PARAMS,
+        cost_estimate=cost(rows, width, 2),
+        name="group_layer",
+    )(y_rows, cotangent.reshape(rows, width), full_gqkv, full_go)
+    grad_banded = exchange(grad_bands.reshape(groups, patches, width)).reshape(all_patches, width)
+    grad_first = pl.pallas_call(
+        spatial_backward,
+        out_shape=shape(all_patches, width),
+        in_specs=[VMEM_SPEC] * 4 + [ANY_SPEC, ANY_SPEC],
+        out_specs=VMEM_SPEC,
+        scratch_shapes=weight_scratch(width)
+        + [pltpu.VMEM((all_patches, 3 * width), jnp.bfloat16), pltpu.SemaphoreType.DMA((2,))],
+        compiler_params=PARAMS,
+        cost_estimate=cost(all_patches, width, 1),
+        name="spatial_backward",
+    )(banded, grad_banded, qkv, probs, full_sqkv, full_so)
+    grad_first = exchange(grad_first.reshape(groups, patches, width)).transpose(1, 0, 2)
+    whole = (patches, groups, width)
+    return (mixed.reshape(whole), grad_y.reshape(whole) + grad_first)
+
+
+def local(tokens, cotangent, w_sqkv, w_so, w_gqkv, w_go, keep):
+    patches, groups, width = tokens.shape
+    size = lax.axis_size("grid")
+    fits = size == groups and width == 64 * H and patches * groups % 128 == 0 and patches * size % 128 == 0
+    layer = banded_layer if fits else general_layer
+    return layer(tokens, cotangent, w_sqkv, w_so, w_gqkv, w_go, keep)
+
+
 def solution(mesh):
     placed = (
         P(("parts", "grid"), None, None),

time: 411 us -> 326 us (0.79)
  local copies, waits for them, and re-layouts: 179 us -> 13.4 us
  waiting for transfers between devices: 125 us -> 232 us
  matrix products: 62.1 us -> 0 us
  blocking collectives: 12.8 us -> 40.8 us
  Pallas kernels: 0 us -> 17.9 us
  other arithmetic: 4.5 us -> 0.25 us
    all_gather x4, waiting for transfers between devices: 71 us -> 218 us  [the longest x1 71.3 us: banded_layer(): lax.all_gather(w_sqkv, 'grid', axis=0, tiled=True)]
    dot_general x127 -> x0, matrix products: 62.1 us -> none  [the longest x48 19.4 us: pair_attention(): jnp.dot(probs, valued, preferred_element_type=jnp.float32)]
    unnamed x19 -> x22, local copies, waits for them, and re-layouts: 68.7 us -> 12.9 us
    all_to_all x4 -> x0, local copies, waits for them, and re-layouts: 44.1 us -> none  [the longest x1 42.8 us: local(): lax.all_to_all(stacked, 'grid', split_axis=2, concat_axis=1, tiled=True)]
    reshape x9 -> x6, local copies, waits for them, and re-layouts: 44.1 us -> 0.51 us  [the longest x1 0.11 us: banded_layer(): grad_first.reshape(groups, patches, width)]
    all_to_all x3 -> x1, waiting for transfers between devices: 51.1 us -> 11 us  [exchange(): lax.all_to_all(values, 'grid', split_axis=0, concat_axis=0, tiled=True)]
    all_to_all x1 -> x3, blocking collectives: 12.8 us -> 40.8 us  [exchange(): lax.all_to_all(values, 'grid', split_axis=0, concat_axis=0, tiled=True)]
    pallas_call x0 -> x3, Pallas kernels: none -> 17.9 us  [the longest x1 7.77 us: banded_layer(): pl.pallas_call(partial(group_layer, patches), out_shape=(shape(rows, widt...]
  transfers between devices with their start and end apart: 7 -> 5, of which waited for: 4 -> 5; matrix products, arithmetic and copies ran while one was open for 45% -> 1% of each run, Pallas kernels for 0% -> 1%
where the time goes in v1:
time: 326 us
  waiting for transfers between devices  232 us (71%)
  blocking collectives  40.8 us (13%)
  Pallas kernels  17.9 us (5%)
  between operations  13.9 us (4%)
  local copies, waits for them, and re-layouts  13.4 us (4%)
  starting transfers between devices  7.45 us (2%)
    all_gather x1, waiting for transfers between devices, banded_layer(): lax.all_gather(w_sqkv, 'grid', axis=0, tiled=True)  71.3 us
    all_gather x1, waiting for transfers between devices, banded_layer(): lax.all_gather(w_gqkv, 'grid', axis=0, tiled=True)  71.1 us
    all_to_all x3, blocking collectives, exchange(): lax.all_to_all(values, 'grid', split_axis=0, concat_axis=0, tiled=True)  40.8 us
    all_gather x1, waiting for transfers between devices, banded_layer(): lax.all_gather(w_so, 'grid', axis=0, tiled=True)  40.3 us
    all_gather x1, waiting for transfers between devices, banded_layer(): lax.all_gather(w_go, 'grid', axis=0, tiled=True)  35.7 us
    unnamed x22, local copies, waits for them, and re-layouts  12.9 us
    all_to_all x1, waiting for transfers between devices, exchange(): lax.all_to_all(values, 'grid', split_axis=0, concat_axis=0, tiled=True)  11 us
    pallas_call x1, Pallas kernels, banded_layer(): pl.pallas_call(partial(group_layer, patches), out_shape=(shape(rows, widt...  7.77 us
  transfers between devices with their start and end apart: 5, of which 5 were waited for; matrix products, arithmetic and copies ran while one was open for 1% of the time, Pallas kernels for 1%

profile of v1, /device:TPU:0, one launch (start us, length us, event | category | flops | bytes accessed | tf_op | source)
XLA Modules:
  0.0 325.6 jit_solution(13939208671634710843)
XLA Ops:
  7.2 0.0 copy-start
  7.2 0.0 copy-start.9
  7.2 0.0 all-gather.7.cloned.1.call-start
  7.2 0.7 all-gather.7.cloned.1.call-update
  7.9 0.0 all-gather.5.cloned.1.call-start
  8.0 0.7 all-gather.5.cloned.1.call-update
  8.7 0.0 all-gather.11.cloned.1.call-start
  8.7 0.7 all-gather.11.cloned.1.call-update
  9.4 0.0 all-gather.9.cloned.1.call-start
  9.5 0.5 all-gather.9.cloned.1.call-update
  10.0 1.9 copy.16
  11.8 7.3 %all-to-all-start = ((bf16[32,4,1024]{2,1,0:T(4,128)(2,1)}), bf16[32,4,1024]{2,1,0:T(4,128)(2,1)S(1)}, u32[]{:S(2)}, u32[]{:S(2)}) async-start(bf16[32,4,1024]{2,1,0:T(4,128)(2,1)} %bitcast.7), calls=%async_computation | async-start | bytes 524288 | tf_op jit(solution)/shard_map/all_to_all | solution.py:288
  19.1 0.0 copy-done
  19.2 11.0 %all-to-all-done = bf16[32,4,1024]{2,1,0:T(4,128)(2,1)S(1)} async-done(((bf16[32,4,1024]{2,1,0:T(4,128)(2,1)}), bf16[32,4,1024]{2,1,0:T(4,128)(2,1)S(1)}, u32[]{:S(2)}, u32[]{:S(2)}) %all-to-all-start) | async-done | bytes 262176 | tf_op jit(solution)/shard_map/all_to_all | solution.py:288
  30.2 0.1 reshape.31.tokens
  30.3 40.3 %all-gather.7.cloned.1.call-done.w_out = bf16[1024,1024]{1,0:T(8,128)(2,1)} async-done(((bf16[32,1024]{1,0:T(8,128)(2,1)}), bf16[1024,1024]{1,0:T(8,128)(2,1)}) %all-gather.7.cloned.1.call-update) | async-done | bytes 2097168 | tf_op jit(solution)/shard_map/all_gather | solution.py:298
  70.6 71.3 %all-gather.5.cloned.1.call-done.w_qkv = bf16[1024,3072]{1,0:T(8,128)(2,1)} async-done(((bf16[32,3072]{1,0:T(8,128)(2,1)}), bf16[1024,3072]{1,0:T(8,128)(2,1)}) %all-gather.5.cloned.1.call-update) | async-done | bytes 6291472 | tf_op jit(solution)/shard_map/all_gather | solution.py:297
  141.8 0.0 copy-start.1
  141.8 1.6 copy-done.1
  143.4 4.8 %spatial_forward.1 = (bf16[128,1024]{1,0:T(8,128)(2,1)S(1)}, bf16[128,3072]{1,0:T(8,128)(2,1)S(1)}, f32[128,2048]{1,0:T(8,128)S(1)}) custom-call(bf16[128,1024]{1,0:T(8,128)(2,1)S(1)} %reshape.31.tokens, s32[1,256]{1,0:T(1,128)S(1)} %pad_add_fusion.keep, bf16[1024,3072]{1,0:T(8,128)(2,1)} %all-gather.5.cloned.1.call-done.w_qkv, bf16[1024,1024]{1,0:T(8,128)(2,1)S(1)} %copy-done.1), custom_call_target="tpu_custom_call" | custom-call | flops 1073741824 | bytes 8388608 | tf_op jit(solution)/shard_map/spatial_forward/pallas_call | solution.py:306
  148.2 0.0 copy-start.5
  148.2 1.0 copy-done.5
  149.2 0.0 copy-start.7
  149.2 0.9 copy-done.7
  150.1 0.0 copy-start.2
  150.1 0.1 reshape.32
  150.2 14.5 %all_to_all.20 = bf16[32,4,1024]{2,1,0:T(4,128)(2,1)S(1)} all-to-all(bf16[32,4,1024]{2,1,0:T(4,128)(2,1)S(1)} %reshape.32), channel_id=1, replica_groups=mesh['parts'=1,'grid'=32] {'grid'}, dimensions={0} | all-to-all | bytes 524288 | tf_op jit(solution)/shard_map/all_to_all | solution.py:288
  164.7 0.1 reshape.33.y_in
  164.8 35.7 %all-gather.11.cloned.1.call-done.w_out = bf16[1024,1024]{1,0:T(8,128)(2,1)} async-done(((bf16[32,1024]{1,0:T(8,128)(2,1)}), bf16[1024,1024]{1,0:T(8,128)(2,1)}) %all-gather.11.cloned.1.call-update) | async-done | bytes 2097168 | tf_op jit(solution)/shard_map/all_gather | solution.py:300
  200.5 71.1 %all-gather.9.cloned.1.call-done.w_qkv = bf16[1024,3072]{1,0:T(8,128)(2,1)} async-done(((bf16[32,3072]{1,0:T(8,128)(2,1)}), bf16[1024,3072]{1,0:T(8,128)(2,1)}) %all-gather.9.cloned.1.call-update) | async-done | bytes 6291472 | tf_op jit(solution)/shard_map/all_gather | solution.py:299
  271.6 0.0 copy-done.9
  271.6 0.0 copy-start.3
  271.6 2.8 copy-done.3
  274.4 0.0 copy-start.4
  274.4 1.6 copy-done.4
  276.0 7.8 %group_layer.1 = (bf16[128,1024]{1,0:T(8,128)(2,1)}, bf16[128,1024]{1,0:T(8,128)(2,1)S(1)}, bf16[128,1024]{1,0:T(8,128)(2,1)S(1)}) custom-call(bf16[128,1024]{1,0:T(8,128)(2,1)S(1)} %reshape.33.y_in, bf16[128,1024]{1,0:T(8,128)(2,1)S(1)} %bitcast.8, bf16[1024,3072]{1,0:T(8,128)(2,1)S(1)} %copy-done.3, bf16[1024,1024]{1,0:T(8,128)(2,1)S(1)} %copy-done.4), custom_call_target="tpu_custom_call" | custom-call | flops 2147483648 | bytes 8388608 | tf_op jit(solution)/shard_map/group_layer/pallas_call | solution.py:321
  283.7 0.1 reshape.37
  283.9 13.5 %all_to_all.21 = bf16[32,4,1024]{2,1,0:T(4,128)(2,1)S(1)} all-to-all(bf16[32,4,1024]{2,1,0:T(4,128)(2,1)S(1)} %reshape.37), channel_id=1, replica_groups=mesh['parts'=1,'grid'=32] {'grid'}, dimensions={0} | all-to-all | bytes 524288 | tf_op jit(solution)/shard_map/all_to_all | solution.py:288
  297.4 0.1 reshape.38.grad
  297.4 0.0 copy-done.2
  297.4 0.0 copy-start.6
  297.5 1.2 copy-done.6
  298.7 0.0 copy-start.8
  298.7 1.1 copy-done.8
  299.8 5.3 %spatial_backward.1 = bf16[128,1024]{1,0:T(8,128)(2,1)S(1)} custom-call(bf16[128,1024]{1,0:T(8,128)(2,1)S(1)} %reshape.31.tokens, bf16[128,1024]{1,0:T(8,128)(2,1)S(1)} %reshape.38.grad, bf16[128,3072]{1,0:T(8,128)(2,1)S(1)} %copy-done.8, f32[128,2048]{1,0:T(8,128)S(1)} %copy-done.6, bf16[1024,3072]{1,0:T(8,128)(2,1)} %all-gather.5.cloned.1.call-done.w_qkv, ...), custom_call_target="tpu_custom_call" | custom-call | flops 1073741824 | bytes 8388608 | tf_op jit(solution)/shard_map/spatial_backward/pallas_call | solution.py:338
  305.1 0.1 reshape.39
  305.2 12.8 %all_to_all.22 = bf16[32,4,1024]{2,1,0:T(4,128)(2,1)S(1)} all-to-all(bf16[32,4,1024]{2,1,0:T(4,128)(2,1)S(1)} %reshape.39), channel_id=1, replica_groups=mesh['parts'=1,'grid'=32] {'grid'}, dimensions={0} | all-to-all | bytes 524288 | tf_op jit(solution)/shard_map/all_to_all | solution.py:288
  318.1 0.2 bitcast_add_fusion
  318.3 0.8 copy.13
  (2 shorter events, 0.0 us)
Async XLA Ops:
  7.2 12.0 %copy-start = (s32[32,128]{1,0:T(8,128)S(1)}, s32[32,128]{1,0:T(8,128)}, u32[]{:S(2)}) copy-start(s32[32,128]{1,0:T(8,128)} %param.13) | copy-start | bytes 49156
  7.2 264.4 %copy-start.9 = (bf16[4,32,1024]{2,1,0:T(8,128)(2,1)S(1)}, bf16[4,32,1024]{2,1,0:T(8,128)(2,1)}, u32[]{:S(2)}) copy-start(bf16[4,32,1024]{2,1,0:T(8,128)(2,1)} %param.8) | copy-start | bytes 786436
  7.2 63.4 %all-gather.7.cloned.1.call-start = ((), (), s32[]{:S(2)}) async-start(), calls=%async_computation.5 | async-start | bytes 2162688 | tf_op jit(solution)/shard_map/all_gather | solution.py:298
  7.9 133.9 %all-gather.5.cloned.1.call-start = ((), (), s32[]{:S(2)}) async-start(), calls=%async_computation.4 | async-start | bytes 6488064 | tf_op jit(solution)/shard_map/all_gather | solution.py:297
  8.7 191.8 %all-gather.11.cloned.1.call-start = ((), (), s32[]{:S(2)}) async-start(), calls=%async_computation.7 | async-start | bytes 2162688 | tf_op jit(solution)/shard_map/all_gather | solution.py:300
  9.4 262.2 %all-gather.9.cloned.1.call-start = ((), (), s32[]{:S(2)}) async-start(), calls=%async_computation.6 | async-start | bytes 6488064 | tf_op jit(solution)/shard_map/all_gather | solution.py:299
  11.8 18.4 %all-to-all-start = ((bf16[32,4,1024]{2,1,0:T(4,128)(2,1)}), bf16[32,4,1024]{2,1,0:T(4,128)(2,1)S(1)}, u32[]{:S(2)}, u32[]{:S(2)}) async-start(bf16[32,4,1024]{2,1,0:T(4,128)(2,1)} %bitcast.7), calls=%async_computation | async-start | bytes 524288 | tf_op jit(solution)/shard_map/all_to_all | solution.py:288
  141.8 1.6 copy-start.1
  148.2 1.0 copy-start.5
  149.2 0.9 copy-start.7
  150.1 147.3 %copy-start.2 = (bf16[1024,1024]{1,0:T(8,128)(2,1)S(1)}, bf16[1024,1024]{1,0:T(8,128)(2,1)}, u32[]{:S(2)}) copy-start(bf16[1024,1024]{1,0:T(8,128)(2,1)} %all-gather.7.cloned.1.call-done.w_out) | copy-start | bytes 6291460
  271.6 2.8 copy-start.3
  274.4 1.6 copy-start.4
  297.4 1.2 copy-start.6
  298.7 1.1 copy-start.8
Sparse Core Ops, SparseCore 0:
  10.9 59.6 all-gather.6
  73.5 68.3 all-gather.4
  144.7 55.7 all-gather.10
  203.2 68.3 all-gather.8

commit v2 on v1

--- a/solution.py
+++ b/solution.py
@@ -168,49 +168,63 @@
     return grad_query, grad_key, grad_value
 
 
-def spatial_forward(tokens, keep, w_qkv, w_out, y_out, qkv_out, probs_out, qkv_buf, out_buf, sems):
+def place_rows(pieces, first, buffer, sem, rows_each):
+    position = lax.axis_index("grid")
+    size = buffer.shape[0] // rows_each
+    core = position % 2
+    one, other = 2 * (core + 1), 4 // (core + 1)
+    own = (0, one, other, 6)
+    sibling = (0, other, one, 6)
+    depth = len(pieces) // 2
+    for at, piece in enumerate(pieces):
+        flip = own[at] if at < depth else sibling[at - depth]
+        base = (position if at < depth else position + 1 - 2 * core) ^ flip
+        for step in range(piece.shape[0] // rows_each):
+            shard = lax.rem(base + size - 8 * step, size)
+            pltpu.make_async_copy(
+                piece.at[pl.ds(step * rows_each, rows_each), pl.ds(first, buffer.shape[1])],
+                buffer.at[pl.ds(pl.multiple_of(shard * rows_each, rows_each), rows_each)],
+                sem,
+            ).start()
+
+
+def wait_rows(buffer, sem):
+    pltpu.make_async_copy(buffer, buffer, sem).wait()
+
+
+def spatial_forward(tokens, keep, *refs):
+    pieces, (result_out, qkv_out, probs_out, qkv_buf, sems) = refs[:-5], refs[-5:]
     rows, width = tokens.shape
     span = 2 * rows
-    load_qkv = pltpu.make_async_copy(w_qkv, qkv_buf, sems.at[0])
-    load_out = pltpu.make_async_copy(w_out, out_buf, sems.at[1])
-    load_qkv.start()
-    load_out.start()
+    place_rows(pieces, 0, qkv_buf, sems.at[0], width // lax.axis_size("grid"))
     wide = tokens[...].astype(jnp.float32)
     normed = (wide * inverse_rms(wide)).astype(jnp.bfloat16)
     allowed = keep[...] > 0
     low = low_lanes(rows)
-    load_qkv.wait()
+    wait_rows(qkv_buf, sems.at[0])
     qkv_out[...] = nn(normed, qkv_buf[...]).astype(jnp.bfloat16)
-    results = []
     for pair in range(width // 128):
         probs, result = pair_forward(qkv_out, allowed, low, width, pair)
         probs_out[:, pair * span : pair * span + span] = probs
-        results.append(result)
-    load_out.wait()
-    total = wide + nn(jnp.concatenate(results, axis=1), out_buf[...])
-    y_out[...] = total.astype(jnp.bfloat16)
-
-
-def spatial_backward(tokens, grad, qkv, probs, w_qkv, w_out, grad_out, qkv_buf, out_buf, grads, sems):
+        result_out[:, pair * 128 : pair * 128 + 128] = result
+
+
+def spatial_backward(tokens, grad, qkv, probs, *refs):
+    pieces, (grad_out, qkv_buf, grads, sems) = refs[:-4], refs[-4:]
     rows, width = tokens.shape
     span = 2 * rows
-    load_out = pltpu.make_async_copy(w_out, out_buf, sems.at[1])
-    load_qkv = pltpu.make_async_copy(w_qkv, qkv_buf, sems.at[0])
-    load_out.start()
-    load_qkv.start()
+    place_rows(pieces, 0, qkv_buf, sems.at[0], width // lax.axis_size("grid"))
     low = low_lanes(rows)
-    load_out.wait()
-    grad_attended = nt(grad[...], out_buf[...]).astype(jnp.bfloat16)
     for pair in range(width // 128):
         at = pair * 128
         parts = pair_backward(
-            qkv, probs[:, pair * span : pair * span + span], grad_attended[:, at : at + 128], low, width, pair
+            qkv, probs[:, pair * span : pair * span + span], grad[:, at : at + 128], low, width, pair
         )
         for which, part in enumerate(parts):
             grads[:, which * width + at : which * width + at + 128] = part
     wide = tokens[...].astype(jnp.float32)
     inverse = inverse_rms(wide)
-    load_qkv.wait()
+    wait_rows(qkv_buf, sems.at[0])
     grad_normed = nt(grads[...], qkv_buf[...]).astype(jnp.bfloat16).astype(jnp.float32)
     grad_out[...] = norm_grad(wide, inverse, grad_normed).astype(jnp.bfloat16)
 
@@ -223,34 +237,38 @@
     return (there == group * patches + patch).astype(jnp.bfloat16)
 
 
-def group_layer(
-    patches, y_in, cotangent, w_qkv, w_out, mixed, grad_y, grad_bands, qkv_buf, out_buf, qkv, grads, probs_buf, sems
-):
-    rows, width = y_in.shape
+def group_layer(patches, tokens, attended, cotangent, w_go, *refs):
+    pieces, rest = refs[:-12], refs[-12:]
+    mixed, grad_y, grad_bands, so_buf, qkv_buf, go_buf, qkv, grads, probs_buf, y_buf, go_sem, sems = rest
+    rows, width = tokens.shape
     groups = rows // patches
     span = 2 * rows
-    load_qkv = pltpu.make_async_copy(w_qkv, qkv_buf, sems.at[0])
-    load_out = pltpu.make_async_copy(w_out, out_buf, sems.at[1])
-    load_qkv.start()
-    load_out.start()
-    y_first = nn(reorder(patches, groups, False), y_in[...]).astype(jnp.bfloat16)
+    each = width // lax.axis_size("grid")
+    place_rows(pieces, 0, so_buf, sems.at[0], each)
+    place_rows(pieces, width, qkv_buf, sems.at[1], each)
+    load_go = pltpu.make_async_copy(w_go, go_buf, go_sem)
+    load_go.start()
+    ordered = nn(reorder(patches, groups, False), attended[...]).astype(jnp.bfloat16)
+    low = low_lanes(rows)
+    row_patch = lax.broadcasted_iota(jnp.int32, (rows, span), 0) // groups
+    column_patch = (lax.broadcasted_iota(jnp.int32, (rows, span), 1) % rows) // groups
+    allowed = row_patch == column_patch
+    wait_rows(so_buf, sems.at[0])
+    y_first = (tokens[...].astype(jnp.float32) + nn(ordered, so_buf[...])).astype(jnp.bfloat16)
     wide = y_first.astype(jnp.float32)
+    y_buf[...] = wide
     inverse = inverse_rms(wide)
     normed = (wide * inverse).astype(jnp.bfloat16)
-    low = low_lanes(rows)
-    row_patch = lax.broadcasted_iota(jnp.int32, (rows, 2 * rows), 0) // groups
-    column_patch = (lax.broadcasted_iota(jnp.int32, (rows, 2 * rows), 1) % rows) // groups
-    allowed = row_patch == column_patch
-    load_qkv.wait()
+    wait_rows(qkv_buf, sems.at[1])
     qkv[...] = nn(normed, qkv_buf[...]).astype(jnp.bfloat16)
     results = []
     for pair in range(width // 128):
         probs, result = pair_forward(qkv, allowed, low, width, pair)
         probs_buf[:, pair * span : pair * span + span] = probs
         results.append(result)
-    load_out.wait()
-    mixed[...] = (wide + nn(jnp.concatenate(results, axis=1), out_buf[...])).astype(jnp.bfloat16)
-    grad_attended = nt(cotangent[...], out_buf[...]).astype(jnp.bfloat16)
+    load_go.wait()
+    mixed[...] = (y_buf[...] + nn(jnp.concatenate(results, axis=1), go_buf[...])).astype(jnp.bfloat16)
+    grad_attended = nt(cotangent[...], go_buf[...]).astype(jnp.bfloat16)
     for pair in range(width // 128):
         at = pair * 128
         parts = pair_backward(
@@ -259,23 +277,20 @@
         for which, part in enumerate(parts):
             grads[:, which * width + at : which * width + at + 128] = part
     grad_normed = nt(grads[...], qkv_buf[...]).astype(jnp.bfloat16).astype(jnp.float32)
-    through = norm_grad(wide, inverse, grad_normed).astype(jnp.bfloat16)
+    through = norm_grad(y_buf[...], inverse, grad_normed).astype(jnp.bfloat16)
     total = cotangent[...] + through
     grad_y[...] = total
-    grad_bands[...] = nn(reorder(patches, groups, True), total).astype(jnp.bfloat16)
+    spread = nt(total, so_buf[...]).astype(jnp.bfloat16)
+    grad_bands[...] = nn(reorder(patches, groups, True), spread).astype(jnp.bfloat16)
 
 
 VMEM_SPEC = pl.BlockSpec(memory_space=pltpu.VMEM)
 ANY_SPEC = pl.BlockSpec(memory_space=pl.ANY)
-PARAMS = pltpu.CompilerParams(vmem_limit_bytes=44 * 1024 * 1024)
+PARAMS = pltpu.CompilerParams(vmem_limit_bytes=56 * 1024 * 1024)
 
 
 def shape(rows, columns, dtype=jnp.bfloat16):
     return jax.ShapeDtypeStruct((rows, columns), dtype)
-
-
-def weight_scratch(width):
-    return [pltpu.VMEM((width, 3 * width), jnp.bfloat16), pltpu.VMEM((width, width), jnp.bfloat16)]
 
 
 def cost(rows, width, passes):
@@ -286,6 +301,29 @@
 
 def exchange(values):
     return lax.all_to_all(values, "grid", split_axis=0, concat_axis=0, tiled=True)
+
+
+def mesh_moves(size):
+    everyone = range(size)
+    first = [(i, i ^ (2 if i % 2 == 0 else 4)) for i in everyone]
+    second = [(i, i ^ (4 if i % 2 == 0 else 2)) for i in everyone]
+    sibling = [(i, i ^ 1) for i in everyone]
+    along = [[(i, (i + 8 * step) % size) for i in everyone] for step in range(1, size // 8)]
+    return first, second, sibling, along
+
+
+def move(values, table):
+    return lax.ppermute(values, "grid", table)
+
+
+def gather_rows(shard):
+    first, second, sibling, along = mesh_moves(lax.axis_size("grid"))
+    line = jnp.concatenate([shard] + [move(shard, table) for table in along], axis=0)
+    one = move(line, first)
+    other = move(line, second)
+    both = move(one, second)
+    held = [line, one, other, both]
+    return held + [move(block, sibling) for block in held]
 
 
 def banded_layer(tokens, cotangent, w_sqkv, w_so, w_gqkv, w_go, keep):
@@ -293,59 +331,63 @@
     rows = patches * groups
     all_patches = patches * lax.axis_size("grid")
     position = lax.axis_index("grid")
-    full_sqkv, full_so, full_gqkv, full_go = (
-        lax.all_gather(w_sqkv, "grid", axis=0, tiled=True),
-        lax.all_gather(w_so, "grid", axis=0, tiled=True),
-        lax.all_gather(w_gqkv, "grid", axis=0, tiled=True),
-        lax.all_gather(w_go, "grid", axis=0, tiled=True),
-    )
+    spatial_rows = gather_rows(w_sqkv)
+    group_rows = gather_rows(jnp.concatenate([w_so, w_gqkv], axis=1))
+    full_go = lax.all_gather(w_go, "grid", axis=0, tiled=True)
     banded = exchange(tokens.transpose(1, 0, 2)).reshape(all_patches, width)
     keep_row = lax.dynamic_slice_in_dim(keep, position, 1, 0)
     keep_row = jnp.concatenate([keep_row, keep_row], axis=1)
     pairs = width // 128
-    y_bands, qkv, probs = pl.pallas_call(
+    attended, qkv, probs = pl.pallas_call(
         spatial_forward,
         out_shape=(
             shape(all_patches, width),
             shape(all_patches, 3 * width),
             shape(all_patches, 2 * pairs * all_patches, jnp.float32),
         ),
-        in_specs=[VMEM_SPEC, VMEM_SPEC, ANY_SPEC, ANY_SPEC],
+        in_specs=[VMEM_SPEC] * 2 + [ANY_SPEC] * len(spatial_rows),
         out_specs=(VMEM_SPEC,) * 3,
-        scratch_shapes=weight_scratch(width) + [pltpu.SemaphoreType.DMA((2,))],
+        scratch_shapes=[pltpu.VMEM((width, 3 * width), jnp.bfloat16), pltpu.SemaphoreType.DMA((1,))],
         compiler_params=PARAMS,
         cost_estimate=cost(all_patches, width, 1),
         name="spatial_forward",
-    )(banded, keep_row, full_sqkv, full_so)
-    y_rows = exchange(y_bands.reshape(groups, patches, width)).reshape(rows, width)
+    )(banded, keep_row, *spatial_rows)
+    attended = exchange(attended.reshape(groups, patches, width)).reshape(rows, width)
     mixed, grad_y, grad_bands = pl.pallas_call(
         partial(group_layer, patches),
         out_shape=(shape(rows, width),) * 3,
-        in_specs=[VMEM_SPEC, VMEM_SPEC, ANY_SPEC, ANY_SPEC],
+        in_specs=[VMEM_SPEC] * 3 + [ANY_SPEC] * (1 + len(group_rows)),
         out_specs=(VMEM_SPEC,) * 3,
-        scratch_shapes=weight_scratch(width)
-        + [
+        scratch_shapes=[
+            pltpu.VMEM((width, width), jnp.bfloat16),
+            pltpu.VMEM((width, 3 * width), jnp.bfloat16),
+            pltpu.VMEM((width, width), jnp.bfloat16),
             pltpu.VMEM((rows, 3 * width), jnp.bfloat16),
             pltpu.VMEM((rows, 3 * width), jnp.bfloat16),
             pltpu.VMEM((rows, 2 * pairs * rows), jnp.float32),
+            pltpu.VMEM((rows, width), jnp.float32),
+            pltpu.SemaphoreType.DMA,
             pltpu.SemaphoreType.DMA((2,)),
         ],
         compiler_params=PARAMS,
         cost_estimate=cost(rows, width, 2),
         name="group_layer",
-    )(y_rows, cotangent.reshape(rows, width), full_gqkv, full_go)
+    )(tokens.reshape(rows, width), attended, cotangent.reshape(rows, width), full_go, *group_rows)
     grad_banded = exchange(grad_bands.reshape(groups, patches, width)).reshape(all_patches, width)
     grad_first = pl.pallas_call(
         spatial_backward,
         out_shape=shape(all_patches, width),
-        in_specs=[VMEM_SPEC] * 4 + [ANY_SPEC, ANY_SPEC],
+        in_specs=[VMEM_SPEC] * 4 + [ANY_SPEC] * len(spatial_rows),
         out_specs=VMEM_SPEC,
-        scratch_shapes=weight_scratch(width)
-        + [pltpu.VMEM((all_patches, 3 * width), jnp.bfloat16), pltpu.SemaphoreType.DMA((2,))],
+        scratch_shapes=[
+            pltpu.VMEM((width, 3 * width), jnp.bfloat16),
+            pltpu.VMEM((all_patches, 3 * width), jnp.bfloat16),
+            pltpu.SemaphoreType.DMA((1,)),
+        ],
         compiler_params=PARAMS,
         cost_estimate=cost(all_patches, width, 1),
         name="spatial_backward",
-    )(banded, grad_banded, qkv, probs, full_sqkv, full_so)
+    )(banded, grad_banded, qkv, probs, *spatial_rows)
     grad_first = exchange(grad_first.reshape(groups, patches, width)).transpose(1, 0, 2)
     whole = (patches, groups, width)
     return (mixed.reshape(whole), grad_y.reshape(whole) + grad_first)
@@ -354,7 +396,7 @@
 def local(tokens, cotangent, w_sqkv, w_so, w_gqkv, w_go, keep):
     patches, groups, width = tokens.shape
     size = lax.axis_size("grid")
-    fits = size == groups and width == 64 * H and patches * groups % 128 == 0 and patches * size % 128 == 0
+    fits = size == groups and size % 8 == 0 and width % (16 * size) == 0 and width == 64 * H and patches * groups % 128 == 0 and patches * size % 128 == 0
     layer = banded_layer if fits else general_layer
     return layer(tokens, cotangent, w_sqkv, w_so, w_gqkv, w_go, keep)
 

time: 326 us -> 210 us (0.64)
  waiting for transfers between devices: 232 us -> 71.9 us
  starting transfers between devices: 7.45 us -> 42.7 us
  Pallas kernels: 17.9 us -> 26.8 us
    all_gather x4 -> x1, waiting for transfers between devices: 218 us -> 0.02 us  [banded_layer(): full_go = lax.all_gather(w_go, 'grid', axis=0, tiled=True)]
    ppermute x0 -> x20, waiting for transfers between devices: none -> 71.9 us  [move(): return lax.ppermute(values, 'grid', table)]
    ppermute x0 -> x20, starting transfers between devices: none -> 36.9 us  [move(): return lax.ppermute(values, 'grid', table)]
    all_to_all x1, waiting for transfers between devices: 11 us -> 0.01 us  [exchange(): lax.all_to_all(values, 'grid', split_axis=0, concat_axis=0, tiled=True)]
    unnamed x22, local copies, waits for them, and re-layouts: 12.9 us -> 3.59 us
    pallas_call x1, Pallas kernels: 7.77 us -> 12.9 us  [banded_layer(): pl.pallas_call(partial(group_layer, patches), out_shape=(shape(rows, widt...]
  transfers between devices with their start and end apart: 5 -> 22, of which waited for: 5 -> 6; matrix products, arithmetic and copies ran while one was open for 1% -> 4% of each run, Pallas kernels for 1% -> 3%
where the time goes in v2:
time: 210 us; the launch traced here: 209 us
  waiting for transfers between devices  71.9 us (34%)
  starting transfers between devices  42.7 us (20%)
  blocking collectives  41.7 us (20%)
  Pallas kernels  26.8 us (13%)
  between operations  14.2 us (7%)
  local copies, waits for them, and re-layouts  11 us (5%)
    ppermute x20, waiting for transfers between devices, move(): return lax.ppermute(values, 'grid', table)  71.9 us
    all_to_all x3, blocking collectives, exchange(): lax.all_to_all(values, 'grid', split_axis=0, concat_axis=0, tiled=True)  41.7 us
    ppermute x20, starting transfers between devices, move(): return lax.ppermute(values, 'grid', table)  36.9 us
    pallas_call x1, Pallas kernels, banded_layer(): pl.pallas_call(partial(group_layer, patches), out_shape=(shape(rows, widt...  12.9 us
    pallas_call x1, Pallas kernels, banded_layer(): pl.pallas_call(spatial_backward, out_shape=shape(all_patches, width), in_...  7.56 us
    pallas_call x1, Pallas kernels, banded_layer(): pl.pallas_call(spatial_forward, out_shape=(shape(all_patches, width), sha...  6.32 us
    all_to_all x1, starting transfers between devices, exchange(): lax.all_to_all(values, 'grid', split_axis=0, concat_axis=0, tiled=True)  5.78 us
  transfers between devices with their start and end apart: 22, of which 6 were waited for; matrix products, arithmetic and copies ran while one was open for 4% of the time, Pallas kernels for 3%

profile of v2, /device:TPU:0, one launch (start us, length us, event | category | flops | bytes accessed | tf_op | source)
XLA Modules:
  0.0 209.3 jit_solution(11731336231602968930)
XLA Ops:
  7.2 0.0 copy-start
  7.2 0.0 all-gather.2.cloned.1.call-start
  7.2 4.1 %collective-permute-start.1 = (bf16[32,3072]{1,0:T(8,128)(2,1)}, bf16[32,3072]{1,0:T(8,128)(2,1)S(1)}, u32[]{:S(2)}, u32[]{:S(2)}) collective-permute-start(bf16[32,3072]{1,0:T(8,128)(2,1)} %param.9), channel_id=1, source_target_pairs={{0,16},{1,17},{2,18},{3,19},{4,20},{5,21},{6,22},{7,23},{8,24},{9,... | collective-permute-start | bytes 589832 | tf_op jit(solution)/shard_map/ppermute | solution.py:316
  11.3 1.6 collective-permute-start
  12.9 2.2 %collective-permute-start.2 = (bf16[32,3072]{1,0:T(8,128)(2,1)}, bf16[32,3072]{1,0:T(8,128)(2,1)S(1)}, u32[]{:S(2)}, u32[]{:S(2)}) collective-permute-start(bf16[32,3072]{1,0:T(8,128)(2,1)} %param.9), channel_id=1, source_target_pairs={{0,24},{1,25},{2,26},{3,27},{4,28},{5,29},{6,30},{7,31},{8,0},{9,1... | collective-permute-start | bytes 589832 | tf_op jit(solution)/shard_map/ppermute | solution.py:316
  15.2 0.8 constant_dynamic-update-slice_fusion.5
  16.0 0.9 constant_dynamic-update-slice_fusion.4
  16.9 0.1 collective-permute-start.12
  17.0 1.2 collective-permute-start.11
  18.2 0.0 all-gather.2.cloned.1.call-update
  18.3 0.0 copy-start.6
  18.3 1.0 constant_dynamic-update-slice_fusion.3
  19.3 3.7 %collective-permute-done = bf16[32,3072]{1,0:T(8,128)(2,1)S(1)} collective-permute-done((bf16[32,3072]{1,0:T(8,128)(2,1)}, bf16[32,3072]{1,0:T(8,128)(2,1)S(1)}, u32[]{:S(2)}, u32[]{:S(2)}) %collective-permute-start) | collective-permute-done | bytes 196640 | tf_op jit(solution)/shard_map/ppermute | solution.py:316
  23.0 19.4 %collective-permute-start.10 = (bf16[32,4096]{1,0:T(8,128)(2,1)S(1)}, bf16[32,4096]{1,0:T(8,128)(2,1)S(1)}, u32[]{:S(2)}, u32[]{:S(2)}) collective-permute-start(bf16[32,4096]{1,0:T(8,128)(2,1)S(1)} %constant_dynamic-update-slice_fusion.4), channel_id=1, source_target_pairs={{0,8},{1,9},{2,10},{3,11},{4,12},{5,13},{6,14},{7,15},{8,16},{9,17... | collective-permute-start | bytes 786440 | tf_op jit(solution)/shard_map/ppermute | solution.py:316
  42.4 0.0 collective-permute-done.1
  42.4 0.0 collective-permute-done.12
  42.4 10.5 %collective-permute-done.11 = bf16[32,4096]{1,0:T(8,128)(2,1)S(1)} collective-permute-done((bf16[32,4096]{1,0:T(8,128)(2,1)S(1)}, bf16[32,4096]{1,0:T(8,128)(2,1)S(1)}, u32[]{:S(2)}, u32[]{:S(2)}) %collective-permute-start.11) | collective-permute-done | bytes 262176 | tf_op jit(solution)/shard_map/ppermute | solution.py:316
  53.0 0.0 collective-permute-done.10
  53.0 0.1 pad_maximum_fusion.refs_0_
  53.1 1.6 collective-permute-start.13
  54.7 0.0 collective-permute-done.2
  54.7 0.6 collective-permute-start.3
  55.3 1.6 collective-permute-start.4
  56.9 0.0 collective-permute-start.6
  56.9 31.7 %collective-permute-done.3.refs_1_ = bf16[128,3072]{1,0:T(8,128)(2,1)S(1)} collective-permute-done((bf16[128,3072]{1,0:T(8,128)(2,1)S(1)}, bf16[128,3072]{1,0:T(8,128)(2,1)S(1)}, u32[]{:S(2)}, u32[]{:S(2)}) %collective-permute-start.3) | collective-permute-done | bytes 786464 | tf_op jit(solution)/shard_map/ppermute | solution.py:316
  88.6 1.5 collective-permute-start.5
  90.1 0.6 collective-permute-start.14
  90.6 0.0 collective-permute-done.13.refs_1_
  90.6 1.5 collective-permute-start.15
  92.1 0.0 collective-permute-done.4.refs_2_
  92.1 0.0 collective-permute-start.8
  92.1 0.0 collective-permute-done.6.refs_4_
  92.1 0.5 collective-permute-start.7
  92.6 8.1 %collective-permute-done.5.refs_3_ = bf16[128,3072]{1,0:T(8,128)(2,1)} collective-permute-done((bf16[128,3072]{1,0:T(8,128)(2,1)S(1)}, bf16[128,3072]{1,0:T(8,128)(2,1)}, u32[]{:S(2)}, u32[]{:S(2)}) %collective-permute-start.5) | collective-permute-done | bytes 786464 | tf_op jit(solution)/shard_map/ppermute | solution.py:316
  100.7 0.0 collective-permute-start.9
  100.7 0.9 copy.16
  101.6 5.8 %all-to-all-start = ((bf16[32,4,1024]{2,1,0:T(4,128)(2,1)}), bf16[32,4,1024]{2,1,0:T(4,128)(2,1)}, u32[]{:S(2)}, u32[]{:S(2)}) async-start(bf16[32,4,1024]{2,1,0:T(4,128)(2,1)} %bitcast.10), calls=%async_computation | async-start | bytes 524288 | tf_op jit(solution)/shard_map/all_to_all | solution.py:303
  107.4 5.7 %collective-permute-done.14.refs_2_ = bf16[128,4096]{1,0:T(8,128)(2,1)} collective-permute-done((bf16[128,4096]{1,0:T(8,128)(2,1)S(1)}, bf16[128,4096]{1,0:T(8,128)(2,1)}, u32[]{:S(2)}, u32[]{:S(2)}) %collective-permute-start.14) | collective-permute-done | bytes 1048608 | tf_op jit(solution)/shard_map/ppermute | solution.py:316
  113.0 0.0 collective-permute-start.16
  113.0 0.0 collective-permute-done.8.refs_6_
  113.1 0.5 collective-permute-start.17
  113.6 0.1 collective-permute-start.18
  113.6 12.2 %collective-permute-done.15.refs_3_ = bf16[128,4096]{1,0:T(8,128)(2,1)} collective-permute-done((bf16[128,4096]{1,0:T(8,128)(2,1)}, bf16[128,4096]{1,0:T(8,128)(2,1)}, u32[]{:S(2)}, u32[]{:S(2)}) %collective-permute-start.15) | collective-permute-done | bytes 1048608 | tf_op jit(solution)/shard_map/ppermute | solution.py:316
  125.8 0.0 collective-permute-start.19
  125.8 0.6 pad_add_fusion.keep
  126.4 0.0 all-to-all-done
  126.4 1.7 reshape.35.tokens
  128.1 6.3 %spatial_forward.1 = (bf16[128,1024]{1,0:T(8,128)(2,1)}, bf16[128,3072]{1,0:T(8,128)(2,1)}, f32[128,2048]{1,0:T(8,128)}) custom-call(bf16[128,1024]{1,0:T(8,128)(2,1)} %reshape.35.tokens, s32[1,256]{1,0:T(1,128)} %pad_add_fusion.keep, bf16[128,3072]{1,0:T(8,128)(2,1)} %copy-done.2, bf16[128,3072]{1,0:T(8,128)(2,1)} %copy-done.3, ...), custom_call_target="tpu_custom_call" | custom-call | flops 1073741824 | bytes 8388608 | tf_op jit(solution)/shard_map/spatial_forward/pallas_call | solution.py:341
  134.5 1.1 reshape.36
  135.5 16.0 %all_to_all.20 = bf16[32,4,1024]{2,1,0:T(4,128)(2,1)S(1)} all-to-all(bf16[32,4,1024]{2,1,0:T(4,128)(2,1)S(1)} %reshape.36), channel_id=1, replica_groups=mesh['parts'=1,'grid'=32] {'grid'}, dimensions={0} | all-to-all | bytes 524288 | tf_op jit(solution)/shard_map/all_to_all | solution.py:303
  151.6 0.8 reshape.37.attended
  152.4 0.0 collective-permute-done.16.refs_4_
  152.4 0.0 collective-permute-done.18.refs_6_
  152.4 0.0 collective-permute-done.17.refs_5_
  152.4 0.0 all-gather.2.cloned.1.call-done.w_go
  152.4 12.9 %group_layer.1 = (bf16[128,1024]{1,0:T(8,128)(2,1)}, bf16[128,1024]{1,0:T(8,128)(2,1)}, bf16[128,1024]{1,0:T(8,128)(2,1)}) custom-call(bf16[128,1024]{1,0:T(8,128)(2,1)} %bitcast.9, bf16[128,1024]{1,0:T(8,128)(2,1)} %reshape.37.attended, bf16[128,1024]{1,0:T(8,128)(2,1)} %bitcast.11, bf16[1024,1024]{1,0:T(8,128)(2,1)} %all-gather.2.cloned.1.call-done.w_go, ...), custom_call_target="tpu_custom_call" | custom-call | flops 2147483648 | bytes 8388608 | tf_op jit(solution)/shard_map/group_layer/pallas_call | solution.py:356
  165.4 1.1 reshape.41
  166.4 12.8 %all_to_all.21 = bf16[32,4,1024]{2,1,0:T(4,128)(2,1)S(1)} all-to-all(bf16[32,4,1024]{2,1,0:T(4,128)(2,1)S(1)} %reshape.41), channel_id=1, replica_groups=mesh['parts'=1,'grid'=32] {'grid'}, dimensions={0} | all-to-all | bytes 524288 | tf_op jit(solution)/shard_map/all_to_all | solution.py:303
  179.2 0.8 reshape.42.grad
  180.0 7.6 %spatial_backward.1 = bf16[128,1024]{1,0:T(8,128)(2,1)} custom-call(bf16[128,1024]{1,0:T(8,128)(2,1)} %reshape.35.tokens, bf16[128,1024]{1,0:T(8,128)(2,1)} %reshape.42.grad, bf16[128,3072]{1,0:T(8,128)(2,1)} %get-tuple-element.12.qkv, f32[128,2048]{1,0:T(8,128)} %get-tuple-element.13.probs, bf16[128,3072]{1,0:T(8,128)(2,1)} %copy-done.2, ...), custom_call_target="tpu_custom_call" | custom-call | flops 1073741824 | bytes 8388608 | tf_op jit(solution)/shard_map/spatial_backward/pallas_call | solution.py:377
  187.6 1.1 reshape.43
  188.6 12.8 %all_to_all.22 = bf16[32,4,1024]{2,1,0:T(4,128)(2,1)S(1)} all-to-all(bf16[32,4,1024]{2,1,0:T(4,128)(2,1)S(1)} %reshape.43), channel_id=1, replica_groups=mesh['parts'=1,'grid'=32] {'grid'}, dimensions={0} | all-to-all | bytes 524288 | tf_op jit(solution)/shard_map/all_to_all | solution.py:303
  201.4 0.2 bitcast_add_fusion
  201.7 0.8 copy.13
  (21 shorter events, 0.1 us)
Async XLA Ops:
  7.2 118.6 %copy-start = (s32[32,128]{1,0:T(8,128)S(1)}, s32[32,128]{1,0:T(8,128)}, u32[]{:S(2)}) copy-start(s32[32,128]{1,0:T(8,128)} %param.13) | copy-start | bytes 49156
  7.2 145.2 %all-gather.2.cloned.1.call-start = ((), (), s32[]{:S(2)}) async-start(), calls=%async_computation.4 | async-start | bytes 2162688 | tf_op jit(solution)/shard_map/all_gather | solution.py:336
  7.2 35.2 %collective-permute-start.1 = (bf16[32,3072]{1,0:T(8,128)(2,1)}, bf16[32,3072]{1,0:T(8,128)(2,1)S(1)}, u32[]{:S(2)}, u32[]{:S(2)}) collective-permute-start(bf16[32,3072]{1,0:T(8,128)(2,1)} %param.9), channel_id=1, source_target_pairs={{0,16},{1,17},{2,18},{3,19},{4,20},{5,21},{6,22},{7,23},{8,24},{9,... | collective-permute-start | bytes 589832 | tf_op jit(solution)/shard_map/ppermute | solution.py:316
  11.3 11.6 %collective-permute-start = (bf16[32,3072]{1,0:T(8,128)(2,1)}, bf16[32,3072]{1,0:T(8,128)(2,1)S(1)}, u32[]{:S(2)}, u32[]{:S(2)}) collective-permute-start(bf16[32,3072]{1,0:T(8,128)(2,1)} %param.9), channel_id=1, source_target_pairs={{0,8},{1,9},{2,10},{3,11},{4,12},{5,13},{6,14},{7,15},{8,16},{9,17... | collective-permute-start | bytes 589832 | tf_op jit(solution)/shard_map/ppermute | solution.py:316
  12.9 41.8 %collective-permute-start.2 = (bf16[32,3072]{1,0:T(8,128)(2,1)}, bf16[32,3072]{1,0:T(8,128)(2,1)S(1)}, u32[]{:S(2)}, u32[]{:S(2)}) collective-permute-start(bf16[32,3072]{1,0:T(8,128)(2,1)} %param.9), channel_id=1, source_target_pairs={{0,24},{1,25},{2,26},{3,27},{4,28},{5,29},{6,30},{7,31},{8,0},{9,1... | collective-permute-start | bytes 589832 | tf_op jit(solution)/shard_map/ppermute | solution.py:316
  16.9 25.5 %collective-permute-start.12 = (bf16[32,4096]{1,0:T(8,128)(2,1)S(1)}, bf16[32,4096]{1,0:T(8,128)(2,1)S(1)}, u32[]{:S(2)}, u32[]{:S(2)}) collective-permute-start(bf16[32,4096]{1,0:T(8,128)(2,1)S(1)} %constant_dynamic-update-slice_fusion.4), channel_id=1, source_target_pairs={{0,24},{1,25},{2,26},{3,27},{4,28},{5,29},{6,30},{7,31},{8,0},{9,1... | collective-permute-start | bytes 786440 | tf_op jit(solution)/shard_map/ppermute | solution.py:316
  17.0 36.0 %collective-permute-start.11 = (bf16[32,4096]{1,0:T(8,128)(2,1)S(1)}, bf16[32,4096]{1,0:T(8,128)(2,1)S(1)}, u32[]{:S(2)}, u32[]{:S(2)}) collective-permute-start(bf16[32,4096]{1,0:T(8,128)(2,1)S(1)} %constant_dynamic-update-slice_fusion.4), channel_id=1, source_target_pairs={{0,16},{1,17},{2,18},{3,19},{4,20},{5,21},{6,22},{7,23},{8,24},{9,... | collective-permute-start | bytes 786440 | tf_op jit(solution)/shard_map/ppermute | solution.py:316
  18.3 82.4 %copy-start.6 = (bf16[4,32,1024]{2,1,0:T(8,128)(2,1)S(1)}, bf16[4,32,1024]{2,1,0:T(8,128)(2,1)}, u32[]{:S(2)}) copy-start(bf16[4,32,1024]{2,1,0:T(8,128)(2,1)} %param.7) | copy-start | bytes 786436
  23.0 30.0 %collective-permute-start.10 = (bf16[32,4096]{1,0:T(8,128)(2,1)S(1)}, bf16[32,4096]{1,0:T(8,128)(2,1)S(1)}, u32[]{:S(2)}, u32[]{:S(2)}) collective-permute-start(bf16[32,4096]{1,0:T(8,128)(2,1)S(1)} %constant_dynamic-update-slice_fusion.4), channel_id=1, source_target_pairs={{0,8},{1,9},{2,10},{3,11},{4,12},{5,13},{6,14},{7,15},{8,16},{9,17... | collective-permute-start | bytes 786440 | tf_op jit(solution)/shard_map/ppermute | solution.py:316
  53.1 81.4 %copy-start.1 = (bf16[128,4096]{1,0:T(8,128)(2,1)}, bf16[128,4096]{1,0:T(8,128)(2,1)S(1)}, u32[]{:S(2)}) copy-start(bf16[128,4096]{1,0:T(8,128)(2,1)S(1)} %pad_maximum_fusion.refs_0_) | copy-start | bytes 3145732
  53.1 37.5 %collective-permute-start.13 = (bf16[128,4096]{1,0:T(8,128)(2,1)S(1)}, bf16[128,4096]{1,0:T(8,128)(2,1)}, u32[]{:S(2)}, u32[]{:S(2)}) collective-permute-start(bf16[128,4096]{1,0:T(8,128)(2,1)S(1)} %pad_maximum_fusion.refs_0_), channel_id=1, source_target_pairs={{0,2},{1,5},{2,0},{3,7},{4,6},{5,1},{6,4},{7,3},{8,10},{9,13},{10,... | collective-permute-start | bytes 3145736 | tf_op jit(solution)/shard_map/ppermute | solution.py:316
  54.7 73.4 %copy-start.2 = (bf16[128,3072]{1,0:T(8,128)(2,1)}, bf16[128,3072]{1,0:T(8,128)(2,1)S(1)}, u32[]{:S(2)}) copy-start(bf16[128,3072]{1,0:T(8,128)(2,1)S(1)} %constant_dynamic-update-slice_fusion.refs_0_) | copy-start | bytes 2359300
  54.7 33.9 %collective-permute-start.3 = (bf16[128,3072]{1,0:T(8,128)(2,1)S(1)}, bf16[128,3072]{1,0:T(8,128)(2,1)S(1)}, u32[]{:S(2)}, u32[]{:S(2)}) collective-permute-start(bf16[128,3072]{1,0:T(8,128)(2,1)S(1)} %constant_dynamic-update-slice_fusion.refs_0_), channel_id=1, source_target_pairs={{0,2},{1,5},{2,0},{3,7},{4,6},{5,1},{6,4},{7,3},{8,10},{9,13},{10,... | collective-permute-start | bytes 2359304 | tf_op jit(solution)/shard_map/ppermute | solution.py:316
  55.3 36.8 %collective-permute-start.4 = (bf16[128,3072]{1,0:T(8,128)(2,1)S(1)}, bf16[128,3072]{1,0:T(8,128)(2,1)S(1)}, u32[]{:S(2)}, u32[]{:S(2)}) collective-permute-start(bf16[128,3072]{1,0:T(8,128)(2,1)S(1)} %constant_dynamic-update-slice_fusion.refs_0_), channel_id=1, source_target_pairs={{0,4},{1,3},{2,6},{3,1},{4,0},{5,7},{6,2},{7,5},{8,12},{9,11},{10,... | collective-permute-start | bytes 2359304 | tf_op jit(solution)/shard_map/ppermute | solution.py:316
  56.9 35.3 %collective-permute-start.6 = (bf16[128,3072]{1,0:T(8,128)(2,1)S(1)}, bf16[128,3072]{1,0:T(8,128)(2,1)S(1)}, u32[]{:S(2)}, u32[]{:S(2)}) collective-permute-start(bf16[128,3072]{1,0:T(8,128)(2,1)S(1)} %constant_dynamic-update-slice_fusion.refs_0_), channel_id=1, source_target_pairs={{0,1},{1,0},{2,3},{3,2},{4,5},{5,4},{6,7},{7,6},{8,9},{9,8},{10,11... | collective-permute-start | bytes 2359304 | tf_op jit(solution)/shard_map/ppermute | solution.py:316
  88.6 39.5 %copy-start.3 = (bf16[128,3072]{1,0:T(8,128)(2,1)}, bf16[128,3072]{1,0:T(8,128)(2,1)S(1)}, u32[]{:S(2)}) copy-start(bf16[128,3072]{1,0:T(8,128)(2,1)S(1)} %collective-permute-done.3.refs_1_) | copy-start | bytes 2359300
  88.6 12.1 %collective-permute-start.5 = (bf16[128,3072]{1,0:T(8,128)(2,1)S(1)}, bf16[128,3072]{1,0:T(8,128)(2,1)}, u32[]{:S(2)}, u32[]{:S(2)}) collective-permute-start(bf16[128,3072]{1,0:T(8,128)(2,1)S(1)} %collective-permute-done.3.refs_1_), channel_id=1, source_target_pairs={{0,4},{1,3},{2,6},{3,1},{4,0},{5,7},{6,2},{7,5},{8,12},{9,11},{10,... | collective-permute-start | bytes 2359304 | tf_op jit(solution)/shard_map/ppermute | solution.py:316
  90.1 23.0 %collective-permute-start.14 = (bf16[128,4096]{1,0:T(8,128)(2,1)S(1)}, bf16[128,4096]{1,0:T(8,128)(2,1)}, u32[]{:S(2)}, u32[]{:S(2)}) collective-permute-start(bf16[128,4096]{1,0:T(8,128)(2,1)S(1)} %pad_maximum_fusion.refs_0_), channel_id=1, source_target_pairs={{0,4},{1,3},{2,6},{3,1},{4,0},{5,7},{6,2},{7,5},{8,12},{9,11},{10,... | collective-permute-start | bytes 3145736 | tf_op jit(solution)/shard_map/ppermute | solution.py:316
  90.6 35.2 %collective-permute-start.15 = (bf16[128,4096]{1,0:T(8,128)(2,1)}, bf16[128,4096]{1,0:T(8,128)(2,1)}, u32[]{:S(2)}, u32[]{:S(2)}) collective-permute-start(bf16[128,4096]{1,0:T(8,128)(2,1)} %collective-permute-done.13.refs_1_), channel_id=1, source_target_pairs={{0,4},{1,3},{2,6},{3,1},{4,0},{5,7},{6,2},{7,5},{8,12},{9,11},{10,... | collective-permute-start | bytes 3145736 | tf_op jit(solution)/shard_map/ppermute | solution.py:316
  92.1 36.0 %copy-start.4 = (bf16[128,3072]{1,0:T(8,128)(2,1)}, bf16[128,3072]{1,0:T(8,128)(2,1)S(1)}, u32[]{:S(2)}) copy-start(bf16[128,3072]{1,0:T(8,128)(2,1)S(1)} %collective-permute-done.4.refs_2_) | copy-start | bytes 2359300
  92.1 21.0 %collective-permute-start.8 = (bf16[128,3072]{1,0:T(8,128)(2,1)S(1)}, bf16[128,3072]{1,0:T(8,128)(2,1)}, u32[]{:S(2)}, u32[]{:S(2)}) collective-permute-start(bf16[128,3072]{1,0:T(8,128)(2,1)S(1)} %collective-permute-done.4.refs_2_), channel_id=1, source_target_pairs={{0,1},{1,0},{2,3},{3,2},{4,5},{5,4},{6,7},{7,6},{8,9},{9,8},{10,11... | collective-permute-start | bytes 2359304 | tf_op jit(solution)/shard_map/ppermute | solution.py:316
  92.1 8.6 %copy-start.5 = (bf16[128,3072]{1,0:T(8,128)(2,1)}, bf16[128,3072]{1,0:T(8,128)(2,1)S(1)}, u32[]{:S(2)}) copy-start(bf16[128,3072]{1,0:T(8,128)(2,1)S(1)} %collective-permute-done.6.refs_4_) | copy-start | bytes 2359300
  92.1 21.4 %collective-permute-start.7 = (bf16[128,3072]{1,0:T(8,128)(2,1)S(1)}, bf16[128,3072]{1,0:T(8,128)(2,1)}, u32[]{:S(2)}, u32[]{:S(2)}) collective-permute-start(bf16[128,3072]{1,0:T(8,128)(2,1)S(1)} %collective-permute-done.3.refs_1_), channel_id=1, source_target_pairs={{0,1},{1,0},{2,3},{3,2},{4,5},{5,4},{6,7},{7,6},{8,9},{9,8},{10,11... | collective-permute-start | bytes 2359304 | tf_op jit(solution)/shard_map/ppermute | solution.py:316
  100.7 27.4 %collective-permute-start.9 = (bf16[128,3072]{1,0:T(8,128)(2,1)}, bf16[128,3072]{1,0:T(8,128)(2,1)}, u32[]{:S(2)}, u32[]{:S(2)}) collective-permute-start(bf16[128,3072]{1,0:T(8,128)(2,1)} %collective-permute-done.5.refs_3_), channel_id=1, source_target_pairs={{0,1},{1,0},{2,3},{3,2},{4,5},{5,4},{6,7},{7,6},{8,9},{9,8},{10,11... | collective-permute-start | bytes 2359304 | tf_op jit(solution)/shard_map/ppermute | solution.py:316
  101.6 24.8 %all-to-all-start = ((bf16[32,4,1024]{2,1,0:T(4,128)(2,1)}), bf16[32,4,1024]{2,1,0:T(4,128)(2,1)}, u32[]{:S(2)}, u32[]{:S(2)}) async-start(bf16[32,4,1024]{2,1,0:T(4,128)(2,1)} %bitcast.10), calls=%async_computation | async-start | bytes 524288 | tf_op jit(solution)/shard_map/all_to_all | solution.py:303
  113.0 39.3 %collective-permute-start.16 = (bf16[128,4096]{1,0:T(8,128)(2,1)S(1)}, bf16[128,4096]{1,0:T(8,128)(2,1)}, u32[]{:S(2)}, u32[]{:S(2)}) collective-permute-start(bf16[128,4096]{1,0:T(8,128)(2,1)S(1)} %pad_maximum_fusion.refs_0_), channel_id=1, source_target_pairs={{0,1},{1,0},{2,3},{3,2},{4,5},{5,4},{6,7},{7,6},{8,9},{9,8},{10,11... | collective-permute-start | bytes 3145736 | tf_op jit(solution)/shard_map/ppermute | solution.py:316
  113.1 39.3 %collective-permute-start.17 = (bf16[128,4096]{1,0:T(8,128)(2,1)}, bf16[128,4096]{1,0:T(8,128)(2,1)}, u32[]{:S(2)}, u32[]{:S(2)}) collective-permute-start(bf16[128,4096]{1,0:T(8,128)(2,1)} %collective-permute-done.13.refs_1_), channel_id=1, source_target_pairs={{0,1},{1,0},{2,3},{3,2},{4,5},{5,4},{6,7},{7,6},{8,9},{9,8},{10,11... | collective-permute-start | bytes 3145736 | tf_op jit(solution)/shard_map/ppermute | solution.py:316
  113.6 38.8 %collective-permute-start.18 = (bf16[128,4096]{1,0:T(8,128)(2,1)}, bf16[128,4096]{1,0:T(8,128)(2,1)}, u32[]{:S(2)}, u32[]{:S(2)}) collective-permute-start(bf16[128,4096]{1,0:T(8,128)(2,1)} %collective-permute-done.14.refs_2_), channel_id=1, source_target_pairs={{0,1},{1,0},{2,3},{3,2},{4,5},{5,4},{6,7},{7,6},{8,9},{9,8},{10,11... | collective-permute-start | bytes 3145736 | tf_op jit(solution)/shard_map/ppermute | solution.py:316
  125.8 26.6 %collective-permute-start.19 = (bf16[128,4096]{1,0:T(8,128)(2,1)}, bf16[128,4096]{1,0:T(8,128)(2,1)}, u32[]{:S(2)}, u32[]{:S(2)}) collective-permute-start(bf16[128,4096]{1,0:T(8,128)(2,1)} %collective-permute-done.15.refs_3_), channel_id=1, source_target_pairs={{0,1},{1,0},{2,3},{3,2},{4,5},{5,4},{6,7},{7,6},{8,9},{9,8},{10,11... | collective-permute-start | bytes 3145736 | tf_op jit(solution)/shard_map/ppermute | solution.py:316
  180.0 21.4 %copy-start.7 = (bf16[128,1024]{1,0:T(8,128)(2,1)S(1)}, bf16[128,1024]{1,0:T(8,128)(2,1)}, u32[]{:S(2)}) copy-start(bf16[128,1024]{1,0:T(8,128)(2,1)} %get-tuple-element.10) | copy-start | bytes 786436
Sparse Core Ops, SparseCore 0:
  18.4 68.6 all-gather.1

commit v3 on v2

--- a/solution.py
+++ b/solution.py
@@ -168,22 +168,20 @@
     return grad_query, grad_key, grad_value
 
 
-def place_rows(pieces, first, buffer, sem, rows_each):
+def place_rows(refs, plan, first, buffer, sem):
     position = lax.axis_index("grid")
-    size = buffer.shape[0] // rows_each
-    core = position % 2
-    one, other = 2 * (core + 1), 4 // (core + 1)
-    own = (0, one, other, 6)
-    sibling = (0, other, one, 6)
-    depth = len(pieces) // 2
-    for at, piece in enumerate(pieces):
-        flip = own[at] if at < depth else sibling[at - depth]
-        base = (position if at < depth else position + 1 - 2 * core) ^ flip
-        for step in range(piece.shape[0] // rows_each):
-            shard = lax.rem(base + size - 8 * step, size)
+    size = lax.axis_size("grid")
+    each = buffer.shape[0] // size
+    core = lax.rem(position, 2)
+    for ref, (from_sibling, blocks) in zip(refs, plan):
+        side = 1 - core if from_sibling else core
+        holder = position + 1 - 2 * core if from_sibling else position
+        flips = (0, 2 * (side + 1), 4 - 2 * side, 6)
+        for at, (step, flip) in enumerate(blocks):
+            shard = lax.rem((holder ^ flips[flip]) + (size - 8 * step), size)
             pltpu.make_async_copy(
-                piece.at[pl.ds(step * rows_each, rows_each), pl.ds(first, buffer.shape[1])],
-                buffer.at[pl.ds(pl.multiple_of(shard * rows_each, rows_each), rows_each)],
+                ref.at[pl.ds(at * each, each), pl.ds(first, buffer.shape[1])],
+                buffer.at[pl.ds(pl.multiple_of(shard * each, each), each)],
                 sem,
             ).start()
 
@@ -192,29 +190,74 @@
     pltpu.make_async_copy(buffer, buffer, sem).wait()
 
 
-def spatial_forward(tokens, keep, *refs):
+def packed_row(row, half, patches, groups, by_band):
+    band, patch = (row // patches, row % patches) if by_band else (row % groups, row // groups)
+    return (band * 2 + half) * patches + patch
+
+
+def unpack(packed, patches, groups, by_band):
+    rows = packed.shape[0] // 2
+    row = lax.broadcasted_iota(jnp.int32, (rows, 2 * rows), 0)
+    there = lax.broadcasted_iota(jnp.int32, (rows, 2 * rows), 1)
+    parts = []
+    for half in range(2):
+        chosen = (there == packed_row(row, half, patches, groups, by_band)).astype(jnp.bfloat16)
+        parts.append(nn(chosen, packed))
+    return jnp.concatenate(parts, axis=1).astype(jnp.bfloat16)
+
+
+def pack(values, patches, groups, by_band):
+    rows, width = values.shape
+    row = lax.broadcasted_iota(jnp.int32, (2 * rows, rows), 1)
+    there = lax.broadcasted_iota(jnp.int32, (2 * rows, rows), 0)
+    total = 0.0
+    for half in range(2):
+        chosen = (there == packed_row(row, half, patches, groups, by_band)).astype(jnp.bfloat16)
+        total += nn(chosen, values[:, half * (width // 2) : (half + 1) * (width // 2)])
+    return total.astype(jnp.bfloat16)
+
+
+def prepare(patches, groups, tokens, w_so, w_gqkv, w_go, packed, joined, first_two):
+    packed[...] = pack(tokens[...], patches, groups, False)
+    width = w_so.shape[1]
+    joined[:, :width] = w_so[...]
+    joined[:, width : 4 * width] = w_gqkv[...]
+    joined[:, 4 * width :] = w_go[...]
+    first_two[:, :width] = w_so[...]
+    first_two[:, width:] = w_gqkv[...]
+
+
+def add_packed(patches, groups, values, packed, total):
+    total[...] = values[...] + unpack(packed[...], patches, groups, False)
+
+
+def spatial_forward(plan, patches, groups, packed, keep, *refs):
     pieces, (result_out, qkv_out, probs_out, qkv_buf, sems) = refs[:-5], refs[-5:]
-    rows, width = tokens.shape
+    rows, width = packed.shape[0] // 2, packed.shape[1] * 2
     span = 2 * rows
-    place_rows(pieces, 0, qkv_buf, sems.at[0], width // lax.axis_size("grid"))
-    wide = tokens[...].astype(jnp.float32)
+    place_rows(pieces, plan, 0, qkv_buf, sems.at[0])
+    wide = unpack(packed[...], patches, groups, True).astype(jnp.float32)
     normed = (wide * inverse_rms(wide)).astype(jnp.bfloat16)
-    allowed = keep[...] > 0
+    kept = keep[pl.ds(lax.axis_index("grid"), 1), :]
+    allowed = jnp.concatenate([kept, kept], axis=1) > 0
     low = low_lanes(rows)
     wait_rows(qkv_buf, sems.at[0])
     qkv_out[...] = nn(normed, qkv_buf[...]).astype(jnp.bfloat16)
+    results = []
     for pair in range(width // 128):
         probs, result = pair_forward(qkv_out, allowed, low, width, pair)
         probs_out[:, pair * span : pair * span + span] = probs
-        result_out[:, pair * 128 : pair * 128 + 128] = result
-
-
-def spatial_backward(tokens, grad, qkv, probs, *refs):
+        results.append(result)
+    result_out[...] = pack(jnp.concatenate(results, axis=1), patches, groups, True)
+
+
+def spatial_backward(plan, patches, groups, packed, grad_packed, qkv, probs, *refs):
     pieces, (grad_out, qkv_buf, grads, sems) = refs[:-4], refs[-4:]
-    rows, width = tokens.shape
+    rows, width = packed.shape[0] // 2, packed.shape[1] * 2
     span = 2 * rows
-    place_rows(pieces, 0, qkv_buf, sems.at[0], width // lax.axis_size("grid"))
+    place_rows(pieces, plan, 0, qkv_buf, sems.at[0])
     low = low_lanes(rows)
+    grad = unpack(grad_packed[...], patches, groups, True)
     for pair in range(width // 128):
         at = pair * 128
         parts = pair_backward(
@@ -222,33 +265,27 @@
         )
         for which, part in enumerate(parts):
             grads[:, which * width + at : which * width + at + 128] = part
-    wide = tokens[...].astype(jnp.float32)
+    wide = unpack(packed[...], patches, groups, True).astype(jnp.float32)
     inverse = inverse_rms(wide)
     wait_rows(qkv_buf, sems.at[0])
     grad_normed = nt(grads[...], qkv_buf[...]).astype(jnp.bfloat16).astype(jnp.float32)
-    grad_out[...] = norm_grad(wide, inverse, grad_normed).astype(jnp.bfloat16)
-
-
-def reorder(patches, groups, backward):
-    rows = patches * groups
-    here = lax.broadcasted_iota(jnp.int32, (rows, rows), 1 if backward else 0)
-    there = lax.broadcasted_iota(jnp.int32, (rows, rows), 0 if backward else 1)
-    patch, group = here // groups, here % groups
-    return (there == group * patches + patch).astype(jnp.bfloat16)
-
-
-def group_layer(patches, tokens, attended, cotangent, w_go, *refs):
-    pieces, rest = refs[:-12], refs[-12:]
-    mixed, grad_y, grad_bands, so_buf, qkv_buf, go_buf, qkv, grads, probs_buf, y_buf, go_sem, sems = rest
+    grad_out[...] = pack(norm_grad(wide, inverse, grad_normed).astype(jnp.bfloat16), patches, groups, True)
+
+
+def group_layer(patches, own_plan, plan, go_plan, tokens, attended, cotangent, *refs):
+    pieces, rest = refs[:-11], refs[-11:]
+    mixed, grad_y, grad_bands, so_buf, qkv_buf, go_buf, qkv, grads, probs_buf, y_buf, sems = rest
     rows, width = tokens.shape
     groups = rows // patches
     span = 2 * rows
-    each = width // lax.axis_size("grid")
-    place_rows(pieces, 0, so_buf, sems.at[0], each)
-    place_rows(pieces, width, qkv_buf, sems.at[1], each)
-    load_go = pltpu.make_async_copy(w_go, go_buf, go_sem)
-    load_go.start()
-    ordered = nn(reorder(patches, groups, False), attended[...]).astype(jnp.bfloat16)
+    own, pieces, out = pieces[:2], pieces[2:-4], pieces[-4:]
+    place_rows(own, own_plan, 0, so_buf, sems.at[0])
+    place_rows(pieces, plan, 0, so_buf, sems.at[0])
+    place_rows(own, own_plan, width, qkv_buf, sems.at[1])
+    place_rows(pieces, plan, width, qkv_buf, sems.at[1])
+    place_rows(own, own_plan, 4 * width, go_buf, sems.at[2])
+    place_rows(out, go_plan, 0, go_buf, sems.at[2])
+    ordered = unpack(attended[...], patches, groups, False)
     low = low_lanes(rows)
     row_patch = lax.broadcasted_iota(jnp.int32, (rows, span), 0) // groups
     column_patch = (lax.broadcasted_iota(jnp.int32, (rows, span), 1) % rows) // groups
@@ -266,7 +303,7 @@
         probs, result = pair_forward(qkv, allowed, low, width, pair)
         probs_buf[:, pair * span : pair * span + span] = probs
         results.append(result)
-    load_go.wait()
+    wait_rows(go_buf, sems.at[2])
     mixed[...] = (y_buf[...] + nn(jnp.concatenate(results, axis=1), go_buf[...])).astype(jnp.bfloat16)
     grad_attended = nt(cotangent[...], go_buf[...]).astype(jnp.bfloat16)
     for pair in range(width // 128):
@@ -281,11 +318,11 @@
     total = cotangent[...] + through
     grad_y[...] = total
     spread = nt(total, so_buf[...]).astype(jnp.bfloat16)
-    grad_bands[...] = nn(reorder(patches, groups, True), spread).astype(jnp.bfloat16)
+    grad_bands[...] = pack(spread, patches, groups, False)
 
 
 VMEM_SPEC = pl.BlockSpec(memory_space=pltpu.VMEM)
-ANY_SPEC = pl.BlockSpec(memory_space=pl.ANY)
+ANY_SPEC = pl.BlockSpec(memory_space=pltpu.HBM)
 PARAMS = pltpu.CompilerParams(vmem_limit_bytes=56 * 1024 * 1024)
 
 
@@ -299,8 +336,11 @@
     )
 
 
-def exchange(values):
-    return lax.all_to_all(values, "grid", split_axis=0, concat_axis=0, tiled=True)
+def exchange(packed):
+    size = lax.axis_size("grid")
+    rows, columns = packed.shape
+    blocks = packed.reshape(size, rows // size, columns)
+    return lax.all_to_all(blocks, "grid", split_axis=0, concat_axis=0, tiled=True).reshape(rows, columns)
 
 
 def mesh_moves(size):
@@ -316,32 +356,75 @@
     return lax.ppermute(values, "grid", table)
 
 
-def gather_rows(shard):
-    first, second, sibling, along = mesh_moves(lax.axis_size("grid"))
-    line = jnp.concatenate([shard] + [move(shard, table) for table in along], axis=0)
-    one = move(line, first)
-    other = move(line, second)
-    both = move(one, second)
-    held = [line, one, other, both]
-    return held + [move(block, sibling) for block in held]
+def together(*values):
+    return lax.optimization_barrier(values)
+
+
+def stack(*values):
+    return jnp.concatenate(values, axis=0)
+
+
+def plans(size):
+    steps = range(size // 8)
+    line = [[(step, flip) for step in steps] for flip in range(4)]
+    own, rest = [(0, flip) for flip in range(4)], [[(step, flip) for step in steps[1:]] for flip in range(4)]
+    out = [(step, flip) for step in steps[1:] for flip in range(4)]
+
+    def plan(held, across):
+        return [(False, blocks) for blocks in held] + [(True, blocks) for blocks in across]
+
+    return (
+        plan(line, [line[0], line[1] + line[2], line[3]]),
+        plan([own], [own]),
+        plan([rest[0] + rest[1] + rest[2], rest[3]], [rest[0] + rest[1] + rest[2], rest[3]]),
+        plan([out[:-4], out[-4:]], [out[:-4], out[-4:]]),
+    )
 
 
 def banded_layer(tokens, cotangent, w_sqkv, w_so, w_gqkv, w_go, keep):
     patches, groups, width = tokens.shape
     rows = patches * groups
     all_patches = patches * lax.axis_size("grid")
-    position = lax.axis_index("grid")
-    spatial_rows = gather_rows(w_sqkv)
-    group_rows = gather_rows(jnp.concatenate([w_so, w_gqkv], axis=1))
-    full_go = lax.all_gather(w_go, "grid", axis=0, tiled=True)
-    banded = exchange(tokens.transpose(1, 0, 2)).reshape(all_patches, width)
-    keep_row = lax.dynamic_slice_in_dim(keep, position, 1, 0)
-    keep_row = jnp.concatenate([keep_row, keep_row], axis=1)
+    first, second, sibling, along = mesh_moves(lax.axis_size("grid"))
+    spatial_plan, *group_plans = plans(lax.axis_size("grid"))
     pairs = width // 128
+    packed_shape = shape(2 * rows, width // 2)
+
+    tokens = tokens.reshape(rows, width)
+    packed, own, group = pl.pallas_call(
+        partial(prepare, patches, groups),
+        out_shape=(packed_shape, shape(w_so.shape[0], 5 * width), shape(w_so.shape[0], 4 * width)),
+        in_specs=[VMEM_SPEC] * 4,
+        out_specs=(VMEM_SPEC,) * 3,
+        name="prepare",
+    )(tokens, w_so, w_gqkv, w_go)
+    spatial_line = [w_sqkv] + [move(w_sqkv, table) for table in along]
+    own_one, own_other = move(own, first), move(own, second)
+    spatial_line, own_one, own_other, banded, group = together(
+        stack(*spatial_line), own_one, own_other, exchange(packed), group
+    )
+    spatial_one, spatial_other = move(spatial_line, first), move(spatial_line, second)
+    group_parts = [move(group, table) for table in along[:-1]]
+    own_both = move(own_one, second)
+    spatial_one, spatial_other, own_plane, group, spatial_line, *group_parts = together(
+        spatial_one, spatial_other, stack(own, own_one, own_other, own_both), group, spatial_line, *group_parts
+    )
+    out_plane = own_plane[:, 4 * width :]
+    spatial_both = move(spatial_one, second)
+    spatial_line_x = move(spatial_line, sibling)
+    spatial_pair_x = move(stack(spatial_one, spatial_other), sibling)
+    group_parts.append(move(group, along[-1]))
+    spatial_both, spatial_line_x, spatial_pair_x, group_line, out_plane = together(
+        spatial_both, spatial_line_x, spatial_pair_x, stack(*group_parts), out_plane
+    )
+    group_one, group_other = move(group_line, first), move(group_line, second)
+    out_parts = [move(out_plane, table) for table in along[:-1]]
+    spatial_rows = [spatial_line, spatial_one, spatial_other, spatial_both]
+    spatial_rows += [spatial_line_x, spatial_pair_x, move(spatial_both, sibling)]
     attended, qkv, probs = pl.pallas_call(
-        spatial_forward,
+        partial(spatial_forward, spatial_plan, patches, groups),
         out_shape=(
-            shape(all_patches, width),
+            packed_shape,
             shape(all_patches, 3 * width),
             shape(all_patches, 2 * pairs * all_patches, jnp.float32),
         ),
@@ -351,12 +434,27 @@
         compiler_params=PARAMS,
         cost_estimate=cost(all_patches, width, 1),
         name="spatial_forward",
-    )(banded, keep_row, *spatial_rows)
-    attended = exchange(attended.reshape(groups, patches, width)).reshape(rows, width)
+    )(banded, keep, *spatial_rows)
+    group_one, group_other, attended, own_plane, group_line, out_plane, *out_parts = together(
+        group_one, group_other, attended, own_plane, group_line, out_plane, *out_parts
+    )
+    group_both = move(group_one, second)
+    out_last = move(out_plane, along[-1])
+    group_most, out_most = stack(group_line, group_one, group_other), stack(*out_parts)
+    group_both, attended, own_plane_x, group_most_x, out_last, out_most_x = together(
+        group_both,
+        exchange(attended),
+        move(own_plane, sibling),
+        move(group_most, sibling),
+        out_last,
+        move(out_most, sibling),
+    )
+    group_rows = [own_plane, own_plane_x, group_most, group_both, group_most_x, move(group_both, sibling)]
+    group_rows += [out_most, out_last, out_most_x, move(out_last, sibling)]
     mixed, grad_y, grad_bands = pl.pallas_call(
-        partial(group_layer, patches),
-        out_shape=(shape(rows, width),) * 3,
-        in_specs=[VMEM_SPEC] * 3 + [ANY_SPEC] * (1 + len(group_rows)),
+        partial(group_layer, patches, *group_plans),
+        out_shape=(shape(rows, width), shape(rows, width), packed_shape),
+        in_specs=[VMEM_SPEC] * 3 + [ANY_SPEC] * len(group_rows),
         out_specs=(VMEM_SPEC,) * 3,
         scratch_shapes=[
             pltpu.VMEM((width, width), jnp.bfloat16),
@@ -366,17 +464,15 @@
             pltpu.VMEM((rows, 3 * width), jnp.bfloat16),
             pltpu.VMEM((rows, 2 * pairs * rows), jnp.float32),
             pltpu.VMEM((rows, width), jnp.float32),
-            pltpu.SemaphoreType.DMA,
-            pltpu.SemaphoreType.DMA((2,)),
+            pltpu.SemaphoreType.DMA((3,)),
         ],
         compiler_params=PARAMS,
         cost_estimate=cost(rows, width, 2),
         name="group_layer",
-    )(tokens.reshape(rows, width), attended, cotangent.reshape(rows, width), full_go, *group_rows)
-    grad_banded = exchange(grad_bands.reshape(groups, patches, width)).reshape(all_patches, width)
+    )(tokens, attended, cotangent.reshape(rows, width), *group_rows)
     grad_first = pl.pallas_call(
-        spatial_backward,
-        out_shape=shape(all_patches, width),
+        partial(spatial_backward, spatial_plan, patches, groups),
+        out_shape=packed_shape,
         in_specs=[VMEM_SPEC] * 4 + [ANY_SPEC] * len(spatial_rows),
         out_specs=VMEM_SPEC,
         scratch_shapes=[
@@ -387,16 +483,22 @@
         compiler_params=PARAMS,
         cost_estimate=cost(all_patches, width, 1),
         name="spatial_backward",
-    )(banded, grad_banded, qkv, probs, *spatial_rows)
-    grad_first = exchange(grad_first.reshape(groups, patches, width)).transpose(1, 0, 2)
+    )(banded, exchange(grad_bands), qkv, probs, *spatial_rows)
+    token_grad = pl.pallas_call(
+        partial(add_packed, patches, groups),
+        out_shape=shape(rows, width),
+        in_specs=[VMEM_SPEC] * 2,
+        out_specs=VMEM_SPEC,
+        name="add_packed",
+    )(grad_y, exchange(grad_first))
     whole = (patches, groups, width)
-    return (mixed.reshape(whole), grad_y.reshape(whole) + grad_first)
+    return (mixed.reshape(whole), token_grad.reshape(whole))
 
 
 def local(tokens, cotangent, w_sqkv, w_so, w_gqkv, w_go, keep):
     patches, groups, width = tokens.shape
     size = lax.axis_size("grid")
-    fits = size == groups and size % 8 == 0 and width % (16 * size) == 0 and width == 64 * H and patches * groups % 128 == 0 and patches * size % 128 == 0
+    fits = size == groups and size % 8 == 0 and width % (16 * size) == 0 and width == 64 * H and patches * groups % 128 == 0 and 2 * patches % 8 == 0
     layer = banded_layer if fits else general_layer
     return layer(tokens, cotangent, w_sqkv, w_so, w_gqkv, w_go, keep)
 

time: 210 us -> 166 us (0.79)
  waiting for transfers between devices: 71.9 us -> 53.5 us
  between operations: 14.2 us -> 0.91 us
  blocking collectives: 41.7 us -> 30.5 us
  local copies, waits for them, and re-layouts: 11 us -> 4.9 us
  Pallas kernels: 26.8 us -> 31.4 us
  other arithmetic: 0.93 us -> 3.25 us
    ppermute x20 -> x26, waiting for transfers between devices: 71.9 us -> 49.8 us  [move(): return lax.ppermute(values, 'grid', table)]
    all_to_all x3 -> x2, blocking collectives: 41.7 us -> 30.5 us  [exchange(): lax.all_to_all(blocks, 'grid', split_axis=0, concat_axis=0, tiled=True)]
    reshape x6 -> x0, local copies, waits for them, and re-layouts: 6.42 us -> none  [the longest x1 1.72 us: banded_layer(): banded = exchange(tokens.transpose(1, 0, 2)).reshape(all_patches, width)]
    pallas_call x3 -> x5, Pallas kernels: 26.8 us -> 31.4 us  [the longest x1 13 us: banded_layer(): pl.pallas_call(partial(group_layer, patches, *group_plans), out_shape=(sh...]
    all_to_all x1 -> x2, waiting for transfers between devices: 0.01 us -> 3.74 us  [exchange(): lax.all_to_all(blocks, 'grid', split_axis=0, concat_axis=0, tiled=True)]
    concatenate x2 -> x4, other arithmetic: 0.69 us -> 3.25 us  [stack(): return jnp.concatenate(values, axis=0)]
    ppermute x20 -> x26, starting transfers between devices: 36.9 us -> 34.9 us  [move(): return lax.ppermute(values, 'grid', table)]
    all_to_all x1 -> x2, starting transfers between devices: 5.78 us -> 6.28 us  [exchange(): lax.all_to_all(blocks, 'grid', split_axis=0, concat_axis=0, tiled=True)]
  transfers between devices with their start and end apart: 22 -> 28, of which waited for: 6 -> 13; matrix products, arithmetic and copies ran while one was open for 4% -> 3% of each run, Pallas kernels for 3% -> 5%
where the time goes in v3:
time: 166 us
  waiting for transfers between devices  53.5 us (32%)
  starting transfers between devices  41.2 us (25%)
  Pallas kernels  31.4 us (19%)
  blocking collectives  30.5 us (18%)
  local copies, waits for them, and re-layouts  4.9 us (3%)
  other arithmetic  3.25 us (2%)
    ppermute x26, waiting for transfers between devices, move(): return lax.ppermute(values, 'grid', table)  49.8 us
    ppermute x26, starting transfers between devices, move(): return lax.ppermute(values, 'grid', table)  34.9 us
    all_to_all x2, blocking collectives, exchange(): lax.all_to_all(blocks, 'grid', split_axis=0, concat_axis=0, tiled=True)  30.5 us
    pallas_call x1, Pallas kernels, banded_layer(): pl.pallas_call(partial(group_layer, patches, *group_plans), out_shape=(sh...  13 us
    pallas_call x1, Pallas kernels, banded_layer(): pl.pallas_call(partial(spatial_backward, spatial_plan, patches, groups),...  7.85 us
    pallas_call x1, Pallas kernels, banded_layer(): pl.pallas_call(partial(spatial_forward, spatial_plan, patches, groups), o...  6.39 us
    all_to_all x2, starting transfers between devices, exchange(): lax.all_to_all(blocks, 'grid', split_axis=0, concat_axis=0, tiled=True)  6.28 us
    unnamed x37, local copies, waits for them, and re-layouts  3.86 us
  transfers between devices with their start and end apart: 28, of which 13 were waited for; matrix products, arithmetic and copies ran while one was open for 3% of the time, Pallas kernels for 5%

profile of v3, /device:TPU:0, one launch (start us, length us, event | category | flops | bytes accessed | tf_op | source)
XLA Modules:
  0.0 165.7 jit_solution(17271417203919330306)
XLA Ops:
  0.6 4.1 %collective-permute-start.1 = (bf16[32,3072]{1,0:T(8,128)(2,1)}, bf16[32,3072]{1,0:T(8,128)(2,1)S(1)}, u32[]{:S(2)}, u32[]{:S(2)}) collective-permute-start(bf16[32,3072]{1,0:T(8,128)(2,1)} %param.9), channel_id=1, source_target_pairs={{0,16},{1,17},{2,18},{3,19},{4,20},{5,21},{6,22},{7,23},{8,24},{9,... | collective-permute-start | bytes 589832 | tf_op jit(solution)/shard_map/ppermute | solution.py:356
  4.7 1.6 collective-permute-start
  6.3 2.2 %collective-permute-start.2 = (bf16[32,3072]{1,0:T(8,128)(2,1)}, bf16[32,3072]{1,0:T(8,128)(2,1)S(1)}, u32[]{:S(2)}, u32[]{:S(2)}) collective-permute-start(bf16[32,3072]{1,0:T(8,128)(2,1)} %param.9), channel_id=1, source_target_pairs={{0,24},{1,25},{2,26},{3,27},{4,28},{5,29},{6,30},{7,31},{8,0},{9,1... | collective-permute-start | bytes 589832 | tf_op jit(solution)/shard_map/ppermute | solution.py:356
  8.6 2.2 %prepare.1 = (bf16[256,512]{1,0:T(8,128)(2,1)}, bf16[32,5120]{1,0:T(8,128)(2,1)}, bf16[32,4096]{1,0:T(8,128)(2,1)}) custom-call(bf16[128,1024]{1,0:T(8,128)(2,1)} %bitcast.14, bf16[32,1024]{1,0:T(8,128)(2,1)} %w_so.1, bf16[32,3072]{1,0:T(8,128)(2,1)} %w_gqkv.1, bf16[32,1024]{1,0:T(8,128)(2,1)} %w_go.1), custom_call_target="tpu_custom_call" | custom-call | tf_op jit(solution)/shard_map/prepare/pallas_call | solution.py:394
  10.7 2.8 %all-to-all-start = ((bf16[32,8,512]{2,1,0:T(8,128)(2,1)}), bf16[32,8,512]{2,1,0:T(8,128)(2,1)S(1)}, u32[]{:S(2)}, u32[]{:S(2)}) async-start(bf16[32,8,512]{2,1,0:T(8,128)(2,1)} %bitcast.22), calls=%async_computation | async-start | bytes 524288 | tf_op jit(solution)/shard_map/all_to_all | solution.py:343
  13.6 1.8 %collective-permute-start.4 = (bf16[32,5120]{1,0:T(8,128)(2,1)}, bf16[32,5120]{1,0:T(8,128)(2,1)S(1)}, u32[]{:S(2)}, u32[]{:S(2)}) collective-permute-start(bf16[32,5120]{1,0:T(8,128)(2,1)} %get-tuple-element.42), channel_id=1, source_target_pairs={{0,4},{1,3},{2,6},{3,1},{4,0},{5,7},{6,2},{7,5},{8,12},{9,11},{10,... | collective-permute-start | bytes 983048 | tf_op jit(solution)/shard_map/ppermute | solution.py:356
  15.4 1.5 collective-permute-start.3
  16.8 2.6 %collective-permute-done.1 = bf16[32,3072]{1,0:T(8,128)(2,1)S(1)} collective-permute-done((bf16[32,3072]{1,0:T(8,128)(2,1)}, bf16[32,3072]{1,0:T(8,128)(2,1)S(1)}, u32[]{:S(2)}, u32[]{:S(2)}) %collective-permute-start.1) | collective-permute-done | bytes 196640 | tf_op jit(solution)/shard_map/ppermute | solution.py:356
  19.4 1.6 collective-permute-done.2
  21.1 1.0 pad_maximum_fusion.2.refs_0_
  22.1 3.8 %collective-permute-done.4 = bf16[32,5120]{1,0:T(8,128)(2,1)S(1)} collective-permute-done((bf16[32,5120]{1,0:T(8,128)(2,1)}, bf16[32,5120]{1,0:T(8,128)(2,1)S(1)}, u32[]{:S(2)}, u32[]{:S(2)}) %collective-permute-start.4) | collective-permute-done | bytes 327712 | tf_op jit(solution)/shard_map/ppermute | solution.py:356
  25.9 3.7 %all-to-all-done = bf16[32,8,512]{2,1,0:T(8,128)(2,1)S(1)} async-done(((bf16[32,8,512]{2,1,0:T(8,128)(2,1)}), bf16[32,8,512]{2,1,0:T(8,128)(2,1)S(1)}, u32[]{:S(2)}, u32[]{:S(2)}) %all-to-all-start) | async-done | bytes 262176 | tf_op jit(solution)/shard_map/all_to_all | solution.py:343
  29.6 0.7 collective-permute-start.7
  30.3 1.3 collective-permute-start.6
  31.7 0.2 collective-permute-start.5
  31.9 3.1 %collective-permute-start.9 = (bf16[32,4096]{1,0:T(8,128)(2,1)S(1)}, bf16[32,4096]{1,0:T(8,128)(2,1)S(1)}, u32[]{:S(2)}, u32[]{:S(2)}) collective-permute-start(bf16[32,4096]{1,0:T(8,128)(2,1)S(1)} %copy-done.16), channel_id=1, source_target_pairs={{0,16},{1,17},{2,18},{3,19},{4,20},{5,21},{6,22},{7,23},{8,24},{9,... | collective-permute-start | bytes 786440 | tf_op jit(solution)/shard_map/ppermute | solution.py:356
  34.9 1.1 collective-permute-start.8
  36.0 4.4 %collective-permute-done.7 = bf16[32,5120]{1,0:T(8,128)(2,1)S(1)} collective-permute-done((bf16[32,5120]{1,0:T(8,128)(2,1)}, bf16[32,5120]{1,0:T(8,128)(2,1)S(1)}, u32[]{:S(2)}, u32[]{:S(2)}) %collective-permute-start.7) | collective-permute-done | bytes 327712 | tf_op jit(solution)/shard_map/ppermute | solution.py:356
  40.4 2.1 %pad_maximum_fusion.1.refs_0_ = bf16[128,5120]{1,0:T(8,128)(2,1)} fusion(bf16[32,5120]{1,0:T(8,128)(2,1)S(1)} %collective-permute-done.7, bf16[32,5120]{1,0:T(8,128)(2,1)S(1)} %collective-permute-done.4, bf16[32,5120]{1,0:T(8,128)(2,1)} %collective-permute-done.3, bf16[32,5120]{1,0:T(8,128)(2,1)S(1)} %copy-done.12), kind=kLoop, calls=%fused_computation.1 | loop fusion | flops 5242880 | bytes 2621440 | tf_op jit(solution)/shard_map/concatenate | solution.py:364
  42.5 9.3 %collective-permute-done.9 = bf16[32,4096]{1,0:T(8,128)(2,1)S(1)} collective-permute-done((bf16[32,4096]{1,0:T(8,128)(2,1)S(1)}, bf16[32,4096]{1,0:T(8,128)(2,1)S(1)}, u32[]{:S(2)}, u32[]{:S(2)}) %collective-permute-start.9) | collective-permute-done | bytes 262176 | tf_op jit(solution)/shard_map/ppermute | solution.py:356
  51.8 0.0 collective-permute-done.8
  51.8 1.4 collective-permute-done.6.refs_2_
  53.1 0.1 pad_maximum_fusion
  53.3 0.8 copy-done.1
  54.0 0.0 collective-permute-start.12
  54.1 0.5 collective-permute-start.11
  54.6 1.3 collective-permute-start.10
  55.9 3.1 %collective-permute-start.13 = (bf16[32,4096]{1,0:T(8,128)(2,1)S(1)}, bf16[32,4096]{1,0:T(8,128)(2,1)S(1)}, u32[]{:S(2)}, u32[]{:S(2)}) collective-permute-start(bf16[32,4096]{1,0:T(8,128)(2,1)S(1)} %copy-done.16), channel_id=1, source_target_pairs={{0,24},{1,25},{2,26},{3,27},{4,28},{5,29},{6,30},{7,31},{8,0},{9,1... | collective-permute-start | bytes 786440 | tf_op jit(solution)/shard_map/ppermute | solution.py:356
  59.0 1.0 slice.3
  60.0 4.5 %collective-permute-done.13 = bf16[32,4096]{1,0:T(8,128)(2,1)S(1)} collective-permute-done((bf16[32,4096]{1,0:T(8,128)(2,1)S(1)}, bf16[32,4096]{1,0:T(8,128)(2,1)S(1)}, u32[]{:S(2)}, u32[]{:S(2)}) %collective-permute-start.13) | collective-permute-done | bytes 262176 | tf_op jit(solution)/shard_map/ppermute | solution.py:356
  64.5 0.1 pad_maximum_fusion.3
  64.6 2.0 %collective-permute-done.10.refs_3_ = bf16[128,3072]{1,0:T(8,128)(2,1)S(1)} collective-permute-done((bf16[128,3072]{1,0:T(8,128)(2,1)S(1)}, bf16[128,3072]{1,0:T(8,128)(2,1)S(1)}, u32[]{:S(2)}, u32[]{:S(2)}) %collective-permute-start.10) | collective-permute-done | bytes 786464 | tf_op jit(solution)/shard_map/ppermute | solution.py:356
  66.6 0.1 collective-permute-start.16
  66.6 1.4 collective-permute-start.15
  68.0 0.9 collective-permute-start.14
  68.9 2.2 %collective-permute-start.18 = (bf16[128,1024]{1,0:T(8,128)(2,1)S(1)}, bf16[128,1024]{1,0:T(8,128)(2,1)S(1)}, u32[]{:S(2)}, u32[]{:S(2)}) collective-permute-start(bf16[128,1024]{1,0:T(8,128)(2,1)S(1)} %slice.3), channel_id=1, source_target_pairs={{0,16},{1,17},{2,18},{3,19},{4,20},{5,21},{6,22},{7,23},{8,24},{9,... | collective-permute-start | bytes 786440 | tf_op jit(solution)/shard_map/ppermute | solution.py:356
  71.1 1.8 %collective-permute-start.17 = (bf16[128,1024]{1,0:T(8,128)(2,1)S(1)}, bf16[128,1024]{1,0:T(8,128)(2,1)S(1)}, u32[]{:S(2)}, u32[]{:S(2)}) collective-permute-start(bf16[128,1024]{1,0:T(8,128)(2,1)S(1)} %slice.3), channel_id=1, source_target_pairs={{0,8},{1,9},{2,10},{3,11},{4,12},{5,13},{6,14},{7,15},{8,16},{9,17... | collective-permute-start | bytes 786440 | tf_op jit(solution)/shard_map/ppermute | solution.py:356
  73.0 0.9 copy-done.7
  73.8 6.4 %spatial_forward.1 = (bf16[256,512]{1,0:T(8,128)(2,1)}, bf16[128,3072]{1,0:T(8,128)(2,1)}, f32[128,2048]{1,0:T(8,128)}) custom-call(bf16[256,512]{1,0:T(8,128)(2,1)} %bitcast.12, s32[32,128]{1,0:T(8,128)} %keep.1, bf16[128,3072]{1,0:T(8,128)(2,1)} %copy-done, bf16[128,3072]{1,0:T(8,128)(2,1)} %copy-done.2, bf16[128,3072]{1,0:T(8,128)(2,1)} %copy-done.1, ...), custom_call_target="tpu_custom_call" | custom-call | flops 1073741824 | bytes 8388608 | tf_op jit(solution)/shard_map/spatial_forward/pallas_call | solution.py:424
  80.2 8.9 %collective-permute-done.18 = bf16[128,1024]{1,0:T(8,128)(2,1)S(1)} collective-permute-done((bf16[128,1024]{1,0:T(8,128)(2,1)S(1)}, bf16[128,1024]{1,0:T(8,128)(2,1)S(1)}, u32[]{:S(2)}, u32[]{:S(2)}) %collective-permute-start.18) | collective-permute-done | bytes 262176 | tf_op jit(solution)/shard_map/ppermute | solution.py:356
  89.1 0.0 collective-permute-done.17
  89.1 0.0 collective-permute-done.15
  89.1 0.1 constant_dynamic-update-slice_fusion.2
  89.2 1.2 constant_dynamic-update-slice_fusion.1
  90.4 0.1 constant_dynamic-update-slice_fusion.refs_2_
  90.5 0.1 collective-permute-start.21
  90.5 0.5 collective-permute-start.20
  91.0 1.1 collective-permute-start.19
  92.2 0.1 collective-permute-start.23
  92.3 3.5 %all-to-all-start.1 = ((bf16[32,8,512]{2,1,0:T(8,128)(2,1)}), bf16[32,8,512]{2,1,0:T(8,128)(2,1)S(1)}, u32[]{:S(2)}, u32[]{:S(2)}) async-start(bf16[32,8,512]{2,1,0:T(8,128)(2,1)} %bitcast.3), calls=%async_computation.1 | async-start | bytes 524288 | tf_op jit(solution)/shard_map/all_to_all | solution.py:343
  95.7 3.7 %collective-permute-start.22 = (bf16[128,1024]{1,0:T(8,128)(2,1)}, bf16[128,1024]{1,0:T(8,128)(2,1)S(1)}, u32[]{:S(2)}, u32[]{:S(2)}) collective-permute-start(bf16[128,1024]{1,0:T(8,128)(2,1)} %copy-done.15), channel_id=1, source_target_pairs={{0,24},{1,25},{2,26},{3,27},{4,28},{5,29},{6,30},{7,31},{8,0},{9,1... | collective-permute-start | bytes 786440 | tf_op jit(solution)/shard_map/ppermute | solution.py:356
  99.4 9.0 %collective-permute-done.22.refs_7_ = bf16[128,1024]{1,0:T(8,128)(2,1)S(1)} collective-permute-done((bf16[128,1024]{1,0:T(8,128)(2,1)}, bf16[128,1024]{1,0:T(8,128)(2,1)S(1)}, u32[]{:S(2)}, u32[]{:S(2)}) %collective-permute-start.22) | collective-permute-done | bytes 262176 | tf_op jit(solution)/shard_map/ppermute | solution.py:356
  108.4 0.0 all-to-all-done.1
  108.5 0.1 collective-permute-start.24
  108.6 0.5 collective-permute-start.25
  109.1 2.1 %collective-permute-done.25.refs_9_ = bf16[128,1024]{1,0:T(8,128)(2,1)S(1)} collective-permute-done((bf16[128,1024]{1,0:T(8,128)(2,1)S(1)}, bf16[128,1024]{1,0:T(8,128)(2,1)S(1)}, u32[]{:S(2)}, u32[]{:S(2)}) %collective-permute-start.25) | collective-permute-done | bytes 262176 | tf_op jit(solution)/shard_map/ppermute | solution.py:356
  111.2 0.2 collective-permute-done.24.refs_5_
  111.4 0.5 copy-done.14
  111.9 0.4 copy-done.11
  112.3 13.0 %group_layer.1 = (bf16[128,1024]{1,0:T(8,128)(2,1)}, bf16[128,1024]{1,0:T(8,128)(2,1)}, bf16[256,512]{1,0:T(8,128)(2,1)}) custom-call(bf16[128,1024]{1,0:T(8,128)(2,1)} %bitcast.15, bf16[256,512]{1,0:T(8,128)(2,1)} %bitcast.16, bf16[128,1024]{1,0:T(8,128)(2,1)} %bitcast.20, bf16[128,5120]{1,0:T(8,128)(2,1)} %pad_maximum_fusion.1.refs_0_, ...), custom_call_target="tpu_custom_call" | custom-call | flops 2147483648 | bytes 8388608 | tf_op jit(solution)/shard_map/group_layer/pallas_call | solution.py:454
  125.3 16.6 %all_to_all.20 = bf16[32,8,512]{2,1,0:T(8,128)(2,1)} all-to-all(bf16[32,8,512]{2,1,0:T(8,128)(2,1)} %bitcast.23), channel_id=1, replica_groups=mesh['parts'=1,'grid'=32] {'grid'}, dimensions={0} | all-to-all | bytes 524288 | tf_op jit(solution)/shard_map/all_to_all | solution.py:343
  142.0 7.8 %spatial_backward.1 = bf16[256,512]{1,0:T(8,128)(2,1)} custom-call(bf16[256,512]{1,0:T(8,128)(2,1)} %bitcast.13, bf16[256,512]{1,0:T(8,128)(2,1)} %bitcast.17, bf16[128,3072]{1,0:T(8,128)(2,1)} %get-tuple-element.80.qkv, f32[128,2048]{1,0:T(8,128)} %get-tuple-element.81.probs, bf16[128,3072]{1,0:T(8,128)(2,1)} %copy-done, bf16[128,3072]{1,0:T(8,128)(2,1)} %copy-done.2, ...), custom_call_target="tpu_custom_call" | custom-call | flops 1073741824 | bytes 8388608 | tf_op jit(solution)/shard_map/spatial_backward/pallas_call | solution.py:473
  149.8 13.9 %all_to_all.21 = bf16[32,8,512]{2,1,0:T(8,128)(2,1)} all-to-all(bf16[32,8,512]{2,1,0:T(8,128)(2,1)} %bitcast.18), channel_id=1, replica_groups=mesh['parts'=1,'grid'=32] {'grid'}, dimensions={0} | all-to-all | bytes 524288 | tf_op jit(solution)/shard_map/all_to_all | solution.py:343
  163.7 2.0 %add_packed.1 = bf16[128,1024]{1,0:T(8,128)(2,1)} custom-call(bf16[128,1024]{1,0:T(8,128)(2,1)} %get-tuple-element.78.values, bf16[256,512]{1,0:T(8,128)(2,1)} %bitcast.19), custom_call_target="tpu_custom_call" | custom-call | tf_op jit(solution)/shard_map/add_packed/pallas_call | solution.py:487
  (43 shorter events, 0.1 us)
Async XLA Ops:
  0.6 18.8 %collective-permute-start.1 = (bf16[32,3072]{1,0:T(8,128)(2,1)}, bf16[32,3072]{1,0:T(8,128)(2,1)S(1)}, u32[]{:S(2)}, u32[]{:S(2)}) collective-permute-start(bf16[32,3072]{1,0:T(8,128)(2,1)} %param.9), channel_id=1, source_target_pairs={{0,16},{1,17},{2,18},{3,19},{4,20},{5,21},{6,22},{7,23},{8,24},{9,... | collective-permute-start | bytes 589832 | tf_op jit(solution)/shard_map/ppermute | solution.py:356
  4.7 14.7 %collective-permute-start = (bf16[32,3072]{1,0:T(8,128)(2,1)}, bf16[32,3072]{1,0:T(8,128)(2,1)S(1)}, u32[]{:S(2)}, u32[]{:S(2)}) collective-permute-start(bf16[32,3072]{1,0:T(8,128)(2,1)} %param.9), channel_id=1, source_target_pairs={{0,8},{1,9},{2,10},{3,11},{4,12},{5,13},{6,14},{7,15},{8,16},{9,17... | collective-permute-start | bytes 589832 | tf_op jit(solution)/shard_map/ppermute | solution.py:356
  6.3 14.8 %collective-permute-start.2 = (bf16[32,3072]{1,0:T(8,128)(2,1)}, bf16[32,3072]{1,0:T(8,128)(2,1)S(1)}, u32[]{:S(2)}, u32[]{:S(2)}) collective-permute-start(bf16[32,3072]{1,0:T(8,128)(2,1)} %param.9), channel_id=1, source_target_pairs={{0,24},{1,25},{2,26},{3,27},{4,28},{5,29},{6,30},{7,31},{8,0},{9,1... | collective-permute-start | bytes 589832 | tf_op jit(solution)/shard_map/ppermute | solution.py:356
  10.7 21.2 %copy-start.16 = (bf16[32,4096]{1,0:T(8,128)(2,1)S(1)}, bf16[32,4096]{1,0:T(8,128)(2,1)}, u32[]{:S(2)}) copy-start(bf16[32,4096]{1,0:T(8,128)(2,1)} %get-tuple-element.54) | copy-start | bytes 786436
  10.7 29.7 %copy-start.12 = (bf16[32,5120]{1,0:T(8,128)(2,1)S(1)}, bf16[32,5120]{1,0:T(8,128)(2,1)}, u32[]{:S(2)}) copy-start(bf16[32,5120]{1,0:T(8,128)(2,1)} %get-tuple-element.42) | copy-start | bytes 983044
  10.7 18.9 %all-to-all-start = ((bf16[32,8,512]{2,1,0:T(8,128)(2,1)}), bf16[32,8,512]{2,1,0:T(8,128)(2,1)S(1)}, u32[]{:S(2)}, u32[]{:S(2)}) async-start(bf16[32,8,512]{2,1,0:T(8,128)(2,1)} %bitcast.22), calls=%async_computation | async-start | bytes 524288 | tf_op jit(solution)/shard_map/all_to_all | solution.py:343
  13.6 12.3 %collective-permute-start.4 = (bf16[32,5120]{1,0:T(8,128)(2,1)}, bf16[32,5120]{1,0:T(8,128)(2,1)S(1)}, u32[]{:S(2)}, u32[]{:S(2)}) collective-permute-start(bf16[32,5120]{1,0:T(8,128)(2,1)} %get-tuple-element.42), channel_id=1, source_target_pairs={{0,4},{1,3},{2,6},{3,1},{4,0},{5,7},{6,2},{7,5},{8,12},{9,11},{10,... | collective-permute-start | bytes 983048 | tf_op jit(solution)/shard_map/ppermute | solution.py:356
  15.4 10.5 %collective-permute-start.3 = (bf16[32,5120]{1,0:T(8,128)(2,1)}, bf16[32,5120]{1,0:T(8,128)(2,1)}, u32[]{:S(2)}, u32[]{:S(2)}) collective-permute-start(bf16[32,5120]{1,0:T(8,128)(2,1)} %get-tuple-element.42), channel_id=1, source_target_pairs={{0,2},{1,5},{2,0},{3,7},{4,6},{5,1},{6,4},{7,3},{8,10},{9,13},{10,... | collective-permute-start | bytes 983048 | tf_op jit(solution)/shard_map/ppermute | solution.py:356
  22.1 32.0 %copy-start = (bf16[128,3072]{1,0:T(8,128)(2,1)}, bf16[128,3072]{1,0:T(8,128)(2,1)S(1)}, u32[]{:S(2)}) copy-start(bf16[128,3072]{1,0:T(8,128)(2,1)S(1)} %pad_maximum_fusion.2.refs_0_) | copy-start | bytes 2359300
  29.6 23.6 %copy-start.8 = (bf16[32,8,512]{2,1,0:T(8,128)(2,1)}, bf16[32,8,512]{2,1,0:T(8,128)(2,1)S(1)}, u32[]{:S(2)}) copy-start(bf16[32,8,512]{2,1,0:T(8,128)(2,1)S(1)} %all-to-all-done) | copy-start | bytes 786436
  29.6 10.7 %collective-permute-start.7 = (bf16[32,5120]{1,0:T(8,128)(2,1)}, bf16[32,5120]{1,0:T(8,128)(2,1)S(1)}, u32[]{:S(2)}, u32[]{:S(2)}) collective-permute-start(bf16[32,5120]{1,0:T(8,128)(2,1)} %collective-permute-done.3), channel_id=1, source_target_pairs={{0,4},{1,3},{2,6},{3,1},{4,0},{5,7},{6,2},{7,5},{8,12},{9,11},{10,... | collective-permute-start | bytes 983048 | tf_op jit(solution)/shard_map/ppermute | solution.py:356
  30.3 22.8 %collective-permute-start.6 = (bf16[128,3072]{1,0:T(8,128)(2,1)S(1)}, bf16[128,3072]{1,0:T(8,128)(2,1)S(1)}, u32[]{:S(2)}, u32[]{:S(2)}) collective-permute-start(bf16[128,3072]{1,0:T(8,128)(2,1)S(1)} %pad_maximum_fusion.2.refs_0_), channel_id=1, source_target_pairs={{0,4},{1,3},{2,6},{3,1},{4,0},{5,7},{6,2},{7,5},{8,12},{9,11},{10,... | collective-permute-start | bytes 2359304 | tf_op jit(solution)/shard_map/ppermute | solution.py:356
  31.7 21.5 %collective-permute-start.5 = (bf16[128,3072]{1,0:T(8,128)(2,1)S(1)}, bf16[128,3072]{1,0:T(8,128)(2,1)S(1)}, u32[]{:S(2)}, u32[]{:S(2)}) collective-permute-start(bf16[128,3072]{1,0:T(8,128)(2,1)S(1)} %pad_maximum_fusion.2.refs_0_), channel_id=1, source_target_pairs={{0,2},{1,5},{2,0},{3,7},{4,6},{5,1},{6,4},{7,3},{8,10},{9,13},{10,... | collective-permute-start | bytes 2359304 | tf_op jit(solution)/shard_map/ppermute | solution.py:356
  31.9 19.9 %collective-permute-start.9 = (bf16[32,4096]{1,0:T(8,128)(2,1)S(1)}, bf16[32,4096]{1,0:T(8,128)(2,1)S(1)}, u32[]{:S(2)}, u32[]{:S(2)}) collective-permute-start(bf16[32,4096]{1,0:T(8,128)(2,1)S(1)} %copy-done.16), channel_id=1, source_target_pairs={{0,16},{1,17},{2,18},{3,19},{4,20},{5,21},{6,22},{7,23},{8,24},{9,... | collective-permute-start | bytes 786440 | tf_op jit(solution)/shard_map/ppermute | solution.py:356
  34.9 16.8 %collective-permute-start.8 = (bf16[32,4096]{1,0:T(8,128)(2,1)S(1)}, bf16[32,4096]{1,0:T(8,128)(2,1)S(1)}, u32[]{:S(2)}, u32[]{:S(2)}) collective-permute-start(bf16[32,4096]{1,0:T(8,128)(2,1)S(1)} %copy-done.16), channel_id=1, source_target_pairs={{0,8},{1,9},{2,10},{3,11},{4,12},{5,13},{6,14},{7,15},{8,16},{9,17... | collective-permute-start | bytes 786440 | tf_op jit(solution)/shard_map/ppermute | solution.py:356
  53.1 0.9 copy-start.1
  53.1 1.4 copy-start.2
  54.0 12.5 %collective-permute-start.12 = (bf16[256,3072]{1,0:T(8,128)(2,1)S(1)}, bf16[256,3072]{1,0:T(8,128)(2,1)S(1)}, u32[]{:S(2)}, u32[]{:S(2)}) collective-permute-start(bf16[256,3072]{1,0:T(8,128)(2,1)S(1)} %pad_maximum_fusion), channel_id=1, source_target_pairs={{0,1},{1,0},{2,3},{3,2},{4,5},{5,4},{6,7},{7,6},{8,9},{9,8},{10,11... | collective-permute-start | bytes 4718600 | tf_op jit(solution)/shard_map/ppermute | solution.py:356
  54.1 10.5 %collective-permute-start.11 = (bf16[128,3072]{1,0:T(8,128)(2,1)S(1)}, bf16[128,3072]{1,0:T(8,128)(2,1)S(1)}, u32[]{:S(2)}, u32[]{:S(2)}) collective-permute-start(bf16[128,3072]{1,0:T(8,128)(2,1)S(1)} %pad_maximum_fusion.2.refs_0_), channel_id=1, source_target_pairs={{0,1},{1,0},{2,3},{3,2},{4,5},{5,4},{6,7},{7,6},{8,9},{9,8},{10,11... | collective-permute-start | bytes 2359304 | tf_op jit(solution)/shard_map/ppermute | solution.py:356
  54.6 12.0 %collective-permute-start.10 = (bf16[128,3072]{1,0:T(8,128)(2,1)S(1)}, bf16[128,3072]{1,0:T(8,128)(2,1)S(1)}, u32[]{:S(2)}, u32[]{:S(2)}) collective-permute-start(bf16[128,3072]{1,0:T(8,128)(2,1)S(1)} %collective-permute-done.5.refs_1_), channel_id=1, source_target_pairs={{0,4},{1,3},{2,6},{3,1},{4,0},{5,7},{6,2},{7,5},{8,12},{9,11},{10,... | collective-permute-start | bytes 2359304 | tf_op jit(solution)/shard_map/ppermute | solution.py:356
  55.9 8.6 %collective-permute-start.13 = (bf16[32,4096]{1,0:T(8,128)(2,1)S(1)}, bf16[32,4096]{1,0:T(8,128)(2,1)S(1)}, u32[]{:S(2)}, u32[]{:S(2)}) collective-permute-start(bf16[32,4096]{1,0:T(8,128)(2,1)S(1)} %copy-done.16), channel_id=1, source_target_pairs={{0,24},{1,25},{2,26},{3,27},{4,28},{5,29},{6,30},{7,31},{8,0},{9,1... | collective-permute-start | bytes 786440 | tf_op jit(solution)/shard_map/ppermute | solution.py:356
  60.0 20.2 %copy-start.15 = (bf16[128,1024]{1,0:T(8,128)(2,1)}, bf16[128,1024]{1,0:T(8,128)(2,1)S(1)}, u32[]{:S(2)}) copy-start(bf16[128,1024]{1,0:T(8,128)(2,1)S(1)} %slice.3) | copy-start | bytes 786436
  64.6 8.3 %copy-start.5 = (bf16[128,3072]{1,0:T(8,128)(2,1)}, bf16[128,3072]{1,0:T(8,128)(2,1)S(1)}, u32[]{:S(2)}) copy-start(bf16[128,3072]{1,0:T(8,128)(2,1)S(1)} %collective-permute-done.11.refs_4_) | copy-start | bytes 2359300
  66.6 6.4 %copy-start.6 = (bf16[128,3072]{1,0:T(8,128)(2,1)}, bf16[128,3072]{1,0:T(8,128)(2,1)S(1)}, u32[]{:S(2)}) copy-start(bf16[128,3072]{1,0:T(8,128)(2,1)S(1)} %collective-permute-done.10.refs_3_) | copy-start | bytes 2359300
  66.6 6.4 %copy-start.3 = (bf16[256,3072]{1,0:T(8,128)(2,1)}, bf16[256,3072]{1,0:T(8,128)(2,1)S(1)}, u32[]{:S(2)}) copy-start(bf16[256,3072]{1,0:T(8,128)(2,1)S(1)} %collective-permute-done.12.refs_5_) | copy-start | bytes 4718596
  66.6 6.4 %collective-permute-start.16 = (bf16[128,3072]{1,0:T(8,128)(2,1)S(1)}, bf16[128,3072]{1,0:T(8,128)(2,1)S(1)}, u32[]{:S(2)}, u32[]{:S(2)}) collective-permute-start(bf16[128,3072]{1,0:T(8,128)(2,1)S(1)} %collective-permute-done.10.refs_3_), channel_id=1, source_target_pairs={{0,1},{1,0},{2,3},{3,2},{4,5},{5,4},{6,7},{7,6},{8,9},{9,8},{10,11... | collective-permute-start | bytes 2359304 | tf_op jit(solution)/shard_map/ppermute | solution.py:356
  66.6 22.5 %collective-permute-start.15 = (bf16[96,4096]{1,0:T(8,128)(2,1)S(1)}, bf16[96,4096]{1,0:T(8,128)(2,1)S(1)}, u32[]{:S(2)}, u32[]{:S(2)}) collective-permute-start(bf16[96,4096]{1,0:T(8,128)(2,1)S(1)} %pad_maximum_fusion.3), channel_id=1, source_target_pairs={{0,4},{1,3},{2,6},{3,1},{4,0},{5,7},{6,2},{7,5},{8,12},{9,11},{10,... | collective-permute-start | bytes 2359304 | tf_op jit(solution)/shard_map/ppermute | solution.py:356
  68.0 21.1 %collective-permute-start.14 = (bf16[96,4096]{1,0:T(8,128)(2,1)S(1)}, bf16[96,4096]{1,0:T(8,128)(2,1)}, u32[]{:S(2)}, u32[]{:S(2)}) collective-permute-start(bf16[96,4096]{1,0:T(8,128)(2,1)S(1)} %pad_maximum_fusion.3), channel_id=1, source_target_pairs={{0,2},{1,5},{2,0},{3,7},{4,6},{5,1},{6,4},{7,3},{8,10},{9,13},{10,... | collective-permute-start | bytes 2359304 | tf_op jit(solution)/shard_map/ppermute | solution.py:356
  68.9 20.2 %collective-permute-start.18 = (bf16[128,1024]{1,0:T(8,128)(2,1)S(1)}, bf16[128,1024]{1,0:T(8,128)(2,1)S(1)}, u32[]{:S(2)}, u32[]{:S(2)}) collective-permute-start(bf16[128,1024]{1,0:T(8,128)(2,1)S(1)} %slice.3), channel_id=1, source_target_pairs={{0,16},{1,17},{2,18},{3,19},{4,20},{5,21},{6,22},{7,23},{8,24},{9,... | collective-permute-start | bytes 786440 | tf_op jit(solution)/shard_map/ppermute | solution.py:356
  71.1 18.0 %collective-permute-start.17 = (bf16[128,1024]{1,0:T(8,128)(2,1)S(1)}, bf16[128,1024]{1,0:T(8,128)(2,1)S(1)}, u32[]{:S(2)}, u32[]{:S(2)}) collective-permute-start(bf16[128,1024]{1,0:T(8,128)(2,1)S(1)} %slice.3), channel_id=1, source_target_pairs={{0,8},{1,9},{2,10},{3,11},{4,12},{5,13},{6,14},{7,15},{8,16},{9,17... | collective-permute-start | bytes 786440 | tf_op jit(solution)/shard_map/ppermute | solution.py:356
  72.9 0.9 copy-start.7
  90.5 20.9 %copy-start.4 = (bf16[288,4096]{1,0:T(8,128)(2,1)}, bf16[288,4096]{1,0:T(8,128)(2,1)S(1)}, u32[]{:S(2)}) copy-start(bf16[288,4096]{1,0:T(8,128)(2,1)S(1)} %constant_dynamic-update-slice_fusion.refs_2_) | copy-start | bytes 7077892
  90.5 18.0 %collective-permute-start.21 = (bf16[288,4096]{1,0:T(8,128)(2,1)S(1)}, bf16[288,4096]{1,0:T(8,128)(2,1)}, u32[]{:S(2)}, u32[]{:S(2)}) collective-permute-start(bf16[288,4096]{1,0:T(8,128)(2,1)S(1)} %constant_dynamic-update-slice_fusion.refs_2_), channel_id=1, source_target_pairs={{0,1},{1,0},{2,3},{3,2},{4,5},{5,4},{6,7},{7,6},{8,9},{9,8},{10,11... | collective-permute-start | bytes 7077896 | tf_op jit(solution)/shard_map/ppermute | solution.py:356
  90.5 17.9 %collective-permute-start.20 = (bf16[128,5120]{1,0:T(8,128)(2,1)}, bf16[128,5120]{1,0:T(8,128)(2,1)}, u32[]{:S(2)}, u32[]{:S(2)}) collective-permute-start(bf16[128,5120]{1,0:T(8,128)(2,1)} %pad_maximum_fusion.1.refs_0_), channel_id=1, source_target_pairs={{0,1},{1,0},{2,3},{3,2},{4,5},{5,4},{6,7},{7,6},{8,9},{9,8},{10,11... | collective-permute-start | bytes 3932168 | tf_op jit(solution)/shard_map/ppermute | solution.py:356
  91.0 17.4 %collective-permute-start.19 = (bf16[96,4096]{1,0:T(8,128)(2,1)}, bf16[96,4096]{1,0:T(8,128)(2,1)}, u32[]{:S(2)}, u32[]{:S(2)}) collective-permute-start(bf16[96,4096]{1,0:T(8,128)(2,1)} %collective-permute-done.14), channel_id=1, source_target_pairs={{0,4},{1,3},{2,6},{3,1},{4,0},{5,7},{6,2},{7,5},{8,12},{9,11},{10,... | collective-permute-start | bytes 2359304 | tf_op jit(solution)/shard_map/ppermute | solution.py:356
  92.2 19.2 %copy-start.9 = (bf16[256,1024]{1,0:T(8,128)(2,1)}, bf16[256,1024]{1,0:T(8,128)(2,1)S(1)}, u32[]{:S(2)}) copy-start(bf16[256,1024]{1,0:T(8,128)(2,1)S(1)} %constant_dynamic-update-slice_fusion.3.refs_6_) | copy-start | bytes 1572868
  92.2 16.3 %collective-permute-start.23 = (bf16[256,1024]{1,0:T(8,128)(2,1)S(1)}, bf16[256,1024]{1,0:T(8,128)(2,1)}, u32[]{:S(2)}, u32[]{:S(2)}) collective-permute-start(bf16[256,1024]{1,0:T(8,128)(2,1)S(1)} %constant_dynamic-update-slice_fusion.3.refs_6_), channel_id=1, source_target_pairs={{0,1},{1,0},{2,3},{3,2},{4,5},{5,4},{6,7},{7,6},{8,9},{9,8},{10,11... | collective-permute-start | bytes 1572872 | tf_op jit(solution)/shard_map/ppermute | solution.py:356
  92.3 16.2 %all-to-all-start.1 = ((bf16[32,8,512]{2,1,0:T(8,128)(2,1)}), bf16[32,8,512]{2,1,0:T(8,128)(2,1)S(1)}, u32[]{:S(2)}, u32[]{:S(2)}) async-start(bf16[32,8,512]{2,1,0:T(8,128)(2,1)} %bitcast.3), calls=%async_computation.1 | async-start | bytes 524288 | tf_op jit(solution)/shard_map/all_to_all | solution.py:343
  95.7 12.7 %collective-permute-start.22 = (bf16[128,1024]{1,0:T(8,128)(2,1)}, bf16[128,1024]{1,0:T(8,128)(2,1)S(1)}, u32[]{:S(2)}, u32[]{:S(2)}) collective-permute-start(bf16[128,1024]{1,0:T(8,128)(2,1)} %copy-done.15), channel_id=1, source_target_pairs={{0,24},{1,25},{2,26},{3,27},{4,28},{5,29},{6,30},{7,31},{8,0},{9,1... | collective-permute-start | bytes 786440 | tf_op jit(solution)/shard_map/ppermute | solution.py:356
  108.4 3.0 %copy-start.13 = (bf16[128,1024]{1,0:T(8,128)(2,1)}, bf16[128,1024]{1,0:T(8,128)(2,1)S(1)}, u32[]{:S(2)}) copy-start(bf16[128,1024]{1,0:T(8,128)(2,1)S(1)} %collective-permute-done.22.refs_7_) | copy-start | bytes 786436
  108.4 3.0 %copy-start.10 = (bf16[32,8,512]{2,1,0:T(8,128)(2,1)}, bf16[32,8,512]{2,1,0:T(8,128)(2,1)S(1)}, u32[]{:S(2)}) copy-start(bf16[32,8,512]{2,1,0:T(8,128)(2,1)S(1)} %all-to-all-done.1) | copy-start | bytes 786436
  108.5 2.9 %collective-permute-start.24 = (bf16[96,4096]{1,0:T(8,128)(2,1)}, bf16[96,4096]{1,0:T(8,128)(2,1)S(1)}, u32[]{:S(2)}, u32[]{:S(2)}) collective-permute-start(bf16[96,4096]{1,0:T(8,128)(2,1)} %collective-permute-done.19.refs_3_), channel_id=1, source_target_pairs={{0,1},{1,0},{2,3},{3,2},{4,5},{5,4},{6,7},{7,6},{8,9},{9,8},{10,11... | collective-permute-start | bytes 2359304 | tf_op jit(solution)/shard_map/ppermute | solution.py:356
  108.6 2.6 %collective-permute-start.25 = (bf16[128,1024]{1,0:T(8,128)(2,1)S(1)}, bf16[128,1024]{1,0:T(8,128)(2,1)S(1)}, u32[]{:S(2)}, u32[]{:S(2)}) collective-permute-start(bf16[128,1024]{1,0:T(8,128)(2,1)S(1)} %collective-permute-done.22.refs_7_), channel_id=1, source_target_pairs={{0,1},{1,0},{2,3},{3,2},{4,5},{5,4},{6,7},{7,6},{8,9},{9,8},{10,11... | collective-permute-start | bytes 786440 | tf_op jit(solution)/shard_map/ppermute | solution.py:356
  111.2 0.7 copy-start.14
  111.4 0.9 copy-start.11

commit v4 on v3

--- a/solution.py
+++ b/solution.py
@@ -168,7 +168,7 @@
     return grad_query, grad_key, grad_value
 
 
-def place_rows(refs, plan, first, buffer, sem):
+def place_rows(refs, plan, first, buffer):
     position = lax.axis_index("grid")
     size = lax.axis_size("grid")
     each = buffer.shape[0] // size
@@ -179,15 +179,8 @@
         flips = (0, 2 * (side + 1), 4 - 2 * side, 6)
         for at, (step, flip) in enumerate(blocks):
             shard = lax.rem((holder ^ flips[flip]) + (size - 8 * step), size)
-            pltpu.make_async_copy(
-                ref.at[pl.ds(at * each, each), pl.ds(first, buffer.shape[1])],
-                buffer.at[pl.ds(pl.multiple_of(shard * each, each), each)],
-                sem,
-            ).start()
-
-
-def wait_rows(buffer, sem):
-    pltpu.make_async_copy(buffer, buffer, sem).wait()
+            rows = pl.ds(pl.multiple_of(shard * each, each), each)
+            buffer[rows, :] = ref[at * each : at * each + each, first : first + buffer.shape[1]]
 
 
 def packed_row(row, half, patches, groups, by_band):
@@ -217,14 +210,12 @@
     return total.astype(jnp.bfloat16)
 
 
-def prepare(patches, groups, tokens, w_so, w_gqkv, w_go, packed, joined, first_two):
+def prepare(patches, groups, tokens, w_so, w_gqkv, w_go, packed, joined):
     packed[...] = pack(tokens[...], patches, groups, False)
     width = w_so.shape[1]
     joined[:, :width] = w_so[...]
     joined[:, width : 4 * width] = w_gqkv[...]
     joined[:, 4 * width :] = w_go[...]
-    first_two[:, :width] = w_so[...]
-    first_two[:, width:] = w_gqkv[...]
 
 
 def add_packed(patches, groups, values, packed, total):
@@ -232,16 +223,15 @@
 
 
 def spatial_forward(plan, patches, groups, packed, keep, *refs):
-    pieces, (result_out, qkv_out, probs_out, qkv_buf, sems) = refs[:-5], refs[-5:]
+    pieces, (result_out, qkv_out, probs_out, qkv_buf) = refs[:-4], refs[-4:]
     rows, width = packed.shape[0] // 2, packed.shape[1] * 2
     span = 2 * rows
-    place_rows(pieces, plan, 0, qkv_buf, sems.at[0])
+    place_rows(pieces, plan, 0, qkv_buf)
     wide = unpack(packed[...], patches, groups, True).astype(jnp.float32)
     normed = (wide * inverse_rms(wide)).astype(jnp.bfloat16)
     kept = keep[pl.ds(lax.axis_index("grid"), 1), :]
     allowed = jnp.concatenate([kept, kept], axis=1) > 0
     low = low_lanes(rows)
-    wait_rows(qkv_buf, sems.at[0])
     qkv_out[...] = nn(normed, qkv_buf[...]).astype(jnp.bfloat16)
     results = []
     for pair in range(width // 128):
@@ -252,10 +242,10 @@
 
 
 def spatial_backward(plan, patches, groups, packed, grad_packed, qkv, probs, *refs):
-    pieces, (grad_out, qkv_buf, grads, sems) = refs[:-4], refs[-4:]
+    pieces, (grad_out, qkv_buf, grads) = refs[:-3], refs[-3:]
     rows, width = packed.shape[0] // 2, packed.shape[1] * 2
     span = 2 * rows
-    place_rows(pieces, plan, 0, qkv_buf, sems.at[0])
+    place_rows(pieces, plan, 0, qkv_buf)
     low = low_lanes(rows)
     grad = unpack(grad_packed[...], patches, groups, True)
     for pair in range(width // 128):
@@ -267,43 +257,35 @@
             grads[:, which * width + at : which * width + at + 128] = part
     wide = unpack(packed[...], patches, groups, True).astype(jnp.float32)
     inverse = inverse_rms(wide)
-    wait_rows(qkv_buf, sems.at[0])
     grad_normed = nt(grads[...], qkv_buf[...]).astype(jnp.bfloat16).astype(jnp.float32)
     grad_out[...] = pack(norm_grad(wide, inverse, grad_normed).astype(jnp.bfloat16), patches, groups, True)
 
 
-def group_layer(patches, own_plan, plan, go_plan, tokens, attended, cotangent, *refs):
-    pieces, rest = refs[:-11], refs[-11:]
-    mixed, grad_y, grad_bands, so_buf, qkv_buf, go_buf, qkv, grads, probs_buf, y_buf, sems = rest
+def group_layer(patches, plan, tokens, attended, cotangent, *refs):
+    pieces, rest = refs[:-10], refs[-10:]
+    mixed, grad_y, grad_bands, so_buf, qkv_buf, go_buf, qkv, grads, probs_buf, y_buf = rest
     rows, width = tokens.shape
     groups = rows // patches
     span = 2 * rows
-    own, pieces, out = pieces[:2], pieces[2:-4], pieces[-4:]
-    place_rows(own, own_plan, 0, so_buf, sems.at[0])
-    place_rows(pieces, plan, 0, so_buf, sems.at[0])
-    place_rows(own, own_plan, width, qkv_buf, sems.at[1])
-    place_rows(pieces, plan, width, qkv_buf, sems.at[1])
-    place_rows(own, own_plan, 4 * width, go_buf, sems.at[2])
-    place_rows(out, go_plan, 0, go_buf, sems.at[2])
+    place_rows(pieces, plan, 0, so_buf)
+    place_rows(pieces, plan, width, qkv_buf)
+    place_rows(pieces, plan, 4 * width, go_buf)
     ordered = unpack(attended[...], patches, groups, False)
     low = low_lanes(rows)
     row_patch = lax.broadcasted_iota(jnp.int32, (rows, span), 0) // groups
     column_patch = (lax.broadcasted_iota(jnp.int32, (rows, span), 1) % rows) // groups
     allowed = row_patch == column_patch
-    wait_rows(so_buf, sems.at[0])
     y_first = (tokens[...].astype(jnp.float32) + nn(ordered, so_buf[...])).astype(jnp.bfloat16)
     wide = y_first.astype(jnp.float32)
     y_buf[...] = wide
     inverse = inverse_rms(wide)
     normed = (wide * inverse).astype(jnp.bfloat16)
-    wait_rows(qkv_buf, sems.at[1])
     qkv[...] = nn(normed, qkv_buf[...]).astype(jnp.bfloat16)
     results = []
     for pair in range(width // 128):
         probs, result = pair_forward(qkv, allowed, low, width, pair)
         probs_buf[:, pair * span : pair * span + span] = probs
         results.append(result)
-    wait_rows(go_buf, sems.at[2])
     mixed[...] = (y_buf[...] + nn(jnp.concatenate(results, axis=1), go_buf[...])).astype(jnp.bfloat16)
     grad_attended = nt(cotangent[...], go_buf[...]).astype(jnp.bfloat16)
     for pair in range(width // 128):
@@ -322,17 +304,21 @@
 
 
 VMEM_SPEC = pl.BlockSpec(memory_space=pltpu.VMEM)
-ANY_SPEC = pl.BlockSpec(memory_space=pltpu.HBM)
-PARAMS = pltpu.CompilerParams(vmem_limit_bytes=56 * 1024 * 1024)
+
+
+def room(mebibytes):
+    return pltpu.CompilerParams(vmem_limit_bytes=mebibytes * 1024 * 1024)
 
 
 def shape(rows, columns, dtype=jnp.bfloat16):
     return jax.ShapeDtypeStruct((rows, columns), dtype)
 
 
-def cost(rows, width, passes):
+def cost(rows, width, weights, passes):
     return pl.CostEstimate(
-        flops=passes * 8 * rows * width * width, bytes_accessed=8 * width * width, transcendentals=16 * rows * rows
+        flops=2 * passes * weights * rows * width * width,
+        bytes_accessed=2 * passes * weights * width * width + 16 * rows * width,
+        transcendentals=16 * rows * rows,
     )
 
 
@@ -367,18 +353,12 @@
 def plans(size):
     steps = range(size // 8)
     line = [[(step, flip) for step in steps] for flip in range(4)]
-    own, rest = [(0, flip) for flip in range(4)], [[(step, flip) for step in steps[1:]] for flip in range(4)]
-    out = [(step, flip) for step in steps[1:] for flip in range(4)]
-
-    def plan(held, across):
-        return [(False, blocks) for blocks in held] + [(True, blocks) for blocks in across]
-
-    return (
-        plan(line, [line[0], line[1] + line[2], line[3]]),
-        plan([own], [own]),
-        plan([rest[0] + rest[1] + rest[2], rest[3]], [rest[0] + rest[1] + rest[2], rest[3]]),
-        plan([out[:-4], out[-4:]], [out[:-4], out[-4:]]),
-    )
+    own, rest = [(0, flip) for flip in range(4)], [blocks[1:] for blocks in line]
+
+    def both_cores(held):
+        return [(False, blocks) for blocks in held] + [(True, blocks) for blocks in held]
+
+    return both_cores(line), both_cores([own] + rest)
 
 
 def banded_layer(tokens, cotangent, w_sqkv, w_so, w_gqkv, w_go, keep):
@@ -386,41 +366,39 @@
     rows = patches * groups
     all_patches = patches * lax.axis_size("grid")
     first, second, sibling, along = mesh_moves(lax.axis_size("grid"))
-    spatial_plan, *group_plans = plans(lax.axis_size("grid"))
+    spatial_plan, group_plan = plans(lax.axis_size("grid"))
     pairs = width // 128
     packed_shape = shape(2 * rows, width // 2)
 
     tokens = tokens.reshape(rows, width)
-    packed, own, group = pl.pallas_call(
+    packed, group = pl.pallas_call(
         partial(prepare, patches, groups),
-        out_shape=(packed_shape, shape(w_so.shape[0], 5 * width), shape(w_so.shape[0], 4 * width)),
+        out_shape=(packed_shape, shape(w_so.shape[0], 5 * width)),
         in_specs=[VMEM_SPEC] * 4,
-        out_specs=(VMEM_SPEC,) * 3,
+        out_specs=(VMEM_SPEC,) * 2,
         name="prepare",
     )(tokens, w_so, w_gqkv, w_go)
     spatial_line = [w_sqkv] + [move(w_sqkv, table) for table in along]
-    own_one, own_other = move(own, first), move(own, second)
-    spatial_line, own_one, own_other, banded, group = together(
-        stack(*spatial_line), own_one, own_other, exchange(packed), group
+    group_one, group_other = move(group, first), move(group, second)
+    spatial_line, group_one, group_other, banded, group = together(
+        stack(*spatial_line), group_one, group_other, exchange(packed), group
     )
     spatial_one, spatial_other = move(spatial_line, first), move(spatial_line, second)
+    group_both = move(group_one, second)
     group_parts = [move(group, table) for table in along[:-1]]
-    own_both = move(own_one, second)
-    spatial_one, spatial_other, own_plane, group, spatial_line, *group_parts = together(
-        spatial_one, spatial_other, stack(own, own_one, own_other, own_both), group, spatial_line, *group_parts
-    )
-    out_plane = own_plane[:, 4 * width :]
+    spatial_one, spatial_other, group_plane, group, spatial_line, *group_parts = together(
+        spatial_one, spatial_other, stack(group, group_one, group_other, group_both), group, spatial_line, *group_parts
+    )
     spatial_both = move(spatial_one, second)
-    spatial_line_x = move(spatial_line, sibling)
-    spatial_pair_x = move(stack(spatial_one, spatial_other), sibling)
+    spatial_across = [move(part, sibling) for part in (spatial_line, spatial_one, spatial_other)]
     group_parts.append(move(group, along[-1]))
-    spatial_both, spatial_line_x, spatial_pair_x, group_line, out_plane = together(
-        spatial_both, spatial_line_x, spatial_pair_x, stack(*group_parts), out_plane
+    spatial_both, group_line, group_plane, *spatial_across = together(
+        spatial_both, stack(*group_parts), group_plane, *spatial_across
     )
     group_one, group_other = move(group_line, first), move(group_line, second)
-    out_parts = [move(out_plane, table) for table in along[:-1]]
+    group_across = [move(group_plane, sibling), move(group_line, sibling)]
     spatial_rows = [spatial_line, spatial_one, spatial_other, spatial_both]
-    spatial_rows += [spatial_line_x, spatial_pair_x, move(spatial_both, sibling)]
+    spatial_rows += [*spatial_across, move(spatial_both, sibling)]
     attended, qkv, probs = pl.pallas_call(
         partial(spatial_forward, spatial_plan, patches, groups),
         out_shape=(
@@ -428,33 +406,23 @@
             shape(all_patches, 3 * width),
             shape(all_patches, 2 * pairs * all_patches, jnp.float32),
         ),
-        in_specs=[VMEM_SPEC] * 2 + [ANY_SPEC] * len(spatial_rows),
+        in_specs=[VMEM_SPEC] * (2 + len(spatial_rows)),
         out_specs=(VMEM_SPEC,) * 3,
-        scratch_shapes=[pltpu.VMEM((width, 3 * width), jnp.bfloat16), pltpu.SemaphoreType.DMA((1,))],
-        compiler_params=PARAMS,
-        cost_estimate=cost(all_patches, width, 1),
+        scratch_shapes=[pltpu.VMEM((width, 3 * width), jnp.bfloat16)],
+        compiler_params=room(18),
+        cost_estimate=cost(all_patches, width, 3, 1),
         name="spatial_forward",
     )(banded, keep, *spatial_rows)
-    group_one, group_other, attended, own_plane, group_line, out_plane, *out_parts = together(
-        group_one, group_other, attended, own_plane, group_line, out_plane, *out_parts
-    )
+    group_one, group_other, attended, *group_across = together(group_one, group_other, attended, *group_across)
     group_both = move(group_one, second)
-    out_last = move(out_plane, along[-1])
-    group_most, out_most = stack(group_line, group_one, group_other), stack(*out_parts)
-    group_both, attended, own_plane_x, group_most_x, out_last, out_most_x = together(
-        group_both,
-        exchange(attended),
-        move(own_plane, sibling),
-        move(group_most, sibling),
-        out_last,
-        move(out_most, sibling),
-    )
-    group_rows = [own_plane, own_plane_x, group_most, group_both, group_most_x, move(group_both, sibling)]
-    group_rows += [out_most, out_last, out_most_x, move(out_last, sibling)]
+    group_across += [move(group_one, sibling), move(group_other, sibling)]
+    group_both, attended, *group_across = together(group_both, exchange(attended), *group_across)
+    group_rows = [group_plane, group_line, group_one, group_other, group_both]
+    group_rows += [*group_across, move(group_both, sibling)]
     mixed, grad_y, grad_bands = pl.pallas_call(
-        partial(group_layer, patches, *group_plans),
+        partial(group_layer, patches, group_plan),
         out_shape=(shape(rows, width), shape(rows, width), packed_shape),
-        in_specs=[VMEM_SPEC] * 3 + [ANY_SPEC] * len(group_rows),
+        in_specs=[VMEM_SPEC] * (3 + len(group_rows)),
         out_specs=(VMEM_SPEC,) * 3,
         scratch_shapes=[
             pltpu.VMEM((width, width), jnp.bfloat16),
@@ -464,24 +432,22 @@
             pltpu.VMEM((rows, 3 * width), jnp.bfloat16),
             pltpu.VMEM((rows, 2 * pairs * rows), jnp.float32),
             pltpu.VMEM((rows, width), jnp.float32),
-            pltpu.SemaphoreType.DMA((3,)),
         ],
-        compiler_params=PARAMS,
-        cost_estimate=cost(rows, width, 2),
+        compiler_params=room(32),
+        cost_estimate=cost(rows, width, 5, 2),
         name="group_layer",
     )(tokens, attended, cotangent.reshape(rows, width), *group_rows)
     grad_first = pl.pallas_call(
         partial(spatial_backward, spatial_plan, patches, groups),
         out_shape=packed_shape,
-        in_specs=[VMEM_SPEC] * 4 + [ANY_SPEC] * len(spatial_rows),
+        in_specs=[VMEM_SPEC] * (4 + len(spatial_rows)),
         out_specs=VMEM_SPEC,
         scratch_shapes=[
             pltpu.VMEM((width, 3 * width), jnp.bfloat16),
             pltpu.VMEM((all_patches, 3 * width), jnp.bfloat16),
-            pltpu.SemaphoreType.DMA((1,)),
         ],
-        compiler_params=PARAMS,
-        cost_estimate=cost(all_patches, width, 1),
+        compiler_params=room(18),
+        cost_estimate=cost(all_patches, width, 3, 1),
         name="spatial_backward",
     )(banded, exchange(grad_bands), qkv, probs, *spatial_rows)
     token_grad = pl.pallas_call(
@@ -489,6 +455,7 @@
         out_shape=shape(rows, width),
         in_specs=[VMEM_SPEC] * 2,
         out_specs=VMEM_SPEC,
+        compiler_params=room(8),
         name="add_packed",
     )(grad_y, exchange(grad_first))
     whole = (patches, groups, width)

time: 166 us -> 157 us (0.946)
  starting transfers between devices: 41.2 us -> 26.8 us
  blocking collectives: 30.5 us -> 43.5 us
  Pallas kernels: 31.4 us -> 19 us
  waiting for transfers between devices: 53.5 us -> 64.9 us
  local copies, waits for them, and re-layouts: 4.9 us -> 0.02 us
  other arithmetic: 3.25 us -> 1.13 us
    all_to_all x2 -> x3, blocking collectives: 30.5 us -> 43.5 us  [exchange(): lax.all_to_all(blocks, 'grid', split_axis=0, concat_axis=0, tiled=True)]
    ppermute x26 -> x24, waiting for transfers between devices: 49.8 us -> 61.1 us  [move(): return lax.ppermute(values, 'grid', table)]
    ppermute x26 -> x24, starting transfers between devices: 34.9 us -> 24 us  [move(): return lax.ppermute(values, 'grid', table)]
    pallas_call x1, Pallas kernels: 13 us -> 8.51 us  [banded_layer(): pl.pallas_call(partial(group_layer, patches, group_plan), out_shape=(shap...]
    pallas_call x1, Pallas kernels: 6.39 us -> 2.37 us  [banded_layer(): pl.pallas_call(partial(spatial_forward, spatial_plan, patches, groups), o...]
    unnamed x37 -> x8, local copies, waits for them, and re-layouts: 3.86 us -> 0.02 us
    all_to_all x2 -> x1, starting transfers between devices: 6.28 us -> 2.81 us  [exchange(): lax.all_to_all(blocks, 'grid', split_axis=0, concat_axis=0, tiled=True)]
    pallas_call x1, Pallas kernels: 7.85 us -> 5.13 us  [banded_layer(): pl.pallas_call(partial(spatial_backward, spatial_plan, patches, groups),...]
  transfers between devices with their start and end apart: 28 -> 25, of which waited for: 13 -> 11; matrix products, arithmetic and copies ran while one was open for 3% -> 1% of each run, Pallas kernels for 5% -> 3%
where the time goes in v4:
time: 157 us; the launch traced here: 156 us
  waiting for transfers between devices  64.9 us (41%)
  blocking collectives  43.5 us (28%)
  starting transfers between devices  26.8 us (17%)
  Pallas kernels  19 us (12%)
    ppermute x24, waiting for transfers between devices, move(): return lax.ppermute(values, 'grid', table)  61.1 us
    all_to_all x3, blocking collectives, exchange(): lax.all_to_all(blocks, 'grid', split_axis=0, concat_axis=0, tiled=True)  43.5 us
    ppermute x24, starting transfers between devices, move(): return lax.ppermute(values, 'grid', table)  24 us
    pallas_call x1, Pallas kernels, banded_layer(): pl.pallas_call(partial(group_layer, patches, group_plan), out_shape=(shap...  8.51 us
    pallas_call x1, Pallas kernels, banded_layer(): pl.pallas_call(partial(spatial_backward, spatial_plan, patches, groups),...  5.13 us
    all_to_all x1, waiting for transfers between devices, exchange(): lax.all_to_all(blocks, 'grid', split_axis=0, concat_axis=0, tiled=True)  3.83 us
  transfers between devices with their start and end apart: 25, of which 11 were waited for; matrix products, arithmetic and copies ran while one was open for 1% of the time, Pallas kernels for 3%

profile of v4, /device:TPU:0, one launch (start us, length us, event | category | flops | bytes accessed | tf_op | source)
XLA Modules:
  0.0 156.3 jit_solution(9679606018270337806)
XLA Ops:
  0.6 4.1 %collective-permute-start.1 = (bf16[32,3072]{1,0:T(8,128)(2,1)}, bf16[32,3072]{1,0:T(8,128)(2,1)S(1)}, u32[]{:S(2)}, u32[]{:S(2)}) collective-permute-start(bf16[32,3072]{1,0:T(8,128)(2,1)} %param.9), channel_id=1, source_target_pairs={{0,16},{1,17},{2,18},{3,19},{4,20},{5,21},{6,22},{7,23},{8,24},{9,... | collective-permute-start | bytes 589832 | tf_op jit(solution)/shard_map/ppermute | solution.py:342
  4.7 1.6 %collective-permute-start = (bf16[32,3072]{1,0:T(8,128)(2,1)}, bf16[32,3072]{1,0:T(8,128)(2,1)S(1)}, u32[]{:S(2)}, u32[]{:S(2)}) collective-permute-start(bf16[32,3072]{1,0:T(8,128)(2,1)} %param.9), channel_id=1, source_target_pairs={{0,8},{1,9},{2,10},{3,11},{4,12},{5,13},{6,14},{7,15},{8,16},{9,17... | collective-permute-start | bytes 589832 | tf_op jit(solution)/shard_map/ppermute | solution.py:342
  6.3 2.2 %collective-permute-start.2 = (bf16[32,3072]{1,0:T(8,128)(2,1)}, bf16[32,3072]{1,0:T(8,128)(2,1)S(1)}, u32[]{:S(2)}, u32[]{:S(2)}) collective-permute-start(bf16[32,3072]{1,0:T(8,128)(2,1)} %param.9), channel_id=1, source_target_pairs={{0,24},{1,25},{2,26},{3,27},{4,28},{5,29},{6,30},{7,31},{8,0},{9,1... | collective-permute-start | bytes 589832 | tf_op jit(solution)/shard_map/ppermute | solution.py:342
  8.6 2.1 %prepare.1 = (bf16[256,512]{1,0:T(8,128)(2,1)}, bf16[32,5120]{1,0:T(8,128)(2,1)}) custom-call(bf16[128,1024]{1,0:T(8,128)(2,1)} %bitcast.14, bf16[32,1024]{1,0:T(8,128)(2,1)} %w_so.1, bf16[32,3072]{1,0:T(8,128)(2,1)} %w_gqkv.1, bf16[32,1024]{1,0:T(8,128)(2,1)} %w_go.1), custom_call_target="tpu_custom_call" | custom-call | tf_op jit(solution)/shard_map/prepare/pallas_call | solution.py:374
  10.6 2.8 %all-to-all-start = ((bf16[32,8,512]{2,1,0:T(8,128)(2,1)}), bf16[32,8,512]{2,1,0:T(8,128)(2,1)S(1)}, u32[]{:S(2)}, u32[]{:S(2)}) async-start(bf16[32,8,512]{2,1,0:T(8,128)(2,1)} %bitcast.24), calls=%async_computation | async-start | bytes 524288 | tf_op jit(solution)/shard_map/all_to_all | solution.py:329
  13.5 1.8 %collective-permute-start.4 = (bf16[32,5120]{1,0:T(8,128)(2,1)}, bf16[32,5120]{1,0:T(8,128)(2,1)S(1)}, u32[]{:S(2)}, u32[]{:S(2)}) collective-permute-start(bf16[32,5120]{1,0:T(8,128)(2,1)} %get-tuple-element.48), channel_id=1, source_target_pairs={{0,4},{1,3},{2,6},{3,1},{4,0},{5,7},{6,2},{7,5},{8,12},{9,11},{10,... | collective-permute-start | bytes 983048 | tf_op jit(solution)/shard_map/ppermute | solution.py:342
  15.3 1.5 collective-permute-start.3
  16.8 2.7 %collective-permute-done.1 = bf16[32,3072]{1,0:T(8,128)(2,1)S(1)} collective-permute-done((bf16[32,3072]{1,0:T(8,128)(2,1)}, bf16[32,3072]{1,0:T(8,128)(2,1)S(1)}, u32[]{:S(2)}, u32[]{:S(2)}) %collective-permute-start.1) | collective-permute-done | bytes 196640 | tf_op jit(solution)/shard_map/ppermute | solution.py:342
  19.4 0.0 collective-permute-done
  19.4 1.6 %collective-permute-done.2 = bf16[32,3072]{1,0:T(8,128)(2,1)S(1)} collective-permute-done((bf16[32,3072]{1,0:T(8,128)(2,1)}, bf16[32,3072]{1,0:T(8,128)(2,1)S(1)}, u32[]{:S(2)}, u32[]{:S(2)}) %collective-permute-start.2) | collective-permute-done | bytes 196640 | tf_op jit(solution)/shard_map/ppermute | solution.py:342
  21.1 1.0 pad_maximum_fusion.2.refs_0_
  22.1 3.7 %collective-permute-done.4 = bf16[32,5120]{1,0:T(8,128)(2,1)S(1)} collective-permute-done((bf16[32,5120]{1,0:T(8,128)(2,1)}, bf16[32,5120]{1,0:T(8,128)(2,1)S(1)}, u32[]{:S(2)}, u32[]{:S(2)}) %collective-permute-start.4) | collective-permute-done | bytes 327712 | tf_op jit(solution)/shard_map/ppermute | solution.py:342
  25.8 0.0 collective-permute-done.3
  25.8 3.8 %all-to-all-done = bf16[32,8,512]{2,1,0:T(8,128)(2,1)S(1)} async-done(((bf16[32,8,512]{2,1,0:T(8,128)(2,1)}), bf16[32,8,512]{2,1,0:T(8,128)(2,1)S(1)}, u32[]{:S(2)}, u32[]{:S(2)}) %all-to-all-start) | async-done | bytes 262176 | tf_op jit(solution)/shard_map/all_to_all | solution.py:329
  29.6 0.7 collective-permute-start.7
  30.3 1.3 collective-permute-start.6
  31.7 0.2 collective-permute-start.5
  31.9 3.1 %collective-permute-start.9 = (bf16[32,5120]{1,0:T(8,128)(2,1)S(1)}, bf16[32,5120]{1,0:T(8,128)(2,1)S(1)}, u32[]{:S(2)}, u32[]{:S(2)}) collective-permute-start(bf16[32,5120]{1,0:T(8,128)(2,1)S(1)} %copy-done.3), channel_id=1, source_target_pairs={{0,16},{1,17},{2,18},{3,19},{4,20},{5,21},{6,22},{7,23},{8,24},{9,... | collective-permute-start | bytes 983048 | tf_op jit(solution)/shard_map/ppermute | solution.py:342
  34.9 1.1 collective-permute-start.8
  36.0 4.1 %collective-permute-done.7 = bf16[32,5120]{1,0:T(8,128)(2,1)S(1)} collective-permute-done((bf16[32,5120]{1,0:T(8,128)(2,1)S(1)}, bf16[32,5120]{1,0:T(8,128)(2,1)S(1)}, u32[]{:S(2)}, u32[]{:S(2)}) %collective-permute-start.7) | collective-permute-done | bytes 327712 | tf_op jit(solution)/shard_map/ppermute | solution.py:342
  40.1 0.1 pad_maximum_fusion.refs_0_
  40.2 0.0 copy-start.2
  40.2 15.7 %collective-permute-done.9 = bf16[32,5120]{1,0:T(8,128)(2,1)S(1)} collective-permute-done((bf16[32,5120]{1,0:T(8,128)(2,1)S(1)}, bf16[32,5120]{1,0:T(8,128)(2,1)S(1)}, u32[]{:S(2)}, u32[]{:S(2)}) %collective-permute-start.9) | collective-permute-done | bytes 327712 | tf_op jit(solution)/shard_map/ppermute | solution.py:342
  56.0 0.0 collective-permute-done.8
  56.0 0.0 collective-permute-done.6.refs_2_
  56.0 0.0 collective-permute-done.5.refs_1_
  56.0 0.7 collective-permute-start.11
  56.7 0.0 collective-permute-start.12
  56.7 0.5 collective-permute-start.14
  57.2 0.0 collective-permute-start.13
  57.2 1.0 collective-permute-start.10
  58.2 6.7 %collective-permute-done.11 = bf16[32,5120]{1,0:T(8,128)(2,1)S(1)} collective-permute-done((bf16[32,5120]{1,0:T(8,128)(2,1)S(1)}, bf16[32,5120]{1,0:T(8,128)(2,1)S(1)}, u32[]{:S(2)}, u32[]{:S(2)}) %collective-permute-start.11) | collective-permute-done | bytes 327712 | tf_op jit(solution)/shard_map/ppermute | solution.py:342
  65.0 0.1 pad_maximum_fusion.1.refs_1_
  65.0 0.0 copy-start
  65.1 0.0 copy-start.1
  65.1 0.0 collective-permute-done.12.refs_4_
  65.1 0.0 collective-permute-done.14.refs_6_
  65.1 0.0 collective-permute-done.13.refs_5_
  65.1 4.1 %collective-permute-done.10.refs_3_ = bf16[128,3072]{1,0:T(8,128)(2,1)S(1)} collective-permute-done((bf16[128,3072]{1,0:T(8,128)(2,1)S(1)}, bf16[128,3072]{1,0:T(8,128)(2,1)S(1)}, u32[]{:S(2)}, u32[]{:S(2)}) %collective-permute-start.10) | collective-permute-done | bytes 786464 | tf_op jit(solution)/shard_map/ppermute | solution.py:342
  69.2 0.0 collective-permute-start.18
  69.2 0.5 collective-permute-start.19
  69.7 1.0 collective-permute-start.16
  70.7 0.9 collective-permute-start.15
  71.6 0.0 collective-permute-start.17
  71.6 3.1 %collective-permute-done.17.refs_7_ = bf16[128,3072]{1,0:T(8,128)(2,1)S(1)} collective-permute-done((bf16[128,3072]{1,0:T(8,128)(2,1)S(1)}, bf16[128,3072]{1,0:T(8,128)(2,1)S(1)}, u32[]{:S(2)}, u32[]{:S(2)}) %collective-permute-start.17) | collective-permute-done | bytes 786464 | tf_op jit(solution)/shard_map/ppermute | solution.py:342
  74.7 2.4 %spatial_forward.1 = (bf16[256,512]{1,0:T(8,128)(2,1)S(1)}, bf16[128,3072]{1,0:T(8,128)(2,1)S(1)}, f32[128,2048]{1,0:T(8,128)S(1)}) custom-call(bf16[256,512]{1,0:T(8,128)(2,1)S(1)} %bitcast.12, s32[32,128]{1,0:T(8,128)S(1)} %copy-done.2, bf16[128,3072]{1,0:T(8,128)(2,1)S(1)} %pad_maximum_fusion.2.refs_0_, ...), custom_call_target="tpu_custom_call" | custom-call | flops 805306368 | bytes 8388608 | tf_op jit(solution)/shard_map/spatial_forward/pallas_call | solution.py:402
  77.1 0.0 collective-permute-done.19.refs_6_
  77.1 16.6 %collective-permute-done.16.refs_3_ = bf16[96,5120]{1,0:T(8,128)(2,1)S(1)} collective-permute-done((bf16[96,5120]{1,0:T(8,128)(2,1)S(1)}, bf16[96,5120]{1,0:T(8,128)(2,1)S(1)}, u32[]{:S(2)}, u32[]{:S(2)}) %collective-permute-start.16) | collective-permute-done | bytes 983072 | tf_op jit(solution)/shard_map/ppermute | solution.py:342
  93.8 0.0 collective-permute-done.15.refs_2_
  93.8 0.0 collective-permute-done.18.refs_5_
  93.8 0.0 collective-permute-start.22
  93.8 0.5 collective-permute-start.21
  94.3 1.2 collective-permute-start.20
  95.5 15.7 %all_to_all.20 = bf16[32,8,512]{2,1,0:T(8,128)(2,1)S(1)} all-to-all(bf16[32,8,512]{2,1,0:T(8,128)(2,1)S(1)} %bitcast.21), channel_id=1, replica_groups=mesh['parts'=1,'grid'=32] {'grid'}, dimensions={0} | all-to-all | bytes 524288 | tf_op jit(solution)/shard_map/all_to_all | solution.py:329
  111.2 0.0 collective-permute-done.22.refs_8_
  111.2 0.0 collective-permute-done.21.refs_7_
  111.2 0.0 collective-permute-done.20.refs_4_
  111.2 0.1 collective-permute-start.23
  111.3 2.6 %collective-permute-done.23.refs_9_ = bf16[96,5120]{1,0:T(8,128)(2,1)S(1)} collective-permute-done((bf16[96,5120]{1,0:T(8,128)(2,1)S(1)}, bf16[96,5120]{1,0:T(8,128)(2,1)S(1)}, u32[]{:S(2)}, u32[]{:S(2)}) %collective-permute-start.23) | collective-permute-done | bytes 983072 | tf_op jit(solution)/shard_map/ppermute | solution.py:342
  113.9 8.5 %group_layer.1 = (bf16[128,1024]{1,0:T(8,128)(2,1)}, bf16[128,1024]{1,0:T(8,128)(2,1)S(1)}, bf16[256,512]{1,0:T(8,128)(2,1)S(1)}) custom-call(bf16[128,1024]{1,0:T(8,128)(2,1)S(1)} %bitcast.15, bf16[256,512]{1,0:T(8,128)(2,1)S(1)} %bitcast.16, bf16[128,1024]{1,0:T(8,128)(2,1)S(1)} %bitcast.20, bf16[128,5120]{1,0:T(8,128)(2,1)S(1)} %pad_maximum_fusion.refs_0_, ...), custom_call_target="tpu_custom_call" | custom-call | flops 2684354560 | bytes 23068672 | tf_op jit(solution)/shard_map/group_layer/pallas_call | solution.py:422
  122.4 15.0 %all_to_all.21 = bf16[32,8,512]{2,1,0:T(8,128)(2,1)S(1)} all-to-all(bf16[32,8,512]{2,1,0:T(8,128)(2,1)S(1)} %bitcast.22), channel_id=1, replica_groups=mesh['parts'=1,'grid'=32] {'grid'}, dimensions={0} | all-to-all | bytes 524288 | tf_op jit(solution)/shard_map/all_to_all | solution.py:329
  137.4 5.1 %spatial_backward.1 = bf16[256,512]{1,0:T(8,128)(2,1)S(1)} custom-call(bf16[256,512]{1,0:T(8,128)(2,1)S(1)} %bitcast.13, bf16[256,512]{1,0:T(8,128)(2,1)S(1)} %bitcast.17, bf16[128,3072]{1,0:T(8,128)(2,1)S(1)} %get-tuple-element.74.qkv, f32[128,2048]{1,0:T(8,128)S(1)} %get-tuple-element.75.probs, bf16[128,3072]{1,0:T(8,128)(2,1)S(1)} %pad_maximum_fusion.2.refs_0_, ...), custom_call_target="tpu_custom_call" | custom-call | flops 805306368 | bytes 8388608 | tf_op jit(solution)/shard_map/spatial_backward/pallas_call | solution.py:440
  142.5 12.8 %all_to_all.22 = bf16[32,8,512]{2,1,0:T(8,128)(2,1)S(1)} all-to-all(bf16[32,8,512]{2,1,0:T(8,128)(2,1)S(1)} %bitcast.18), channel_id=1, replica_groups=mesh['parts'=1,'grid'=32] {'grid'}, dimensions={0} | all-to-all | bytes 524288 | tf_op jit(solution)/shard_map/all_to_all | solution.py:329
  155.3 0.9 add_packed.1
  (5 shorter events, 0.0 us)
Async XLA Ops:
  0.6 18.8 %collective-permute-start.1 = (bf16[32,3072]{1,0:T(8,128)(2,1)}, bf16[32,3072]{1,0:T(8,128)(2,1)S(1)}, u32[]{:S(2)}, u32[]{:S(2)}) collective-permute-start(bf16[32,3072]{1,0:T(8,128)(2,1)} %param.9), channel_id=1, source_target_pairs={{0,16},{1,17},{2,18},{3,19},{4,20},{5,21},{6,22},{7,23},{8,24},{9,... | collective-permute-start | bytes 589832 | tf_op jit(solution)/shard_map/ppermute | solution.py:342
  4.7 14.7 %collective-permute-start = (bf16[32,3072]{1,0:T(8,128)(2,1)}, bf16[32,3072]{1,0:T(8,128)(2,1)S(1)}, u32[]{:S(2)}, u32[]{:S(2)}) collective-permute-start(bf16[32,3072]{1,0:T(8,128)(2,1)} %param.9), channel_id=1, source_target_pairs={{0,8},{1,9},{2,10},{3,11},{4,12},{5,13},{6,14},{7,15},{8,16},{9,17... | collective-permute-start | bytes 589832 | tf_op jit(solution)/shard_map/ppermute | solution.py:342
  6.3 14.8 %collective-permute-start.2 = (bf16[32,3072]{1,0:T(8,128)(2,1)}, bf16[32,3072]{1,0:T(8,128)(2,1)S(1)}, u32[]{:S(2)}, u32[]{:S(2)}) collective-permute-start(bf16[32,3072]{1,0:T(8,128)(2,1)} %param.9), channel_id=1, source_target_pairs={{0,24},{1,25},{2,26},{3,27},{4,28},{5,29},{6,30},{7,31},{8,0},{9,1... | collective-permute-start | bytes 589832 | tf_op jit(solution)/shard_map/ppermute | solution.py:342
  10.6 21.2 %copy-start.3 = (bf16[32,5120]{1,0:T(8,128)(2,1)S(1)}, bf16[32,5120]{1,0:T(8,128)(2,1)}, u32[]{:S(2)}) copy-start(bf16[32,5120]{1,0:T(8,128)(2,1)} %get-tuple-element.48) | copy-start | bytes 983044
  10.6 19.0 %all-to-all-start = ((bf16[32,8,512]{2,1,0:T(8,128)(2,1)}), bf16[32,8,512]{2,1,0:T(8,128)(2,1)S(1)}, u32[]{:S(2)}, u32[]{:S(2)}) async-start(bf16[32,8,512]{2,1,0:T(8,128)(2,1)} %bitcast.24), calls=%async_computation | async-start | bytes 524288 | tf_op jit(solution)/shard_map/all_to_all | solution.py:329
  13.5 12.3 %collective-permute-start.4 = (bf16[32,5120]{1,0:T(8,128)(2,1)}, bf16[32,5120]{1,0:T(8,128)(2,1)S(1)}, u32[]{:S(2)}, u32[]{:S(2)}) collective-permute-start(bf16[32,5120]{1,0:T(8,128)(2,1)} %get-tuple-element.48), channel_id=1, source_target_pairs={{0,4},{1,3},{2,6},{3,1},{4,0},{5,7},{6,2},{7,5},{8,12},{9,11},{10,... | collective-permute-start | bytes 983048 | tf_op jit(solution)/shard_map/ppermute | solution.py:342
  15.3 10.5 %collective-permute-start.3 = (bf16[32,5120]{1,0:T(8,128)(2,1)}, bf16[32,5120]{1,0:T(8,128)(2,1)S(1)}, u32[]{:S(2)}, u32[]{:S(2)}) collective-permute-start(bf16[32,5120]{1,0:T(8,128)(2,1)} %get-tuple-element.48), channel_id=1, source_target_pairs={{0,2},{1,5},{2,0},{3,7},{4,6},{5,1},{6,4},{7,3},{8,10},{9,13},{10,... | collective-permute-start | bytes 983048 | tf_op jit(solution)/shard_map/ppermute | solution.py:342
  29.6 10.5 %collective-permute-start.7 = (bf16[32,5120]{1,0:T(8,128)(2,1)S(1)}, bf16[32,5120]{1,0:T(8,128)(2,1)S(1)}, u32[]{:S(2)}, u32[]{:S(2)}) collective-permute-start(bf16[32,5120]{1,0:T(8,128)(2,1)S(1)} %collective-permute-done.3), channel_id=1, source_target_pairs={{0,4},{1,3},{2,6},{3,1},{4,0},{5,7},{6,2},{7,5},{8,12},{9,11},{10,... | collective-permute-start | bytes 983048 | tf_op jit(solution)/shard_map/ppermute | solution.py:342
  30.3 25.7 %collective-permute-start.6 = (bf16[128,3072]{1,0:T(8,128)(2,1)S(1)}, bf16[128,3072]{1,0:T(8,128)(2,1)S(1)}, u32[]{:S(2)}, u32[]{:S(2)}) collective-permute-start(bf16[128,3072]{1,0:T(8,128)(2,1)S(1)} %pad_maximum_fusion.2.refs_0_), channel_id=1, source_target_pairs={{0,4},{1,3},{2,6},{3,1},{4,0},{5,7},{6,2},{7,5},{8,12},{9,11},{10,... | collective-permute-start | bytes 2359304 | tf_op jit(solution)/shard_map/ppermute | solution.py:342
  31.7 24.3 %collective-permute-start.5 = (bf16[128,3072]{1,0:T(8,128)(2,1)S(1)}, bf16[128,3072]{1,0:T(8,128)(2,1)S(1)}, u32[]{:S(2)}, u32[]{:S(2)}) collective-permute-start(bf16[128,3072]{1,0:T(8,128)(2,1)S(1)} %pad_maximum_fusion.2.refs_0_), channel_id=1, source_target_pairs={{0,2},{1,5},{2,0},{3,7},{4,6},{5,1},{6,4},{7,3},{8,10},{9,13},{10,... | collective-permute-start | bytes 2359304 | tf_op jit(solution)/shard_map/ppermute | solution.py:342
  31.9 24.1 %collective-permute-start.9 = (bf16[32,5120]{1,0:T(8,128)(2,1)S(1)}, bf16[32,5120]{1,0:T(8,128)(2,1)S(1)}, u32[]{:S(2)}, u32[]{:S(2)}) collective-permute-start(bf16[32,5120]{1,0:T(8,128)(2,1)S(1)} %copy-done.3), channel_id=1, source_target_pairs={{0,16},{1,17},{2,18},{3,19},{4,20},{5,21},{6,22},{7,23},{8,24},{9,... | collective-permute-start | bytes 983048 | tf_op jit(solution)/shard_map/ppermute | solution.py:342
  34.9 21.0 %collective-permute-start.8 = (bf16[32,5120]{1,0:T(8,128)(2,1)S(1)}, bf16[32,5120]{1,0:T(8,128)(2,1)S(1)}, u32[]{:S(2)}, u32[]{:S(2)}) collective-permute-start(bf16[32,5120]{1,0:T(8,128)(2,1)S(1)} %copy-done.3), channel_id=1, source_target_pairs={{0,8},{1,9},{2,10},{3,11},{4,12},{5,13},{6,14},{7,15},{8,16},{9,17... | collective-permute-start | bytes 983048 | tf_op jit(solution)/shard_map/ppermute | solution.py:342
  40.2 34.5 %copy-start.2 = (s32[32,128]{1,0:T(8,128)S(1)}, s32[32,128]{1,0:T(8,128)}, u32[]{:S(2)}) copy-start(s32[32,128]{1,0:T(8,128)} %keep.1) | copy-start | bytes 49156
  56.0 9.0 %collective-permute-start.11 = (bf16[32,5120]{1,0:T(8,128)(2,1)S(1)}, bf16[32,5120]{1,0:T(8,128)(2,1)S(1)}, u32[]{:S(2)}, u32[]{:S(2)}) collective-permute-start(bf16[32,5120]{1,0:T(8,128)(2,1)S(1)} %copy-done.3), channel_id=1, source_target_pairs={{0,24},{1,25},{2,26},{3,27},{4,28},{5,29},{6,30},{7,31},{8,0},{9,1... | collective-permute-start | bytes 983048 | tf_op jit(solution)/shard_map/ppermute | solution.py:342
  56.7 8.4 %collective-permute-start.12 = (bf16[128,3072]{1,0:T(8,128)(2,1)S(1)}, bf16[128,3072]{1,0:T(8,128)(2,1)S(1)}, u32[]{:S(2)}, u32[]{:S(2)}) collective-permute-start(bf16[128,3072]{1,0:T(8,128)(2,1)S(1)} %pad_maximum_fusion.2.refs_0_), channel_id=1, source_target_pairs={{0,1},{1,0},{2,3},{3,2},{4,5},{5,4},{6,7},{7,6},{8,9},{9,8},{10,11... | collective-permute-start | bytes 2359304 | tf_op jit(solution)/shard_map/ppermute | solution.py:342
  56.7 8.4 %collective-permute-start.14 = (bf16[128,3072]{1,0:T(8,128)(2,1)S(1)}, bf16[128,3072]{1,0:T(8,128)(2,1)S(1)}, u32[]{:S(2)}, u32[]{:S(2)}) collective-permute-start(bf16[128,3072]{1,0:T(8,128)(2,1)S(1)} %collective-permute-done.6.refs_2_), channel_id=1, source_target_pairs={{0,1},{1,0},{2,3},{3,2},{4,5},{5,4},{6,7},{7,6},{8,9},{9,8},{10,11... | collective-permute-start | bytes 2359304 | tf_op jit(solution)/shard_map/ppermute | solution.py:342
  57.2 7.9 %collective-permute-start.13 = (bf16[128,3072]{1,0:T(8,128)(2,1)S(1)}, bf16[128,3072]{1,0:T(8,128)(2,1)S(1)}, u32[]{:S(2)}, u32[]{:S(2)}) collective-permute-start(bf16[128,3072]{1,0:T(8,128)(2,1)S(1)} %collective-permute-done.5.refs_1_), channel_id=1, source_target_pairs={{0,1},{1,0},{2,3},{3,2},{4,5},{5,4},{6,7},{7,6},{8,9},{9,8},{10,11... | collective-permute-start | bytes 2359304 | tf_op jit(solution)/shard_map/ppermute | solution.py:342
  57.2 12.0 %collective-permute-start.10 = (bf16[128,3072]{1,0:T(8,128)(2,1)S(1)}, bf16[128,3072]{1,0:T(8,128)(2,1)S(1)}, u32[]{:S(2)}, u32[]{:S(2)}) collective-permute-start(bf16[128,3072]{1,0:T(8,128)(2,1)S(1)} %collective-permute-done.5.refs_1_), channel_id=1, source_target_pairs={{0,4},{1,3},{2,6},{3,1},{4,0},{5,7},{6,2},{7,5},{8,12},{9,11},{10,... | collective-permute-start | bytes 2359304 | tf_op jit(solution)/shard_map/ppermute | solution.py:342
  65.0 48.8 %copy-start = (bf16[4,32,1024]{2,1,0:T(8,128)(2,1)S(1)}, bf16[4,32,1024]{2,1,0:T(8,128)(2,1)}, u32[]{:S(2)}) copy-start(bf16[4,32,1024]{2,1,0:T(8,128)(2,1)} %param.7) | copy-start | bytes 786436
  65.1 48.8 %copy-start.1 = (bf16[4,32,1024]{2,1,0:T(8,128)(2,1)S(1)}, bf16[4,32,1024]{2,1,0:T(8,128)(2,1)}, u32[]{:S(2)}) copy-start(bf16[4,32,1024]{2,1,0:T(8,128)(2,1)} %param.8) | copy-start | bytes 786436
  69.2 24.6 %collective-permute-start.18 = (bf16[128,5120]{1,0:T(8,128)(2,1)S(1)}, bf16[128,5120]{1,0:T(8,128)(2,1)S(1)}, u32[]{:S(2)}, u32[]{:S(2)}) collective-permute-start(bf16[128,5120]{1,0:T(8,128)(2,1)S(1)} %pad_maximum_fusion.refs_0_), channel_id=1, source_target_pairs={{0,1},{1,0},{2,3},{3,2},{4,5},{5,4},{6,7},{7,6},{8,9},{9,8},{10,11... | collective-permute-start | bytes 3932168 | tf_op jit(solution)/shard_map/ppermute | solution.py:342
  69.2 7.9 %collective-permute-start.19 = (bf16[96,5120]{1,0:T(8,128)(2,1)S(1)}, bf16[96,5120]{1,0:T(8,128)(2,1)S(1)}, u32[]{:S(2)}, u32[]{:S(2)}) collective-permute-start(bf16[96,5120]{1,0:T(8,128)(2,1)S(1)} %pad_maximum_fusion.1.refs_1_), channel_id=1, source_target_pairs={{0,1},{1,0},{2,3},{3,2},{4,5},{5,4},{6,7},{7,6},{8,9},{9,8},{10,11... | collective-permute-start | bytes 2949128 | tf_op jit(solution)/shard_map/ppermute | solution.py:342
  69.7 24.1 %collective-permute-start.16 = (bf16[96,5120]{1,0:T(8,128)(2,1)S(1)}, bf16[96,5120]{1,0:T(8,128)(2,1)S(1)}, u32[]{:S(2)}, u32[]{:S(2)}) collective-permute-start(bf16[96,5120]{1,0:T(8,128)(2,1)S(1)} %pad_maximum_fusion.1.refs_1_), channel_id=1, source_target_pairs={{0,4},{1,3},{2,6},{3,1},{4,0},{5,7},{6,2},{7,5},{8,12},{9,11},{10,... | collective-permute-start | bytes 2949128 | tf_op jit(solution)/shard_map/ppermute | solution.py:342
  70.7 23.1 %collective-permute-start.15 = (bf16[96,5120]{1,0:T(8,128)(2,1)S(1)}, bf16[96,5120]{1,0:T(8,128)(2,1)S(1)}, u32[]{:S(2)}, u32[]{:S(2)}) collective-permute-start(bf16[96,5120]{1,0:T(8,128)(2,1)S(1)} %pad_maximum_fusion.1.refs_1_), channel_id=1, source_target_pairs={{0,2},{1,5},{2,0},{3,7},{4,6},{5,1},{6,4},{7,3},{8,10},{9,13},{10,... | collective-permute-start | bytes 2949128 | tf_op jit(solution)/shard_map/ppermute | solution.py:342
  71.6 3.1 %collective-permute-start.17 = (bf16[128,3072]{1,0:T(8,128)(2,1)S(1)}, bf16[128,3072]{1,0:T(8,128)(2,1)S(1)}, u32[]{:S(2)}, u32[]{:S(2)}) collective-permute-start(bf16[128,3072]{1,0:T(8,128)(2,1)S(1)} %collective-permute-done.10.refs_3_), channel_id=1, source_target_pairs={{0,1},{1,0},{2,3},{3,2},{4,5},{5,4},{6,7},{7,6},{8,9},{9,8},{10,11... | collective-permute-start | bytes 2359304 | tf_op jit(solution)/shard_map/ppermute | solution.py:342
  93.8 17.4 %collective-permute-start.22 = (bf16[96,5120]{1,0:T(8,128)(2,1)S(1)}, bf16[96,5120]{1,0:T(8,128)(2,1)S(1)}, u32[]{:S(2)}, u32[]{:S(2)}) collective-permute-start(bf16[96,5120]{1,0:T(8,128)(2,1)S(1)} %collective-permute-done.16.refs_3_), channel_id=1, source_target_pairs={{0,1},{1,0},{2,3},{3,2},{4,5},{5,4},{6,7},{7,6},{8,9},{9,8},{10,11... | collective-permute-start | bytes 2949128 | tf_op jit(solution)/shard_map/ppermute | solution.py:342
  93.8 17.4 %collective-permute-start.21 = (bf16[96,5120]{1,0:T(8,128)(2,1)S(1)}, bf16[96,5120]{1,0:T(8,128)(2,1)S(1)}, u32[]{:S(2)}, u32[]{:S(2)}) collective-permute-start(bf16[96,5120]{1,0:T(8,128)(2,1)S(1)} %collective-permute-done.15.refs_2_), channel_id=1, source_target_pairs={{0,1},{1,0},{2,3},{3,2},{4,5},{5,4},{6,7},{7,6},{8,9},{9,8},{10,11... | collective-permute-start | bytes 2949128 | tf_op jit(solution)/shard_map/ppermute | solution.py:342
  94.3 16.9 %collective-permute-start.20 = (bf16[96,5120]{1,0:T(8,128)(2,1)S(1)}, bf16[96,5120]{1,0:T(8,128)(2,1)S(1)}, u32[]{:S(2)}, u32[]{:S(2)}) collective-permute-start(bf16[96,5120]{1,0:T(8,128)(2,1)S(1)} %collective-permute-done.15.refs_2_), channel_id=1, source_target_pairs={{0,4},{1,3},{2,6},{3,1},{4,0},{5,7},{6,2},{7,5},{8,12},{9,11},{10,... | collective-permute-start | bytes 2949128 | tf_op jit(solution)/shard_map/ppermute | solution.py:342
  111.2 2.6 %collective-permute-start.23 = (bf16[96,5120]{1,0:T(8,128)(2,1)S(1)}, bf16[96,5120]{1,0:T(8,128)(2,1)S(1)}, u32[]{:S(2)}, u32[]{:S(2)}) collective-permute-start(bf16[96,5120]{1,0:T(8,128)(2,1)S(1)} %collective-permute-done.20.refs_4_), channel_id=1, source_target_pairs={{0,1},{1,0},{2,3},{3,2},{4,5},{5,4},{6,7},{7,6},{8,9},{9,8},{10,11... | collective-permute-start | bytes 2949128 | tf_op jit(solution)/shard_map/ppermute | solution.py:342

commit v5 on v4

--- a/solution.py
+++ b/solution.py
@@ -131,41 +131,52 @@
     return jnp.where(low, stacked[:rows], stacked[rows:])
 
 
-def halves(values):
-    width = values.shape[1] // 2
-    first = jnp.sum(values[:, :width], axis=-1, keepdims=True)
-    second = jnp.sum(values[:, width:], axis=-1, keepdims=True)
-    rows = values.shape[0]
-    return jnp.concatenate(
-        [jnp.broadcast_to(first, (rows, width)), jnp.broadcast_to(second, (rows, width))], axis=1
-    )
-
-
 def low_lanes(rows):
     return lax.broadcasted_iota(jnp.int32, (rows, 128), 1) < 64
 
 
-def pair_forward(qkv, allowed, low, width, pair):
-    query = qkv[:, pair * 128 : pair * 128 + 128]
-    keyed = head_pair(qkv[:, width + pair * 128 : width + pair * 128 + 128], low)
-    valued = head_pair(qkv[:, 2 * width + pair * 128 : 2 * width + pair * 128 + 128], low)
-    weights = jnp.where(allowed, jnp.exp(nt(query, keyed) * 0.125), 0.0)
-    probs = weights / halves(weights)
-    result = nn(probs.astype(jnp.bfloat16), valued).astype(jnp.bfloat16)
-    return probs, result
-
-
-def pair_backward(qkv, probs, grad, low, width, pair):
-    query = qkv[:, pair * 128 : pair * 128 + 128]
-    keyed = head_pair(qkv[:, width + pair * 128 : width + pair * 128 + 128], low)
-    valued = head_pair(qkv[:, 2 * width + pair * 128 : 2 * width + pair * 128 + 128], low)
-    grad_probs = nt(grad, valued).astype(jnp.bfloat16).astype(jnp.float32)
-    grad_scores = probs * (grad_probs - halves(grad_probs * probs))
-    grad_scores = (grad_scores * 0.125).astype(jnp.bfloat16)
-    grad_value = join_pair(tn(probs.astype(jnp.bfloat16), grad), low).astype(jnp.bfloat16)
-    grad_query = nn(grad_scores, keyed).astype(jnp.bfloat16)
-    grad_key = join_pair(tn(grad_scores, query), low).astype(jnp.bfloat16)
-    return grad_query, grad_key, grad_value
+def columns(which, pair, width):
+    return slice(which * width + pair * 128, which * width + pair * 128 + 128)
+
+
+def attention_forward(qkv, allowed, probs):
+    rows, width = qkv.shape[0], qkv.shape[1] // 3
+    span, pairs, low = 2 * rows, width // 128, low_lanes(rows)
+    for pair in range(pairs):
+        keyed = head_pair(qkv[:, columns(1, pair, width)], low)
+        probs[:, pair * span : pair * span + span] = nt(qkv[:, columns(0, pair, width)], keyed)
+    for head in range(2 * pairs):
+        at = slice(head * rows, head * rows + rows)
+        weights = jnp.where(allowed, jnp.exp(probs[:, at] * 0.125), 0.0)
+        probs[:, at] = weights * (1.0 / jnp.sum(weights, axis=-1, keepdims=True))
+    results = []
+    for pair in range(pairs):
+        valued = head_pair(qkv[:, columns(2, pair, width)], low)
+        results.append(nn(probs[:, pair * span : pair * span + span].astype(jnp.bfloat16), valued).astype(jnp.bfloat16))
+    return jnp.concatenate(results, axis=1)
+
+
+def attention_backward(qkv, probs, grad, grad_probs, grad_scores, grads):
+    rows, width = qkv.shape[0], qkv.shape[1] // 3
+    span, pairs, low = 2 * rows, width // 128, low_lanes(rows)
+    for pair in range(pairs):
+        valued = head_pair(qkv[:, columns(2, pair, width)], low)
+        part = nt(grad[:, columns(0, pair, width)], valued)
+        grad_probs[:, pair * span : pair * span + span] = part.astype(jnp.bfloat16)
+    for head in range(2 * pairs):
+        at = slice(head * rows, head * rows + rows)
+        share, part = probs[:, at], grad_probs[:, at].astype(jnp.float32)
+        inner = jnp.sum(part * share, axis=-1, keepdims=True)
+        grad_scores[:, at] = (share * (part - inner) * 0.125).astype(jnp.bfloat16)
+    for pair in range(pairs):
+        at = slice(pair * span, pair * span + span)
+        keyed = head_pair(qkv[:, columns(1, pair, width)], low)
+        query, part = qkv[:, columns(0, pair, width)], grad[:, columns(0, pair, width)]
+        scored = grad_scores[:, at]
+        grads[:, columns(0, pair, width)] = nn(scored, keyed).astype(jnp.bfloat16)
+        grads[:, columns(1, pair, width)] = join_pair(tn(scored, query), low).astype(jnp.bfloat16)
+        shares = probs[:, at].astype(jnp.bfloat16)
+        grads[:, columns(2, pair, width)] = join_pair(tn(shares, part), low).astype(jnp.bfloat16)
 
 
 def place_rows(refs, plan, first, buffer):
@@ -223,78 +234,49 @@
 
 
 def spatial_forward(plan, patches, groups, packed, keep, *refs):
-    pieces, (result_out, qkv_out, probs_out, qkv_buf) = refs[:-4], refs[-4:]
-    rows, width = packed.shape[0] // 2, packed.shape[1] * 2
-    span = 2 * rows
-    place_rows(pieces, plan, 0, qkv_buf)
-    wide = unpack(packed[...], patches, groups, True).astype(jnp.float32)
+    pieces, (result_out, qkv_out, probs_out, banded_out, weight_out) = refs[:-5], refs[-5:]
+    place_rows(pieces, plan, 0, weight_out)
+    banded = unpack(packed[...], patches, groups, True)
+    banded_out[...] = banded
+    wide = banded.astype(jnp.float32)
     normed = (wide * inverse_rms(wide)).astype(jnp.bfloat16)
-    kept = keep[pl.ds(lax.axis_index("grid"), 1), :]
-    allowed = jnp.concatenate([kept, kept], axis=1) > 0
-    low = low_lanes(rows)
-    qkv_out[...] = nn(normed, qkv_buf[...]).astype(jnp.bfloat16)
-    results = []
-    for pair in range(width // 128):
-        probs, result = pair_forward(qkv_out, allowed, low, width, pair)
-        probs_out[:, pair * span : pair * span + span] = probs
-        results.append(result)
-    result_out[...] = pack(jnp.concatenate(results, axis=1), patches, groups, True)
-
-
-def spatial_backward(plan, patches, groups, packed, grad_packed, qkv, probs, *refs):
-    pieces, (grad_out, qkv_buf, grads) = refs[:-3], refs[-3:]
-    rows, width = packed.shape[0] // 2, packed.shape[1] * 2
-    span = 2 * rows
-    place_rows(pieces, plan, 0, qkv_buf)
-    low = low_lanes(rows)
+    allowed = keep[pl.ds(lax.axis_index("grid"), 1), :] > 0
+    qkv_out[...] = nn(normed, weight_out[...]).astype(jnp.bfloat16)
+    result_out[...] = pack(attention_forward(qkv_out, allowed, probs_out), patches, groups, True)
+
+
+def spatial_backward(
+    patches, groups, grad_packed, banded, qkv, probs, weight, grad_out, grads, grad_probs, grad_scores
+):
     grad = unpack(grad_packed[...], patches, groups, True)
-    for pair in range(width // 128):
-        at = pair * 128
-        parts = pair_backward(
-            qkv, probs[:, pair * span : pair * span + span], grad[:, at : at + 128], low, width, pair
-        )
-        for which, part in enumerate(parts):
-            grads[:, which * width + at : which * width + at + 128] = part
-    wide = unpack(packed[...], patches, groups, True).astype(jnp.float32)
+    attention_backward(qkv, probs, grad, grad_probs, grad_scores, grads)
+    wide = banded[...].astype(jnp.float32)
     inverse = inverse_rms(wide)
-    grad_normed = nt(grads[...], qkv_buf[...]).astype(jnp.bfloat16).astype(jnp.float32)
+    grad_normed = nt(grads[...], weight[...]).astype(jnp.bfloat16).astype(jnp.float32)
     grad_out[...] = pack(norm_grad(wide, inverse, grad_normed).astype(jnp.bfloat16), patches, groups, True)
 
 
 def group_layer(patches, plan, tokens, attended, cotangent, *refs):
-    pieces, rest = refs[:-10], refs[-10:]
-    mixed, grad_y, grad_bands, so_buf, qkv_buf, go_buf, qkv, grads, probs_buf, y_buf = rest
+    pieces, rest = refs[:-12], refs[-12:]
+    mixed, grad_y, grad_bands, so_buf, qkv_buf, go_buf, qkv, probs, y_buf, grads, grad_probs, grad_scores = rest
     rows, width = tokens.shape
     groups = rows // patches
-    span = 2 * rows
     place_rows(pieces, plan, 0, so_buf)
-    place_rows(pieces, plan, width, qkv_buf)
-    place_rows(pieces, plan, 4 * width, go_buf)
     ordered = unpack(attended[...], patches, groups, False)
-    low = low_lanes(rows)
-    row_patch = lax.broadcasted_iota(jnp.int32, (rows, span), 0) // groups
-    column_patch = (lax.broadcasted_iota(jnp.int32, (rows, span), 1) % rows) // groups
-    allowed = row_patch == column_patch
     y_first = (tokens[...].astype(jnp.float32) + nn(ordered, so_buf[...])).astype(jnp.bfloat16)
     wide = y_first.astype(jnp.float32)
     y_buf[...] = wide
     inverse = inverse_rms(wide)
     normed = (wide * inverse).astype(jnp.bfloat16)
+    place_rows(pieces, plan, width, qkv_buf)
     qkv[...] = nn(normed, qkv_buf[...]).astype(jnp.bfloat16)
-    results = []
-    for pair in range(width // 128):
-        probs, result = pair_forward(qkv, allowed, low, width, pair)
-        probs_buf[:, pair * span : pair * span + span] = probs
-        results.append(result)
-    mixed[...] = (y_buf[...] + nn(jnp.concatenate(results, axis=1), go_buf[...])).astype(jnp.bfloat16)
+    place_rows(pieces, plan, 4 * width, go_buf)
     grad_attended = nt(cotangent[...], go_buf[...]).astype(jnp.bfloat16)
-    for pair in range(width // 128):
-        at = pair * 128
-        parts = pair_backward(
-            qkv, probs_buf[:, pair * span : pair * span + span], grad_attended[:, at : at + 128], low, width, pair
-        )
-        for which, part in enumerate(parts):
-            grads[:, which * width + at : which * width + at + 128] = part
+    row_patch = lax.broadcasted_iota(jnp.int32, (rows, rows), 0) // groups
+    allowed = row_patch == lax.broadcasted_iota(jnp.int32, (rows, rows), 1) // groups
+    results = attention_forward(qkv, allowed, probs)
+    mixed[...] = (y_buf[...] + nn(results, go_buf[...])).astype(jnp.bfloat16)
+    attention_backward(qkv, probs, grad_attended, grad_probs, grad_scores, grads)
     grad_normed = nt(grads[...], qkv_buf[...]).astype(jnp.bfloat16).astype(jnp.float32)
     through = norm_grad(y_buf[...], inverse, grad_normed).astype(jnp.bfloat16)
     total = cotangent[...] + through
@@ -399,16 +381,18 @@
     group_across = [move(group_plane, sibling), move(group_line, sibling)]
     spatial_rows = [spatial_line, spatial_one, spatial_other, spatial_both]
     spatial_rows += [*spatial_across, move(spatial_both, sibling)]
-    attended, qkv, probs = pl.pallas_call(
+    probs_shape = shape(all_patches, 2 * pairs * all_patches, jnp.float32)
+    attended, qkv, probs, banded, full_sqkv = pl.pallas_call(
         partial(spatial_forward, spatial_plan, patches, groups),
         out_shape=(
             packed_shape,
             shape(all_patches, 3 * width),
-            shape(all_patches, 2 * pairs * all_patches, jnp.float32),
+            probs_shape,
+            shape(all_patches, width),
+            shape(width, 3 * width),
         ),
         in_specs=[VMEM_SPEC] * (2 + len(spatial_rows)),
-        out_specs=(VMEM_SPEC,) * 3,
-        scratch_shapes=[pltpu.VMEM((width, 3 * width), jnp.bfloat16)],
+        out_specs=(VMEM_SPEC,) * 5,
         compiler_params=room(18),
         cost_estimate=cost(all_patches, width, 3, 1),
         name="spatial_forward",
@@ -419,6 +403,7 @@
     group_both, attended, *group_across = together(group_both, exchange(attended), *group_across)
     group_rows = [group_plane, group_line, group_one, group_other, group_both]
     group_rows += [*group_across, move(group_both, sibling)]
+    heads_wide = 2 * pairs * rows
     mixed, grad_y, grad_bands = pl.pallas_call(
         partial(group_layer, patches, group_plan),
         out_shape=(shape(rows, width), shape(rows, width), packed_shape),
@@ -429,27 +414,31 @@
             pltpu.VMEM((width, 3 * width), jnp.bfloat16),
             pltpu.VMEM((width, width), jnp.bfloat16),
             pltpu.VMEM((rows, 3 * width), jnp.bfloat16),
+            pltpu.VMEM((rows, heads_wide), jnp.float32),
+            pltpu.VMEM((rows, width), jnp.float32),
             pltpu.VMEM((rows, 3 * width), jnp.bfloat16),
-            pltpu.VMEM((rows, 2 * pairs * rows), jnp.float32),
-            pltpu.VMEM((rows, width), jnp.float32),
+            pltpu.VMEM((rows, heads_wide), jnp.bfloat16),
+            pltpu.VMEM((rows, heads_wide), jnp.bfloat16),
         ],
         compiler_params=room(32),
         cost_estimate=cost(rows, width, 5, 2),
         name="group_layer",
     )(tokens, attended, cotangent.reshape(rows, width), *group_rows)
+    heads_wide = 2 * pairs * all_patches
     grad_first = pl.pallas_call(
-        partial(spatial_backward, spatial_plan, patches, groups),
+        partial(spatial_backward, patches, groups),
         out_shape=packed_shape,
-        in_specs=[VMEM_SPEC] * (4 + len(spatial_rows)),
+        in_specs=[VMEM_SPEC] * 5,
         out_specs=VMEM_SPEC,
         scratch_shapes=[
-            pltpu.VMEM((width, 3 * width), jnp.bfloat16),
             pltpu.VMEM((all_patches, 3 * width), jnp.bfloat16),
+            pltpu.VMEM((all_patches, heads_wide), jnp.bfloat16),
+            pltpu.VMEM((all_patches, heads_wide), jnp.bfloat16),
         ],
         compiler_params=room(18),
         cost_estimate=cost(all_patches, width, 3, 1),
         name="spatial_backward",
-    )(banded, exchange(grad_bands), qkv, probs, *spatial_rows)
+    )(exchange(grad_bands), banded, qkv, probs, full_sqkv)
     token_grad = pl.pallas_call(
         partial(add_packed, patches, groups),
         out_shape=shape(rows, width),

time: 157 us -> 152 us (0.968)
  Pallas kernels: 19 us -> 16.4 us
  blocking collectives: 43.5 us -> 41.4 us
  waiting for transfers between devices: 64.9 us -> 66.7 us
    all_to_all x3, blocking collectives: 43.5 us -> 41.4 us  [exchange(): lax.all_to_all(blocks, 'grid', split_axis=0, concat_axis=0, tiled=True)]
    all_to_all x1, waiting for transfers between devices: 3.83 us -> 5.59 us  [exchange(): lax.all_to_all(blocks, 'grid', split_axis=0, concat_axis=0, tiled=True)]
    pallas_call x1, Pallas kernels: 5.13 us -> 3.4 us  [banded_layer(): pl.pallas_call(partial(spatial_backward, patches, groups), out_shape=pack...]
  transfers between devices with their start and end apart: 25 -> 25, of which waited for: 11 -> 13; matrix products, arithmetic and copies ran while one was open for 1% -> 1% of each run, Pallas kernels for 3% -> 3%
where the time goes in v5:
time: 152 us
  waiting for transfers between devices  66.7 us (44%)
  blocking collectives  41.4 us (27%)
  starting transfers between devices  25.7 us (17%)
  Pallas kernels  16.4 us (11%)
    ppermute x24, waiting for transfers between devices, move(): return lax.ppermute(values, 'grid', table)  61.1 us
    all_to_all x3, blocking collectives, exchange(): lax.all_to_all(blocks, 'grid', split_axis=0, concat_axis=0, tiled=True)  41.4 us
    ppermute x24, starting transfers between devices, move(): return lax.ppermute(values, 'grid', table)  22.8 us
    pallas_call x1, Pallas kernels, banded_layer(): pl.pallas_call(partial(group_layer, patches, group_plan), out_shape=(shap...  7.57 us
    all_to_all x1, waiting for transfers between devices, exchange(): lax.all_to_all(blocks, 'grid', split_axis=0, concat_axis=0, tiled=True)  5.59 us
    pallas_call x1, Pallas kernels, banded_layer(): pl.pallas_call(partial(spatial_backward, patches, groups), out_shape=pack...  3.4 us
  transfers between devices with their start and end apart: 25, of which 13 were waited for; matrix products, arithmetic and copies ran while one was open for 1% of the time, Pallas kernels for 3%

profile of v5, /device:TPU:0, one launch (start us, length us, event | category | flops | bytes accessed | tf_op | source)
XLA Modules:
  0.0 152.1 jit_solution(15512162304554400310)
XLA Ops:
  0.6 3.1 %collective-permute-start = (bf16[32,3072]{1,0:T(8,128)(2,1)}, bf16[32,3072]{1,0:T(8,128)(2,1)S(1)}, u32[]{:S(2)}, u32[]{:S(2)}) collective-permute-start(bf16[32,3072]{1,0:T(8,128)(2,1)} %param.9), channel_id=1, source_target_pairs={{0,8},{1,9},{2,10},{3,11},{4,12},{5,13},{6,14},{7,15},{8,16},{9,17... | collective-permute-start | bytes 589832 | tf_op jit(solution)/shard_map/ppermute | solution.py:324
  3.7 2.6 %collective-permute-start.1 = (bf16[32,3072]{1,0:T(8,128)(2,1)}, bf16[32,3072]{1,0:T(8,128)(2,1)S(1)}, u32[]{:S(2)}, u32[]{:S(2)}) collective-permute-start(bf16[32,3072]{1,0:T(8,128)(2,1)} %param.9), channel_id=1, source_target_pairs={{0,16},{1,17},{2,18},{3,19},{4,20},{5,21},{6,22},{7,23},{8,24},{9,... | collective-permute-start | bytes 589832 | tf_op jit(solution)/shard_map/ppermute | solution.py:324
  6.3 1.3 collective-permute-start.2
  7.6 2.1 %prepare.1 = (bf16[256,512]{1,0:T(8,128)(2,1)}, bf16[32,5120]{1,0:T(8,128)(2,1)}) custom-call(bf16[128,1024]{1,0:T(8,128)(2,1)} %bitcast.12, bf16[32,1024]{1,0:T(8,128)(2,1)} %w_so.1, bf16[32,3072]{1,0:T(8,128)(2,1)} %w_gqkv.1, bf16[32,1024]{1,0:T(8,128)(2,1)} %w_go.1), custom_call_target="tpu_custom_call" | custom-call | tf_op jit(solution)/shard_map/prepare/pallas_call | solution.py:356
  9.7 2.9 %all-to-all-start = ((bf16[32,8,512]{2,1,0:T(8,128)(2,1)}), bf16[32,8,512]{2,1,0:T(8,128)(2,1)S(1)}, u32[]{:S(2)}, u32[]{:S(2)}) async-start(bf16[32,8,512]{2,1,0:T(8,128)(2,1)} %bitcast.23), calls=%async_computation | async-start | bytes 524288 | tf_op jit(solution)/shard_map/all_to_all | solution.py:311
  12.7 1.8 %collective-permute-start.3 = (bf16[32,5120]{1,0:T(8,128)(2,1)}, bf16[32,5120]{1,0:T(8,128)(2,1)S(1)}, u32[]{:S(2)}, u32[]{:S(2)}) collective-permute-start(bf16[32,5120]{1,0:T(8,128)(2,1)} %get-tuple-element.50), channel_id=1, source_target_pairs={{0,2},{1,5},{2,0},{3,7},{4,6},{5,1},{6,4},{7,3},{8,10},{9,13},{10,... | collective-permute-start | bytes 983048 | tf_op jit(solution)/shard_map/ppermute | solution.py:324
  14.5 1.5 collective-permute-start.4
  16.0 0.0 collective-permute-done
  16.0 3.9 %collective-permute-done.1 = bf16[32,3072]{1,0:T(8,128)(2,1)S(1)} collective-permute-done((bf16[32,3072]{1,0:T(8,128)(2,1)}, bf16[32,3072]{1,0:T(8,128)(2,1)S(1)}, u32[]{:S(2)}, u32[]{:S(2)}) %collective-permute-start.1) | collective-permute-done | bytes 196640 | tf_op jit(solution)/shard_map/ppermute | solution.py:324
  19.8 0.0 collective-permute-done.2
  19.8 1.0 pad_maximum_fusion.2.refs_0_
  20.8 3.5 %collective-permute-done.3 = bf16[32,5120]{1,0:T(8,128)(2,1)S(1)} collective-permute-done((bf16[32,5120]{1,0:T(8,128)(2,1)}, bf16[32,5120]{1,0:T(8,128)(2,1)S(1)}, u32[]{:S(2)}, u32[]{:S(2)}) %collective-permute-start.3) | collective-permute-done | bytes 327712 | tf_op jit(solution)/shard_map/ppermute | solution.py:324
  24.3 0.3 collective-permute-done.4
  24.7 5.6 %all-to-all-done = bf16[32,8,512]{2,1,0:T(8,128)(2,1)S(1)} async-done(((bf16[32,8,512]{2,1,0:T(8,128)(2,1)}), bf16[32,8,512]{2,1,0:T(8,128)(2,1)S(1)}, u32[]{:S(2)}, u32[]{:S(2)}) %all-to-all-start) | async-done | bytes 262176 | tf_op jit(solution)/shard_map/all_to_all | solution.py:311
  30.2 0.9 collective-permute-start.7
  31.1 1.0 collective-permute-start.5
  32.2 0.8 collective-permute-start.6
  33.0 0.9 collective-permute-start.8
  33.9 1.1 collective-permute-start.9
  35.0 5.8 %collective-permute-done.7 = bf16[32,5120]{1,0:T(8,128)(2,1)S(1)} collective-permute-done((bf16[32,5120]{1,0:T(8,128)(2,1)S(1)}, bf16[32,5120]{1,0:T(8,128)(2,1)S(1)}, u32[]{:S(2)}, u32[]{:S(2)}) %collective-permute-start.7) | collective-permute-done | bytes 327712 | tf_op jit(solution)/shard_map/ppermute | solution.py:324
  40.8 0.1 pad_maximum_fusion.refs_0_
  40.9 0.0 copy-start.2
  40.9 4.5 %collective-permute-done.8 = bf16[32,5120]{1,0:T(8,128)(2,1)S(1)} collective-permute-done((bf16[32,5120]{1,0:T(8,128)(2,1)S(1)}, bf16[32,5120]{1,0:T(8,128)(2,1)S(1)}, u32[]{:S(2)}, u32[]{:S(2)}) %collective-permute-start.8) | collective-permute-done | bytes 327712 | tf_op jit(solution)/shard_map/ppermute | solution.py:324
  45.5 11.7 %collective-permute-done.9 = bf16[32,5120]{1,0:T(8,128)(2,1)S(1)} collective-permute-done((bf16[32,5120]{1,0:T(8,128)(2,1)S(1)}, bf16[32,5120]{1,0:T(8,128)(2,1)S(1)}, u32[]{:S(2)}, u32[]{:S(2)}) %collective-permute-start.9) | collective-permute-done | bytes 327712 | tf_op jit(solution)/shard_map/ppermute | solution.py:324
  57.1 0.0 collective-permute-done.5.refs_1_
  57.1 0.0 collective-permute-done.6.refs_2_
  57.1 0.4 collective-permute-start.11
  57.5 1.7 %collective-permute-start.10 = (bf16[128,3072]{1,0:T(8,128)(2,1)S(1)}, bf16[128,3072]{1,0:T(8,128)(2,1)S(1)}, u32[]{:S(2)}, u32[]{:S(2)}) collective-permute-start(bf16[128,3072]{1,0:T(8,128)(2,1)S(1)} %collective-permute-done.5.refs_1_), channel_id=1, source_target_pairs={{0,4},{1,3},{2,6},{3,1},{4,0},{5,7},{6,2},{7,5},{8,12},{9,11},{10,... | collective-permute-start | bytes 2359304 | tf_op jit(solution)/shard_map/ppermute | solution.py:324
  59.3 0.0 collective-permute-start.13
  59.3 0.5 collective-permute-start.12
  59.8 0.0 collective-permute-start.14
  59.8 6.8 %collective-permute-done.11 = bf16[32,5120]{1,0:T(8,128)(2,1)S(1)} collective-permute-done((bf16[32,5120]{1,0:T(8,128)(2,1)S(1)}, bf16[32,5120]{1,0:T(8,128)(2,1)S(1)}, u32[]{:S(2)}, u32[]{:S(2)}) %collective-permute-start.11) | collective-permute-done | bytes 327712 | tf_op jit(solution)/shard_map/ppermute | solution.py:324
  66.6 0.1 pad_maximum_fusion.1.refs_1_
  66.7 0.0 copy-start
  66.7 0.0 copy-start.1
  66.7 2.8 %collective-permute-done.10.refs_3_ = bf16[128,3072]{1,0:T(8,128)(2,1)S(1)} collective-permute-done((bf16[128,3072]{1,0:T(8,128)(2,1)S(1)}, bf16[128,3072]{1,0:T(8,128)(2,1)S(1)}, u32[]{:S(2)}, u32[]{:S(2)}) %collective-permute-start.10) | collective-permute-done | bytes 786464 | tf_op jit(solution)/shard_map/ppermute | solution.py:324
  69.5 0.0 collective-permute-done.12.refs_4_
  69.5 0.0 collective-permute-done.13.refs_5_
  69.5 0.0 collective-permute-done.14.refs_6_
  69.5 0.1 collective-permute-start.18
  69.6 0.8 collective-permute-start.15
  70.4 1.3 collective-permute-start.16
  71.7 0.0 collective-permute-start.19
  71.7 0.5 collective-permute-start.17
  72.2 3.2 %collective-permute-done.17.refs_7_ = bf16[128,3072]{1,0:T(8,128)(2,1)S(1)} collective-permute-done((bf16[128,3072]{1,0:T(8,128)(2,1)S(1)}, bf16[128,3072]{1,0:T(8,128)(2,1)S(1)}, u32[]{:S(2)}, u32[]{:S(2)}) %collective-permute-start.17) | collective-permute-done | bytes 786464 | tf_op jit(solution)/shard_map/ppermute | solution.py:324
  75.4 2.4 %spatial_forward.1 = (bf16[256,512]{1,0:T(8,128)(2,1)S(1)}, bf16[128,3072]{1,0:T(8,128)(2,1)S(1)}, f32[128,2048]{1,0:T(8,128)S(1)}, bf16[128,1024]{1,0:T(8,128)(2,1)S(1)}, bf16[1024,3072]{1,0:T(8,128)(2,1)S(1)}) custom-call(bf16[256,512]{1,0:T(8,128)(2,1)S(1)} %bitcast.14, s32[32,128]{1,0:T(8,128)S(1)} %copy-done.2, ...), custom_call_target="tpu_custom_call" | custom-call | flops 805306368 | bytes 8388608 | tf_op jit(solution)/shard_map/spatial_forward/pallas_call | solution.py:385
  77.8 15.6 %collective-permute-done.15.refs_2_ = bf16[96,5120]{1,0:T(8,128)(2,1)S(1)} collective-permute-done((bf16[96,5120]{1,0:T(8,128)(2,1)S(1)}, bf16[96,5120]{1,0:T(8,128)(2,1)S(1)}, u32[]{:S(2)}, u32[]{:S(2)}) %collective-permute-start.15) | collective-permute-done | bytes 983072 | tf_op jit(solution)/shard_map/ppermute | solution.py:324
  93.4 0.4 collective-permute-done.16.refs_3_
  93.8 0.0 collective-permute-done.19.refs_6_
  93.8 0.0 collective-permute-done.18.refs_5_
  93.8 1.8 %collective-permute-start.20 = (bf16[96,5120]{1,0:T(8,128)(2,1)S(1)}, bf16[96,5120]{1,0:T(8,128)(2,1)S(1)}, u32[]{:S(2)}, u32[]{:S(2)}) collective-permute-start(bf16[96,5120]{1,0:T(8,128)(2,1)S(1)} %collective-permute-done.15.refs_2_), channel_id=1, source_target_pairs={{0,4},{1,3},{2,6},{3,1},{4,0},{5,7},{6,2},{7,5},{8,12},{9,11},{10,... | collective-permute-start | bytes 2949128 | tf_op jit(solution)/shard_map/ppermute | solution.py:324
  95.6 0.0 collective-permute-start.21
  95.6 0.5 collective-permute-start.22
  96.1 14.6 %all_to_all.20 = bf16[32,8,512]{2,1,0:T(8,128)(2,1)S(1)} all-to-all(bf16[32,8,512]{2,1,0:T(8,128)(2,1)S(1)} %bitcast.20), channel_id=1, replica_groups=mesh['parts'=1,'grid'=32] {'grid'}, dimensions={0} | all-to-all | bytes 524288 | tf_op jit(solution)/shard_map/all_to_all | solution.py:311
  110.7 0.0 collective-permute-done.20.refs_4_
  110.7 0.0 collective-permute-done.21.refs_7_
  110.7 0.0 collective-permute-done.22.refs_8_
  110.7 0.1 collective-permute-start.23
  110.8 2.6 %collective-permute-done.23.refs_9_ = bf16[96,5120]{1,0:T(8,128)(2,1)S(1)} collective-permute-done((bf16[96,5120]{1,0:T(8,128)(2,1)S(1)}, bf16[96,5120]{1,0:T(8,128)(2,1)S(1)}, u32[]{:S(2)}, u32[]{:S(2)}) %collective-permute-start.23) | collective-permute-done | bytes 983072 | tf_op jit(solution)/shard_map/ppermute | solution.py:324
  113.3 7.6 %group_layer.1 = (bf16[128,1024]{1,0:T(8,128)(2,1)}, bf16[128,1024]{1,0:T(8,128)(2,1)S(1)}, bf16[256,512]{1,0:T(8,128)(2,1)S(1)}) custom-call(bf16[128,1024]{1,0:T(8,128)(2,1)S(1)} %bitcast.13, bf16[256,512]{1,0:T(8,128)(2,1)S(1)} %bitcast.15, bf16[128,1024]{1,0:T(8,128)(2,1)S(1)} %bitcast.19, bf16[128,5120]{1,0:T(8,128)(2,1)S(1)} %pad_maximum_fusion.refs_0_, ...), custom_call_target="tpu_custom_call" | custom-call | flops 2684354560 | bytes 23068672 | tf_op jit(solution)/shard_map/group_layer/pallas_call | solution.py:407
  120.9 14.0 %all_to_all.21 = bf16[32,8,512]{2,1,0:T(8,128)(2,1)S(1)} all-to-all(bf16[32,8,512]{2,1,0:T(8,128)(2,1)S(1)} %bitcast.21), channel_id=1, replica_groups=mesh['parts'=1,'grid'=32] {'grid'}, dimensions={0} | all-to-all | bytes 524288 | tf_op jit(solution)/shard_map/all_to_all | solution.py:311
  134.9 3.4 %spatial_backward.1 = bf16[256,512]{1,0:T(8,128)(2,1)S(1)} custom-call(bf16[256,512]{1,0:T(8,128)(2,1)S(1)} %bitcast.16, bf16[128,1024]{1,0:T(8,128)(2,1)S(1)} %get-tuple-element.76.banded, bf16[128,3072]{1,0:T(8,128)(2,1)S(1)} %get-tuple-element.77.qkv, f32[128,2048]{1,0:T(8,128)S(1)} %get-tuple-element.78.probs, ...), custom_call_target="tpu_custom_call" | custom-call | flops 805306368 | bytes 8388608 | tf_op jit(solution)/shard_map/spatial_backward/pallas_call | solution.py:428
  138.4 12.8 %all_to_all.22 = bf16[32,8,512]{2,1,0:T(8,128)(2,1)S(1)} all-to-all(bf16[32,8,512]{2,1,0:T(8,128)(2,1)S(1)} %bitcast.17), channel_id=1, replica_groups=mesh['parts'=1,'grid'=32] {'grid'}, dimensions={0} | all-to-all | bytes 524288 | tf_op jit(solution)/shard_map/all_to_all | solution.py:311
  151.2 0.9 add_packed.1
  (5 shorter events, 0.0 us)
Async XLA Ops:
  0.6 15.3 %collective-permute-start = (bf16[32,3072]{1,0:T(8,128)(2,1)}, bf16[32,3072]{1,0:T(8,128)(2,1)S(1)}, u32[]{:S(2)}, u32[]{:S(2)}) collective-permute-start(bf16[32,3072]{1,0:T(8,128)(2,1)} %param.9), channel_id=1, source_target_pairs={{0,8},{1,9},{2,10},{3,11},{4,12},{5,13},{6,14},{7,15},{8,16},{9,17... | collective-permute-start | bytes 589832 | tf_op jit(solution)/shard_map/ppermute | solution.py:324
  3.7 16.1 %collective-permute-start.1 = (bf16[32,3072]{1,0:T(8,128)(2,1)}, bf16[32,3072]{1,0:T(8,128)(2,1)S(1)}, u32[]{:S(2)}, u32[]{:S(2)}) collective-permute-start(bf16[32,3072]{1,0:T(8,128)(2,1)} %param.9), channel_id=1, source_target_pairs={{0,16},{1,17},{2,18},{3,19},{4,20},{5,21},{6,22},{7,23},{8,24},{9,... | collective-permute-start | bytes 589832 | tf_op jit(solution)/shard_map/ppermute | solution.py:324
  6.3 13.5 %collective-permute-start.2 = (bf16[32,3072]{1,0:T(8,128)(2,1)}, bf16[32,3072]{1,0:T(8,128)(2,1)S(1)}, u32[]{:S(2)}, u32[]{:S(2)}) collective-permute-start(bf16[32,3072]{1,0:T(8,128)(2,1)} %param.9), channel_id=1, source_target_pairs={{0,24},{1,25},{2,26},{3,27},{4,28},{5,29},{6,30},{7,31},{8,0},{9,1... | collective-permute-start | bytes 589832 | tf_op jit(solution)/shard_map/ppermute | solution.py:324
  9.7 23.2 %copy-start.3 = (bf16[32,5120]{1,0:T(8,128)(2,1)S(1)}, bf16[32,5120]{1,0:T(8,128)(2,1)}, u32[]{:S(2)}) copy-start(bf16[32,5120]{1,0:T(8,128)(2,1)} %get-tuple-element.50) | copy-start | bytes 983044
  9.7 20.5 %all-to-all-start = ((bf16[32,8,512]{2,1,0:T(8,128)(2,1)}), bf16[32,8,512]{2,1,0:T(8,128)(2,1)S(1)}, u32[]{:S(2)}, u32[]{:S(2)}) async-start(bf16[32,8,512]{2,1,0:T(8,128)(2,1)} %bitcast.23), calls=%async_computation | async-start | bytes 524288 | tf_op jit(solution)/shard_map/all_to_all | solution.py:311
  12.7 11.6 %collective-permute-start.3 = (bf16[32,5120]{1,0:T(8,128)(2,1)}, bf16[32,5120]{1,0:T(8,128)(2,1)S(1)}, u32[]{:S(2)}, u32[]{:S(2)}) collective-permute-start(bf16[32,5120]{1,0:T(8,128)(2,1)} %get-tuple-element.50), channel_id=1, source_target_pairs={{0,2},{1,5},{2,0},{3,7},{4,6},{5,1},{6,4},{7,3},{8,10},{9,13},{10,... | collective-permute-start | bytes 983048 | tf_op jit(solution)/shard_map/ppermute | solution.py:324
  14.5 10.2 %collective-permute-start.4 = (bf16[32,5120]{1,0:T(8,128)(2,1)}, bf16[32,5120]{1,0:T(8,128)(2,1)S(1)}, u32[]{:S(2)}, u32[]{:S(2)}) collective-permute-start(bf16[32,5120]{1,0:T(8,128)(2,1)} %get-tuple-element.50), channel_id=1, source_target_pairs={{0,4},{1,3},{2,6},{3,1},{4,0},{5,7},{6,2},{7,5},{8,12},{9,11},{10,... | collective-permute-start | bytes 983048 | tf_op jit(solution)/shard_map/ppermute | solution.py:324
  30.2 10.6 %collective-permute-start.7 = (bf16[32,5120]{1,0:T(8,128)(2,1)S(1)}, bf16[32,5120]{1,0:T(8,128)(2,1)S(1)}, u32[]{:S(2)}, u32[]{:S(2)}) collective-permute-start(bf16[32,5120]{1,0:T(8,128)(2,1)S(1)} %collective-permute-done.3), channel_id=1, source_target_pairs={{0,4},{1,3},{2,6},{3,1},{4,0},{5,7},{6,2},{7,5},{8,12},{9,11},{10,... | collective-permute-start | bytes 983048 | tf_op jit(solution)/shard_map/ppermute | solution.py:324
  31.1 26.0 %collective-permute-start.5 = (bf16[128,3072]{1,0:T(8,128)(2,1)S(1)}, bf16[128,3072]{1,0:T(8,128)(2,1)S(1)}, u32[]{:S(2)}, u32[]{:S(2)}) collective-permute-start(bf16[128,3072]{1,0:T(8,128)(2,1)S(1)} %pad_maximum_fusion.2.refs_0_), channel_id=1, source_target_pairs={{0,2},{1,5},{2,0},{3,7},{4,6},{5,1},{6,4},{7,3},{8,10},{9,13},{10,... | collective-permute-start | bytes 2359304 | tf_op jit(solution)/shard_map/ppermute | solution.py:324
  32.2 25.0 %collective-permute-start.6 = (bf16[128,3072]{1,0:T(8,128)(2,1)S(1)}, bf16[128,3072]{1,0:T(8,128)(2,1)S(1)}, u32[]{:S(2)}, u32[]{:S(2)}) collective-permute-start(bf16[128,3072]{1,0:T(8,128)(2,1)S(1)} %pad_maximum_fusion.2.refs_0_), channel_id=1, source_target_pairs={{0,4},{1,3},{2,6},{3,1},{4,0},{5,7},{6,2},{7,5},{8,12},{9,11},{10,... | collective-permute-start | bytes 2359304 | tf_op jit(solution)/shard_map/ppermute | solution.py:324
  33.0 12.5 %collective-permute-start.8 = (bf16[32,5120]{1,0:T(8,128)(2,1)S(1)}, bf16[32,5120]{1,0:T(8,128)(2,1)S(1)}, u32[]{:S(2)}, u32[]{:S(2)}) collective-permute-start(bf16[32,5120]{1,0:T(8,128)(2,1)S(1)} %copy-done.3), channel_id=1, source_target_pairs={{0,8},{1,9},{2,10},{3,11},{4,12},{5,13},{6,14},{7,15},{8,16},{9,17... | collective-permute-start | bytes 983048 | tf_op jit(solution)/shard_map/ppermute | solution.py:324
  33.9 23.2 %collective-permute-start.9 = (bf16[32,5120]{1,0:T(8,128)(2,1)S(1)}, bf16[32,5120]{1,0:T(8,128)(2,1)S(1)}, u32[]{:S(2)}, u32[]{:S(2)}) collective-permute-start(bf16[32,5120]{1,0:T(8,128)(2,1)S(1)} %copy-done.3), channel_id=1, source_target_pairs={{0,16},{1,17},{2,18},{3,19},{4,20},{5,21},{6,22},{7,23},{8,24},{9,... | collective-permute-start | bytes 983048 | tf_op jit(solution)/shard_map/ppermute | solution.py:324
  40.9 34.5 %copy-start.2 = (s32[32,128]{1,0:T(8,128)S(1)}, s32[32,128]{1,0:T(8,128)}, u32[]{:S(2)}) copy-start(s32[32,128]{1,0:T(8,128)} %keep.1) | copy-start | bytes 49156
  57.1 9.4 %collective-permute-start.11 = (bf16[32,5120]{1,0:T(8,128)(2,1)S(1)}, bf16[32,5120]{1,0:T(8,128)(2,1)S(1)}, u32[]{:S(2)}, u32[]{:S(2)}) collective-permute-start(bf16[32,5120]{1,0:T(8,128)(2,1)S(1)} %copy-done.3), channel_id=1, source_target_pairs={{0,24},{1,25},{2,26},{3,27},{4,28},{5,29},{6,30},{7,31},{8,0},{9,1... | collective-permute-start | bytes 983048 | tf_op jit(solution)/shard_map/ppermute | solution.py:324
  57.5 12.0 %collective-permute-start.10 = (bf16[128,3072]{1,0:T(8,128)(2,1)S(1)}, bf16[128,3072]{1,0:T(8,128)(2,1)S(1)}, u32[]{:S(2)}, u32[]{:S(2)}) collective-permute-start(bf16[128,3072]{1,0:T(8,128)(2,1)S(1)} %collective-permute-done.5.refs_1_), channel_id=1, source_target_pairs={{0,4},{1,3},{2,6},{3,1},{4,0},{5,7},{6,2},{7,5},{8,12},{9,11},{10,... | collective-permute-start | bytes 2359304 | tf_op jit(solution)/shard_map/ppermute | solution.py:324
  59.3 10.3 %collective-permute-start.13 = (bf16[128,3072]{1,0:T(8,128)(2,1)S(1)}, bf16[128,3072]{1,0:T(8,128)(2,1)S(1)}, u32[]{:S(2)}, u32[]{:S(2)}) collective-permute-start(bf16[128,3072]{1,0:T(8,128)(2,1)S(1)} %collective-permute-done.5.refs_1_), channel_id=1, source_target_pairs={{0,1},{1,0},{2,3},{3,2},{4,5},{5,4},{6,7},{7,6},{8,9},{9,8},{10,11... | collective-permute-start | bytes 2359304 | tf_op jit(solution)/shard_map/ppermute | solution.py:324
  59.3 10.2 %collective-permute-start.12 = (bf16[128,3072]{1,0:T(8,128)(2,1)S(1)}, bf16[128,3072]{1,0:T(8,128)(2,1)S(1)}, u32[]{:S(2)}, u32[]{:S(2)}) collective-permute-start(bf16[128,3072]{1,0:T(8,128)(2,1)S(1)} %pad_maximum_fusion.2.refs_0_), channel_id=1, source_target_pairs={{0,1},{1,0},{2,3},{3,2},{4,5},{5,4},{6,7},{7,6},{8,9},{9,8},{10,11... | collective-permute-start | bytes 2359304 | tf_op jit(solution)/shard_map/ppermute | solution.py:324
  59.8 9.7 %collective-permute-start.14 = (bf16[128,3072]{1,0:T(8,128)(2,1)S(1)}, bf16[128,3072]{1,0:T(8,128)(2,1)S(1)}, u32[]{:S(2)}, u32[]{:S(2)}) collective-permute-start(bf16[128,3072]{1,0:T(8,128)(2,1)S(1)} %collective-permute-done.6.refs_2_), channel_id=1, source_target_pairs={{0,1},{1,0},{2,3},{3,2},{4,5},{5,4},{6,7},{7,6},{8,9},{9,8},{10,11... | collective-permute-start | bytes 2359304 | tf_op jit(solution)/shard_map/ppermute | solution.py:324
  66.7 46.7 %copy-start = (bf16[4,32,1024]{2,1,0:T(8,128)(2,1)S(1)}, bf16[4,32,1024]{2,1,0:T(8,128)(2,1)}, u32[]{:S(2)}) copy-start(bf16[4,32,1024]{2,1,0:T(8,128)(2,1)} %param.7) | copy-start | bytes 786436
  66.7 46.7 %copy-start.1 = (bf16[4,32,1024]{2,1,0:T(8,128)(2,1)S(1)}, bf16[4,32,1024]{2,1,0:T(8,128)(2,1)}, u32[]{:S(2)}) copy-start(bf16[4,32,1024]{2,1,0:T(8,128)(2,1)} %param.8) | copy-start | bytes 786436
  69.5 24.2 %collective-permute-start.18 = (bf16[128,5120]{1,0:T(8,128)(2,1)S(1)}, bf16[128,5120]{1,0:T(8,128)(2,1)S(1)}, u32[]{:S(2)}, u32[]{:S(2)}) collective-permute-start(bf16[128,5120]{1,0:T(8,128)(2,1)S(1)} %pad_maximum_fusion.refs_0_), channel_id=1, source_target_pairs={{0,1},{1,0},{2,3},{3,2},{4,5},{5,4},{6,7},{7,6},{8,9},{9,8},{10,11... | collective-permute-start | bytes 3932168 | tf_op jit(solution)/shard_map/ppermute | solution.py:324
  69.6 23.8 %collective-permute-start.15 = (bf16[96,5120]{1,0:T(8,128)(2,1)S(1)}, bf16[96,5120]{1,0:T(8,128)(2,1)S(1)}, u32[]{:S(2)}, u32[]{:S(2)}) collective-permute-start(bf16[96,5120]{1,0:T(8,128)(2,1)S(1)} %pad_maximum_fusion.1.refs_1_), channel_id=1, source_target_pairs={{0,2},{1,5},{2,0},{3,7},{4,6},{5,1},{6,4},{7,3},{8,10},{9,13},{10,... | collective-permute-start | bytes 2949128 | tf_op jit(solution)/shard_map/ppermute | solution.py:324
  70.4 23.3 %collective-permute-start.16 = (bf16[96,5120]{1,0:T(8,128)(2,1)S(1)}, bf16[96,5120]{1,0:T(8,128)(2,1)S(1)}, u32[]{:S(2)}, u32[]{:S(2)}) collective-permute-start(bf16[96,5120]{1,0:T(8,128)(2,1)S(1)} %pad_maximum_fusion.1.refs_1_), channel_id=1, source_target_pairs={{0,4},{1,3},{2,6},{3,1},{4,0},{5,7},{6,2},{7,5},{8,12},{9,11},{10,... | collective-permute-start | bytes 2949128 | tf_op jit(solution)/shard_map/ppermute | solution.py:324
  71.7 22.1 %collective-permute-start.19 = (bf16[96,5120]{1,0:T(8,128)(2,1)S(1)}, bf16[96,5120]{1,0:T(8,128)(2,1)S(1)}, u32[]{:S(2)}, u32[]{:S(2)}) collective-permute-start(bf16[96,5120]{1,0:T(8,128)(2,1)S(1)} %pad_maximum_fusion.1.refs_1_), channel_id=1, source_target_pairs={{0,1},{1,0},{2,3},{3,2},{4,5},{5,4},{6,7},{7,6},{8,9},{9,8},{10,11... | collective-permute-start | bytes 2949128 | tf_op jit(solution)/shard_map/ppermute | solution.py:324
  71.7 3.7 %collective-permute-start.17 = (bf16[128,3072]{1,0:T(8,128)(2,1)S(1)}, bf16[128,3072]{1,0:T(8,128)(2,1)S(1)}, u32[]{:S(2)}, u32[]{:S(2)}) collective-permute-start(bf16[128,3072]{1,0:T(8,128)(2,1)S(1)} %collective-permute-done.10.refs_3_), channel_id=1, source_target_pairs={{0,1},{1,0},{2,3},{3,2},{4,5},{5,4},{6,7},{7,6},{8,9},{9,8},{10,11... | collective-permute-start | bytes 2359304 | tf_op jit(solution)/shard_map/ppermute | solution.py:324
  93.8 16.9 %collective-permute-start.20 = (bf16[96,5120]{1,0:T(8,128)(2,1)S(1)}, bf16[96,5120]{1,0:T(8,128)(2,1)S(1)}, u32[]{:S(2)}, u32[]{:S(2)}) collective-permute-start(bf16[96,5120]{1,0:T(8,128)(2,1)S(1)} %collective-permute-done.15.refs_2_), channel_id=1, source_target_pairs={{0,4},{1,3},{2,6},{3,1},{4,0},{5,7},{6,2},{7,5},{8,12},{9,11},{10,... | collective-permute-start | bytes 2949128 | tf_op jit(solution)/shard_map/ppermute | solution.py:324
  95.6 15.1 %collective-permute-start.21 = (bf16[96,5120]{1,0:T(8,128)(2,1)S(1)}, bf16[96,5120]{1,0:T(8,128)(2,1)S(1)}, u32[]{:S(2)}, u32[]{:S(2)}) collective-permute-start(bf16[96,5120]{1,0:T(8,128)(2,1)S(1)} %collective-permute-done.15.refs_2_), channel_id=1, source_target_pairs={{0,1},{1,0},{2,3},{3,2},{4,5},{5,4},{6,7},{7,6},{8,9},{9,8},{10,11... | collective-permute-start | bytes 2949128 | tf_op jit(solution)/shard_map/ppermute | solution.py:324
  95.6 15.1 %collective-permute-start.22 = (bf16[96,5120]{1,0:T(8,128)(2,1)S(1)}, bf16[96,5120]{1,0:T(8,128)(2,1)S(1)}, u32[]{:S(2)}, u32[]{:S(2)}) collective-permute-start(bf16[96,5120]{1,0:T(8,128)(2,1)S(1)} %collective-permute-done.16.refs_3_), channel_id=1, source_target_pairs={{0,1},{1,0},{2,3},{3,2},{4,5},{5,4},{6,7},{7,6},{8,9},{9,8},{10,11... | collective-permute-start | bytes 2949128 | tf_op jit(solution)/shard_map/ppermute | solution.py:324
  110.7 2.6 %collective-permute-start.23 = (bf16[96,5120]{1,0:T(8,128)(2,1)S(1)}, bf16[96,5120]{1,0:T(8,128)(2,1)S(1)}, u32[]{:S(2)}, u32[]{:S(2)}) collective-permute-start(bf16[96,5120]{1,0:T(8,128)(2,1)S(1)} %collective-permute-done.20.refs_4_), channel_id=1, source_target_pairs={{0,1},{1,0},{2,3},{3,2},{4,5},{5,4},{6,7},{7,6},{8,9},{9,8},{10,11... | collective-permute-start | bytes 2949128 | tf_op jit(solution)/shard_map/ppermute | solution.py:324

commit v6 on v5

--- a/solution.py
+++ b/solution.py
@@ -234,25 +234,26 @@
 
 
 def spatial_forward(plan, patches, groups, packed, keep, *refs):
-    pieces, (result_out, qkv_out, probs_out, banded_out, weight_out) = refs[:-5], refs[-5:]
-    place_rows(pieces, plan, 0, weight_out)
+    pieces, (result_out, qkv_out, probs_out, banded_out, turned_out, weight) = refs[:-6], refs[-6:]
+    place_rows(pieces, plan, 0, weight)
     banded = unpack(packed[...], patches, groups, True)
     banded_out[...] = banded
     wide = banded.astype(jnp.float32)
     normed = (wide * inverse_rms(wide)).astype(jnp.bfloat16)
     allowed = keep[pl.ds(lax.axis_index("grid"), 1), :] > 0
-    qkv_out[...] = nn(normed, weight_out[...]).astype(jnp.bfloat16)
+    qkv_out[...] = nn(normed, weight[...]).astype(jnp.bfloat16)
     result_out[...] = pack(attention_forward(qkv_out, allowed, probs_out), patches, groups, True)
+    turned_out[...] = weight[...].T
 
 
 def spatial_backward(
-    patches, groups, grad_packed, banded, qkv, probs, weight, grad_out, grads, grad_probs, grad_scores
+    patches, groups, grad_packed, banded, qkv, probs, turned, grad_out, grads, grad_probs, grad_scores
 ):
     grad = unpack(grad_packed[...], patches, groups, True)
     attention_backward(qkv, probs, grad, grad_probs, grad_scores, grads)
     wide = banded[...].astype(jnp.float32)
     inverse = inverse_rms(wide)
-    grad_normed = nt(grads[...], weight[...]).astype(jnp.bfloat16).astype(jnp.float32)
+    grad_normed = nn(grads[...], turned[...]).astype(jnp.bfloat16).astype(jnp.float32)
     grad_out[...] = pack(norm_grad(wide, inverse, grad_normed).astype(jnp.bfloat16), patches, groups, True)
 
 
@@ -362,38 +363,45 @@
     )(tokens, w_so, w_gqkv, w_go)
     spatial_line = [w_sqkv] + [move(w_sqkv, table) for table in along]
     group_one, group_other = move(group, first), move(group, second)
-    spatial_line, group_one, group_other, banded, group = together(
-        stack(*spatial_line), group_one, group_other, exchange(packed), group
+    spatial_line, group_one, group_other, packed, group = together(
+        stack(*spatial_line), group_one, group_other, packed, group
     )
     spatial_one, spatial_other = move(spatial_line, first), move(spatial_line, second)
     group_both = move(group_one, second)
     group_parts = [move(group, table) for table in along[:-1]]
-    spatial_one, spatial_other, group_plane, group, spatial_line, *group_parts = together(
-        spatial_one, spatial_other, stack(group, group_one, group_other, group_both), group, spatial_line, *group_parts
+    spatial_one, spatial_other, group_plane, group, spatial_line, packed, group_part = together(
+        spatial_one,
+        spatial_other,
+        stack(group, group_one, group_other, group_both),
+        group,
+        spatial_line,
+        packed,
+        stack(*group_parts),
     )
     spatial_both = move(spatial_one, second)
     spatial_across = [move(part, sibling) for part in (spatial_line, spatial_one, spatial_other)]
-    group_parts.append(move(group, along[-1]))
-    spatial_both, group_line, group_plane, *spatial_across = together(
-        spatial_both, stack(*group_parts), group_plane, *spatial_across
+    group_line = stack(group_part, move(group, along[-1]))
+    spatial_both, group_line, group_plane, banded, *spatial_across = together(
+        spatial_both, group_line, group_plane, exchange(packed), *spatial_across
     )
     group_one, group_other = move(group_line, first), move(group_line, second)
     group_across = [move(group_plane, sibling), move(group_line, sibling)]
     spatial_rows = [spatial_line, spatial_one, spatial_other, spatial_both]
     spatial_rows += [*spatial_across, move(spatial_both, sibling)]
     probs_shape = shape(all_patches, 2 * pairs * all_patches, jnp.float32)
-    attended, qkv, probs, banded, full_sqkv = pl.pallas_call(
+    attended, qkv, probs, banded, turned = pl.pallas_call(
         partial(spatial_forward, spatial_plan, patches, groups),
         out_shape=(
             packed_shape,
             shape(all_patches, 3 * width),
             probs_shape,
             shape(all_patches, width),
-            shape(width, 3 * width),
+            shape(3 * width, width),
         ),
         in_specs=[VMEM_SPEC] * (2 + len(spatial_rows)),
         out_specs=(VMEM_SPEC,) * 5,
-        compiler_params=room(18),
+        scratch_shapes=[pltpu.VMEM((width, 3 * width), jnp.bfloat16)],
+        compiler_params=room(28),
         cost_estimate=cost(all_patches, width, 3, 1),
         name="spatial_forward",
     )(banded, keep, *spatial_rows)
@@ -438,7 +446,7 @@
         compiler_params=room(18),
         cost_estimate=cost(all_patches, width, 3, 1),
         name="spatial_backward",
-    )(exchange(grad_bands), banded, qkv, probs, full_sqkv)
+    )(exchange(grad_bands), banded, qkv, probs, turned)
     token_grad = pl.pallas_call(
         partial(add_packed, patches, groups),
         out_shape=shape(rows, width),

time: 152 us -> 149 us (0.980)
  waiting for transfers between devices: 66.7 us -> 52.1 us
  starting transfers between devices: 25.7 us -> 31.4 us
  other arithmetic: 1.14 us -> 3.23 us
  blocking collectives: 41.4 us -> 43.2 us
  Pallas kernels: 16.4 us -> 18.2 us
    ppermute x24, waiting for transfers between devices: 61.1 us -> 46.1 us  [move(): return lax.ppermute(values, 'grid', table)]
    ppermute x24, starting transfers between devices: 22.8 us -> 28.8 us  [move(): return lax.ppermute(values, 'grid', table)]
    pallas_call x1, Pallas kernels: 2.38 us -> 5.19 us  [banded_layer(): pl.pallas_call(partial(spatial_forward, spatial_plan, patches, groups), o...]
    concatenate x3 -> x4, other arithmetic: 1.14 us -> 3.23 us  [stack(): return jnp.concatenate(values, axis=0)]
    all_to_all x3, blocking collectives: 41.4 us -> 43.2 us  [exchange(): lax.all_to_all(blocks, 'grid', split_axis=0, concat_axis=0, tiled=True)]
  transfers between devices with their start and end apart: 25 -> 25, of which waited for: 13 -> 9; matrix products, arithmetic and copies ran while one was open for 1% -> 2% of each run, Pallas kernels for 3% -> 5%
where the time goes in v6:
time: 149 us
  waiting for transfers between devices  52.1 us (35%)
  blocking collectives  43.2 us (29%)
  starting transfers between devices  31.4 us (21%)
  Pallas kernels  18.2 us (12%)
  other arithmetic  3.23 us (2%)
    ppermute x24, waiting for transfers between devices, move(): return lax.ppermute(values, 'grid', table)  46.1 us
    all_to_all x3, blocking collectives, exchange(): lax.all_to_all(blocks, 'grid', split_axis=0, concat_axis=0, tiled=True)  43.2 us
    ppermute x24, starting transfers between devices, move(): return lax.ppermute(values, 'grid', table)  28.8 us
    pallas_call x1, Pallas kernels, banded_layer(): pl.pallas_call(partial(group_layer, patches, group_plan), out_shape=(shap...  7.56 us
    all_to_all x1, waiting for transfers between devices, exchange(): lax.all_to_all(blocks, 'grid', split_axis=0, concat_axis=0, tiled=True)  6 us
    pallas_call x1, Pallas kernels, banded_layer(): pl.pallas_call(partial(spatial_forward, spatial_plan, patches, groups), o...  5.19 us
    concatenate x4, other arithmetic, stack(): return jnp.concatenate(values, axis=0)  3.23 us
  transfers between devices with their start and end apart: 25, of which 9 were waited for; matrix products, arithmetic and copies ran while one was open for 2% of the time, Pallas kernels for 5%

profile of v6, /device:TPU:0, one launch (start us, length us, event | category | flops | bytes accessed | tf_op | source)
XLA Modules:
  0.0 148.9 jit_solution(16129507799869993594)
XLA Ops:
  0.6 3.1 %collective-permute-start = (bf16[32,3072]{1,0:T(8,128)(2,1)}, bf16[32,3072]{1,0:T(8,128)(2,1)S(1)}, u32[]{:S(2)}, u32[]{:S(2)}) collective-permute-start(bf16[32,3072]{1,0:T(8,128)(2,1)} %param.9), channel_id=1, source_target_pairs={{0,8},{1,9},{2,10},{3,11},{4,12},{5,13},{6,14},{7,15},{8,16},{9,17... | collective-permute-start | bytes 589832 | tf_op jit(solution)/shard_map/ppermute | solution.py:325
  3.7 2.6 %collective-permute-start.1 = (bf16[32,3072]{1,0:T(8,128)(2,1)}, bf16[32,3072]{1,0:T(8,128)(2,1)S(1)}, u32[]{:S(2)}, u32[]{:S(2)}) collective-permute-start(bf16[32,3072]{1,0:T(8,128)(2,1)} %param.9), channel_id=1, source_target_pairs={{0,16},{1,17},{2,18},{3,19},{4,20},{5,21},{6,22},{7,23},{8,24},{9,... | collective-permute-start | bytes 589832 | tf_op jit(solution)/shard_map/ppermute | solution.py:325
  6.3 1.3 collective-permute-start.2
  7.6 2.1 %prepare.1 = (bf16[256,512]{1,0:T(8,128)(2,1)}, bf16[32,5120]{1,0:T(8,128)(2,1)}) custom-call(bf16[128,1024]{1,0:T(8,128)(2,1)} %bitcast.12, bf16[32,1024]{1,0:T(8,128)(2,1)} %w_so.1, bf16[32,3072]{1,0:T(8,128)(2,1)} %w_gqkv.1, bf16[32,1024]{1,0:T(8,128)(2,1)} %w_go.1), custom_call_target="tpu_custom_call" | custom-call | tf_op jit(solution)/shard_map/prepare/pallas_call | solution.py:357
  9.7 1.5 %collective-permute-start.3 = (bf16[32,5120]{1,0:T(8,128)(2,1)}, bf16[32,5120]{1,0:T(8,128)(2,1)S(1)}, u32[]{:S(2)}, u32[]{:S(2)}) collective-permute-start(bf16[32,5120]{1,0:T(8,128)(2,1)} %get-tuple-element.51), channel_id=1, source_target_pairs={{0,2},{1,5},{2,0},{3,7},{4,6},{5,1},{6,4},{7,3},{8,10},{9,13},{10,... | collective-permute-start | bytes 983048 | tf_op jit(solution)/shard_map/ppermute | solution.py:325
  11.2 1.5 %collective-permute-start.4 = (bf16[32,5120]{1,0:T(8,128)(2,1)}, bf16[32,5120]{1,0:T(8,128)(2,1)S(1)}, u32[]{:S(2)}, u32[]{:S(2)}) collective-permute-start(bf16[32,5120]{1,0:T(8,128)(2,1)} %get-tuple-element.51), channel_id=1, source_target_pairs={{0,4},{1,3},{2,6},{3,1},{4,0},{5,7},{6,2},{7,5},{8,12},{9,11},{10,... | collective-permute-start | bytes 983048 | tf_op jit(solution)/shard_map/ppermute | solution.py:325
  12.7 0.0 collective-permute-done
  12.8 6.6 %collective-permute-done.1 = bf16[32,3072]{1,0:T(8,128)(2,1)S(1)} collective-permute-done((bf16[32,3072]{1,0:T(8,128)(2,1)}, bf16[32,3072]{1,0:T(8,128)(2,1)S(1)}, u32[]{:S(2)}, u32[]{:S(2)}) %collective-permute-start.1) | collective-permute-done | bytes 196640 | tf_op jit(solution)/shard_map/ppermute | solution.py:325
  19.4 0.0 collective-permute-done.2
  19.4 1.0 pad_maximum_fusion.2.refs_0_
  20.4 0.0 collective-permute-done.3
  20.4 0.0 collective-permute-done.4
  20.4 4.7 %collective-permute-start.8 = (bf16[32,5120]{1,0:T(8,128)(2,1)S(1)}, bf16[32,5120]{1,0:T(8,128)(2,1)S(1)}, u32[]{:S(2)}, u32[]{:S(2)}) collective-permute-start(bf16[32,5120]{1,0:T(8,128)(2,1)S(1)} %copy-done.3), channel_id=1, source_target_pairs={{0,8},{1,9},{2,10},{3,11},{4,12},{5,13},{6,14},{7,15},{8,16},{9,17... | collective-permute-start | bytes 983048 | tf_op jit(solution)/shard_map/ppermute | solution.py:325
  25.1 1.6 %collective-permute-start.9 = (bf16[32,5120]{1,0:T(8,128)(2,1)S(1)}, bf16[32,5120]{1,0:T(8,128)(2,1)S(1)}, u32[]{:S(2)}, u32[]{:S(2)}) collective-permute-start(bf16[32,5120]{1,0:T(8,128)(2,1)S(1)} %copy-done.3), channel_id=1, source_target_pairs={{0,16},{1,17},{2,18},{3,19},{4,20},{5,21},{6,22},{7,23},{8,24},{9,... | collective-permute-start | bytes 983048 | tf_op jit(solution)/shard_map/ppermute | solution.py:325
  26.7 1.5 %collective-permute-start.5 = (bf16[128,3072]{1,0:T(8,128)(2,1)S(1)}, bf16[128,3072]{1,0:T(8,128)(2,1)}, u32[]{:S(2)}, u32[]{:S(2)}) collective-permute-start(bf16[128,3072]{1,0:T(8,128)(2,1)S(1)} %pad_maximum_fusion.2.refs_0_), channel_id=1, source_target_pairs={{0,2},{1,5},{2,0},{3,7},{4,6},{5,1},{6,4},{7,3},{8,10},{9,13},{10,... | collective-permute-start | bytes 2359304 | tf_op jit(solution)/shard_map/ppermute | solution.py:325
  28.2 1.5 %collective-permute-start.6 = (bf16[128,3072]{1,0:T(8,128)(2,1)S(1)}, bf16[128,3072]{1,0:T(8,128)(2,1)}, u32[]{:S(2)}, u32[]{:S(2)}) collective-permute-start(bf16[128,3072]{1,0:T(8,128)(2,1)S(1)} %pad_maximum_fusion.2.refs_0_), channel_id=1, source_target_pairs={{0,4},{1,3},{2,6},{3,1},{4,0},{5,7},{6,2},{7,5},{8,12},{9,11},{10,... | collective-permute-start | bytes 2359304 | tf_op jit(solution)/shard_map/ppermute | solution.py:325
  29.8 0.5 collective-permute-start.7
  30.3 4.6 %collective-permute-done.8 = bf16[32,5120]{1,0:T(8,128)(2,1)S(1)} collective-permute-done((bf16[32,5120]{1,0:T(8,128)(2,1)S(1)}, bf16[32,5120]{1,0:T(8,128)(2,1)S(1)}, u32[]{:S(2)}, u32[]{:S(2)}) %collective-permute-start.8) | collective-permute-done | bytes 327712 | tf_op jit(solution)/shard_map/ppermute | solution.py:325
  34.9 12.2 %collective-permute-done.9 = bf16[32,5120]{1,0:T(8,128)(2,1)S(1)} collective-permute-done((bf16[32,5120]{1,0:T(8,128)(2,1)S(1)}, bf16[32,5120]{1,0:T(8,128)(2,1)S(1)}, u32[]{:S(2)}, u32[]{:S(2)}) %collective-permute-start.9) | collective-permute-done | bytes 327712 | tf_op jit(solution)/shard_map/ppermute | solution.py:325
  47.1 0.9 pad_maximum_fusion.3
  48.0 0.1 collective-permute-done.7
  48.1 0.1 pad_maximum_fusion.refs_0_
  48.2 0.0 copy-start.2
  48.2 0.0 collective-permute-done.5.refs_1_
  48.2 0.0 collective-permute-done.6.refs_2_
  48.2 2.3 %collective-permute-start.11 = (bf16[32,5120]{1,0:T(8,128)(2,1)S(1)}, bf16[32,5120]{1,0:T(8,128)(2,1)}, u32[]{:S(2)}, u32[]{:S(2)}) collective-permute-start(bf16[32,5120]{1,0:T(8,128)(2,1)S(1)} %copy-done.3), channel_id=1, source_target_pairs={{0,24},{1,25},{2,26},{3,27},{4,28},{5,29},{6,30},{7,31},{8,0},{9,1... | collective-permute-start | bytes 983048 | tf_op jit(solution)/shard_map/ppermute | solution.py:325
  50.5 1.5 %collective-permute-start.10 = (bf16[128,3072]{1,0:T(8,128)(2,1)}, bf16[128,3072]{1,0:T(8,128)(2,1)}, u32[]{:S(2)}, u32[]{:S(2)}) collective-permute-start(bf16[128,3072]{1,0:T(8,128)(2,1)} %collective-permute-done.5.refs_1_), channel_id=1, source_target_pairs={{0,4},{1,3},{2,6},{3,1},{4,0},{5,7},{6,2},{7,5},{8,12},{9,11},{10,... | collective-permute-start | bytes 2359304 | tf_op jit(solution)/shard_map/ppermute | solution.py:325
  52.0 0.4 collective-permute-start.13
  52.4 0.1 collective-permute-start.12
  52.5 0.4 collective-permute-start.14
  52.9 2.6 %all-to-all-start = ((bf16[32,8,512]{2,1,0:T(8,128)(2,1)}), bf16[32,8,512]{2,1,0:T(8,128)(2,1)S(1)}, u32[]{:S(2)}, u32[]{:S(2)}) async-start(bf16[32,8,512]{2,1,0:T(8,128)(2,1)} %bitcast.1), calls=%async_computation | async-start | bytes 524288 | tf_op jit(solution)/shard_map/all_to_all | solution.py:312
  55.5 3.3 %collective-permute-done.11 = bf16[32,5120]{1,0:T(8,128)(2,1)} collective-permute-done((bf16[32,5120]{1,0:T(8,128)(2,1)S(1)}, bf16[32,5120]{1,0:T(8,128)(2,1)}, u32[]{:S(2)}, u32[]{:S(2)}) %collective-permute-start.11) | collective-permute-done | bytes 327712 | tf_op jit(solution)/shard_map/ppermute | solution.py:325
  58.9 1.3 pad_maximum_fusion.1.refs_1_
  60.1 6.0 %all-to-all-done = bf16[32,8,512]{2,1,0:T(8,128)(2,1)S(1)} async-done(((bf16[32,8,512]{2,1,0:T(8,128)(2,1)}), bf16[32,8,512]{2,1,0:T(8,128)(2,1)S(1)}, u32[]{:S(2)}, u32[]{:S(2)}) %all-to-all-start) | async-done | bytes 262176 | tf_op jit(solution)/shard_map/all_to_all | solution.py:312
  66.1 0.0 collective-permute-done.10.refs_3_
  66.1 0.0 collective-permute-done.12.refs_4_
  66.1 0.0 collective-permute-done.13.refs_5_
  66.2 0.0 collective-permute-done.14.refs_6_
  66.2 0.0 copy-start
  66.2 0.0 copy-start.1
  66.2 0.1 collective-permute-start.18
  66.3 0.8 collective-permute-start.15
  67.1 1.6 %collective-permute-start.16 = (bf16[96,5120]{1,0:T(8,128)(2,1)S(1)}, bf16[96,5120]{1,0:T(8,128)(2,1)S(1)}, u32[]{:S(2)}, u32[]{:S(2)}) collective-permute-start(bf16[96,5120]{1,0:T(8,128)(2,1)S(1)} %pad_maximum_fusion.1.refs_1_), channel_id=1, source_target_pairs={{0,4},{1,3},{2,6},{3,1},{4,0},{5,7},{6,2},{7,5},{8,12},{9,11},{10,... | collective-permute-start | bytes 2949128 | tf_op jit(solution)/shard_map/ppermute | solution.py:325
  68.7 0.0 collective-permute-start.19
  68.7 0.5 collective-permute-start.17
  69.2 3.1 %collective-permute-done.17.refs_7_ = bf16[128,3072]{1,0:T(8,128)(2,1)S(1)} collective-permute-done((bf16[128,3072]{1,0:T(8,128)(2,1)}, bf16[128,3072]{1,0:T(8,128)(2,1)S(1)}, u32[]{:S(2)}, u32[]{:S(2)}) %collective-permute-start.17) | collective-permute-done | bytes 786464 | tf_op jit(solution)/shard_map/ppermute | solution.py:325
  72.3 5.2 %spatial_forward.1 = (bf16[256,512]{1,0:T(8,128)(2,1)S(1)}, bf16[128,3072]{1,0:T(8,128)(2,1)S(1)}, f32[128,2048]{1,0:T(8,128)S(1)}, bf16[128,1024]{1,0:T(8,128)(2,1)S(1)}, bf16[3072,1024]{1,0:T(8,128)(2,1)S(1)}) custom-call(bf16[256,512]{1,0:T(8,128)(2,1)S(1)} %bitcast.14, s32[32,128]{1,0:T(8,128)S(1)} %copy-done.2, ...), custom_call_target="tpu_custom_call" | custom-call | flops 805306368 | bytes 8388608 | tf_op jit(solution)/shard_map/spatial_forward/pallas_call | solution.py:392
  77.5 13.4 %collective-permute-done.15.refs_2_ = bf16[96,5120]{1,0:T(8,128)(2,1)S(1)} collective-permute-done((bf16[96,5120]{1,0:T(8,128)(2,1)S(1)}, bf16[96,5120]{1,0:T(8,128)(2,1)S(1)}, u32[]{:S(2)}, u32[]{:S(2)}) %collective-permute-start.15) | collective-permute-done | bytes 983072 | tf_op jit(solution)/shard_map/ppermute | solution.py:325
  91.0 0.0 collective-permute-done.16.refs_3_
  91.0 0.0 collective-permute-done.19.refs_6_
  91.0 0.0 collective-permute-done.18.refs_5_
  91.0 0.7 collective-permute-start.20
  91.6 0.0 collective-permute-start.21
  91.6 0.5 collective-permute-start.22
  92.2 15.8 %all_to_all.20 = bf16[32,8,512]{2,1,0:T(8,128)(2,1)S(1)} all-to-all(bf16[32,8,512]{2,1,0:T(8,128)(2,1)S(1)} %bitcast.20), channel_id=1, replica_groups=mesh['parts'=1,'grid'=32] {'grid'}, dimensions={0} | all-to-all | bytes 524288 | tf_op jit(solution)/shard_map/all_to_all | solution.py:312
  107.9 0.0 collective-permute-done.20.refs_4_
  107.9 0.0 collective-permute-done.22.refs_8_
  108.0 0.1 collective-permute-start.23
  108.0 2.6 %collective-permute-done.23.refs_9_ = bf16[96,5120]{1,0:T(8,128)(2,1)S(1)} collective-permute-done((bf16[96,5120]{1,0:T(8,128)(2,1)S(1)}, bf16[96,5120]{1,0:T(8,128)(2,1)S(1)}, u32[]{:S(2)}, u32[]{:S(2)}) %collective-permute-start.23) | collective-permute-done | bytes 983072 | tf_op jit(solution)/shard_map/ppermute | solution.py:325
  110.6 7.6 %group_layer.1 = (bf16[128,1024]{1,0:T(8,128)(2,1)}, bf16[128,1024]{1,0:T(8,128)(2,1)S(1)}, bf16[256,512]{1,0:T(8,128)(2,1)S(1)}) custom-call(bf16[128,1024]{1,0:T(8,128)(2,1)S(1)} %bitcast.13, bf16[256,512]{1,0:T(8,128)(2,1)S(1)} %bitcast.15, bf16[128,1024]{1,0:T(8,128)(2,1)S(1)} %bitcast.19, bf16[128,5120]{1,0:T(8,128)(2,1)S(1)} %pad_maximum_fusion.refs_0_, ...), custom_call_target="tpu_custom_call" | custom-call | flops 2684354560 | bytes 23068672 | tf_op jit(solution)/shard_map/group_layer/pallas_call | solution.py:415
  118.2 14.6 %all_to_all.21 = bf16[32,8,512]{2,1,0:T(8,128)(2,1)S(1)} all-to-all(bf16[32,8,512]{2,1,0:T(8,128)(2,1)S(1)} %bitcast.21), channel_id=1, replica_groups=mesh['parts'=1,'grid'=32] {'grid'}, dimensions={0} | all-to-all | bytes 524288 | tf_op jit(solution)/shard_map/all_to_all | solution.py:312
  132.8 2.4 %spatial_backward.1 = bf16[256,512]{1,0:T(8,128)(2,1)S(1)} custom-call(bf16[256,512]{1,0:T(8,128)(2,1)S(1)} %bitcast.16, bf16[128,1024]{1,0:T(8,128)(2,1)S(1)} %get-tuple-element.78.banded, bf16[128,3072]{1,0:T(8,128)(2,1)S(1)} %get-tuple-element.79.qkv, f32[128,2048]{1,0:T(8,128)S(1)} %get-tuple-element.80.probs, ...), custom_call_target="tpu_custom_call" | custom-call | flops 805306368 | bytes 8388608 | tf_op jit(solution)/shard_map/spatial_backward/pallas_call | solution.py:436
  135.2 12.8 %all_to_all.22 = bf16[32,8,512]{2,1,0:T(8,128)(2,1)S(1)} all-to-all(bf16[32,8,512]{2,1,0:T(8,128)(2,1)S(1)} %bitcast.17), channel_id=1, replica_groups=mesh['parts'=1,'grid'=32] {'grid'}, dimensions={0} | all-to-all | bytes 524288 | tf_op jit(solution)/shard_map/all_to_all | solution.py:312
  148.0 0.9 add_packed.1
  (6 shorter events, 0.0 us)
Async XLA Ops:
  0.6 12.1 %collective-permute-start = (bf16[32,3072]{1,0:T(8,128)(2,1)}, bf16[32,3072]{1,0:T(8,128)(2,1)S(1)}, u32[]{:S(2)}, u32[]{:S(2)}) collective-permute-start(bf16[32,3072]{1,0:T(8,128)(2,1)} %param.9), channel_id=1, source_target_pairs={{0,8},{1,9},{2,10},{3,11},{4,12},{5,13},{6,14},{7,15},{8,16},{9,17... | collective-permute-start | bytes 589832 | tf_op jit(solution)/shard_map/ppermute | solution.py:325
  3.7 15.7 %collective-permute-start.1 = (bf16[32,3072]{1,0:T(8,128)(2,1)}, bf16[32,3072]{1,0:T(8,128)(2,1)S(1)}, u32[]{:S(2)}, u32[]{:S(2)}) collective-permute-start(bf16[32,3072]{1,0:T(8,128)(2,1)} %param.9), channel_id=1, source_target_pairs={{0,16},{1,17},{2,18},{3,19},{4,20},{5,21},{6,22},{7,23},{8,24},{9,... | collective-permute-start | bytes 589832 | tf_op jit(solution)/shard_map/ppermute | solution.py:325
  6.3 13.1 %collective-permute-start.2 = (bf16[32,3072]{1,0:T(8,128)(2,1)}, bf16[32,3072]{1,0:T(8,128)(2,1)S(1)}, u32[]{:S(2)}, u32[]{:S(2)}) collective-permute-start(bf16[32,3072]{1,0:T(8,128)(2,1)} %param.9), channel_id=1, source_target_pairs={{0,24},{1,25},{2,26},{3,27},{4,28},{5,29},{6,30},{7,31},{8,0},{9,1... | collective-permute-start | bytes 589832 | tf_op jit(solution)/shard_map/ppermute | solution.py:325
  9.7 10.7 %copy-start.3 = (bf16[32,5120]{1,0:T(8,128)(2,1)S(1)}, bf16[32,5120]{1,0:T(8,128)(2,1)}, u32[]{:S(2)}) copy-start(bf16[32,5120]{1,0:T(8,128)(2,1)} %get-tuple-element.51) | copy-start | bytes 983044
  9.7 10.7 %collective-permute-start.3 = (bf16[32,5120]{1,0:T(8,128)(2,1)}, bf16[32,5120]{1,0:T(8,128)(2,1)S(1)}, u32[]{:S(2)}, u32[]{:S(2)}) collective-permute-start(bf16[32,5120]{1,0:T(8,128)(2,1)} %get-tuple-element.51), channel_id=1, source_target_pairs={{0,2},{1,5},{2,0},{3,7},{4,6},{5,1},{6,4},{7,3},{8,10},{9,13},{10,... | collective-permute-start | bytes 983048 | tf_op jit(solution)/shard_map/ppermute | solution.py:325
  11.2 9.2 %collective-permute-start.4 = (bf16[32,5120]{1,0:T(8,128)(2,1)}, bf16[32,5120]{1,0:T(8,128)(2,1)S(1)}, u32[]{:S(2)}, u32[]{:S(2)}) collective-permute-start(bf16[32,5120]{1,0:T(8,128)(2,1)} %get-tuple-element.51), channel_id=1, source_target_pairs={{0,4},{1,3},{2,6},{3,1},{4,0},{5,7},{6,2},{7,5},{8,12},{9,11},{10,... | collective-permute-start | bytes 983048 | tf_op jit(solution)/shard_map/ppermute | solution.py:325
  20.4 14.5 %collective-permute-start.8 = (bf16[32,5120]{1,0:T(8,128)(2,1)S(1)}, bf16[32,5120]{1,0:T(8,128)(2,1)S(1)}, u32[]{:S(2)}, u32[]{:S(2)}) collective-permute-start(bf16[32,5120]{1,0:T(8,128)(2,1)S(1)} %copy-done.3), channel_id=1, source_target_pairs={{0,8},{1,9},{2,10},{3,11},{4,12},{5,13},{6,14},{7,15},{8,16},{9,17... | collective-permute-start | bytes 983048 | tf_op jit(solution)/shard_map/ppermute | solution.py:325
  25.1 21.9 %collective-permute-start.9 = (bf16[32,5120]{1,0:T(8,128)(2,1)S(1)}, bf16[32,5120]{1,0:T(8,128)(2,1)S(1)}, u32[]{:S(2)}, u32[]{:S(2)}) collective-permute-start(bf16[32,5120]{1,0:T(8,128)(2,1)S(1)} %copy-done.3), channel_id=1, source_target_pairs={{0,16},{1,17},{2,18},{3,19},{4,20},{5,21},{6,22},{7,23},{8,24},{9,... | collective-permute-start | bytes 983048 | tf_op jit(solution)/shard_map/ppermute | solution.py:325
  26.7 21.5 %collective-permute-start.5 = (bf16[128,3072]{1,0:T(8,128)(2,1)S(1)}, bf16[128,3072]{1,0:T(8,128)(2,1)}, u32[]{:S(2)}, u32[]{:S(2)}) collective-permute-start(bf16[128,3072]{1,0:T(8,128)(2,1)S(1)} %pad_maximum_fusion.2.refs_0_), channel_id=1, source_target_pairs={{0,2},{1,5},{2,0},{3,7},{4,6},{5,1},{6,4},{7,3},{8,10},{9,13},{10,... | collective-permute-start | bytes 2359304 | tf_op jit(solution)/shard_map/ppermute | solution.py:325
  28.2 20.0 %collective-permute-start.6 = (bf16[128,3072]{1,0:T(8,128)(2,1)S(1)}, bf16[128,3072]{1,0:T(8,128)(2,1)}, u32[]{:S(2)}, u32[]{:S(2)}) collective-permute-start(bf16[128,3072]{1,0:T(8,128)(2,1)S(1)} %pad_maximum_fusion.2.refs_0_), channel_id=1, source_target_pairs={{0,4},{1,3},{2,6},{3,1},{4,0},{5,7},{6,2},{7,5},{8,12},{9,11},{10,... | collective-permute-start | bytes 2359304 | tf_op jit(solution)/shard_map/ppermute | solution.py:325
  29.8 18.3 %collective-permute-start.7 = (bf16[32,5120]{1,0:T(8,128)(2,1)S(1)}, bf16[32,5120]{1,0:T(8,128)(2,1)S(1)}, u32[]{:S(2)}, u32[]{:S(2)}) collective-permute-start(bf16[32,5120]{1,0:T(8,128)(2,1)S(1)} %collective-permute-done.3), channel_id=1, source_target_pairs={{0,4},{1,3},{2,6},{3,1},{4,0},{5,7},{6,2},{7,5},{8,12},{9,11},{10,... | collective-permute-start | bytes 983048 | tf_op jit(solution)/shard_map/ppermute | solution.py:325
  48.2 24.1 %copy-start.2 = (s32[32,128]{1,0:T(8,128)S(1)}, s32[32,128]{1,0:T(8,128)}, u32[]{:S(2)}) copy-start(s32[32,128]{1,0:T(8,128)} %keep.1) | copy-start | bytes 49156
  48.2 10.7 %collective-permute-start.11 = (bf16[32,5120]{1,0:T(8,128)(2,1)S(1)}, bf16[32,5120]{1,0:T(8,128)(2,1)}, u32[]{:S(2)}, u32[]{:S(2)}) collective-permute-start(bf16[32,5120]{1,0:T(8,128)(2,1)S(1)} %copy-done.3), channel_id=1, source_target_pairs={{0,24},{1,25},{2,26},{3,27},{4,28},{5,29},{6,30},{7,31},{8,0},{9,1... | collective-permute-start | bytes 983048 | tf_op jit(solution)/shard_map/ppermute | solution.py:325
  50.5 15.6 %collective-permute-start.10 = (bf16[128,3072]{1,0:T(8,128)(2,1)}, bf16[128,3072]{1,0:T(8,128)(2,1)}, u32[]{:S(2)}, u32[]{:S(2)}) collective-permute-start(bf16[128,3072]{1,0:T(8,128)(2,1)} %collective-permute-done.5.refs_1_), channel_id=1, source_target_pairs={{0,4},{1,3},{2,6},{3,1},{4,0},{5,7},{6,2},{7,5},{8,12},{9,11},{10,... | collective-permute-start | bytes 2359304 | tf_op jit(solution)/shard_map/ppermute | solution.py:325
  52.0 14.1 %collective-permute-start.13 = (bf16[128,3072]{1,0:T(8,128)(2,1)}, bf16[128,3072]{1,0:T(8,128)(2,1)}, u32[]{:S(2)}, u32[]{:S(2)}) collective-permute-start(bf16[128,3072]{1,0:T(8,128)(2,1)} %collective-permute-done.5.refs_1_), channel_id=1, source_target_pairs={{0,1},{1,0},{2,3},{3,2},{4,5},{5,4},{6,7},{7,6},{8,9},{9,8},{10,11... | collective-permute-start | bytes 2359304 | tf_op jit(solution)/shard_map/ppermute | solution.py:325
  52.4 13.7 %collective-permute-start.12 = (bf16[128,3072]{1,0:T(8,128)(2,1)S(1)}, bf16[128,3072]{1,0:T(8,128)(2,1)}, u32[]{:S(2)}, u32[]{:S(2)}) collective-permute-start(bf16[128,3072]{1,0:T(8,128)(2,1)S(1)} %pad_maximum_fusion.2.refs_0_), channel_id=1, source_target_pairs={{0,1},{1,0},{2,3},{3,2},{4,5},{5,4},{6,7},{7,6},{8,9},{9,8},{10,11... | collective-permute-start | bytes 2359304 | tf_op jit(solution)/shard_map/ppermute | solution.py:325
  52.5 13.6 %collective-permute-start.14 = (bf16[128,3072]{1,0:T(8,128)(2,1)}, bf16[128,3072]{1,0:T(8,128)(2,1)}, u32[]{:S(2)}, u32[]{:S(2)}) collective-permute-start(bf16[128,3072]{1,0:T(8,128)(2,1)} %collective-permute-done.6.refs_2_), channel_id=1, source_target_pairs={{0,1},{1,0},{2,3},{3,2},{4,5},{5,4},{6,7},{7,6},{8,9},{9,8},{10,11... | collective-permute-start | bytes 2359304 | tf_op jit(solution)/shard_map/ppermute | solution.py:325
  52.9 13.2 %all-to-all-start = ((bf16[32,8,512]{2,1,0:T(8,128)(2,1)}), bf16[32,8,512]{2,1,0:T(8,128)(2,1)S(1)}, u32[]{:S(2)}, u32[]{:S(2)}) async-start(bf16[32,8,512]{2,1,0:T(8,128)(2,1)} %bitcast.1), calls=%async_computation | async-start | bytes 524288 | tf_op jit(solution)/shard_map/all_to_all | solution.py:312
  66.2 44.4 %copy-start = (bf16[4,32,1024]{2,1,0:T(8,128)(2,1)S(1)}, bf16[4,32,1024]{2,1,0:T(8,128)(2,1)}, u32[]{:S(2)}) copy-start(bf16[4,32,1024]{2,1,0:T(8,128)(2,1)} %param.7) | copy-start | bytes 786436
  66.2 44.4 %copy-start.1 = (bf16[4,32,1024]{2,1,0:T(8,128)(2,1)S(1)}, bf16[4,32,1024]{2,1,0:T(8,128)(2,1)}, u32[]{:S(2)}) copy-start(bf16[4,32,1024]{2,1,0:T(8,128)(2,1)} %param.8) | copy-start | bytes 786436
  66.2 24.8 %collective-permute-start.18 = (bf16[128,5120]{1,0:T(8,128)(2,1)S(1)}, bf16[128,5120]{1,0:T(8,128)(2,1)S(1)}, u32[]{:S(2)}, u32[]{:S(2)}) collective-permute-start(bf16[128,5120]{1,0:T(8,128)(2,1)S(1)} %pad_maximum_fusion.refs_0_), channel_id=1, source_target_pairs={{0,1},{1,0},{2,3},{3,2},{4,5},{5,4},{6,7},{7,6},{8,9},{9,8},{10,11... | collective-permute-start | bytes 3932168 | tf_op jit(solution)/shard_map/ppermute | solution.py:325
  66.3 24.7 %collective-permute-start.15 = (bf16[96,5120]{1,0:T(8,128)(2,1)S(1)}, bf16[96,5120]{1,0:T(8,128)(2,1)S(1)}, u32[]{:S(2)}, u32[]{:S(2)}) collective-permute-start(bf16[96,5120]{1,0:T(8,128)(2,1)S(1)} %pad_maximum_fusion.1.refs_1_), channel_id=1, source_target_pairs={{0,2},{1,5},{2,0},{3,7},{4,6},{5,1},{6,4},{7,3},{8,10},{9,13},{10,... | collective-permute-start | bytes 2949128 | tf_op jit(solution)/shard_map/ppermute | solution.py:325
  67.1 23.9 %collective-permute-start.16 = (bf16[96,5120]{1,0:T(8,128)(2,1)S(1)}, bf16[96,5120]{1,0:T(8,128)(2,1)S(1)}, u32[]{:S(2)}, u32[]{:S(2)}) collective-permute-start(bf16[96,5120]{1,0:T(8,128)(2,1)S(1)} %pad_maximum_fusion.1.refs_1_), channel_id=1, source_target_pairs={{0,4},{1,3},{2,6},{3,1},{4,0},{5,7},{6,2},{7,5},{8,12},{9,11},{10,... | collective-permute-start | bytes 2949128 | tf_op jit(solution)/shard_map/ppermute | solution.py:325
  68.7 22.3 %collective-permute-start.19 = (bf16[96,5120]{1,0:T(8,128)(2,1)S(1)}, bf16[96,5120]{1,0:T(8,128)(2,1)S(1)}, u32[]{:S(2)}, u32[]{:S(2)}) collective-permute-start(bf16[96,5120]{1,0:T(8,128)(2,1)S(1)} %pad_maximum_fusion.1.refs_1_), channel_id=1, source_target_pairs={{0,1},{1,0},{2,3},{3,2},{4,5},{5,4},{6,7},{7,6},{8,9},{9,8},{10,11... | collective-permute-start | bytes 2949128 | tf_op jit(solution)/shard_map/ppermute | solution.py:325
  68.7 3.6 %collective-permute-start.17 = (bf16[128,3072]{1,0:T(8,128)(2,1)}, bf16[128,3072]{1,0:T(8,128)(2,1)S(1)}, u32[]{:S(2)}, u32[]{:S(2)}) collective-permute-start(bf16[128,3072]{1,0:T(8,128)(2,1)} %collective-permute-done.10.refs_3_), channel_id=1, source_target_pairs={{0,1},{1,0},{2,3},{3,2},{4,5},{5,4},{6,7},{7,6},{8,9},{9,8},{10,11... | collective-permute-start | bytes 2359304 | tf_op jit(solution)/shard_map/ppermute | solution.py:325
  91.0 17.0 %collective-permute-start.20 = (bf16[96,5120]{1,0:T(8,128)(2,1)S(1)}, bf16[96,5120]{1,0:T(8,128)(2,1)S(1)}, u32[]{:S(2)}, u32[]{:S(2)}) collective-permute-start(bf16[96,5120]{1,0:T(8,128)(2,1)S(1)} %collective-permute-done.15.refs_2_), channel_id=1, source_target_pairs={{0,4},{1,3},{2,6},{3,1},{4,0},{5,7},{6,2},{7,5},{8,12},{9,11},{10,... | collective-permute-start | bytes 2949128 | tf_op jit(solution)/shard_map/ppermute | solution.py:325
  91.6 16.3 %collective-permute-start.21 = (bf16[96,5120]{1,0:T(8,128)(2,1)S(1)}, bf16[96,5120]{1,0:T(8,128)(2,1)S(1)}, u32[]{:S(2)}, u32[]{:S(2)}) collective-permute-start(bf16[96,5120]{1,0:T(8,128)(2,1)S(1)} %collective-permute-done.15.refs_2_), channel_id=1, source_target_pairs={{0,1},{1,0},{2,3},{3,2},{4,5},{5,4},{6,7},{7,6},{8,9},{9,8},{10,11... | collective-permute-start | bytes 2949128 | tf_op jit(solution)/shard_map/ppermute | solution.py:325
  91.6 16.3 %collective-permute-start.22 = (bf16[96,5120]{1,0:T(8,128)(2,1)S(1)}, bf16[96,5120]{1,0:T(8,128)(2,1)S(1)}, u32[]{:S(2)}, u32[]{:S(2)}) collective-permute-start(bf16[96,5120]{1,0:T(8,128)(2,1)S(1)} %collective-permute-done.16.refs_3_), channel_id=1, source_target_pairs={{0,1},{1,0},{2,3},{3,2},{4,5},{5,4},{6,7},{7,6},{8,9},{9,8},{10,11... | collective-permute-start | bytes 2949128 | tf_op jit(solution)/shard_map/ppermute | solution.py:325
  108.0 2.6 %collective-permute-start.23 = (bf16[96,5120]{1,0:T(8,128)(2,1)S(1)}, bf16[96,5120]{1,0:T(8,128)(2,1)S(1)}, u32[]{:S(2)}, u32[]{:S(2)}) collective-permute-start(bf16[96,5120]{1,0:T(8,128)(2,1)S(1)} %collective-permute-done.20.refs_4_), channel_id=1, source_target_pairs={{0,1},{1,0},{2,3},{3,2},{4,5},{5,4},{6,7},{7,6},{8,9},{9,8},{10,11... | collective-permute-start | bytes 2949128 | tf_op jit(solution)/shard_map/ppermute | solution.py:325

commit v7 on v6

--- a/solution.py
+++ b/solution.py
@@ -366,26 +366,27 @@
     spatial_line, group_one, group_other, packed, group = together(
         stack(*spatial_line), group_one, group_other, packed, group
     )
+    group_parts = [move(group, table) for table in along[:-1]]
     spatial_one, spatial_other = move(spatial_line, first), move(spatial_line, second)
     group_both = move(group_one, second)
-    group_parts = [move(group, table) for table in along[:-1]]
-    spatial_one, spatial_other, group_plane, group, spatial_line, packed, group_part = together(
+    spatial_one, spatial_other, group_plane, group, group_other, spatial_line, packed, *group_parts = together(
         spatial_one,
         spatial_other,
         stack(group, group_one, group_other, group_both),
         group,
+        group_other,
         spatial_line,
         packed,
-        stack(*group_parts),
+        *group_parts,
     )
     spatial_both = move(spatial_one, second)
     spatial_across = [move(part, sibling) for part in (spatial_line, spatial_one, spatial_other)]
-    group_line = stack(group_part, move(group, along[-1]))
-    spatial_both, group_line, group_plane, banded, *spatial_across = together(
-        spatial_both, group_line, group_plane, exchange(packed), *spatial_across
-    )
-    group_one, group_other = move(group_line, first), move(group_line, second)
-    group_across = [move(group_plane, sibling), move(group_line, sibling)]
+    group_line = stack(*group_parts, move(group, along[-1]))
+    spatial_both, group_line, group_plane, group_other, middle, banded, *spatial_across = together(
+        spatial_both, group_line, group_plane, group_other, group_parts[1], exchange(packed), *spatial_across
+    )
+    other_parts = [move(group_other, along[0]), move(middle, second), move(group_other, along[-1])]
+    group_one = move(group_line, first)
     spatial_rows = [spatial_line, spatial_one, spatial_other, spatial_both]
     spatial_rows += [*spatial_across, move(spatial_both, sibling)]
     probs_shape = shape(all_patches, 2 * pairs * all_patches, jnp.float32)
@@ -405,9 +406,12 @@
         cost_estimate=cost(all_patches, width, 3, 1),
         name="spatial_forward",
     )(banded, keep, *spatial_rows)
-    group_one, group_other, attended, *group_across = together(group_one, group_other, attended, *group_across)
+    group_one, attended, group_plane, group_line, *other_parts = together(
+        group_one, attended, group_plane, group_line, *other_parts
+    )
     group_both = move(group_one, second)
-    group_across += [move(group_one, sibling), move(group_other, sibling)]
+    group_other = stack(*other_parts)
+    group_across = [move(part, sibling) for part in (group_plane, group_line, group_one, group_other)]
     group_both, attended, *group_across = together(group_both, exchange(attended), *group_across)
     group_rows = [group_plane, group_line, group_one, group_other, group_both]
     group_rows += [*group_across, move(group_both, sibling)]

time: 149 us -> 146 us (0.980)
  waiting for transfers between devices: 52.1 us -> 49 us
    all_to_all x1, waiting for transfers between devices: 6 us -> 4.02 us  [exchange(): lax.all_to_all(blocks, 'grid', split_axis=0, concat_axis=0, tiled=True)]
    ppermute x24 -> x26, starting transfers between devices: 28.8 us -> 27.6 us  [move(): return lax.ppermute(values, 'grid', table)]
    ppermute x24 -> x26, waiting for transfers between devices: 46.1 us -> 45 us  [move(): return lax.ppermute(values, 'grid', table)]
    concatenate x4 -> x3, other arithmetic: 3.23 us -> 2.3 us  [stack(): return jnp.concatenate(values, axis=0)]
  transfers between devices with their start and end apart: 25 -> 27, of which waited for: 9 -> 9; matrix products, arithmetic and copies ran while one was open for 2% -> 2% of each run, Pallas kernels for 5% -> 5%
where the time goes in v7:
time: 146 us; the launch traced here: 145 us
  waiting for transfers between devices  49 us (34%)
  blocking collectives  42.8 us (29%)
  starting transfers between devices  31.2 us (21%)
  Pallas kernels  18.2 us (12%)
  other arithmetic  2.3 us (2%)
    ppermute x26, waiting for transfers between devices, move(): return lax.ppermute(values, 'grid', table)  45 us
    all_to_all x3, blocking collectives, exchange(): lax.all_to_all(blocks, 'grid', split_axis=0, concat_axis=0, tiled=True)  42.8 us
    ppermute x26, starting transfers between devices, move(): return lax.ppermute(values, 'grid', table)  27.6 us
    pallas_call x1, Pallas kernels, banded_layer(): pl.pallas_call(partial(group_layer, patches, group_plan), out_shape=(shap...  7.56 us
    pallas_call x1, Pallas kernels, banded_layer(): pl.pallas_call(partial(spatial_forward, spatial_plan, patches, groups), o...  5.19 us
    all_to_all x1, waiting for transfers between devices, exchange(): lax.all_to_all(blocks, 'grid', split_axis=0, concat_axis=0, tiled=True)  4.02 us
    all_to_all x1, starting transfers between devices, exchange(): lax.all_to_all(blocks, 'grid', split_axis=0, concat_axis=0, tiled=True)  3.56 us
  transfers between devices with their start and end apart: 27, of which 9 were waited for; matrix products, arithmetic and copies ran while one was open for 2% of the time, Pallas kernels for 5%

profile of v7, /device:TPU:0, one launch (start us, length us, event | category | flops | bytes accessed | tf_op | source)
XLA Modules:
  0.0 145.2 jit_solution(12443207024500250365)
XLA Ops:
  0.6 4.1 %collective-permute-start.1 = (bf16[32,3072]{1,0:T(8,128)(2,1)}, bf16[32,3072]{1,0:T(8,128)(2,1)S(1)}, u32[]{:S(2)}, u32[]{:S(2)}) collective-permute-start(bf16[32,3072]{1,0:T(8,128)(2,1)} %param.9), channel_id=1, source_target_pairs={{0,16},{1,17},{2,18},{3,19},{4,20},{5,21},{6,22},{7,23},{8,24},{9,... | collective-permute-start | bytes 589832 | tf_op jit(solution)/shard_map/ppermute | solution.py:325
  4.7 1.6 %collective-permute-start = (bf16[32,3072]{1,0:T(8,128)(2,1)}, bf16[32,3072]{1,0:T(8,128)(2,1)S(1)}, u32[]{:S(2)}, u32[]{:S(2)}) collective-permute-start(bf16[32,3072]{1,0:T(8,128)(2,1)} %param.9), channel_id=1, source_target_pairs={{0,8},{1,9},{2,10},{3,11},{4,12},{5,13},{6,14},{7,15},{8,16},{9,17... | collective-permute-start | bytes 589832 | tf_op jit(solution)/shard_map/ppermute | solution.py:325
  6.3 2.2 %collective-permute-start.2 = (bf16[32,3072]{1,0:T(8,128)(2,1)}, bf16[32,3072]{1,0:T(8,128)(2,1)S(1)}, u32[]{:S(2)}, u32[]{:S(2)}) collective-permute-start(bf16[32,3072]{1,0:T(8,128)(2,1)} %param.9), channel_id=1, source_target_pairs={{0,24},{1,25},{2,26},{3,27},{4,28},{5,29},{6,30},{7,31},{8,0},{9,1... | collective-permute-start | bytes 589832 | tf_op jit(solution)/shard_map/ppermute | solution.py:325
  8.6 2.1 %prepare.1 = (bf16[256,512]{1,0:T(8,128)(2,1)}, bf16[32,5120]{1,0:T(8,128)(2,1)}) custom-call(bf16[128,1024]{1,0:T(8,128)(2,1)} %bitcast.12, bf16[32,1024]{1,0:T(8,128)(2,1)} %w_so.1, bf16[32,3072]{1,0:T(8,128)(2,1)} %w_gqkv.1, bf16[32,1024]{1,0:T(8,128)(2,1)} %w_go.1), custom_call_target="tpu_custom_call" | custom-call | tf_op jit(solution)/shard_map/prepare/pallas_call | solution.py:357
  10.6 1.5 %collective-permute-start.4 = (bf16[32,5120]{1,0:T(8,128)(2,1)}, bf16[32,5120]{1,0:T(8,128)(2,1)S(1)}, u32[]{:S(2)}, u32[]{:S(2)}) collective-permute-start(bf16[32,5120]{1,0:T(8,128)(2,1)} %get-tuple-element.58), channel_id=1, source_target_pairs={{0,4},{1,3},{2,6},{3,1},{4,0},{5,7},{6,2},{7,5},{8,12},{9,11},{10,... | collective-permute-start | bytes 983048 | tf_op jit(solution)/shard_map/ppermute | solution.py:325
  12.2 1.5 %collective-permute-start.3 = (bf16[32,5120]{1,0:T(8,128)(2,1)}, bf16[32,5120]{1,0:T(8,128)(2,1)S(1)}, u32[]{:S(2)}, u32[]{:S(2)}) collective-permute-start(bf16[32,5120]{1,0:T(8,128)(2,1)} %get-tuple-element.58), channel_id=1, source_target_pairs={{0,2},{1,5},{2,0},{3,7},{4,6},{5,1},{6,4},{7,3},{8,10},{9,13},{10,... | collective-permute-start | bytes 983048 | tf_op jit(solution)/shard_map/ppermute | solution.py:325
  13.7 5.5 %collective-permute-done.1 = bf16[32,3072]{1,0:T(8,128)(2,1)S(1)} collective-permute-done((bf16[32,3072]{1,0:T(8,128)(2,1)}, bf16[32,3072]{1,0:T(8,128)(2,1)S(1)}, u32[]{:S(2)}, u32[]{:S(2)}) %collective-permute-start.1) | collective-permute-done | bytes 196640 | tf_op jit(solution)/shard_map/ppermute | solution.py:325
  19.1 0.0 collective-permute-done
  19.1 0.7 collective-permute-done.2
  19.9 1.0 pad_maximum_fusion.2.refs_0_
  20.8 0.0 collective-permute-done.4
  20.9 0.0 collective-permute-done.3
  20.9 1.6 %collective-permute-start.7 = (bf16[32,5120]{1,0:T(8,128)(2,1)S(1)}, bf16[32,5120]{1,0:T(8,128)(2,1)S(1)}, u32[]{:S(2)}, u32[]{:S(2)}) collective-permute-start(bf16[32,5120]{1,0:T(8,128)(2,1)S(1)} %collective-permute-done.3), channel_id=1, source_target_pairs={{0,4},{1,3},{2,6},{3,1},{4,0},{5,7},{6,2},{7,5},{8,12},{9,11},{10,... | collective-permute-start | bytes 983048 | tf_op jit(solution)/shard_map/ppermute | solution.py:325
  22.5 0.5 collective-permute-start.6
  23.0 1.5 %collective-permute-start.5 = (bf16[128,3072]{1,0:T(8,128)(2,1)S(1)}, bf16[128,3072]{1,0:T(8,128)(2,1)}, u32[]{:S(2)}, u32[]{:S(2)}) collective-permute-start(bf16[128,3072]{1,0:T(8,128)(2,1)S(1)} %pad_maximum_fusion.2.refs_0_), channel_id=1, source_target_pairs={{0,2},{1,5},{2,0},{3,7},{4,6},{5,1},{6,4},{7,3},{8,10},{9,13},{10,... | collective-permute-start | bytes 2359304 | tf_op jit(solution)/shard_map/ppermute | solution.py:325
  24.5 5.2 %collective-permute-start.9 = (bf16[32,5120]{1,0:T(8,128)(2,1)S(1)}, bf16[32,5120]{1,0:T(8,128)(2,1)S(1)}, u32[]{:S(2)}, u32[]{:S(2)}) collective-permute-start(bf16[32,5120]{1,0:T(8,128)(2,1)S(1)} %copy-done.4), channel_id=1, source_target_pairs={{0,16},{1,17},{2,18},{3,19},{4,20},{5,21},{6,22},{7,23},{8,24},{9,... | collective-permute-start | bytes 983048 | tf_op jit(solution)/shard_map/ppermute | solution.py:325
  29.7 0.0 collective-permute-start.8
  29.7 1.7 %collective-permute-done.7 = bf16[32,5120]{1,0:T(8,128)(2,1)S(1)} collective-permute-done((bf16[32,5120]{1,0:T(8,128)(2,1)S(1)}, bf16[32,5120]{1,0:T(8,128)(2,1)S(1)}, u32[]{:S(2)}, u32[]{:S(2)}) %collective-permute-start.7) | collective-permute-done | bytes 327712 | tf_op jit(solution)/shard_map/ppermute | solution.py:325
  31.4 0.1 pad_maximum_fusion.refs_0_
  31.5 0.0 copy-start.2
  31.5 19.3 %collective-permute-done.9 = bf16[32,5120]{1,0:T(8,128)(2,1)S(1)} collective-permute-done((bf16[32,5120]{1,0:T(8,128)(2,1)S(1)}, bf16[32,5120]{1,0:T(8,128)(2,1)S(1)}, u32[]{:S(2)}, u32[]{:S(2)}) %collective-permute-start.9) | collective-permute-done | bytes 327712 | tf_op jit(solution)/shard_map/ppermute | solution.py:325
  50.9 0.0 collective-permute-done.8
  50.9 0.0 collective-permute-done.6.refs_2_
  50.9 0.0 collective-permute-done.5.refs_1_
  50.9 0.1 collective-permute-start.11
  51.0 0.6 copy-done.5
  51.6 0.1 copy-done.6
  51.7 0.4 collective-permute-start.14
  52.1 0.1 collective-permute-start.13
  52.2 0.5 collective-permute-start.10
  52.7 3.6 %all-to-all-start = ((bf16[32,8,512]{2,1,0:T(8,128)(2,1)}), bf16[32,8,512]{2,1,0:T(8,128)(2,1)S(1)}, u32[]{:S(2)}, u32[]{:S(2)}) async-start(bf16[32,8,512]{2,1,0:T(8,128)(2,1)} %bitcast.23), calls=%async_computation | async-start | bytes 524288 | tf_op jit(solution)/shard_map/all_to_all | solution.py:312
  56.3 5.7 %collective-permute-done.11 = bf16[32,5120]{1,0:T(8,128)(2,1)} collective-permute-done((bf16[32,5120]{1,0:T(8,128)(2,1)S(1)}, bf16[32,5120]{1,0:T(8,128)(2,1)}, u32[]{:S(2)}, u32[]{:S(2)}) %collective-permute-start.11) | collective-permute-done | bytes 327712 | tf_op jit(solution)/shard_map/ppermute | solution.py:325
  62.0 1.2 pad_maximum_fusion.1.refs_1_
  63.2 4.0 %all-to-all-done = bf16[32,8,512]{2,1,0:T(8,128)(2,1)S(1)} async-done(((bf16[32,8,512]{2,1,0:T(8,128)(2,1)}), bf16[32,8,512]{2,1,0:T(8,128)(2,1)S(1)}, u32[]{:S(2)}, u32[]{:S(2)}) %all-to-all-start) | async-done | bytes 262176 | tf_op jit(solution)/shard_map/all_to_all | solution.py:312
  67.2 0.0 collective-permute-done.13.refs_5_
  67.3 0.0 collective-permute-done.10.refs_3_
  67.3 1.6 %collective-permute-start.15 = (bf16[96,5120]{1,0:T(8,128)(2,1)S(1)}, bf16[96,5120]{1,0:T(8,128)(2,1)S(1)}, u32[]{:S(2)}, u32[]{:S(2)}) collective-permute-start(bf16[96,5120]{1,0:T(8,128)(2,1)S(1)} %pad_maximum_fusion.1.refs_1_), channel_id=1, source_target_pairs={{0,2},{1,5},{2,0},{3,7},{4,6},{5,1},{6,4},{7,3},{8,10},{9,13},{10,... | collective-permute-start | bytes 2949128 | tf_op jit(solution)/shard_map/ppermute | solution.py:325
  68.8 0.9 collective-permute-start.18
  69.7 1.0 collective-permute-start.19
  70.7 1.0 collective-permute-start.17
  71.7 0.0 collective-permute-done.16.refs_7_
  71.7 5.2 %spatial_forward.1 = (bf16[256,512]{1,0:T(8,128)(2,1)S(1)}, bf16[128,3072]{1,0:T(8,128)(2,1)S(1)}, f32[128,2048]{1,0:T(8,128)S(1)}, bf16[128,1024]{1,0:T(8,128)(2,1)S(1)}, bf16[3072,1024]{1,0:T(8,128)(2,1)S(1)}) custom-call(bf16[256,512]{1,0:T(8,128)(2,1)S(1)} %bitcast.14, s32[32,128]{1,0:T(8,128)S(1)} %copy-done.2, ...), custom_call_target="tpu_custom_call" | custom-call | flops 805306368 | bytes 8388608 | tf_op jit(solution)/shard_map/spatial_forward/pallas_call | solution.py:393
  76.9 0.0 copy-start
  76.9 0.0 copy-start.1
  77.0 2.7 %collective-permute-done.18 = bf16[32,5120]{1,0:T(8,128)(2,1)S(1)} collective-permute-done((bf16[32,5120]{1,0:T(8,128)(2,1)}, bf16[32,5120]{1,0:T(8,128)(2,1)S(1)}, u32[]{:S(2)}, u32[]{:S(2)}) %collective-permute-start.18) | collective-permute-done | bytes 327712 | tf_op jit(solution)/shard_map/ppermute | solution.py:325
  79.7 6.8 %collective-permute-done.19 = bf16[32,5120]{1,0:T(8,128)(2,1)S(1)} collective-permute-done((bf16[32,5120]{1,0:T(8,128)(2,1)}, bf16[32,5120]{1,0:T(8,128)(2,1)S(1)}, u32[]{:S(2)}, u32[]{:S(2)}) %collective-permute-start.19) | collective-permute-done | bytes 327712 | tf_op jit(solution)/shard_map/ppermute | solution.py:325
  86.4 0.0 collective-permute-done.15.refs_2_
  86.5 0.1 collective-permute-start.21
  86.6 0.6 collective-permute-start.24
  87.2 0.1 collective-permute-start.22
  87.2 0.4 collective-permute-start.23
  87.7 1.1 collective-permute-start.20
  88.8 15.8 %all_to_all.20 = bf16[32,8,512]{2,1,0:T(8,128)(2,1)S(1)} all-to-all(bf16[32,8,512]{2,1,0:T(8,128)(2,1)S(1)} %bitcast.20), channel_id=1, replica_groups=mesh['parts'=1,'grid'=32] {'grid'}, dimensions={0} | all-to-all | bytes 524288 | tf_op jit(solution)/shard_map/all_to_all | solution.py:312
  104.6 0.0 collective-permute-done.24.refs_8_
  104.6 0.0 collective-permute-done.22.refs_6_
  104.6 0.0 collective-permute-done.23.refs_7_
  104.6 0.0 collective-permute-done.21.refs_5_
  104.6 0.1 collective-permute-start.25
  104.7 2.6 %collective-permute-done.25.refs_9_ = bf16[96,5120]{1,0:T(8,128)(2,1)S(1)} collective-permute-done((bf16[96,5120]{1,0:T(8,128)(2,1)S(1)}, bf16[96,5120]{1,0:T(8,128)(2,1)S(1)}, u32[]{:S(2)}, u32[]{:S(2)}) %collective-permute-start.25) | collective-permute-done | bytes 983072 | tf_op jit(solution)/shard_map/ppermute | solution.py:325
  107.3 7.6 %group_layer.1 = (bf16[128,1024]{1,0:T(8,128)(2,1)}, bf16[128,1024]{1,0:T(8,128)(2,1)S(1)}, bf16[256,512]{1,0:T(8,128)(2,1)S(1)}) custom-call(bf16[128,1024]{1,0:T(8,128)(2,1)S(1)} %bitcast.13, bf16[256,512]{1,0:T(8,128)(2,1)S(1)} %bitcast.15, bf16[128,1024]{1,0:T(8,128)(2,1)S(1)} %bitcast.19, bf16[128,5120]{1,0:T(8,128)(2,1)S(1)} %pad_maximum_fusion.refs_0_, ...), custom_call_target="tpu_custom_call" | custom-call | flops 2684354560 | bytes 23068672 | tf_op jit(solution)/shard_map/group_layer/pallas_call | solution.py:419
  114.8 14.2 %all_to_all.21 = bf16[32,8,512]{2,1,0:T(8,128)(2,1)S(1)} all-to-all(bf16[32,8,512]{2,1,0:T(8,128)(2,1)S(1)} %bitcast.21), channel_id=1, replica_groups=mesh['parts'=1,'grid'=32] {'grid'}, dimensions={0} | all-to-all | bytes 524288 | tf_op jit(solution)/shard_map/all_to_all | solution.py:312
  129.1 2.4 %spatial_backward.1 = bf16[256,512]{1,0:T(8,128)(2,1)S(1)} custom-call(bf16[256,512]{1,0:T(8,128)(2,1)S(1)} %bitcast.16, bf16[128,1024]{1,0:T(8,128)(2,1)S(1)} %get-tuple-element.90.banded, bf16[128,3072]{1,0:T(8,128)(2,1)S(1)} %get-tuple-element.91.qkv, f32[128,2048]{1,0:T(8,128)S(1)} %get-tuple-element.92.probs, ...), custom_call_target="tpu_custom_call" | custom-call | flops 805306368 | bytes 8388608 | tf_op jit(solution)/shard_map/spatial_backward/pallas_call | solution.py:440
  131.5 12.8 %all_to_all.22 = bf16[32,8,512]{2,1,0:T(8,128)(2,1)S(1)} all-to-all(bf16[32,8,512]{2,1,0:T(8,128)(2,1)S(1)} %bitcast.17), channel_id=1, replica_groups=mesh['parts'=1,'grid'=32] {'grid'}, dimensions={0} | all-to-all | bytes 524288 | tf_op jit(solution)/shard_map/all_to_all | solution.py:312
  144.3 0.9 add_packed.1
  (18 shorter events, 0.1 us)
Async XLA Ops:
  0.6 18.5 %collective-permute-start.1 = (bf16[32,3072]{1,0:T(8,128)(2,1)}, bf16[32,3072]{1,0:T(8,128)(2,1)S(1)}, u32[]{:S(2)}, u32[]{:S(2)}) collective-permute-start(bf16[32,3072]{1,0:T(8,128)(2,1)} %param.9), channel_id=1, source_target_pairs={{0,16},{1,17},{2,18},{3,19},{4,20},{5,21},{6,22},{7,23},{8,24},{9,... | collective-permute-start | bytes 589832 | tf_op jit(solution)/shard_map/ppermute | solution.py:325
  4.7 14.4 %collective-permute-start = (bf16[32,3072]{1,0:T(8,128)(2,1)}, bf16[32,3072]{1,0:T(8,128)(2,1)S(1)}, u32[]{:S(2)}, u32[]{:S(2)}) collective-permute-start(bf16[32,3072]{1,0:T(8,128)(2,1)} %param.9), channel_id=1, source_target_pairs={{0,8},{1,9},{2,10},{3,11},{4,12},{5,13},{6,14},{7,15},{8,16},{9,17... | collective-permute-start | bytes 589832 | tf_op jit(solution)/shard_map/ppermute | solution.py:325
  6.3 13.6 %collective-permute-start.2 = (bf16[32,3072]{1,0:T(8,128)(2,1)}, bf16[32,3072]{1,0:T(8,128)(2,1)S(1)}, u32[]{:S(2)}, u32[]{:S(2)}) collective-permute-start(bf16[32,3072]{1,0:T(8,128)(2,1)} %param.9), channel_id=1, source_target_pairs={{0,24},{1,25},{2,26},{3,27},{4,28},{5,29},{6,30},{7,31},{8,0},{9,1... | collective-permute-start | bytes 589832 | tf_op jit(solution)/shard_map/ppermute | solution.py:325
  10.6 13.9 %copy-start.4 = (bf16[32,5120]{1,0:T(8,128)(2,1)S(1)}, bf16[32,5120]{1,0:T(8,128)(2,1)}, u32[]{:S(2)}) copy-start(bf16[32,5120]{1,0:T(8,128)(2,1)} %get-tuple-element.58) | copy-start | bytes 983044
  10.6 10.2 %collective-permute-start.4 = (bf16[32,5120]{1,0:T(8,128)(2,1)}, bf16[32,5120]{1,0:T(8,128)(2,1)S(1)}, u32[]{:S(2)}, u32[]{:S(2)}) collective-permute-start(bf16[32,5120]{1,0:T(8,128)(2,1)} %get-tuple-element.58), channel_id=1, source_target_pairs={{0,4},{1,3},{2,6},{3,1},{4,0},{5,7},{6,2},{7,5},{8,12},{9,11},{10,... | collective-permute-start | bytes 983048 | tf_op jit(solution)/shard_map/ppermute | solution.py:325
  12.2 8.7 %collective-permute-start.3 = (bf16[32,5120]{1,0:T(8,128)(2,1)}, bf16[32,5120]{1,0:T(8,128)(2,1)S(1)}, u32[]{:S(2)}, u32[]{:S(2)}) collective-permute-start(bf16[32,5120]{1,0:T(8,128)(2,1)} %get-tuple-element.58), channel_id=1, source_target_pairs={{0,2},{1,5},{2,0},{3,7},{4,6},{5,1},{6,4},{7,3},{8,10},{9,13},{10,... | collective-permute-start | bytes 983048 | tf_op jit(solution)/shard_map/ppermute | solution.py:325
  20.9 30.0 %copy-start.3 = (bf16[32,5120]{1,0:T(8,128)(2,1)}, bf16[32,5120]{1,0:T(8,128)(2,1)S(1)}, u32[]{:S(2)}) copy-start(bf16[32,5120]{1,0:T(8,128)(2,1)S(1)} %collective-permute-done.4) | copy-start | bytes 983044
  20.9 10.6 %collective-permute-start.7 = (bf16[32,5120]{1,0:T(8,128)(2,1)S(1)}, bf16[32,5120]{1,0:T(8,128)(2,1)S(1)}, u32[]{:S(2)}, u32[]{:S(2)}) collective-permute-start(bf16[32,5120]{1,0:T(8,128)(2,1)S(1)} %collective-permute-done.3), channel_id=1, source_target_pairs={{0,4},{1,3},{2,6},{3,1},{4,0},{5,7},{6,2},{7,5},{8,12},{9,11},{10,... | collective-permute-start | bytes 983048 | tf_op jit(solution)/shard_map/ppermute | solution.py:325
  22.5 28.3 %collective-permute-start.6 = (bf16[128,3072]{1,0:T(8,128)(2,1)S(1)}, bf16[128,3072]{1,0:T(8,128)(2,1)}, u32[]{:S(2)}, u32[]{:S(2)}) collective-permute-start(bf16[128,3072]{1,0:T(8,128)(2,1)S(1)} %pad_maximum_fusion.2.refs_0_), channel_id=1, source_target_pairs={{0,4},{1,3},{2,6},{3,1},{4,0},{5,7},{6,2},{7,5},{8,12},{9,11},{10,... | collective-permute-start | bytes 2359304 | tf_op jit(solution)/shard_map/ppermute | solution.py:325
  23.0 27.9 %collective-permute-start.5 = (bf16[128,3072]{1,0:T(8,128)(2,1)S(1)}, bf16[128,3072]{1,0:T(8,128)(2,1)}, u32[]{:S(2)}, u32[]{:S(2)}) collective-permute-start(bf16[128,3072]{1,0:T(8,128)(2,1)S(1)} %pad_maximum_fusion.2.refs_0_), channel_id=1, source_target_pairs={{0,2},{1,5},{2,0},{3,7},{4,6},{5,1},{6,4},{7,3},{8,10},{9,13},{10,... | collective-permute-start | bytes 2359304 | tf_op jit(solution)/shard_map/ppermute | solution.py:325
  24.5 26.3 %collective-permute-start.9 = (bf16[32,5120]{1,0:T(8,128)(2,1)S(1)}, bf16[32,5120]{1,0:T(8,128)(2,1)S(1)}, u32[]{:S(2)}, u32[]{:S(2)}) collective-permute-start(bf16[32,5120]{1,0:T(8,128)(2,1)S(1)} %copy-done.4), channel_id=1, source_target_pairs={{0,16},{1,17},{2,18},{3,19},{4,20},{5,21},{6,22},{7,23},{8,24},{9,... | collective-permute-start | bytes 983048 | tf_op jit(solution)/shard_map/ppermute | solution.py:325
  29.7 21.1 %collective-permute-start.8 = (bf16[32,5120]{1,0:T(8,128)(2,1)S(1)}, bf16[32,5120]{1,0:T(8,128)(2,1)S(1)}, u32[]{:S(2)}, u32[]{:S(2)}) collective-permute-start(bf16[32,5120]{1,0:T(8,128)(2,1)S(1)} %copy-done.4), channel_id=1, source_target_pairs={{0,8},{1,9},{2,10},{3,11},{4,12},{5,13},{6,14},{7,15},{8,16},{9,17... | collective-permute-start | bytes 983048 | tf_op jit(solution)/shard_map/ppermute | solution.py:325
  31.5 40.2 %copy-start.2 = (s32[32,128]{1,0:T(8,128)S(1)}, s32[32,128]{1,0:T(8,128)}, u32[]{:S(2)}) copy-start(s32[32,128]{1,0:T(8,128)} %keep.1) | copy-start | bytes 49156
  50.8 0.7 copy-start.5
  50.9 0.9 copy-start.6
  50.9 11.1 %collective-permute-start.11 = (bf16[32,5120]{1,0:T(8,128)(2,1)S(1)}, bf16[32,5120]{1,0:T(8,128)(2,1)}, u32[]{:S(2)}, u32[]{:S(2)}) collective-permute-start(bf16[32,5120]{1,0:T(8,128)(2,1)S(1)} %copy-done.4), channel_id=1, source_target_pairs={{0,24},{1,25},{2,26},{3,27},{4,28},{5,29},{6,30},{7,31},{8,0},{9,1... | collective-permute-start | bytes 983048 | tf_op jit(solution)/shard_map/ppermute | solution.py:325
  51.6 15.7 %collective-permute-start.12 = (bf16[128,3072]{1,0:T(8,128)(2,1)S(1)}, bf16[128,3072]{1,0:T(8,128)(2,1)}, u32[]{:S(2)}, u32[]{:S(2)}) collective-permute-start(bf16[128,3072]{1,0:T(8,128)(2,1)S(1)} %pad_maximum_fusion.2.refs_0_), channel_id=1, source_target_pairs={{0,1},{1,0},{2,3},{3,2},{4,5},{5,4},{6,7},{7,6},{8,9},{9,8},{10,11... | collective-permute-start | bytes 2359304 | tf_op jit(solution)/shard_map/ppermute | solution.py:325
  51.7 15.5 %collective-permute-start.14 = (bf16[128,3072]{1,0:T(8,128)(2,1)}, bf16[128,3072]{1,0:T(8,128)(2,1)}, u32[]{:S(2)}, u32[]{:S(2)}) collective-permute-start(bf16[128,3072]{1,0:T(8,128)(2,1)} %collective-permute-done.6.refs_2_), channel_id=1, source_target_pairs={{0,1},{1,0},{2,3},{3,2},{4,5},{5,4},{6,7},{7,6},{8,9},{9,8},{10,11... | collective-permute-start | bytes 2359304 | tf_op jit(solution)/shard_map/ppermute | solution.py:325
  52.1 15.2 %collective-permute-start.13 = (bf16[128,3072]{1,0:T(8,128)(2,1)}, bf16[128,3072]{1,0:T(8,128)(2,1)}, u32[]{:S(2)}, u32[]{:S(2)}) collective-permute-start(bf16[128,3072]{1,0:T(8,128)(2,1)} %collective-permute-done.5.refs_1_), channel_id=1, source_target_pairs={{0,1},{1,0},{2,3},{3,2},{4,5},{5,4},{6,7},{7,6},{8,9},{9,8},{10,11... | collective-permute-start | bytes 2359304 | tf_op jit(solution)/shard_map/ppermute | solution.py:325
  52.2 15.0 %collective-permute-start.10 = (bf16[128,3072]{1,0:T(8,128)(2,1)}, bf16[128,3072]{1,0:T(8,128)(2,1)}, u32[]{:S(2)}, u32[]{:S(2)}) collective-permute-start(bf16[128,3072]{1,0:T(8,128)(2,1)} %collective-permute-done.5.refs_1_), channel_id=1, source_target_pairs={{0,4},{1,3},{2,6},{3,1},{4,0},{5,7},{6,2},{7,5},{8,12},{9,11},{10,... | collective-permute-start | bytes 2359304 | tf_op jit(solution)/shard_map/ppermute | solution.py:325
  52.7 14.5 %all-to-all-start = ((bf16[32,8,512]{2,1,0:T(8,128)(2,1)}), bf16[32,8,512]{2,1,0:T(8,128)(2,1)S(1)}, u32[]{:S(2)}, u32[]{:S(2)}) async-start(bf16[32,8,512]{2,1,0:T(8,128)(2,1)} %bitcast.23), calls=%async_computation | async-start | bytes 524288 | tf_op jit(solution)/shard_map/all_to_all | solution.py:312
  67.3 19.2 %collective-permute-start.15 = (bf16[96,5120]{1,0:T(8,128)(2,1)S(1)}, bf16[96,5120]{1,0:T(8,128)(2,1)S(1)}, u32[]{:S(2)}, u32[]{:S(2)}) collective-permute-start(bf16[96,5120]{1,0:T(8,128)(2,1)S(1)} %pad_maximum_fusion.1.refs_1_), channel_id=1, source_target_pairs={{0,2},{1,5},{2,0},{3,7},{4,6},{5,1},{6,4},{7,3},{8,10},{9,13},{10,... | collective-permute-start | bytes 2949128 | tf_op jit(solution)/shard_map/ppermute | solution.py:325
  68.8 2.9 %collective-permute-start.16 = (bf16[128,3072]{1,0:T(8,128)(2,1)}, bf16[128,3072]{1,0:T(8,128)(2,1)S(1)}, u32[]{:S(2)}, u32[]{:S(2)}) collective-permute-start(bf16[128,3072]{1,0:T(8,128)(2,1)} %collective-permute-done.10.refs_3_), channel_id=1, source_target_pairs={{0,1},{1,0},{2,3},{3,2},{4,5},{5,4},{6,7},{7,6},{8,9},{9,8},{10,11... | collective-permute-start | bytes 2359304 | tf_op jit(solution)/shard_map/ppermute | solution.py:325
  68.8 10.9 %collective-permute-start.18 = (bf16[32,5120]{1,0:T(8,128)(2,1)}, bf16[32,5120]{1,0:T(8,128)(2,1)S(1)}, u32[]{:S(2)}, u32[]{:S(2)}) collective-permute-start(bf16[32,5120]{1,0:T(8,128)(2,1)} %copy-done.5), channel_id=1, source_target_pairs={{0,4},{1,3},{2,6},{3,1},{4,0},{5,7},{6,2},{7,5},{8,12},{9,11},{10,... | collective-permute-start | bytes 983048 | tf_op jit(solution)/shard_map/ppermute | solution.py:325
  69.7 16.7 %collective-permute-start.19 = (bf16[32,5120]{1,0:T(8,128)(2,1)}, bf16[32,5120]{1,0:T(8,128)(2,1)S(1)}, u32[]{:S(2)}, u32[]{:S(2)}) collective-permute-start(bf16[32,5120]{1,0:T(8,128)(2,1)} %copy-done.3), channel_id=1, source_target_pairs={{0,24},{1,25},{2,26},{3,27},{4,28},{5,29},{6,30},{7,31},{8,0},{9,1... | collective-permute-start | bytes 983048 | tf_op jit(solution)/shard_map/ppermute | solution.py:325
  70.7 15.8 %collective-permute-start.17 = (bf16[32,5120]{1,0:T(8,128)(2,1)}, bf16[32,5120]{1,0:T(8,128)(2,1)S(1)}, u32[]{:S(2)}, u32[]{:S(2)}) collective-permute-start(bf16[32,5120]{1,0:T(8,128)(2,1)} %copy-done.3), channel_id=1, source_target_pairs={{0,8},{1,9},{2,10},{3,11},{4,12},{5,13},{6,14},{7,15},{8,16},{9,17... | collective-permute-start | bytes 983048 | tf_op jit(solution)/shard_map/ppermute | solution.py:325
  76.9 30.3 %copy-start = (bf16[4,32,1024]{2,1,0:T(8,128)(2,1)S(1)}, bf16[4,32,1024]{2,1,0:T(8,128)(2,1)}, u32[]{:S(2)}) copy-start(bf16[4,32,1024]{2,1,0:T(8,128)(2,1)} %param.7) | copy-start | bytes 786436
  76.9 30.3 %copy-start.1 = (bf16[4,32,1024]{2,1,0:T(8,128)(2,1)S(1)}, bf16[4,32,1024]{2,1,0:T(8,128)(2,1)}, u32[]{:S(2)}) copy-start(bf16[4,32,1024]{2,1,0:T(8,128)(2,1)} %param.8) | copy-start | bytes 786436
  86.5 18.1 %collective-permute-start.21 = (bf16[128,5120]{1,0:T(8,128)(2,1)S(1)}, bf16[128,5120]{1,0:T(8,128)(2,1)S(1)}, u32[]{:S(2)}, u32[]{:S(2)}) collective-permute-start(bf16[128,5120]{1,0:T(8,128)(2,1)S(1)} %pad_maximum_fusion.refs_0_), channel_id=1, source_target_pairs={{0,1},{1,0},{2,3},{3,2},{4,5},{5,4},{6,7},{7,6},{8,9},{9,8},{10,11... | collective-permute-start | bytes 3932168 | tf_op jit(solution)/shard_map/ppermute | solution.py:325
  86.6 18.0 %collective-permute-start.24 = (bf16[96,5120]{1,0:T(8,128)(2,1)S(1)}, bf16[96,5120]{1,0:T(8,128)(2,1)S(1)}, u32[]{:S(2)}, u32[]{:S(2)}) collective-permute-start(bf16[96,5120]{1,0:T(8,128)(2,1)S(1)} %constant_dynamic-update-slice_fusion.refs_3_), channel_id=1, source_target_pairs={{0,1},{1,0},{2,3},{3,2},{4,5},{5,4},{6,7},{7,6},{8,9},{9,8},{10,11... | collective-permute-start | bytes 2949128 | tf_op jit(solution)/shard_map/ppermute | solution.py:325
  87.2 17.4 %collective-permute-start.22 = (bf16[96,5120]{1,0:T(8,128)(2,1)S(1)}, bf16[96,5120]{1,0:T(8,128)(2,1)S(1)}, u32[]{:S(2)}, u32[]{:S(2)}) collective-permute-start(bf16[96,5120]{1,0:T(8,128)(2,1)S(1)} %pad_maximum_fusion.1.refs_1_), channel_id=1, source_target_pairs={{0,1},{1,0},{2,3},{3,2},{4,5},{5,4},{6,7},{7,6},{8,9},{9,8},{10,11... | collective-permute-start | bytes 2949128 | tf_op jit(solution)/shard_map/ppermute | solution.py:325
  87.2 17.3 %collective-permute-start.23 = (bf16[96,5120]{1,0:T(8,128)(2,1)S(1)}, bf16[96,5120]{1,0:T(8,128)(2,1)S(1)}, u32[]{:S(2)}, u32[]{:S(2)}) collective-permute-start(bf16[96,5120]{1,0:T(8,128)(2,1)S(1)} %collective-permute-done.15.refs_2_), channel_id=1, source_target_pairs={{0,1},{1,0},{2,3},{3,2},{4,5},{5,4},{6,7},{7,6},{8,9},{9,8},{10,11... | collective-permute-start | bytes 2949128 | tf_op jit(solution)/shard_map/ppermute | solution.py:325
  87.7 16.9 %collective-permute-start.20 = (bf16[96,5120]{1,0:T(8,128)(2,1)S(1)}, bf16[96,5120]{1,0:T(8,128)(2,1)S(1)}, u32[]{:S(2)}, u32[]{:S(2)}) collective-permute-start(bf16[96,5120]{1,0:T(8,128)(2,1)S(1)} %collective-permute-done.15.refs_2_), channel_id=1, source_target_pairs={{0,4},{1,3},{2,6},{3,1},{4,0},{5,7},{6,2},{7,5},{8,12},{9,11},{10,... | collective-permute-start | bytes 2949128 | tf_op jit(solution)/shard_map/ppermute | solution.py:325
  104.6 2.6 %collective-permute-start.25 = (bf16[96,5120]{1,0:T(8,128)(2,1)S(1)}, bf16[96,5120]{1,0:T(8,128)(2,1)S(1)}, u32[]{:S(2)}, u32[]{:S(2)}) collective-permute-start(bf16[96,5120]{1,0:T(8,128)(2,1)S(1)} %collective-permute-done.20.refs_4_), channel_id=1, source_target_pairs={{0,1},{1,0},{2,3},{3,2},{4,5},{5,4},{6,7},{7,6},{8,9},{9,8},{10,11... | collective-permute-start | bytes 2949128 | tf_op jit(solution)/shard_map/ppermute | solution.py:325

commit v8 on v7

--- a/solution.py
+++ b/solution.py
@@ -148,7 +148,7 @@
     for head in range(2 * pairs):
         at = slice(head * rows, head * rows + rows)
         weights = jnp.where(allowed, jnp.exp(probs[:, at] * 0.125), 0.0)
-        probs[:, at] = weights * (1.0 / jnp.sum(weights, axis=-1, keepdims=True))
+        probs[:, at] = weights / jnp.sum(weights, axis=-1, keepdims=True)
     results = []
     for pair in range(pairs):
         valued = head_pair(qkv[:, columns(2, pair, width)], low)

time: 146 us -> 146 us (level)
  no operation moved by 1% of the time
where the time goes in v8:
time: 146 us; the launch traced here: 145 us
  waiting for transfers between devices  49 us (34%)
  blocking collectives  42.8 us (29%)
  starting transfers between devices  31.2 us (21%)
  Pallas kernels  18.2 us (12%)
  other arithmetic  2.3 us (2%)
    ppermute x26, waiting for transfers between devices, move(): return lax.ppermute(values, 'grid', table)  45 us
    all_to_all x3, blocking collectives, exchange(): lax.all_to_all(blocks, 'grid', split_axis=0, concat_axis=0, tiled=True)  42.8 us
    ppermute x26, starting transfers between devices, move(): return lax.ppermute(values, 'grid', table)  27.6 us
    pallas_call x1, Pallas kernels, banded_layer(): pl.pallas_call(partial(group_layer, patches, group_plan), out_shape=(shap...  7.56 us
    pallas_call x1, Pallas kernels, banded_layer(): pl.pallas_call(partial(spatial_forward, spatial_plan, patches, groups), o...  5.19 us
    all_to_all x1, waiting for transfers between devices, exchange(): lax.all_to_all(blocks, 'grid', split_axis=0, concat_axis=0, tiled=True)  4.02 us
    all_to_all x1, starting transfers between devices, exchange(): lax.all_to_all(blocks, 'grid', split_axis=0, concat_axis=0, tiled=True)  3.56 us
  transfers between devices with their start and end apart: 27, of which 9 were waited for; matrix products, arithmetic and copies ran while one was open for 2% of the time, Pallas kernels for 5%

profile of v8, /device:TPU:0, one launch (start us, length us, event | category | flops | bytes accessed | tf_op | source)
XLA Modules:
  0.0 145.2 jit_solution(12443207024500250365)
XLA Ops:
  0.6 4.1 %collective-permute-start.1 = (bf16[32,3072]{1,0:T(8,128)(2,1)}, bf16[32,3072]{1,0:T(8,128)(2,1)S(1)}, u32[]{:S(2)}, u32[]{:S(2)}) collective-permute-start(bf16[32,3072]{1,0:T(8,128)(2,1)} %param.9), channel_id=1, source_target_pairs={{0,16},{1,17},{2,18},{3,19},{4,20},{5,21},{6,22},{7,23},{8,24},{9,... | collective-permute-start | bytes 589832 | tf_op jit(solution)/shard_map/ppermute | solution.py:325
  4.7 1.6 %collective-permute-start = (bf16[32,3072]{1,0:T(8,128)(2,1)}, bf16[32,3072]{1,0:T(8,128)(2,1)S(1)}, u32[]{:S(2)}, u32[]{:S(2)}) collective-permute-start(bf16[32,3072]{1,0:T(8,128)(2,1)} %param.9), channel_id=1, source_target_pairs={{0,8},{1,9},{2,10},{3,11},{4,12},{5,13},{6,14},{7,15},{8,16},{9,17... | collective-permute-start | bytes 589832 | tf_op jit(solution)/shard_map/ppermute | solution.py:325
  6.3 2.2 %collective-permute-start.2 = (bf16[32,3072]{1,0:T(8,128)(2,1)}, bf16[32,3072]{1,0:T(8,128)(2,1)S(1)}, u32[]{:S(2)}, u32[]{:S(2)}) collective-permute-start(bf16[32,3072]{1,0:T(8,128)(2,1)} %param.9), channel_id=1, source_target_pairs={{0,24},{1,25},{2,26},{3,27},{4,28},{5,29},{6,30},{7,31},{8,0},{9,1... | collective-permute-start | bytes 589832 | tf_op jit(solution)/shard_map/ppermute | solution.py:325
  8.6 2.1 %prepare.1 = (bf16[256,512]{1,0:T(8,128)(2,1)}, bf16[32,5120]{1,0:T(8,128)(2,1)}) custom-call(bf16[128,1024]{1,0:T(8,128)(2,1)} %bitcast.12, bf16[32,1024]{1,0:T(8,128)(2,1)} %w_so.1, bf16[32,3072]{1,0:T(8,128)(2,1)} %w_gqkv.1, bf16[32,1024]{1,0:T(8,128)(2,1)} %w_go.1), custom_call_target="tpu_custom_call" | custom-call | tf_op jit(solution)/shard_map/prepare/pallas_call | solution.py:357
  10.6 1.5 %collective-permute-start.4 = (bf16[32,5120]{1,0:T(8,128)(2,1)}, bf16[32,5120]{1,0:T(8,128)(2,1)S(1)}, u32[]{:S(2)}, u32[]{:S(2)}) collective-permute-start(bf16[32,5120]{1,0:T(8,128)(2,1)} %get-tuple-element.58), channel_id=1, source_target_pairs={{0,4},{1,3},{2,6},{3,1},{4,0},{5,7},{6,2},{7,5},{8,12},{9,11},{10,... | collective-permute-start | bytes 983048 | tf_op jit(solution)/shard_map/ppermute | solution.py:325
  12.2 1.5 %collective-permute-start.3 = (bf16[32,5120]{1,0:T(8,128)(2,1)}, bf16[32,5120]{1,0:T(8,128)(2,1)S(1)}, u32[]{:S(2)}, u32[]{:S(2)}) collective-permute-start(bf16[32,5120]{1,0:T(8,128)(2,1)} %get-tuple-element.58), channel_id=1, source_target_pairs={{0,2},{1,5},{2,0},{3,7},{4,6},{5,1},{6,4},{7,3},{8,10},{9,13},{10,... | collective-permute-start | bytes 983048 | tf_op jit(solution)/shard_map/ppermute | solution.py:325
  13.7 5.5 %collective-permute-done.1 = bf16[32,3072]{1,0:T(8,128)(2,1)S(1)} collective-permute-done((bf16[32,3072]{1,0:T(8,128)(2,1)}, bf16[32,3072]{1,0:T(8,128)(2,1)S(1)}, u32[]{:S(2)}, u32[]{:S(2)}) %collective-permute-start.1) | collective-permute-done | bytes 196640 | tf_op jit(solution)/shard_map/ppermute | solution.py:325
  19.1 0.0 collective-permute-done
  19.1 0.7 collective-permute-done.2
  19.9 1.0 pad_maximum_fusion.2.refs_0_
  20.8 0.0 collective-permute-done.4
  20.9 0.0 collective-permute-done.3
  20.9 1.6 %collective-permute-start.7 = (bf16[32,5120]{1,0:T(8,128)(2,1)S(1)}, bf16[32,5120]{1,0:T(8,128)(2,1)S(1)}, u32[]{:S(2)}, u32[]{:S(2)}) collective-permute-start(bf16[32,5120]{1,0:T(8,128)(2,1)S(1)} %collective-permute-done.3), channel_id=1, source_target_pairs={{0,4},{1,3},{2,6},{3,1},{4,0},{5,7},{6,2},{7,5},{8,12},{9,11},{10,... | collective-permute-start | bytes 983048 | tf_op jit(solution)/shard_map/ppermute | solution.py:325
  22.5 0.5 collective-permute-start.6
  23.0 1.5 %collective-permute-start.5 = (bf16[128,3072]{1,0:T(8,128)(2,1)S(1)}, bf16[128,3072]{1,0:T(8,128)(2,1)}, u32[]{:S(2)}, u32[]{:S(2)}) collective-permute-start(bf16[128,3072]{1,0:T(8,128)(2,1)S(1)} %pad_maximum_fusion.2.refs_0_), channel_id=1, source_target_pairs={{0,2},{1,5},{2,0},{3,7},{4,6},{5,1},{6,4},{7,3},{8,10},{9,13},{10,... | collective-permute-start | bytes 2359304 | tf_op jit(solution)/shard_map/ppermute | solution.py:325
  24.5 5.2 %collective-permute-start.9 = (bf16[32,5120]{1,0:T(8,128)(2,1)S(1)}, bf16[32,5120]{1,0:T(8,128)(2,1)S(1)}, u32[]{:S(2)}, u32[]{:S(2)}) collective-permute-start(bf16[32,5120]{1,0:T(8,128)(2,1)S(1)} %copy-done.4), channel_id=1, source_target_pairs={{0,16},{1,17},{2,18},{3,19},{4,20},{5,21},{6,22},{7,23},{8,24},{9,... | collective-permute-start | bytes 983048 | tf_op jit(solution)/shard_map/ppermute | solution.py:325
  29.7 0.0 collective-permute-start.8
  29.7 1.7 %collective-permute-done.7 = bf16[32,5120]{1,0:T(8,128)(2,1)S(1)} collective-permute-done((bf16[32,5120]{1,0:T(8,128)(2,1)S(1)}, bf16[32,5120]{1,0:T(8,128)(2,1)S(1)}, u32[]{:S(2)}, u32[]{:S(2)}) %collective-permute-start.7) | collective-permute-done | bytes 327712 | tf_op jit(solution)/shard_map/ppermute | solution.py:325
  31.4 0.1 pad_maximum_fusion.refs_0_
  31.5 0.0 copy-start.2
  31.5 19.3 %collective-permute-done.9 = bf16[32,5120]{1,0:T(8,128)(2,1)S(1)} collective-permute-done((bf16[32,5120]{1,0:T(8,128)(2,1)S(1)}, bf16[32,5120]{1,0:T(8,128)(2,1)S(1)}, u32[]{:S(2)}, u32[]{:S(2)}) %collective-permute-start.9) | collective-permute-done | bytes 327712 | tf_op jit(solution)/shard_map/ppermute | solution.py:325
  50.9 0.0 collective-permute-done.8
  50.9 0.0 collective-permute-done.6.refs_2_
  50.9 0.0 collective-permute-done.5.refs_1_
  50.9 0.1 collective-permute-start.11
  51.0 0.6 copy-done.5
  51.6 0.1 copy-done.6
  51.7 0.4 collective-permute-start.14
  52.1 0.1 collective-permute-start.13
  52.2 0.5 collective-permute-start.10
  52.7 3.6 %all-to-all-start = ((bf16[32,8,512]{2,1,0:T(8,128)(2,1)}), bf16[32,8,512]{2,1,0:T(8,128)(2,1)S(1)}, u32[]{:S(2)}, u32[]{:S(2)}) async-start(bf16[32,8,512]{2,1,0:T(8,128)(2,1)} %bitcast.23), calls=%async_computation | async-start | bytes 524288 | tf_op jit(solution)/shard_map/all_to_all | solution.py:312
  56.3 5.7 %collective-permute-done.11 = bf16[32,5120]{1,0:T(8,128)(2,1)} collective-permute-done((bf16[32,5120]{1,0:T(8,128)(2,1)S(1)}, bf16[32,5120]{1,0:T(8,128)(2,1)}, u32[]{:S(2)}, u32[]{:S(2)}) %collective-permute-start.11) | collective-permute-done | bytes 327712 | tf_op jit(solution)/shard_map/ppermute | solution.py:325
  62.0 1.2 pad_maximum_fusion.1.refs_1_
  63.2 4.0 %all-to-all-done = bf16[32,8,512]{2,1,0:T(8,128)(2,1)S(1)} async-done(((bf16[32,8,512]{2,1,0:T(8,128)(2,1)}), bf16[32,8,512]{2,1,0:T(8,128)(2,1)S(1)}, u32[]{:S(2)}, u32[]{:S(2)}) %all-to-all-start) | async-done | bytes 262176 | tf_op jit(solution)/shard_map/all_to_all | solution.py:312
  67.2 0.0 collective-permute-done.13.refs_5_
  67.3 0.0 collective-permute-done.10.refs_3_
  67.3 1.6 %collective-permute-start.15 = (bf16[96,5120]{1,0:T(8,128)(2,1)S(1)}, bf16[96,5120]{1,0:T(8,128)(2,1)S(1)}, u32[]{:S(2)}, u32[]{:S(2)}) collective-permute-start(bf16[96,5120]{1,0:T(8,128)(2,1)S(1)} %pad_maximum_fusion.1.refs_1_), channel_id=1, source_target_pairs={{0,2},{1,5},{2,0},{3,7},{4,6},{5,1},{6,4},{7,3},{8,10},{9,13},{10,... | collective-permute-start | bytes 2949128 | tf_op jit(solution)/shard_map/ppermute | solution.py:325
  68.8 0.9 collective-permute-start.18
  69.7 1.0 collective-permute-start.19
  70.7 1.0 collective-permute-start.17
  71.7 0.0 collective-permute-done.16.refs_7_
  71.7 5.2 %spatial_forward.1 = (bf16[256,512]{1,0:T(8,128)(2,1)S(1)}, bf16[128,3072]{1,0:T(8,128)(2,1)S(1)}, f32[128,2048]{1,0:T(8,128)S(1)}, bf16[128,1024]{1,0:T(8,128)(2,1)S(1)}, bf16[3072,1024]{1,0:T(8,128)(2,1)S(1)}) custom-call(bf16[256,512]{1,0:T(8,128)(2,1)S(1)} %bitcast.14, s32[32,128]{1,0:T(8,128)S(1)} %copy-done.2, ...), custom_call_target="tpu_custom_call" | custom-call | flops 805306368 | bytes 8388608 | tf_op jit(solution)/shard_map/spatial_forward/pallas_call | solution.py:393
  76.9 0.0 copy-start
  76.9 0.0 copy-start.1
  77.0 2.7 %collective-permute-done.18 = bf16[32,5120]{1,0:T(8,128)(2,1)S(1)} collective-permute-done((bf16[32,5120]{1,0:T(8,128)(2,1)}, bf16[32,5120]{1,0:T(8,128)(2,1)S(1)}, u32[]{:S(2)}, u32[]{:S(2)}) %collective-permute-start.18) | collective-permute-done | bytes 327712 | tf_op jit(solution)/shard_map/ppermute | solution.py:325
  79.7 6.8 %collective-permute-done.19 = bf16[32,5120]{1,0:T(8,128)(2,1)S(1)} collective-permute-done((bf16[32,5120]{1,0:T(8,128)(2,1)}, bf16[32,5120]{1,0:T(8,128)(2,1)S(1)}, u32[]{:S(2)}, u32[]{:S(2)}) %collective-permute-start.19) | collective-permute-done | bytes 327712 | tf_op jit(solution)/shard_map/ppermute | solution.py:325
  86.4 0.0 collective-permute-done.15.refs_2_
  86.5 0.1 collective-permute-start.21
  86.6 0.6 collective-permute-start.24
  87.2 0.1 collective-permute-start.22
  87.2 0.4 collective-permute-start.23
  87.7 1.1 collective-permute-start.20
  88.8 15.8 %all_to_all.20 = bf16[32,8,512]{2,1,0:T(8,128)(2,1)S(1)} all-to-all(bf16[32,8,512]{2,1,0:T(8,128)(2,1)S(1)} %bitcast.20), channel_id=1, replica_groups=mesh['parts'=1,'grid'=32] {'grid'}, dimensions={0} | all-to-all | bytes 524288 | tf_op jit(solution)/shard_map/all_to_all | solution.py:312
  104.6 0.0 collective-permute-done.24.refs_8_
  104.6 0.0 collective-permute-done.22.refs_6_
  104.6 0.0 collective-permute-done.23.refs_7_
  104.6 0.0 collective-permute-done.21.refs_5_
  104.6 0.1 collective-permute-start.25
  104.7 2.6 %collective-permute-done.25.refs_9_ = bf16[96,5120]{1,0:T(8,128)(2,1)S(1)} collective-permute-done((bf16[96,5120]{1,0:T(8,128)(2,1)S(1)}, bf16[96,5120]{1,0:T(8,128)(2,1)S(1)}, u32[]{:S(2)}, u32[]{:S(2)}) %collective-permute-start.25) | collective-permute-done | bytes 983072 | tf_op jit(solution)/shard_map/ppermute | solution.py:325
  107.3 7.6 %group_layer.1 = (bf16[128,1024]{1,0:T(8,128)(2,1)}, bf16[128,1024]{1,0:T(8,128)(2,1)S(1)}, bf16[256,512]{1,0:T(8,128)(2,1)S(1)}) custom-call(bf16[128,1024]{1,0:T(8,128)(2,1)S(1)} %bitcast.13, bf16[256,512]{1,0:T(8,128)(2,1)S(1)} %bitcast.15, bf16[128,1024]{1,0:T(8,128)(2,1)S(1)} %bitcast.19, bf16[128,5120]{1,0:T(8,128)(2,1)S(1)} %pad_maximum_fusion.refs_0_, ...), custom_call_target="tpu_custom_call" | custom-call | flops 2684354560 | bytes 23068672 | tf_op jit(solution)/shard_map/group_layer/pallas_call | solution.py:419
  114.8 14.2 %all_to_all.21 = bf16[32,8,512]{2,1,0:T(8,128)(2,1)S(1)} all-to-all(bf16[32,8,512]{2,1,0:T(8,128)(2,1)S(1)} %bitcast.21), channel_id=1, replica_groups=mesh['parts'=1,'grid'=32] {'grid'}, dimensions={0} | all-to-all | bytes 524288 | tf_op jit(solution)/shard_map/all_to_all | solution.py:312
  129.1 2.4 %spatial_backward.1 = bf16[256,512]{1,0:T(8,128)(2,1)S(1)} custom-call(bf16[256,512]{1,0:T(8,128)(2,1)S(1)} %bitcast.16, bf16[128,1024]{1,0:T(8,128)(2,1)S(1)} %get-tuple-element.90.banded, bf16[128,3072]{1,0:T(8,128)(2,1)S(1)} %get-tuple-element.91.qkv, f32[128,2048]{1,0:T(8,128)S(1)} %get-tuple-element.92.probs, ...), custom_call_target="tpu_custom_call" | custom-call | flops 805306368 | bytes 8388608 | tf_op jit(solution)/shard_map/spatial_backward/pallas_call | solution.py:440
  131.5 12.8 %all_to_all.22 = bf16[32,8,512]{2,1,0:T(8,128)(2,1)S(1)} all-to-all(bf16[32,8,512]{2,1,0:T(8,128)(2,1)S(1)} %bitcast.17), channel_id=1, replica_groups=mesh['parts'=1,'grid'=32] {'grid'}, dimensions={0} | all-to-all | bytes 524288 | tf_op jit(solution)/shard_map/all_to_all | solution.py:312
  144.3 0.9 add_packed.1
  (18 shorter events, 0.1 us)
Async XLA Ops:
  0.6 18.5 %collective-permute-start.1 = (bf16[32,3072]{1,0:T(8,128)(2,1)}, bf16[32,3072]{1,0:T(8,128)(2,1)S(1)}, u32[]{:S(2)}, u32[]{:S(2)}) collective-permute-start(bf16[32,3072]{1,0:T(8,128)(2,1)} %param.9), channel_id=1, source_target_pairs={{0,16},{1,17},{2,18},{3,19},{4,20},{5,21},{6,22},{7,23},{8,24},{9,... | collective-permute-start | bytes 589832 | tf_op jit(solution)/shard_map/ppermute | solution.py:325
  4.7 14.4 %collective-permute-start = (bf16[32,3072]{1,0:T(8,128)(2,1)}, bf16[32,3072]{1,0:T(8,128)(2,1)S(1)}, u32[]{:S(2)}, u32[]{:S(2)}) collective-permute-start(bf16[32,3072]{1,0:T(8,128)(2,1)} %param.9), channel_id=1, source_target_pairs={{0,8},{1,9},{2,10},{3,11},{4,12},{5,13},{6,14},{7,15},{8,16},{9,17... | collective-permute-start | bytes 589832 | tf_op jit(solution)/shard_map/ppermute | solution.py:325
  6.3 13.6 %collective-permute-start.2 = (bf16[32,3072]{1,0:T(8,128)(2,1)}, bf16[32,3072]{1,0:T(8,128)(2,1)S(1)}, u32[]{:S(2)}, u32[]{:S(2)}) collective-permute-start(bf16[32,3072]{1,0:T(8,128)(2,1)} %param.9), channel_id=1, source_target_pairs={{0,24},{1,25},{2,26},{3,27},{4,28},{5,29},{6,30},{7,31},{8,0},{9,1... | collective-permute-start | bytes 589832 | tf_op jit(solution)/shard_map/ppermute | solution.py:325
  10.6 13.9 %copy-start.4 = (bf16[32,5120]{1,0:T(8,128)(2,1)S(1)}, bf16[32,5120]{1,0:T(8,128)(2,1)}, u32[]{:S(2)}) copy-start(bf16[32,5120]{1,0:T(8,128)(2,1)} %get-tuple-element.58) | copy-start | bytes 983044
  10.6 10.2 %collective-permute-start.4 = (bf16[32,5120]{1,0:T(8,128)(2,1)}, bf16[32,5120]{1,0:T(8,128)(2,1)S(1)}, u32[]{:S(2)}, u32[]{:S(2)}) collective-permute-start(bf16[32,5120]{1,0:T(8,128)(2,1)} %get-tuple-element.58), channel_id=1, source_target_pairs={{0,4},{1,3},{2,6},{3,1},{4,0},{5,7},{6,2},{7,5},{8,12},{9,11},{10,... | collective-permute-start | bytes 983048 | tf_op jit(solution)/shard_map/ppermute | solution.py:325
  12.2 8.7 %collective-permute-start.3 = (bf16[32,5120]{1,0:T(8,128)(2,1)}, bf16[32,5120]{1,0:T(8,128)(2,1)S(1)}, u32[]{:S(2)}, u32[]{:S(2)}) collective-permute-start(bf16[32,5120]{1,0:T(8,128)(2,1)} %get-tuple-element.58), channel_id=1, source_target_pairs={{0,2},{1,5},{2,0},{3,7},{4,6},{5,1},{6,4},{7,3},{8,10},{9,13},{10,... | collective-permute-start | bytes 983048 | tf_op jit(solution)/shard_map/ppermute | solution.py:325
  20.9 30.0 %copy-start.3 = (bf16[32,5120]{1,0:T(8,128)(2,1)}, bf16[32,5120]{1,0:T(8,128)(2,1)S(1)}, u32[]{:S(2)}) copy-start(bf16[32,5120]{1,0:T(8,128)(2,1)S(1)} %collective-permute-done.4) | copy-start | bytes 983044
  20.9 10.6 %collective-permute-start.7 = (bf16[32,5120]{1,0:T(8,128)(2,1)S(1)}, bf16[32,5120]{1,0:T(8,128)(2,1)S(1)}, u32[]{:S(2)}, u32[]{:S(2)}) collective-permute-start(bf16[32,5120]{1,0:T(8,128)(2,1)S(1)} %collective-permute-done.3), channel_id=1, source_target_pairs={{0,4},{1,3},{2,6},{3,1},{4,0},{5,7},{6,2},{7,5},{8,12},{9,11},{10,... | collective-permute-start | bytes 983048 | tf_op jit(solution)/shard_map/ppermute | solution.py:325
  22.5 28.3 %collective-permute-start.6 = (bf16[128,3072]{1,0:T(8,128)(2,1)S(1)}, bf16[128,3072]{1,0:T(8,128)(2,1)}, u32[]{:S(2)}, u32[]{:S(2)}) collective-permute-start(bf16[128,3072]{1,0:T(8,128)(2,1)S(1)} %pad_maximum_fusion.2.refs_0_), channel_id=1, source_target_pairs={{0,4},{1,3},{2,6},{3,1},{4,0},{5,7},{6,2},{7,5},{8,12},{9,11},{10,... | collective-permute-start | bytes 2359304 | tf_op jit(solution)/shard_map/ppermute | solution.py:325
  23.0 27.9 %collective-permute-start.5 = (bf16[128,3072]{1,0:T(8,128)(2,1)S(1)}, bf16[128,3072]{1,0:T(8,128)(2,1)}, u32[]{:S(2)}, u32[]{:S(2)}) collective-permute-start(bf16[128,3072]{1,0:T(8,128)(2,1)S(1)} %pad_maximum_fusion.2.refs_0_), channel_id=1, source_target_pairs={{0,2},{1,5},{2,0},{3,7},{4,6},{5,1},{6,4},{7,3},{8,10},{9,13},{10,... | collective-permute-start | bytes 2359304 | tf_op jit(solution)/shard_map/ppermute | solution.py:325
  24.5 26.3 %collective-permute-start.9 = (bf16[32,5120]{1,0:T(8,128)(2,1)S(1)}, bf16[32,5120]{1,0:T(8,128)(2,1)S(1)}, u32[]{:S(2)}, u32[]{:S(2)}) collective-permute-start(bf16[32,5120]{1,0:T(8,128)(2,1)S(1)} %copy-done.4), channel_id=1, source_target_pairs={{0,16},{1,17},{2,18},{3,19},{4,20},{5,21},{6,22},{7,23},{8,24},{9,... | collective-permute-start | bytes 983048 | tf_op jit(solution)/shard_map/ppermute | solution.py:325
  29.7 21.1 %collective-permute-start.8 = (bf16[32,5120]{1,0:T(8,128)(2,1)S(1)}, bf16[32,5120]{1,0:T(8,128)(2,1)S(1)}, u32[]{:S(2)}, u32[]{:S(2)}) collective-permute-start(bf16[32,5120]{1,0:T(8,128)(2,1)S(1)} %copy-done.4), channel_id=1, source_target_pairs={{0,8},{1,9},{2,10},{3,11},{4,12},{5,13},{6,14},{7,15},{8,16},{9,17... | collective-permute-start | bytes 983048 | tf_op jit(solution)/shard_map/ppermute | solution.py:325
  31.5 40.2 %copy-start.2 = (s32[32,128]{1,0:T(8,128)S(1)}, s32[32,128]{1,0:T(8,128)}, u32[]{:S(2)}) copy-start(s32[32,128]{1,0:T(8,128)} %keep.1) | copy-start | bytes 49156
  50.8 0.7 copy-start.5
  50.9 0.9 copy-start.6
  50.9 11.1 %collective-permute-start.11 = (bf16[32,5120]{1,0:T(8,128)(2,1)S(1)}, bf16[32,5120]{1,0:T(8,128)(2,1)}, u32[]{:S(2)}, u32[]{:S(2)}) collective-permute-start(bf16[32,5120]{1,0:T(8,128)(2,1)S(1)} %copy-done.4), channel_id=1, source_target_pairs={{0,24},{1,25},{2,26},{3,27},{4,28},{5,29},{6,30},{7,31},{8,0},{9,1... | collective-permute-start | bytes 983048 | tf_op jit(solution)/shard_map/ppermute | solution.py:325
  51.6 15.7 %collective-permute-start.12 = (bf16[128,3072]{1,0:T(8,128)(2,1)S(1)}, bf16[128,3072]{1,0:T(8,128)(2,1)}, u32[]{:S(2)}, u32[]{:S(2)}) collective-permute-start(bf16[128,3072]{1,0:T(8,128)(2,1)S(1)} %pad_maximum_fusion.2.refs_0_), channel_id=1, source_target_pairs={{0,1},{1,0},{2,3},{3,2},{4,5},{5,4},{6,7},{7,6},{8,9},{9,8},{10,11... | collective-permute-start | bytes 2359304 | tf_op jit(solution)/shard_map/ppermute | solution.py:325
  51.7 15.5 %collective-permute-start.14 = (bf16[128,3072]{1,0:T(8,128)(2,1)}, bf16[128,3072]{1,0:T(8,128)(2,1)}, u32[]{:S(2)}, u32[]{:S(2)}) collective-permute-start(bf16[128,3072]{1,0:T(8,128)(2,1)} %collective-permute-done.6.refs_2_), channel_id=1, source_target_pairs={{0,1},{1,0},{2,3},{3,2},{4,5},{5,4},{6,7},{7,6},{8,9},{9,8},{10,11... | collective-permute-start | bytes 2359304 | tf_op jit(solution)/shard_map/ppermute | solution.py:325
  52.1 15.2 %collective-permute-start.13 = (bf16[128,3072]{1,0:T(8,128)(2,1)}, bf16[128,3072]{1,0:T(8,128)(2,1)}, u32[]{:S(2)}, u32[]{:S(2)}) collective-permute-start(bf16[128,3072]{1,0:T(8,128)(2,1)} %collective-permute-done.5.refs_1_), channel_id=1, source_target_pairs={{0,1},{1,0},{2,3},{3,2},{4,5},{5,4},{6,7},{7,6},{8,9},{9,8},{10,11... | collective-permute-start | bytes 2359304 | tf_op jit(solution)/shard_map/ppermute | solution.py:325
  52.2 15.0 %collective-permute-start.10 = (bf16[128,3072]{1,0:T(8,128)(2,1)}, bf16[128,3072]{1,0:T(8,128)(2,1)}, u32[]{:S(2)}, u32[]{:S(2)}) collective-permute-start(bf16[128,3072]{1,0:T(8,128)(2,1)} %collective-permute-done.5.refs_1_), channel_id=1, source_target_pairs={{0,4},{1,3},{2,6},{3,1},{4,0},{5,7},{6,2},{7,5},{8,12},{9,11},{10,... | collective-permute-start | bytes 2359304 | tf_op jit(solution)/shard_map/ppermute | solution.py:325
  52.7 14.5 %all-to-all-start = ((bf16[32,8,512]{2,1,0:T(8,128)(2,1)}), bf16[32,8,512]{2,1,0:T(8,128)(2,1)S(1)}, u32[]{:S(2)}, u32[]{:S(2)}) async-start(bf16[32,8,512]{2,1,0:T(8,128)(2,1)} %bitcast.23), calls=%async_computation | async-start | bytes 524288 | tf_op jit(solution)/shard_map/all_to_all | solution.py:312
  67.3 19.2 %collective-permute-start.15 = (bf16[96,5120]{1,0:T(8,128)(2,1)S(1)}, bf16[96,5120]{1,0:T(8,128)(2,1)S(1)}, u32[]{:S(2)}, u32[]{:S(2)}) collective-permute-start(bf16[96,5120]{1,0:T(8,128)(2,1)S(1)} %pad_maximum_fusion.1.refs_1_), channel_id=1, source_target_pairs={{0,2},{1,5},{2,0},{3,7},{4,6},{5,1},{6,4},{7,3},{8,10},{9,13},{10,... | collective-permute-start | bytes 2949128 | tf_op jit(solution)/shard_map/ppermute | solution.py:325
  68.8 2.9 %collective-permute-start.16 = (bf16[128,3072]{1,0:T(8,128)(2,1)}, bf16[128,3072]{1,0:T(8,128)(2,1)S(1)}, u32[]{:S(2)}, u32[]{:S(2)}) collective-permute-start(bf16[128,3072]{1,0:T(8,128)(2,1)} %collective-permute-done.10.refs_3_), channel_id=1, source_target_pairs={{0,1},{1,0},{2,3},{3,2},{4,5},{5,4},{6,7},{7,6},{8,9},{9,8},{10,11... | collective-permute-start | bytes 2359304 | tf_op jit(solution)/shard_map/ppermute | solution.py:325
  68.8 10.9 %collective-permute-start.18 = (bf16[32,5120]{1,0:T(8,128)(2,1)}, bf16[32,5120]{1,0:T(8,128)(2,1)S(1)}, u32[]{:S(2)}, u32[]{:S(2)}) collective-permute-start(bf16[32,5120]{1,0:T(8,128)(2,1)} %copy-done.5), channel_id=1, source_target_pairs={{0,4},{1,3},{2,6},{3,1},{4,0},{5,7},{6,2},{7,5},{8,12},{9,11},{10,... | collective-permute-start | bytes 983048 | tf_op jit(solution)/shard_map/ppermute | solution.py:325
  69.7 16.7 %collective-permute-start.19 = (bf16[32,5120]{1,0:T(8,128)(2,1)}, bf16[32,5120]{1,0:T(8,128)(2,1)S(1)}, u32[]{:S(2)}, u32[]{:S(2)}) collective-permute-start(bf16[32,5120]{1,0:T(8,128)(2,1)} %copy-done.3), channel_id=1, source_target_pairs={{0,24},{1,25},{2,26},{3,27},{4,28},{5,29},{6,30},{7,31},{8,0},{9,1... | collective-permute-start | bytes 983048 | tf_op jit(solution)/shard_map/ppermute | solution.py:325
  70.7 15.8 %collective-permute-start.17 = (bf16[32,5120]{1,0:T(8,128)(2,1)}, bf16[32,5120]{1,0:T(8,128)(2,1)S(1)}, u32[]{:S(2)}, u32[]{:S(2)}) collective-permute-start(bf16[32,5120]{1,0:T(8,128)(2,1)} %copy-done.3), channel_id=1, source_target_pairs={{0,8},{1,9},{2,10},{3,11},{4,12},{5,13},{6,14},{7,15},{8,16},{9,17... | collective-permute-start | bytes 983048 | tf_op jit(solution)/shard_map/ppermute | solution.py:325
  76.9 30.3 %copy-start = (bf16[4,32,1024]{2,1,0:T(8,128)(2,1)S(1)}, bf16[4,32,1024]{2,1,0:T(8,128)(2,1)}, u32[]{:S(2)}) copy-start(bf16[4,32,1024]{2,1,0:T(8,128)(2,1)} %param.7) | copy-start | bytes 786436
  76.9 30.3 %copy-start.1 = (bf16[4,32,1024]{2,1,0:T(8,128)(2,1)S(1)}, bf16[4,32,1024]{2,1,0:T(8,128)(2,1)}, u32[]{:S(2)}) copy-start(bf16[4,32,1024]{2,1,0:T(8,128)(2,1)} %param.8) | copy-start | bytes 786436
  86.5 18.1 %collective-permute-start.21 = (bf16[128,5120]{1,0:T(8,128)(2,1)S(1)}, bf16[128,5120]{1,0:T(8,128)(2,1)S(1)}, u32[]{:S(2)}, u32[]{:S(2)}) collective-permute-start(bf16[128,5120]{1,0:T(8,128)(2,1)S(1)} %pad_maximum_fusion.refs_0_), channel_id=1, source_target_pairs={{0,1},{1,0},{2,3},{3,2},{4,5},{5,4},{6,7},{7,6},{8,9},{9,8},{10,11... | collective-permute-start | bytes 3932168 | tf_op jit(solution)/shard_map/ppermute | solution.py:325
  86.6 18.0 %collective-permute-start.24 = (bf16[96,5120]{1,0:T(8,128)(2,1)S(1)}, bf16[96,5120]{1,0:T(8,128)(2,1)S(1)}, u32[]{:S(2)}, u32[]{:S(2)}) collective-permute-start(bf16[96,5120]{1,0:T(8,128)(2,1)S(1)} %constant_dynamic-update-slice_fusion.refs_3_), channel_id=1, source_target_pairs={{0,1},{1,0},{2,3},{3,2},{4,5},{5,4},{6,7},{7,6},{8,9},{9,8},{10,11... | collective-permute-start | bytes 2949128 | tf_op jit(solution)/shard_map/ppermute | solution.py:325
  87.2 17.4 %collective-permute-start.22 = (bf16[96,5120]{1,0:T(8,128)(2,1)S(1)}, bf16[96,5120]{1,0:T(8,128)(2,1)S(1)}, u32[]{:S(2)}, u32[]{:S(2)}) collective-permute-start(bf16[96,5120]{1,0:T(8,128)(2,1)S(1)} %pad_maximum_fusion.1.refs_1_), channel_id=1, source_target_pairs={{0,1},{1,0},{2,3},{3,2},{4,5},{5,4},{6,7},{7,6},{8,9},{9,8},{10,11... | collective-permute-start | bytes 2949128 | tf_op jit(solution)/shard_map/ppermute | solution.py:325
  87.2 17.3 %collective-permute-start.23 = (bf16[96,5120]{1,0:T(8,128)(2,1)S(1)}, bf16[96,5120]{1,0:T(8,128)(2,1)S(1)}, u32[]{:S(2)}, u32[]{:S(2)}) collective-permute-start(bf16[96,5120]{1,0:T(8,128)(2,1)S(1)} %collective-permute-done.15.refs_2_), channel_id=1, source_target_pairs={{0,1},{1,0},{2,3},{3,2},{4,5},{5,4},{6,7},{7,6},{8,9},{9,8},{10,11... | collective-permute-start | bytes 2949128 | tf_op jit(solution)/shard_map/ppermute | solution.py:325
  87.7 16.9 %collective-permute-start.20 = (bf16[96,5120]{1,0:T(8,128)(2,1)S(1)}, bf16[96,5120]{1,0:T(8,128)(2,1)S(1)}, u32[]{:S(2)}, u32[]{:S(2)}) collective-permute-start(bf16[96,5120]{1,0:T(8,128)(2,1)S(1)} %collective-permute-done.15.refs_2_), channel_id=1, source_target_pairs={{0,4},{1,3},{2,6},{3,1},{4,0},{5,7},{6,2},{7,5},{8,12},{9,11},{10,... | collective-permute-start | bytes 2949128 | tf_op jit(solution)/shard_map/ppermute | solution.py:325
  104.6 2.6 %collective-permute-start.25 = (bf16[96,5120]{1,0:T(8,128)(2,1)S(1)}, bf16[96,5120]{1,0:T(8,128)(2,1)S(1)}, u32[]{:S(2)}, u32[]{:S(2)}) collective-permute-start(bf16[96,5120]{1,0:T(8,128)(2,1)S(1)} %collective-permute-done.20.refs_4_), channel_id=1, source_target_pairs={{0,1},{1,0},{2,3},{3,2},{4,5},{5,4},{6,7},{7,6},{8,9},{9,8},{10,11... | collective-permute-start | bytes 2949128 | tf_op jit(solution)/shard_map/ppermute | solution.py:325

commit v9 on v8

--- a/solution.py
+++ b/solution.py
@@ -406,11 +406,10 @@
         cost_estimate=cost(all_patches, width, 3, 1),
         name="spatial_forward",
     )(banded, keep, *spatial_rows)
-    group_one, attended, group_plane, group_line, *other_parts = together(
-        group_one, attended, group_plane, group_line, *other_parts
+    group_one, attended, group_plane, group_line, group_other = together(
+        group_one, attended, group_plane, group_line, stack(*other_parts)
     )
     group_both = move(group_one, second)
-    group_other = stack(*other_parts)
     group_across = [move(part, sibling) for part in (group_plane, group_line, group_one, group_other)]
     group_both, attended, *group_across = together(group_both, exchange(attended), *group_across)
     group_rows = [group_plane, group_line, group_one, group_other, group_both]

time: 146 us -> 149 us (1.021)
  waiting for transfers between devices: 49 us -> 52.4 us
    ppermute x26, waiting for transfers between devices: 45 us -> 48.4 us  [move(): return lax.ppermute(values, 'grid', table)]
    concatenate x3 -> x4, other arithmetic: 2.3 us -> 3.33 us  [stack(): return jnp.concatenate(values, axis=0)]
where the time goes in v9:
time: 149 us
  waiting for transfers between devices  52.4 us (35%)
  blocking collectives  42.8 us (29%)
  starting transfers between devices  30.5 us (20%)
  Pallas kernels  18.2 us (12%)
  other arithmetic  3.33 us (2%)
    ppermute x26, waiting for transfers between devices, move(): return lax.ppermute(values, 'grid', table)  48.4 us
    all_to_all x3, blocking collectives, exchange(): lax.all_to_all(blocks, 'grid', split_axis=0, concat_axis=0, tiled=True)  42.8 us
    ppermute x26, starting transfers between devices, move(): return lax.ppermute(values, 'grid', table)  26.9 us
    pallas_call x1, Pallas kernels, banded_layer(): pl.pallas_call(partial(group_layer, patches, group_plan), out_shape=(shap...  7.57 us
    pallas_call x1, Pallas kernels, banded_layer(): pl.pallas_call(partial(spatial_forward, spatial_plan, patches, groups), o...  5.24 us
    all_to_all x1, waiting for transfers between devices, exchange(): lax.all_to_all(blocks, 'grid', split_axis=0, concat_axis=0, tiled=True)  3.99 us
    all_to_all x1, starting transfers between devices, exchange(): lax.all_to_all(blocks, 'grid', split_axis=0, concat_axis=0, tiled=True)  3.6 us
    concatenate x4, other arithmetic, stack(): return jnp.concatenate(values, axis=0)  3.33 us
  transfers between devices with their start and end apart: 27, of which 9 were waited for; matrix products, arithmetic and copies ran while one was open for 2% of the time, Pallas kernels for 5%

profile of v9, /device:TPU:0, one launch (start us, length us, event | category | flops | bytes accessed | tf_op | source)
XLA Modules:
  0.0 148.9 jit_solution(1494614193857841347)
XLA Ops:
  0.6 4.1 %collective-permute-start.1 = (bf16[32,3072]{1,0:T(8,128)(2,1)}, bf16[32,3072]{1,0:T(8,128)(2,1)S(1)}, u32[]{:S(2)}, u32[]{:S(2)}) collective-permute-start(bf16[32,3072]{1,0:T(8,128)(2,1)} %param.9), channel_id=1, source_target_pairs={{0,16},{1,17},{2,18},{3,19},{4,20},{5,21},{6,22},{7,23},{8,24},{9,... | collective-permute-start | bytes 589832 | tf_op jit(solution)/shard_map/ppermute | solution.py:325
  4.7 1.6 %collective-permute-start = (bf16[32,3072]{1,0:T(8,128)(2,1)}, bf16[32,3072]{1,0:T(8,128)(2,1)S(1)}, u32[]{:S(2)}, u32[]{:S(2)}) collective-permute-start(bf16[32,3072]{1,0:T(8,128)(2,1)} %param.9), channel_id=1, source_target_pairs={{0,8},{1,9},{2,10},{3,11},{4,12},{5,13},{6,14},{7,15},{8,16},{9,17... | collective-permute-start | bytes 589832 | tf_op jit(solution)/shard_map/ppermute | solution.py:325
  6.3 2.2 %collective-permute-start.2 = (bf16[32,3072]{1,0:T(8,128)(2,1)}, bf16[32,3072]{1,0:T(8,128)(2,1)S(1)}, u32[]{:S(2)}, u32[]{:S(2)}) collective-permute-start(bf16[32,3072]{1,0:T(8,128)(2,1)} %param.9), channel_id=1, source_target_pairs={{0,24},{1,25},{2,26},{3,27},{4,28},{5,29},{6,30},{7,31},{8,0},{9,1... | collective-permute-start | bytes 589832 | tf_op jit(solution)/shard_map/ppermute | solution.py:325
  8.6 2.1 %prepare.1 = (bf16[256,512]{1,0:T(8,128)(2,1)}, bf16[32,5120]{1,0:T(8,128)(2,1)}) custom-call(bf16[128,1024]{1,0:T(8,128)(2,1)} %bitcast.12, bf16[32,1024]{1,0:T(8,128)(2,1)} %w_so.1, bf16[32,3072]{1,0:T(8,128)(2,1)} %w_gqkv.1, bf16[32,1024]{1,0:T(8,128)(2,1)} %w_go.1), custom_call_target="tpu_custom_call" | custom-call | tf_op jit(solution)/shard_map/prepare/pallas_call | solution.py:357
  10.6 1.5 %collective-permute-start.4 = (bf16[32,5120]{1,0:T(8,128)(2,1)}, bf16[32,5120]{1,0:T(8,128)(2,1)S(1)}, u32[]{:S(2)}, u32[]{:S(2)}) collective-permute-start(bf16[32,5120]{1,0:T(8,128)(2,1)} %get-tuple-element.56), channel_id=1, source_target_pairs={{0,4},{1,3},{2,6},{3,1},{4,0},{5,7},{6,2},{7,5},{8,12},{9,11},{10,... | collective-permute-start | bytes 983048 | tf_op jit(solution)/shard_map/ppermute | solution.py:325
  12.2 1.5 collective-permute-start.3
  13.7 5.5 %collective-permute-done.1 = bf16[32,3072]{1,0:T(8,128)(2,1)S(1)} collective-permute-done((bf16[32,3072]{1,0:T(8,128)(2,1)}, bf16[32,3072]{1,0:T(8,128)(2,1)S(1)}, u32[]{:S(2)}, u32[]{:S(2)}) %collective-permute-start.1) | collective-permute-done | bytes 196640 | tf_op jit(solution)/shard_map/ppermute | solution.py:325
  19.1 0.0 collective-permute-done
  19.1 0.7 collective-permute-done.2
  19.9 1.0 pad_maximum_fusion.3.refs_0_
  20.8 0.0 collective-permute-done.4
  20.9 0.0 collective-permute-done.3
  20.9 1.6 %collective-permute-start.7 = (bf16[32,5120]{1,0:T(8,128)(2,1)S(1)}, bf16[32,5120]{1,0:T(8,128)(2,1)S(1)}, u32[]{:S(2)}, u32[]{:S(2)}) collective-permute-start(bf16[32,5120]{1,0:T(8,128)(2,1)S(1)} %collective-permute-done.3), channel_id=1, source_target_pairs={{0,4},{1,3},{2,6},{3,1},{4,0},{5,7},{6,2},{7,5},{8,12},{9,11},{10,... | collective-permute-start | bytes 983048 | tf_op jit(solution)/shard_map/ppermute | solution.py:325
  22.5 0.5 collective-permute-start.6
  23.0 1.5 %collective-permute-start.5 = (bf16[128,3072]{1,0:T(8,128)(2,1)S(1)}, bf16[128,3072]{1,0:T(8,128)(2,1)}, u32[]{:S(2)}, u32[]{:S(2)}) collective-permute-start(bf16[128,3072]{1,0:T(8,128)(2,1)S(1)} %pad_maximum_fusion.3.refs_0_), channel_id=1, source_target_pairs={{0,2},{1,5},{2,0},{3,7},{4,6},{5,1},{6,4},{7,3},{8,10},{9,13},{10,... | collective-permute-start | bytes 2359304 | tf_op jit(solution)/shard_map/ppermute | solution.py:325
  24.5 5.2 %collective-permute-start.9 = (bf16[32,5120]{1,0:T(8,128)(2,1)}, bf16[32,5120]{1,0:T(8,128)(2,1)S(1)}, u32[]{:S(2)}, u32[]{:S(2)}) collective-permute-start(bf16[32,5120]{1,0:T(8,128)(2,1)} %get-tuple-element.56), channel_id=1, source_target_pairs={{0,16},{1,17},{2,18},{3,19},{4,20},{5,21},{6,22},{7,23},{8,24},{9,... | collective-permute-start | bytes 983048 | tf_op jit(solution)/shard_map/ppermute | solution.py:325
  29.7 0.0 collective-permute-start.8
  29.7 1.7 %collective-permute-done.7 = bf16[32,5120]{1,0:T(8,128)(2,1)S(1)} collective-permute-done((bf16[32,5120]{1,0:T(8,128)(2,1)S(1)}, bf16[32,5120]{1,0:T(8,128)(2,1)S(1)}, u32[]{:S(2)}, u32[]{:S(2)}) %collective-permute-start.7) | collective-permute-done | bytes 327712 | tf_op jit(solution)/shard_map/ppermute | solution.py:325
  31.4 1.1 pad_maximum_fusion.refs_0_
  32.5 18.6 %collective-permute-done.9 = bf16[32,5120]{1,0:T(8,128)(2,1)S(1)} collective-permute-done((bf16[32,5120]{1,0:T(8,128)(2,1)}, bf16[32,5120]{1,0:T(8,128)(2,1)S(1)}, u32[]{:S(2)}, u32[]{:S(2)}) %collective-permute-start.9) | collective-permute-done | bytes 327712 | tf_op jit(solution)/shard_map/ppermute | solution.py:325
  51.1 0.0 collective-permute-done.8
  51.1 0.0 collective-permute-done.6.refs_2_
  51.1 0.0 collective-permute-done.5.refs_1_
  51.1 0.1 collective-permute-start.11
  51.2 0.6 copy-done.5
  51.8 0.0 collective-permute-start.12
  51.8 0.1 copy-done.6
  51.9 0.4 collective-permute-start.14
  52.3 0.1 collective-permute-start.13
  52.4 0.5 collective-permute-start.10
  52.9 3.6 %all-to-all-start = ((bf16[32,8,512]{2,1,0:T(8,128)(2,1)}), bf16[32,8,512]{2,1,0:T(8,128)(2,1)S(1)}, u32[]{:S(2)}, u32[]{:S(2)}) async-start(bf16[32,8,512]{2,1,0:T(8,128)(2,1)} %bitcast.1), calls=%async_computation | async-start | bytes 524288 | tf_op jit(solution)/shard_map/all_to_all | solution.py:312
  56.5 0.0 copy-start.2
  56.5 5.7 %collective-permute-done.11 = bf16[32,5120]{1,0:T(8,128)(2,1)} collective-permute-done((bf16[32,5120]{1,0:T(8,128)(2,1)S(1)}, bf16[32,5120]{1,0:T(8,128)(2,1)}, u32[]{:S(2)}, u32[]{:S(2)}) %collective-permute-start.11) | collective-permute-done | bytes 327712 | tf_op jit(solution)/shard_map/ppermute | solution.py:325
  62.2 1.2 pad_maximum_fusion.1.refs_1_
  63.4 4.0 %all-to-all-done = bf16[32,8,512]{2,1,0:T(8,128)(2,1)S(1)} async-done(((bf16[32,8,512]{2,1,0:T(8,128)(2,1)}), bf16[32,8,512]{2,1,0:T(8,128)(2,1)S(1)}, u32[]{:S(2)}, u32[]{:S(2)}) %all-to-all-start) | async-done | bytes 262176 | tf_op jit(solution)/shard_map/all_to_all | solution.py:312
  67.4 0.0 collective-permute-done.14.refs_6_
  67.4 0.0 collective-permute-done.13.refs_5_
  67.4 0.0 collective-permute-done.10.refs_3_
  67.4 0.8 collective-permute-start.18
  68.2 2.0 %collective-permute-start.19 = (bf16[32,5120]{1,0:T(8,128)(2,1)}, bf16[32,5120]{1,0:T(8,128)(2,1)S(1)}, u32[]{:S(2)}, u32[]{:S(2)}) collective-permute-start(bf16[32,5120]{1,0:T(8,128)(2,1)} %copy-done.3), channel_id=1, source_target_pairs={{0,24},{1,25},{2,26},{3,27},{4,28},{5,29},{6,30},{7,31},{8,0},{9,1... | collective-permute-start | bytes 983048 | tf_op jit(solution)/shard_map/ppermute | solution.py:325
  70.2 0.1 collective-permute-start.17
  70.3 1.7 %collective-permute-start.15 = (bf16[96,5120]{1,0:T(8,128)(2,1)S(1)}, bf16[96,5120]{1,0:T(8,128)(2,1)S(1)}, u32[]{:S(2)}, u32[]{:S(2)}) collective-permute-start(bf16[96,5120]{1,0:T(8,128)(2,1)S(1)} %pad_maximum_fusion.1.refs_1_), channel_id=1, source_target_pairs={{0,2},{1,5},{2,0},{3,7},{4,6},{5,1},{6,4},{7,3},{8,10},{9,13},{10,... | collective-permute-start | bytes 2949128 | tf_op jit(solution)/shard_map/ppermute | solution.py:325
  71.9 4.8 %collective-permute-done.18 = bf16[32,5120]{1,0:T(8,128)(2,1)S(1)} collective-permute-done((bf16[32,5120]{1,0:T(8,128)(2,1)}, bf16[32,5120]{1,0:T(8,128)(2,1)S(1)}, u32[]{:S(2)}, u32[]{:S(2)}) %collective-permute-start.18) | collective-permute-done | bytes 327712 | tf_op jit(solution)/shard_map/ppermute | solution.py:325
  76.7 8.9 %collective-permute-done.19 = bf16[32,5120]{1,0:T(8,128)(2,1)S(1)} collective-permute-done((bf16[32,5120]{1,0:T(8,128)(2,1)}, bf16[32,5120]{1,0:T(8,128)(2,1)S(1)}, u32[]{:S(2)}, u32[]{:S(2)}) %collective-permute-start.19) | collective-permute-done | bytes 327712 | tf_op jit(solution)/shard_map/ppermute | solution.py:325
  85.6 0.1 pad_maximum_fusion.2.refs_3_
  85.7 0.0 copy-start
  85.7 0.0 copy-start.1
  85.7 5.2 %spatial_forward.1 = (bf16[256,512]{1,0:T(8,128)(2,1)S(1)}, bf16[128,3072]{1,0:T(8,128)(2,1)S(1)}, f32[128,2048]{1,0:T(8,128)S(1)}, bf16[128,1024]{1,0:T(8,128)(2,1)S(1)}, bf16[3072,1024]{1,0:T(8,128)(2,1)S(1)}) custom-call(bf16[256,512]{1,0:T(8,128)(2,1)S(1)} %bitcast.14, s32[32,128]{1,0:T(8,128)S(1)} %copy-done.2, ...), custom_call_target="tpu_custom_call" | custom-call | flops 805306368 | bytes 8388608 | tf_op jit(solution)/shard_map/spatial_forward/pallas_call | solution.py:393
  91.0 0.1 collective-permute-start.21
  91.1 0.5 collective-permute-start.22
  91.6 0.1 collective-permute-start.24
  91.7 0.4 collective-permute-start.23
  92.1 0.4 collective-permute-start.20
  92.5 16.5 %all_to_all.20 = bf16[32,8,512]{2,1,0:T(8,128)(2,1)S(1)} all-to-all(bf16[32,8,512]{2,1,0:T(8,128)(2,1)S(1)} %bitcast.20), channel_id=1, replica_groups=mesh['parts'=1,'grid'=32] {'grid'}, dimensions={0} | all-to-all | bytes 524288 | tf_op jit(solution)/shard_map/all_to_all | solution.py:312
  109.0 0.0 collective-permute-done.22.refs_6_
  109.0 0.0 collective-permute-done.24.refs_8_
  109.0 0.0 collective-permute-done.21.refs_5_
  109.0 0.1 collective-permute-start.25
  109.1 2.6 %collective-permute-done.25.refs_9_ = bf16[96,5120]{1,0:T(8,128)(2,1)S(1)} collective-permute-done((bf16[96,5120]{1,0:T(8,128)(2,1)S(1)}, bf16[96,5120]{1,0:T(8,128)(2,1)S(1)}, u32[]{:S(2)}, u32[]{:S(2)}) %collective-permute-start.25) | collective-permute-done | bytes 983072 | tf_op jit(solution)/shard_map/ppermute | solution.py:325
  111.7 7.6 %group_layer.1 = (bf16[128,1024]{1,0:T(8,128)(2,1)}, bf16[128,1024]{1,0:T(8,128)(2,1)S(1)}, bf16[256,512]{1,0:T(8,128)(2,1)S(1)}) custom-call(bf16[128,1024]{1,0:T(8,128)(2,1)S(1)} %bitcast.13, bf16[256,512]{1,0:T(8,128)(2,1)S(1)} %bitcast.15, bf16[128,1024]{1,0:T(8,128)(2,1)S(1)} %bitcast.19, bf16[128,5120]{1,0:T(8,128)(2,1)S(1)} %pad_maximum_fusion.refs_0_, ...), custom_call_target="tpu_custom_call" | custom-call | flops 2684354560 | bytes 23068672 | tf_op jit(solution)/shard_map/group_layer/pallas_call | solution.py:418
  119.2 13.5 %all_to_all.21 = bf16[32,8,512]{2,1,0:T(8,128)(2,1)S(1)} all-to-all(bf16[32,8,512]{2,1,0:T(8,128)(2,1)S(1)} %bitcast.21), channel_id=1, replica_groups=mesh['parts'=1,'grid'=32] {'grid'}, dimensions={0} | all-to-all | bytes 524288 | tf_op jit(solution)/shard_map/all_to_all | solution.py:312
  132.7 2.4 %spatial_backward.1 = bf16[256,512]{1,0:T(8,128)(2,1)S(1)} custom-call(bf16[256,512]{1,0:T(8,128)(2,1)S(1)} %bitcast.16, bf16[128,1024]{1,0:T(8,128)(2,1)S(1)} %get-tuple-element.86.banded, bf16[128,3072]{1,0:T(8,128)(2,1)S(1)} %get-tuple-element.87.qkv, f32[128,2048]{1,0:T(8,128)S(1)} %get-tuple-element.88.probs, ...), custom_call_target="tpu_custom_call" | custom-call | flops 805306368 | bytes 8388608 | tf_op jit(solution)/shard_map/spatial_backward/pallas_call | solution.py:439
  135.1 12.8 %all_to_all.22 = bf16[32,8,512]{2,1,0:T(8,128)(2,1)S(1)} all-to-all(bf16[32,8,512]{2,1,0:T(8,128)(2,1)S(1)} %bitcast.17), channel_id=1, replica_groups=mesh['parts'=1,'grid'=32] {'grid'}, dimensions={0} | all-to-all | bytes 524288 | tf_op jit(solution)/shard_map/all_to_all | solution.py:312
  147.9 0.9 add_packed.1
  (16 shorter events, 0.0 us)
Async XLA Ops:
  0.6 18.5 %collective-permute-start.1 = (bf16[32,3072]{1,0:T(8,128)(2,1)}, bf16[32,3072]{1,0:T(8,128)(2,1)S(1)}, u32[]{:S(2)}, u32[]{:S(2)}) collective-permute-start(bf16[32,3072]{1,0:T(8,128)(2,1)} %param.9), channel_id=1, source_target_pairs={{0,16},{1,17},{2,18},{3,19},{4,20},{5,21},{6,22},{7,23},{8,24},{9,... | collective-permute-start | bytes 589832 | tf_op jit(solution)/shard_map/ppermute | solution.py:325
  4.7 14.4 %collective-permute-start = (bf16[32,3072]{1,0:T(8,128)(2,1)}, bf16[32,3072]{1,0:T(8,128)(2,1)S(1)}, u32[]{:S(2)}, u32[]{:S(2)}) collective-permute-start(bf16[32,3072]{1,0:T(8,128)(2,1)} %param.9), channel_id=1, source_target_pairs={{0,8},{1,9},{2,10},{3,11},{4,12},{5,13},{6,14},{7,15},{8,16},{9,17... | collective-permute-start | bytes 589832 | tf_op jit(solution)/shard_map/ppermute | solution.py:325
  6.3 13.6 %collective-permute-start.2 = (bf16[32,3072]{1,0:T(8,128)(2,1)}, bf16[32,3072]{1,0:T(8,128)(2,1)S(1)}, u32[]{:S(2)}, u32[]{:S(2)}) collective-permute-start(bf16[32,3072]{1,0:T(8,128)(2,1)} %param.9), channel_id=1, source_target_pairs={{0,24},{1,25},{2,26},{3,27},{4,28},{5,29},{6,30},{7,31},{8,0},{9,1... | collective-permute-start | bytes 589832 | tf_op jit(solution)/shard_map/ppermute | solution.py:325
  10.6 40.4 %copy-start.4 = (bf16[32,5120]{1,0:T(8,128)(2,1)S(1)}, bf16[32,5120]{1,0:T(8,128)(2,1)}, u32[]{:S(2)}) copy-start(bf16[32,5120]{1,0:T(8,128)(2,1)} %get-tuple-element.56) | copy-start | bytes 983044
  10.6 10.2 %collective-permute-start.4 = (bf16[32,5120]{1,0:T(8,128)(2,1)}, bf16[32,5120]{1,0:T(8,128)(2,1)S(1)}, u32[]{:S(2)}, u32[]{:S(2)}) collective-permute-start(bf16[32,5120]{1,0:T(8,128)(2,1)} %get-tuple-element.56), channel_id=1, source_target_pairs={{0,4},{1,3},{2,6},{3,1},{4,0},{5,7},{6,2},{7,5},{8,12},{9,11},{10,... | collective-permute-start | bytes 983048 | tf_op jit(solution)/shard_map/ppermute | solution.py:325
  12.2 8.7 %collective-permute-start.3 = (bf16[32,5120]{1,0:T(8,128)(2,1)}, bf16[32,5120]{1,0:T(8,128)(2,1)S(1)}, u32[]{:S(2)}, u32[]{:S(2)}) collective-permute-start(bf16[32,5120]{1,0:T(8,128)(2,1)} %get-tuple-element.56), channel_id=1, source_target_pairs={{0,2},{1,5},{2,0},{3,7},{4,6},{5,1},{6,4},{7,3},{8,10},{9,13},{10,... | collective-permute-start | bytes 983048 | tf_op jit(solution)/shard_map/ppermute | solution.py:325
  20.9 30.2 %copy-start.3 = (bf16[32,5120]{1,0:T(8,128)(2,1)}, bf16[32,5120]{1,0:T(8,128)(2,1)S(1)}, u32[]{:S(2)}) copy-start(bf16[32,5120]{1,0:T(8,128)(2,1)S(1)} %collective-permute-done.4) | copy-start | bytes 983044
  20.9 10.6 %collective-permute-start.7 = (bf16[32,5120]{1,0:T(8,128)(2,1)S(1)}, bf16[32,5120]{1,0:T(8,128)(2,1)S(1)}, u32[]{:S(2)}, u32[]{:S(2)}) collective-permute-start(bf16[32,5120]{1,0:T(8,128)(2,1)S(1)} %collective-permute-done.3), channel_id=1, source_target_pairs={{0,4},{1,3},{2,6},{3,1},{4,0},{5,7},{6,2},{7,5},{8,12},{9,11},{10,... | collective-permute-start | bytes 983048 | tf_op jit(solution)/shard_map/ppermute | solution.py:325
  22.5 28.6 %collective-permute-start.6 = (bf16[128,3072]{1,0:T(8,128)(2,1)S(1)}, bf16[128,3072]{1,0:T(8,128)(2,1)}, u32[]{:S(2)}, u32[]{:S(2)}) collective-permute-start(bf16[128,3072]{1,0:T(8,128)(2,1)S(1)} %pad_maximum_fusion.3.refs_0_), channel_id=1, source_target_pairs={{0,4},{1,3},{2,6},{3,1},{4,0},{5,7},{6,2},{7,5},{8,12},{9,11},{10,... | collective-permute-start | bytes 2359304 | tf_op jit(solution)/shard_map/ppermute | solution.py:325
  23.0 28.1 %collective-permute-start.5 = (bf16[128,3072]{1,0:T(8,128)(2,1)S(1)}, bf16[128,3072]{1,0:T(8,128)(2,1)}, u32[]{:S(2)}, u32[]{:S(2)}) collective-permute-start(bf16[128,3072]{1,0:T(8,128)(2,1)S(1)} %pad_maximum_fusion.3.refs_0_), channel_id=1, source_target_pairs={{0,2},{1,5},{2,0},{3,7},{4,6},{5,1},{6,4},{7,3},{8,10},{9,13},{10,... | collective-permute-start | bytes 2359304 | tf_op jit(solution)/shard_map/ppermute | solution.py:325
  24.5 26.5 %collective-permute-start.9 = (bf16[32,5120]{1,0:T(8,128)(2,1)}, bf16[32,5120]{1,0:T(8,128)(2,1)S(1)}, u32[]{:S(2)}, u32[]{:S(2)}) collective-permute-start(bf16[32,5120]{1,0:T(8,128)(2,1)} %get-tuple-element.56), channel_id=1, source_target_pairs={{0,16},{1,17},{2,18},{3,19},{4,20},{5,21},{6,22},{7,23},{8,24},{9,... | collective-permute-start | bytes 983048 | tf_op jit(solution)/shard_map/ppermute | solution.py:325
  29.7 21.3 %collective-permute-start.8 = (bf16[32,5120]{1,0:T(8,128)(2,1)}, bf16[32,5120]{1,0:T(8,128)(2,1)S(1)}, u32[]{:S(2)}, u32[]{:S(2)}) collective-permute-start(bf16[32,5120]{1,0:T(8,128)(2,1)} %get-tuple-element.56), channel_id=1, source_target_pairs={{0,8},{1,9},{2,10},{3,11},{4,12},{5,13},{6,14},{7,15},{8,16},{9,17... | collective-permute-start | bytes 983048 | tf_op jit(solution)/shard_map/ppermute | solution.py:325
  51.1 0.7 copy-start.5
  51.1 0.8 copy-start.6
  51.1 11.1 %collective-permute-start.11 = (bf16[32,5120]{1,0:T(8,128)(2,1)S(1)}, bf16[32,5120]{1,0:T(8,128)(2,1)}, u32[]{:S(2)}, u32[]{:S(2)}) collective-permute-start(bf16[32,5120]{1,0:T(8,128)(2,1)S(1)} %copy-done.4), channel_id=1, source_target_pairs={{0,24},{1,25},{2,26},{3,27},{4,28},{5,29},{6,30},{7,31},{8,0},{9,1... | collective-permute-start | bytes 983048 | tf_op jit(solution)/shard_map/ppermute | solution.py:325
  51.8 15.6 %collective-permute-start.12 = (bf16[128,3072]{1,0:T(8,128)(2,1)S(1)}, bf16[128,3072]{1,0:T(8,128)(2,1)}, u32[]{:S(2)}, u32[]{:S(2)}) collective-permute-start(bf16[128,3072]{1,0:T(8,128)(2,1)S(1)} %pad_maximum_fusion.3.refs_0_), channel_id=1, source_target_pairs={{0,1},{1,0},{2,3},{3,2},{4,5},{5,4},{6,7},{7,6},{8,9},{9,8},{10,11... | collective-permute-start | bytes 2359304 | tf_op jit(solution)/shard_map/ppermute | solution.py:325
  51.9 15.5 %collective-permute-start.14 = (bf16[128,3072]{1,0:T(8,128)(2,1)}, bf16[128,3072]{1,0:T(8,128)(2,1)}, u32[]{:S(2)}, u32[]{:S(2)}) collective-permute-start(bf16[128,3072]{1,0:T(8,128)(2,1)} %collective-permute-done.6.refs_2_), channel_id=1, source_target_pairs={{0,1},{1,0},{2,3},{3,2},{4,5},{5,4},{6,7},{7,6},{8,9},{9,8},{10,11... | collective-permute-start | bytes 2359304 | tf_op jit(solution)/shard_map/ppermute | solution.py:325
  52.3 15.1 %collective-permute-start.13 = (bf16[128,3072]{1,0:T(8,128)(2,1)}, bf16[128,3072]{1,0:T(8,128)(2,1)}, u32[]{:S(2)}, u32[]{:S(2)}) collective-permute-start(bf16[128,3072]{1,0:T(8,128)(2,1)} %collective-permute-done.5.refs_1_), channel_id=1, source_target_pairs={{0,1},{1,0},{2,3},{3,2},{4,5},{5,4},{6,7},{7,6},{8,9},{9,8},{10,11... | collective-permute-start | bytes 2359304 | tf_op jit(solution)/shard_map/ppermute | solution.py:325
  52.4 15.0 %collective-permute-start.10 = (bf16[128,3072]{1,0:T(8,128)(2,1)}, bf16[128,3072]{1,0:T(8,128)(2,1)}, u32[]{:S(2)}, u32[]{:S(2)}) collective-permute-start(bf16[128,3072]{1,0:T(8,128)(2,1)} %collective-permute-done.5.refs_1_), channel_id=1, source_target_pairs={{0,4},{1,3},{2,6},{3,1},{4,0},{5,7},{6,2},{7,5},{8,12},{9,11},{10,... | collective-permute-start | bytes 2359304 | tf_op jit(solution)/shard_map/ppermute | solution.py:325
  52.9 14.5 %all-to-all-start = ((bf16[32,8,512]{2,1,0:T(8,128)(2,1)}), bf16[32,8,512]{2,1,0:T(8,128)(2,1)S(1)}, u32[]{:S(2)}, u32[]{:S(2)}) async-start(bf16[32,8,512]{2,1,0:T(8,128)(2,1)} %bitcast.1), calls=%async_computation | async-start | bytes 524288 | tf_op jit(solution)/shard_map/all_to_all | solution.py:312
  56.5 29.2 %copy-start.2 = (s32[32,128]{1,0:T(8,128)S(1)}, s32[32,128]{1,0:T(8,128)}, u32[]{:S(2)}) copy-start(s32[32,128]{1,0:T(8,128)} %keep.1) | copy-start | bytes 49156
  67.4 9.2 %collective-permute-start.18 = (bf16[32,5120]{1,0:T(8,128)(2,1)}, bf16[32,5120]{1,0:T(8,128)(2,1)S(1)}, u32[]{:S(2)}, u32[]{:S(2)}) collective-permute-start(bf16[32,5120]{1,0:T(8,128)(2,1)} %copy-done.5), channel_id=1, source_target_pairs={{0,4},{1,3},{2,6},{3,1},{4,0},{5,7},{6,2},{7,5},{8,12},{9,11},{10,... | collective-permute-start | bytes 983048 | tf_op jit(solution)/shard_map/ppermute | solution.py:325
  68.2 17.4 %collective-permute-start.19 = (bf16[32,5120]{1,0:T(8,128)(2,1)}, bf16[32,5120]{1,0:T(8,128)(2,1)S(1)}, u32[]{:S(2)}, u32[]{:S(2)}) collective-permute-start(bf16[32,5120]{1,0:T(8,128)(2,1)} %copy-done.3), channel_id=1, source_target_pairs={{0,24},{1,25},{2,26},{3,27},{4,28},{5,29},{6,30},{7,31},{8,0},{9,1... | collective-permute-start | bytes 983048 | tf_op jit(solution)/shard_map/ppermute | solution.py:325
  70.2 15.4 %collective-permute-start.17 = (bf16[32,5120]{1,0:T(8,128)(2,1)}, bf16[32,5120]{1,0:T(8,128)(2,1)S(1)}, u32[]{:S(2)}, u32[]{:S(2)}) collective-permute-start(bf16[32,5120]{1,0:T(8,128)(2,1)} %copy-done.3), channel_id=1, source_target_pairs={{0,8},{1,9},{2,10},{3,11},{4,12},{5,13},{6,14},{7,15},{8,16},{9,17... | collective-permute-start | bytes 983048 | tf_op jit(solution)/shard_map/ppermute | solution.py:325
  70.3 20.7 %collective-permute-start.15 = (bf16[96,5120]{1,0:T(8,128)(2,1)S(1)}, bf16[96,5120]{1,0:T(8,128)(2,1)S(1)}, u32[]{:S(2)}, u32[]{:S(2)}) collective-permute-start(bf16[96,5120]{1,0:T(8,128)(2,1)S(1)} %pad_maximum_fusion.1.refs_1_), channel_id=1, source_target_pairs={{0,2},{1,5},{2,0},{3,7},{4,6},{5,1},{6,4},{7,3},{8,10},{9,13},{10,... | collective-permute-start | bytes 2949128 | tf_op jit(solution)/shard_map/ppermute | solution.py:325
  71.9 13.8 %collective-permute-start.16 = (bf16[128,3072]{1,0:T(8,128)(2,1)}, bf16[128,3072]{1,0:T(8,128)(2,1)S(1)}, u32[]{:S(2)}, u32[]{:S(2)}) collective-permute-start(bf16[128,3072]{1,0:T(8,128)(2,1)} %collective-permute-done.10.refs_3_), channel_id=1, source_target_pairs={{0,1},{1,0},{2,3},{3,2},{4,5},{5,4},{6,7},{7,6},{8,9},{9,8},{10,11... | collective-permute-start | bytes 2359304 | tf_op jit(solution)/shard_map/ppermute | solution.py:325
  85.7 26.0 %copy-start = (bf16[4,32,1024]{2,1,0:T(8,128)(2,1)S(1)}, bf16[4,32,1024]{2,1,0:T(8,128)(2,1)}, u32[]{:S(2)}) copy-start(bf16[4,32,1024]{2,1,0:T(8,128)(2,1)} %param.7) | copy-start | bytes 786436
  85.7 26.0 %copy-start.1 = (bf16[4,32,1024]{2,1,0:T(8,128)(2,1)S(1)}, bf16[4,32,1024]{2,1,0:T(8,128)(2,1)}, u32[]{:S(2)}) copy-start(bf16[4,32,1024]{2,1,0:T(8,128)(2,1)} %param.8) | copy-start | bytes 786436
  91.0 18.0 %collective-permute-start.21 = (bf16[128,5120]{1,0:T(8,128)(2,1)S(1)}, bf16[128,5120]{1,0:T(8,128)(2,1)S(1)}, u32[]{:S(2)}, u32[]{:S(2)}) collective-permute-start(bf16[128,5120]{1,0:T(8,128)(2,1)S(1)} %pad_maximum_fusion.refs_0_), channel_id=1, source_target_pairs={{0,1},{1,0},{2,3},{3,2},{4,5},{5,4},{6,7},{7,6},{8,9},{9,8},{10,11... | collective-permute-start | bytes 3932168 | tf_op jit(solution)/shard_map/ppermute | solution.py:325
  91.1 17.9 %collective-permute-start.22 = (bf16[96,5120]{1,0:T(8,128)(2,1)S(1)}, bf16[96,5120]{1,0:T(8,128)(2,1)S(1)}, u32[]{:S(2)}, u32[]{:S(2)}) collective-permute-start(bf16[96,5120]{1,0:T(8,128)(2,1)S(1)} %pad_maximum_fusion.1.refs_1_), channel_id=1, source_target_pairs={{0,1},{1,0},{2,3},{3,2},{4,5},{5,4},{6,7},{7,6},{8,9},{9,8},{10,11... | collective-permute-start | bytes 2949128 | tf_op jit(solution)/shard_map/ppermute | solution.py:325
  91.6 17.4 %collective-permute-start.24 = (bf16[96,5120]{1,0:T(8,128)(2,1)S(1)}, bf16[96,5120]{1,0:T(8,128)(2,1)S(1)}, u32[]{:S(2)}, u32[]{:S(2)}) collective-permute-start(bf16[96,5120]{1,0:T(8,128)(2,1)S(1)} %pad_maximum_fusion.2.refs_3_), channel_id=1, source_target_pairs={{0,1},{1,0},{2,3},{3,2},{4,5},{5,4},{6,7},{7,6},{8,9},{9,8},{10,11... | collective-permute-start | bytes 2949128 | tf_op jit(solution)/shard_map/ppermute | solution.py:325
  91.7 17.3 %collective-permute-start.23 = (bf16[96,5120]{1,0:T(8,128)(2,1)S(1)}, bf16[96,5120]{1,0:T(8,128)(2,1)S(1)}, u32[]{:S(2)}, u32[]{:S(2)}) collective-permute-start(bf16[96,5120]{1,0:T(8,128)(2,1)S(1)} %collective-permute-done.15.refs_2_), channel_id=1, source_target_pairs={{0,1},{1,0},{2,3},{3,2},{4,5},{5,4},{6,7},{7,6},{8,9},{9,8},{10,11... | collective-permute-start | bytes 2949128 | tf_op jit(solution)/shard_map/ppermute | solution.py:325
  92.1 16.9 %collective-permute-start.20 = (bf16[96,5120]{1,0:T(8,128)(2,1)S(1)}, bf16[96,5120]{1,0:T(8,128)(2,1)S(1)}, u32[]{:S(2)}, u32[]{:S(2)}) collective-permute-start(bf16[96,5120]{1,0:T(8,128)(2,1)S(1)} %collective-permute-done.15.refs_2_), channel_id=1, source_target_pairs={{0,4},{1,3},{2,6},{3,1},{4,0},{5,7},{6,2},{7,5},{8,12},{9,11},{10,... | collective-permute-start | bytes 2949128 | tf_op jit(solution)/shard_map/ppermute | solution.py:325
  109.0 2.6 %collective-permute-start.25 = (bf16[96,5120]{1,0:T(8,128)(2,1)S(1)}, bf16[96,5120]{1,0:T(8,128)(2,1)S(1)}, u32[]{:S(2)}, u32[]{:S(2)}) collective-permute-start(bf16[96,5120]{1,0:T(8,128)(2,1)S(1)} %collective-permute-done.20.refs_4_), channel_id=1, source_target_pairs={{0,1},{1,0},{2,3},{3,2},{4,5},{5,4},{6,7},{7,6},{8,9},{9,8},{10,11... | collective-permute-start | bytes 2949128 | tf_op jit(solution)/shard_map/ppermute | solution.py:325
